TPU v7x, 32 devices: a whole 2x2x4 slice. The times are simulated.
32 devices in a mesh: row: 4 (over y, core), col: 8 (over z, x).
Axes of the slice: x: 2, y: 2, z: 4, core: 2. Of those that a mesh axis runs over, the one named last changes fastest.
Arguments:
- tokens: bfloat16 [4096, 768], P(('row', 'col')), may hold values from -6 to 6
- expert_ids: int32 [4096, 2], P(('row', 'col')), may hold values from 0 to 31, all different within a row; in each aligned block of 128 rows (0 to 127, 128 to 255, ...) at most 16 rows name the same one
- keep_mask: int32 [4096, 2], P(('row', 'col')), may hold values 0 or 1
- gate_weights: float32 [4096, 2], P(('row', 'col')), may hold values from 0.2 to 1
- weight_in: bfloat16 [32, 768, 4096], P(('row', 'col')), may hold values from -0.21875 to 0.21875
- weight_out: bfloat16 [32, 4096, 768], P(('row', 'col')), may hold values from -0.09375 to 0.09375
- grad_output: bfloat16 [4096, 768], P(('row', 'col')), may hold values from -6 to 6
Outputs:
- combined: bfloat16 [4096, 768], P(('row', 'col'))
- grad_tokens: bfloat16 [4096, 768], P(('row', 'col'))
- grad_gates: float32 [4096, 2], P(('row', 'col'))
- grad_weight_in: bfloat16 [32, 768, 4096], P(('row', 'col'))
- grad_weight_out: bfloat16 [32, 4096, 768], P(('row', 'col'))
Inputs may be any that keep to these rules, and one draw needn't show every extreme that they name: `expert_ids`: the two experts of a token differ. Among the choices of one device's tokens, at most 16 name one expert, and in every draw some expert is named by exactly 16 choices of some device.
All inputs are finite; a program needn't handle non-finite values. Where the computation divides by a largest or mean magnitude, that divisor is 1e-20 or more. No bound on the sum of `keep_mask` on one device may be relied on, other than what follows from the above.
Results may differ from a plain program's by a relative error of at most 0.0067.
Values may be sent and summed in bfloat16 or wider, within the bound.
No kernel may reach another device: no remote copies, remote signals or barrier semaphores. Data moves between devices by JAX's collectives and lax.ppermute only.
A program may use at most 128 MiB of HBM per device.

v0:
```python
import jax
import jax.numpy as jnp
from jax import lax
from jax.sharding import PartitionSpec as P

BLOCK = 128


def arrival_slots(expert_rows):
    flattened = expert_rows.reshape(-1)
    count_all = flattened.shape[0]
    matching = flattened[:, None] == flattened[None, :]
    positions = jnp.arange(count_all, dtype=jnp.int32)
    earlier = positions[:, None] > positions[None, :]
    return jnp.sum((matching & earlier).astype(jnp.int32), axis=1).reshape(expert_rows.shape)


def expert_work(quantized, scales, cotangent, weight_in, weight_out):
    block_count = scales.shape[-1]
    restored = (
        (
            quantized.astype(jnp.float32).reshape(-1, block_count, BLOCK)
            * scales.astype(jnp.float32)[:, :, None]
        )
        .reshape(quantized.shape)
        .astype(jnp.bfloat16)
    )
    preact = jnp.dot(restored, weight_in, preferred_element_type=jnp.float32)
    hidden_full, hidden_vjp = jax.vjp(jax.nn.gelu, preact)
    hidden = hidden_full.astype(jnp.bfloat16)
    outputs = jnp.dot(hidden, weight_out, preferred_element_type=jnp.float32).astype(jnp.bfloat16)
    grad_out_w = jnp.dot(hidden.T, cotangent, preferred_element_type=jnp.float32).astype(
        jnp.bfloat16
    )
    grad_hidden = jnp.dot(cotangent, weight_out.T, preferred_element_type=jnp.float32)
    grad_preact = hidden_vjp(grad_hidden)[0].astype(jnp.bfloat16)
    grad_in_w = jnp.dot(restored.T, grad_preact, preferred_element_type=jnp.float32).astype(
        jnp.bfloat16
    )
    grad_rows = jnp.dot(grad_preact, weight_in.T, preferred_element_type=jnp.float32).astype(
        jnp.bfloat16
    )
    return (outputs, grad_rows, grad_in_w, grad_out_w)


def place_rows(values, slot_rows, slot_total):
    empty = jnp.zeros((slot_total,) + values.shape[1:], values.dtype)
    return empty.at[slot_rows].set(values, mode="drop")


def body(tokens, expert_ids, keep_mask, gate_weights, weight_in, weight_out, grad_output):
    token_rows, width = tokens.shape
    top_count = expert_ids.shape[1]
    row_count = lax.axis_size("row")
    col_count = lax.axis_size("col")
    experts = row_count * col_count
    capacity = 2 * top_count * token_rows // experts
    slot_total = experts * capacity
    block_count = width // BLOCK
    slot_ids = arrival_slots(expert_ids)
    blocks = tokens.astype(jnp.float32).reshape(token_rows, block_count, BLOCK)
    scales = (jnp.max(jnp.abs(blocks), axis=2) + 1e-06).astype(jnp.bfloat16)
    quantized = (
        (blocks / scales.astype(jnp.float32)[:, :, None])
        .astype(jnp.bfloat16)
        .reshape(token_rows, width)
    )
    cotangent = (
        (gate_weights[:, :, None] * grad_output.astype(jnp.float32)[:, None, :])
        .astype(jnp.bfloat16)
        .reshape(token_rows * top_count, width)
    )
    kept = keep_mask > 0
    slot_index = expert_ids * capacity + slot_ids
    slot_rows = jnp.where(kept, slot_index, slot_total).reshape(-1)
    send_quant = place_rows(jnp.repeat(quantized, top_count, axis=0), slot_rows, slot_total)
    send_scales = place_rows(jnp.repeat(scales, top_count, axis=0), slot_rows, slot_total)
    send_cot = place_rows(cotangent, slot_rows, slot_total)
    flat_shape = (experts, capacity)
    got_quant, got_scales, got_cot = (
        lax.all_to_all(
            send_quant.reshape(flat_shape + (width,)),
            ("row", "col"),
            split_axis=0,
            concat_axis=0,
            tiled=True,
        ),
        lax.all_to_all(
            send_scales.reshape(flat_shape + (block_count,)),
            ("row", "col"),
            split_axis=0,
            concat_axis=0,
            tiled=True,
        ),
        lax.all_to_all(
            send_cot.reshape(flat_shape + (width,)),
            ("row", "col"),
            split_axis=0,
            concat_axis=0,
            tiled=True,
        ),
    )
    outputs, grad_rows, grad_in_w, grad_out_w = expert_work(
        got_quant.reshape(slot_total, width),
        got_scales.reshape(slot_total, block_count),
        got_cot.reshape(slot_total, width),
        weight_in[0],
        weight_out[0],
    )
    flat_shape = (experts, capacity, width)
    back_out, back_grad = (
        lax.all_to_all(
            outputs.reshape(flat_shape), ("row", "col"), split_axis=0, concat_axis=0, tiled=True
        ),
        lax.all_to_all(
            grad_rows.reshape(flat_shape), ("row", "col"), split_axis=0, concat_axis=0, tiled=True
        ),
    )
    pick_rows = jnp.where(kept, slot_index, 0)
    picked_out = back_out.reshape(slot_total, width)[pick_rows].astype(jnp.float32)
    weight_kept = jnp.where(kept, gate_weights, 0.0)
    combined = jnp.sum(weight_kept[:, :, None] * picked_out, axis=1).astype(jnp.bfloat16)
    grad_gates = jnp.where(
        kept, jnp.sum(grad_output.astype(jnp.float32)[:, None, :] * picked_out, axis=2), 0.0
    )
    picked_grad = back_grad.reshape(slot_total, width)[pick_rows].astype(jnp.float32)
    grad_tokens = jnp.sum(jnp.where(kept[:, :, None], picked_grad, 0.0), axis=1).astype(
        jnp.bfloat16
    )
    return (combined, grad_tokens, grad_gates, grad_in_w[None], grad_out_w[None])


def solution(mesh):
    placed = (
        P(("row", "col"), None),
        P(("row", "col"), None),
        P(("row", "col"), None),
        P(("row", "col"), None),
        P(("row", "col"), None, None),
        P(("row", "col"), None, None),
        P(("row", "col"), None),
    )
    return jax.shard_map(
        body,
        mesh=mesh,
        in_specs=placed,
        out_specs=(
            P(("row", "col"), None),
            P(("row", "col"), None),
            P(("row", "col"), None),
            P(("row", "col"), None, None),
            P(("row", "col"), None, None),
        ),
        check_vma=False,
    )
```

profile of v0, /device:TPU:0, one launch (start us, length us, event | category | flops | bytes accessed | tf_op | source)
XLA Modules:
  0.0 126.5 jit_solution(7054237778260468327)
XLA Ops:
  0.6 0.8 copy.121
  1.4 0.1 eq.15
  1.6 0.2 convert_reduce_fusion
  1.7 0.1 reshape.125
  1.9 0.1 copy.122
  2.0 0.7 broadcast_select_fusion.2
  2.7 0.7 compare_select_fusion.1
  3.4 0.1 copy.123
  3.5 0.1 reshape.126
  3.6 1.1 copy.124
  4.8 0.1 copy.126
  5.0 1.2 scatter_custom_fusion.1
  6.2 0.9 copy.128
  7.1 7.3 %all-to-all-start.1 = ((bf16[32,16,6]{1,2,0:T(8,128)(2,1)}), bf16[32,16,6]{1,2,0:T(8,128)(2,1)S(1)}, u32[]{:S(2)}, u32[]{:S(2)}) async-start(bf16[32,16,6]{1,2,0:T(8,128)(2,1)} %copy.128), calls=%async_computation.1 | async-start | bytes 131072 | tf_op jit(solution)/shard_map/all_to_all | solution.py:88
  14.5 0.1 copy.125
  14.6 0.2 broadcast_in_dim.55
  14.8 0.1 reshape.160
  15.0 2.6 %scatter_custom_fusion = bf16[512,768]{1,0:T(8,128)(2,1)} fusion(s32[256]{0:T(256)S(1)} %bitcast.61, bf16[256,768]{1,0:T(8,128)(2,1)S(1)} %reshape.160, bf16[]{:T(256)} %constant.15.clone.1), kind=kCustom, calls=%fused_computation.42 | custom fusion | bytes 786434 | tf_op jit(solution)/shard_map/scatter | solution.py:48
  17.6 4.1 %all-to-all-done.1 = bf16[32,16,6]{1,2,0:T(8,128)(2,1)S(1)} async-done(((bf16[32,16,6]{1,2,0:T(8,128)(2,1)}), bf16[32,16,6]{1,2,0:T(8,128)(2,1)S(1)}, u32[]{:S(2)}, u32[]{:S(2)}) %all-to-all-start.1) | async-done | bytes 6176 | tf_op jit(solution)/shard_map/all_to_all | solution.py:88
  21.7 2.6 %all-to-all-start = ((bf16[32,16,768]{2,1,0:T(8,128)(2,1)}), bf16[32,16,768]{2,1,0:T(8,128)(2,1)S(1)}, u32[]{:S(2)}, u32[]{:S(2)}) async-start(bf16[32,16,768]{2,1,0:T(8,128)(2,1)} %bitcast.3), calls=%async_computation | async-start | bytes 1572864 | tf_op jit(solution)/shard_map/all_to_all | solution.py:81
  24.3 0.7 copy.134
  25.1 0.8 copy.135
  25.8 0.7 copy.120
  26.6 0.1 copy.133
  26.7 0.1 reshape.142
  26.8 0.1 mul.112
  27.0 1.0 convert_element_type.121
  27.9 1.1 mul.114
  29.1 0.5 mul.115
  29.6 2.6 %scatter_custom_fusion.2 = bf16[512,768]{1,0:T(8,128)(2,1)} fusion(s32[256]{0:T(256)S(1)} %bitcast.62, f32[256,768]{1,0:T(8,128)S(1)} %mul.115, f32[256]{0:T(256)S(1)} %mul.112, bf16[]{:T(256)} %constant.15.clone.1), kind=kCustom, calls=%fused_computation.39 | custom fusion | flops 393216 | bytes 1573890 | tf_op jit(solution)/shard_map/scatter | solution.py:48
  32.3 0.1 copy.129
  32.4 0.2 copy.141
  32.6 0.1 copy.143
  32.7 0.2 mul.105.clone
  32.9 1.6 %copy.138 = f32[512,768]{1,0:T(8,128)} copy(f32[512,768]{0,1:T(8,128)S(1)} %bitcast.51) | data formatting | bytes 3145728 | tf_op jit(solution)/shard_map/mul | solution.py:22
  34.5 11.8 %all-to-all-done = bf16[32,16,768]{2,1,0:T(8,128)(2,1)S(1)} async-done(((bf16[32,16,768]{2,1,0:T(8,128)(2,1)}), bf16[32,16,768]{2,1,0:T(8,128)(2,1)S(1)}, u32[]{:S(2)}, u32[]{:S(2)}) %all-to-all-start) | async-done | bytes 786464 | tf_op jit(solution)/shard_map/all_to_all | solution.py:81
  46.3 3.5 %all-to-all-start.3 = ((bf16[32,16,768]{2,1,0:T(8,128)(2,1)}), bf16[32,16,768]{2,1,0:T(8,128)(2,1)}, u32[]{:S(2)}, u32[]{:S(2)}) async-start(bf16[32,16,768]{2,1,0:T(8,128)(2,1)} %bitcast.12), calls=%async_computation.3 | async-start | bytes 1572864 | tf_op jit(solution)/shard_map/all_to_all | solution.py:95
  49.8 0.8 reshape.137
  50.7 1.5 %multiply_convert_fusion.1 = bf16[512,6,128]{2,1,0:T(8,128)(2,1)} fusion(f32[512,6,128]{2,1,0:T(8,128)S(1)} %reshape.137, f32[512,6]{1,0:T(8,128)S(1)} %bitcast.56), kind=kLoop, calls=%fused_computation.27 | loop fusion | flops 786432 | bytes 2371584 | tf_op jit(solution)/shard_map/convert_element_type | solution.py:26
  52.1 1.6 %copy.132 = bf16[512,6,128]{0,2,1:T(8,128)(2,1)S(1)} copy(bf16[512,6,128]{2,1,0:T(8,128)(2,1)} %multiply_convert_fusion.1) | data formatting | bytes 1572864 | tf_op jit(solution)/shard_map/convert_element_type | solution.py:26
  53.7 0.0 slice-start.2
  53.7 5.8 %fusion.13 = f32[512,4096]{1,0:T(8,128)S(1)} fusion(bf16[512,768]{0,1:T(8,128)(2,1)S(1)} %bitcast.54, bf16[1,768,4096]{2,1,0:T(8,128)(2,1)} %param.11), kind=kOutput, calls=%fused_computation.23 | convolution fusion | flops 3221225472 | bytes 15466496 | tf_op jit(solution)/shard_map/dot_general | solution.py:28
  59.6 3.2 %copy-done = f32[512,4096]{1,0:T(8,128)} copy-done((f32[512,4096]{1,0:T(8,128)}, f32[512,4096]{1,0:T(8,128)S(1)}, u32[]{:S(2)}) %copy-start) | copy-done | bytes 8388632
  62.8 5.9 %fusion.23 = bf16[512,768]{1,0:T(8,128)(2,1)} fusion(bf16[1,4096,768]{2,1,0:T(8,128)(2,1)S(1)} %bitcast.64, f32[512,4096]{1,0:T(8,128)S(1)} %fusion.13), kind=kOutput, calls=%fused_computation.31 | convolution fusion | flops 3240493056 | bytes 15466496 | tf_op jit(solution)/shard_map/dot_general | solution.py:31
  68.7 2.9 %all-to-all-done.3 = bf16[32,16,768]{2,1,0:T(8,128)(2,1)} async-done(((bf16[32,16,768]{2,1,0:T(8,128)(2,1)}), bf16[32,16,768]{2,1,0:T(8,128)(2,1)}, u32[]{:S(2)}, u32[]{:S(2)}) %all-to-all-start.3) | async-done | bytes 786464 | tf_op jit(solution)/shard_map/all_to_all | solution.py:95
  71.6 2.9 %all-to-all-start.2 = ((bf16[32,16,768]{2,1,0:T(8,128)(2,1)}), bf16[32,16,768]{2,1,0:T(8,128)(2,1)S(1)}, u32[]{:S(2)}, u32[]{:S(2)}) async-start(bf16[32,16,768]{2,1,0:T(8,128)(2,1)} %bitcast.10), calls=%async_computation.2 | async-start | bytes 1572864 | tf_op jit(solution)/shard_map/all_to_all | solution.py:112
  74.5 11.0 %fusion.6 = bf16[512,4096]{1,0:T(8,128)(2,1)S(1)} fusion(f32[512,4096]{1,0:T(8,128)} %copy-done, bf16[512,768]{1,0:T(8,128)(2,1)} %bitcast.13, bf16[1,4096,768]{2,1,0:T(8,128)(2,1)} %param.12), kind=kOutput, calls=%fused_computation.13 | convolution fusion | flops 3263168512 | bytes 19660800 | tf_op jit(solution)/shard_map/dot_general | solution.py:35
  85.5 0.0 slice-start
  85.5 0.2 fusion.19
  85.8 5.4 %fusion.15 = bf16[1,768,4096]{2,1,0:T(8,128)(2,1)} fusion(bf16[512,768]{1,0:T(8,128)(2,1)S(1)} %fusion.19, bf16[512,4096]{1,0:T(8,128)(2,1)S(1)} %fusion.6), kind=kOutput, calls=%fused_computation.25 | convolution fusion | flops 3224371200 | bytes 11272192 | tf_op jit(solution)/shard_map/dot_general | solution.py:37
  91.2 4.4 %fusion.20 = bf16[512,768]{1,0:T(8,128)(2,1)} fusion(bf16[512,4096]{1,0:T(8,128)(2,1)S(1)} %fusion.6, bf16[1,768,4096]{2,1,0:T(8,128)(2,1)S(1)} %bitcast.53), kind=kOutput, calls=%fused_computation.30 | convolution fusion | flops 3221618688 | bytes 11272192 | tf_op jit(solution)/shard_map/dot_general | solution.py:40
  95.5 0.7 all-to-all-done.2
  96.3 5.1 %all-to-all-start.4 = ((bf16[32,16,768]{2,1,0:T(8,128)(2,1)}), bf16[32,16,768]{2,1,0:T(8,128)(2,1)S(1)}, u32[]{:S(2)}, u32[]{:S(2)}) async-start(bf16[32,16,768]{2,1,0:T(8,128)(2,1)} %bitcast.14), calls=%async_computation.4 | async-start | bytes 1572864 | tf_op jit(solution)/shard_map/all_to_all | solution.py:115
  101.4 0.0 copy-start.2
  101.4 10.6 %fusion.16 = bf16[1,4096,768]{2,1,0:T(8,128)(2,1)} fusion(bf16[512,768]{1,0:T(8,128)(2,1)} %bitcast.13, f32[512,4096]{1,0:T(8,128)} %copy-done), kind=kOutput, calls=%fused_computation.26 | convolution fusion | flops 3243245568 | bytes 15466496 | tf_op jit(solution)/shard_map/dot_general | solution.py:32
  112.0 1.2 gather_fusion
  113.2 0.4 reshape.184
  113.6 2.1 %multiply_reduce_fusion = (f32[128,2]{1,0:T(8,128)S(1)}, bf16[128,768]{1,0:T(8,128)(2,1)}) fusion(f32[128,2,768]{2,1,0:T(2,128)S(1)} %reshape.184, f32[128,768]{1,0:T(8,128)S(1)} %convert_element_type.121, f32[128,2]{1,0:T(8,128)S(1)} %copy-done.2), kind=kLoop, calls=%fused_computation.32 | loop fusion | flops 687872 | bytes 1378304 | tf_op jit(solution)/shard_map/reduce_sum | solution.py:124
  115.7 0.1 copy.136
  115.8 0.6 broadcast_select_fusion.1
  116.3 6.8 %all-to-all-done.4 = bf16[32,16,768]{2,1,0:T(8,128)(2,1)S(1)} async-done(((bf16[32,16,768]{2,1,0:T(8,128)(2,1)}), bf16[32,16,768]{2,1,0:T(8,128)(2,1)S(1)}, u32[]{:S(2)}, u32[]{:S(2)}) %all-to-all-start.4) | async-done | bytes 786464 | tf_op jit(solution)/shard_map/all_to_all | solution.py:115
  123.1 1.2 gather_fusion.1
  124.3 0.4 reshape.185
  124.7 1.8 %select_reduce_fusion = bf16[128,768]{1,0:T(8,128)(2,1)} fusion(f32[128,2,768]{2,1,0:T(2,128)S(1)} %reshape.185, pred[128,2]{1,0:T(8,128)(4,1)S(1)} %copy-done.3), kind=kLoop, calls=%fused_computation.33 | loop fusion | flops 294912 | bytes 983296 | tf_op jit(solution)/shard_map/reduce_sum | solution.py:127
  (21 shorter events, 0.2 us)
Async XLA Ops:
  7.1 14.6 %all-to-all-start.1 = ((bf16[32,16,6]{1,2,0:T(8,128)(2,1)}), bf16[32,16,6]{1,2,0:T(8,128)(2,1)S(1)}, u32[]{:S(2)}, u32[]{:S(2)}) async-start(bf16[32,16,6]{1,2,0:T(8,128)(2,1)} %copy.128), calls=%async_computation.1 | async-start | bytes 131072 | tf_op jit(solution)/shard_map/all_to_all | solution.py:88
  21.7 24.6 %all-to-all-start = ((bf16[32,16,768]{2,1,0:T(8,128)(2,1)}), bf16[32,16,768]{2,1,0:T(8,128)(2,1)S(1)}, u32[]{:S(2)}, u32[]{:S(2)}) async-start(bf16[32,16,768]{2,1,0:T(8,128)(2,1)} %bitcast.3), calls=%async_computation | async-start | bytes 1572864 | tf_op jit(solution)/shard_map/all_to_all | solution.py:81
  46.3 25.3 %all-to-all-start.3 = ((bf16[32,16,768]{2,1,0:T(8,128)(2,1)}), bf16[32,16,768]{2,1,0:T(8,128)(2,1)}, u32[]{:S(2)}, u32[]{:S(2)}) async-start(bf16[32,16,768]{2,1,0:T(8,128)(2,1)} %bitcast.12), calls=%async_computation.3 | async-start | bytes 1572864 | tf_op jit(solution)/shard_map/all_to_all | solution.py:95
  53.7 9.1 %slice-start.2 = ((s8[6291456]{0:T(1024)(128)(4,1)}), s8[4194304]{0:T(1024)(128)(4,1)S(1)}, s32[]{:S(2)}) async-start(s8[6291456]{0:T(1024)(128)(4,1)} %bitcast.63), calls=%async_computation.7 | async-start | bytes 8388608
  53.7 9.1 %slice-start.3 = ((s8[6291456]{0:T(1024)(128)(4,1)}), s8[2097152]{0:T(1024)(128)(4,1)S(1)}, s32[]{:S(2)}) async-start(s8[6291456]{0:T(1024)(128)(4,1)} %bitcast.63), calls=%async_computation.8 | async-start | bytes 4194304
  59.5 3.2 %copy-start = (f32[512,4096]{1,0:T(8,128)}, f32[512,4096]{1,0:T(8,128)S(1)}, u32[]{:S(2)}) copy-start(f32[512,4096]{1,0:T(8,128)S(1)} %fusion.13) | copy-start | bytes 25165828
  71.6 24.6 %all-to-all-start.2 = ((bf16[32,16,768]{2,1,0:T(8,128)(2,1)}), bf16[32,16,768]{2,1,0:T(8,128)(2,1)S(1)}, u32[]{:S(2)}, u32[]{:S(2)}) async-start(bf16[32,16,768]{2,1,0:T(8,128)(2,1)} %bitcast.10), calls=%async_computation.2 | async-start | bytes 1572864 | tf_op jit(solution)/shard_map/all_to_all | solution.py:112
  74.5 11.0 %copy-start.1 = (f32[512,768]{1,0:T(8,128)S(1)}, f32[512,768]{1,0:T(8,128)}, u32[]{:S(2)}) copy-start(f32[512,768]{1,0:T(8,128)} %copy.138) | copy-start | bytes 4718596
  85.5 5.6 %slice-start = ((s8[6291456]{0:T(1024)(128)(4,1)}), s8[4194304]{0:T(1024)(128)(4,1)S(1)}, s32[]{:S(2)}) async-start(s8[6291456]{0:T(1024)(128)(4,1)} %bitcast.52), calls=%async_computation.5 | async-start | bytes 8388608
  85.8 5.4 %slice-start.1 = ((s8[6291456]{0:T(1024)(128)(4,1)}), s8[2097152]{0:T(1024)(128)(4,1)S(1)}, s32[]{:S(2)}) async-start(s8[6291456]{0:T(1024)(128)(4,1)} %bitcast.52), calls=%async_computation.6 | async-start | bytes 4194304
  96.3 26.9 %all-to-all-start.4 = ((bf16[32,16,768]{2,1,0:T(8,128)(2,1)}), bf16[32,16,768]{2,1,0:T(8,128)(2,1)S(1)}, u32[]{:S(2)}, u32[]{:S(2)}) async-start(bf16[32,16,768]{2,1,0:T(8,128)(2,1)} %bitcast.14), calls=%async_computation.4 | async-start | bytes 1572864 | tf_op jit(solution)/shard_map/all_to_all | solution.py:115
  101.4 12.2 %copy-start.2 = (f32[128,2]{1,0:T(8,128)S(1)}, f32[128,2]{1,0:T(8,128)}, u32[]{:S(2)}) copy-start(f32[128,2]{1,0:T(8,128)} %copy.120) | copy-start | bytes 3076
  112.0 12.7 %copy-start.3 = (pred[128,2]{1,0:T(8,128)(4,1)S(1)}, pred[128,2]{1,0:T(8,128)(4,1)}, u32[]{:S(2)}) copy-start(pred[128,2]{1,0:T(8,128)(4,1)} %copy.134) | copy-start | bytes 772
where the time goes:
time: 127 us; the launch traced here: 126 us
  matrix products  43 us (34%)
  waiting for transfers between devices  26.3 us (21%)
  local copies, waits for them, and re-layouts  23.2 us (18%)
  starting transfers between devices  21.5 us (17%)
  other arithmetic  11.5 us (9%)
    all_to_all x1, waiting for transfers between devices, body(): lax.all_to_all(send_quant.reshape(flat_shape + (width,)), ('row', 'col'),...  11.8 us
    dot_general x1, matrix products, expert_work(): jnp.dot(cotangent, weight_out.T, preferred_element_type=jnp.float32)  11 us
    dot_general x1, matrix products, expert_work(): jnp.dot(hidden.T, cotangent, preferred_element_type=jnp.float32)  10.6 us
    all_to_all x1, starting transfers between devices, body(): lax.all_to_all(send_scales.reshape(flat_shape + (block_count,)), ('row',...  7.3 us
    all_to_all x1, waiting for transfers between devices, body(): lax.all_to_all(grad_rows.reshape(flat_shape), ('row', 'col'), split_axis=...  6.78 us
    unnamed x20, local copies, waits for them, and re-layouts  6.03 us
    dot_general x1, matrix products, expert_work(): jnp.dot(hidden, weight_out, preferred_element_type=jnp.float32)  5.9 us
    dot_general x1, matrix products, expert_work(): preact = jnp.dot(restored, weight_in, preferred_element_type=jnp.float32)  5.8 us
  transfers between devices with their start and end apart: 5, of which 5 were waited for; matrix products, arithmetic and copies ran while one was open for 51% of the time, Pallas kernels for 0%

commit v1 on v0

--- a/solution.py
+++ b/solution.py
@@ -15,16 +15,7 @@
     return jnp.sum((matching & earlier).astype(jnp.int32), axis=1).reshape(expert_rows.shape)
 
 
-def expert_work(quantized, scales, cotangent, weight_in, weight_out):
-    block_count = scales.shape[-1]
-    restored = (
-        (
-            quantized.astype(jnp.float32).reshape(-1, block_count, BLOCK)
-            * scales.astype(jnp.float32)[:, :, None]
-        )
-        .reshape(quantized.shape)
-        .astype(jnp.bfloat16)
-    )
+def expert_work(restored, cotangent, weight_in, weight_out):
     preact = jnp.dot(restored, weight_in, preferred_element_type=jnp.float32)
     hidden_full, hidden_vjp = jax.vjp(jax.nn.gelu, preact)
     hidden = hidden_full.astype(jnp.bfloat16)
@@ -60,8 +51,9 @@
     slot_ids = arrival_slots(expert_ids)
     blocks = tokens.astype(jnp.float32).reshape(token_rows, block_count, BLOCK)
     scales = (jnp.max(jnp.abs(blocks), axis=2) + 1e-06).astype(jnp.bfloat16)
-    quantized = (
-        (blocks / scales.astype(jnp.float32)[:, :, None])
+    quantized = (blocks / scales.astype(jnp.float32)[:, :, None]).astype(jnp.bfloat16)
+    restored = (
+        (quantized.astype(jnp.float32) * scales.astype(jnp.float32)[:, :, None])
         .astype(jnp.bfloat16)
         .reshape(token_rows, width)
     )
@@ -73,20 +65,12 @@
     kept = keep_mask > 0
     slot_index = expert_ids * capacity + slot_ids
     slot_rows = jnp.where(kept, slot_index, slot_total).reshape(-1)
-    send_quant = place_rows(jnp.repeat(quantized, top_count, axis=0), slot_rows, slot_total)
-    send_scales = place_rows(jnp.repeat(scales, top_count, axis=0), slot_rows, slot_total)
+    send_rows = place_rows(jnp.repeat(restored, top_count, axis=0), slot_rows, slot_total)
     send_cot = place_rows(cotangent, slot_rows, slot_total)
     flat_shape = (experts, capacity)
-    got_quant, got_scales, got_cot = (
+    got_rows, got_cot = (
         lax.all_to_all(
-            send_quant.reshape(flat_shape + (width,)),
-            ("row", "col"),
-            split_axis=0,
-            concat_axis=0,
-            tiled=True,
-        ),
-        lax.all_to_all(
-            send_scales.reshape(flat_shape + (block_count,)),
+            send_rows.reshape(flat_shape + (width,)),
             ("row", "col"),
             split_axis=0,
             concat_axis=0,
@@ -101,8 +85,7 @@
         ),
     )
     outputs, grad_rows, grad_in_w, grad_out_w = expert_work(
-        got_quant.reshape(slot_total, width),
-        got_scales.reshape(slot_total, block_count),
+        got_rows.reshape(slot_total, width),
         got_cot.reshape(slot_total, width),
         weight_in[0],
         weight_out[0],

time: 127 us -> 119 us (0.937)
  local copies, waits for them, and re-layouts: 23.2 us -> 16.3 us
  starting transfers between devices: 21.5 us -> 18.6 us
  matrix products: 43 us -> 45.3 us
  waiting for transfers between devices: 26.3 us -> 28.1 us
  other arithmetic: 11.5 us -> 9.78 us
    all_to_all x1, waiting for transfers between devices: 2.93 us -> 7.09 us  [body(): lax.all_to_all(send_cot.reshape(flat_shape + (width,)), ('row', 'col'), s...]
    convert_element_type x5 -> x1, local copies, waits for them, and re-layouts: 2.86 us -> 0.14 us  [body(): restored = (quantized.astype(jnp.float32) * scales.astype(jnp.float32)[:,...]
    all_to_all x2 -> x1, starting transfers between devices: 9.92 us -> 7.3 us  [body(): lax.all_to_all(send_rows.reshape(flat_shape + (width,)), ('row', 'col'),...]
    dot_general x1, matrix products: 4.37 us -> 6.59 us  [expert_work(): jnp.dot(grad_preact, weight_in.T, preferred_element_type=jnp.float32)]
    all_to_all x2 -> x1, waiting for transfers between devices: 15.9 us -> 14 us  [body(): lax.all_to_all(send_rows.reshape(flat_shape + (width,)), ('row', 'col'),...]
    mul x2 -> x0, local copies, waits for them, and re-layouts: 1.81 us -> none  [expert_work(): quantized.astype(jnp.float32).reshape(-1, block_count, BLOCK)]
    convert_element_type x3 -> x1, other arithmetic: 1.75 us -> 0.06 us  [body(): restored = (quantized.astype(jnp.float32) * scales.astype(jnp.float32)[:,...]
    scatter x2 -> x1, local copies, waits for them, and re-layouts: 3.79 us -> 2.58 us  [place_rows(): return empty.at[slot_rows].set(values, mode='drop')]
  transfers between devices with their start and end apart: 5 -> 4, of which waited for: 5 -> 3; matrix products, arithmetic and copies ran while one was open for 51% -> 48% of each run, Pallas kernels for 0% -> 0%
where the time goes in v1:
time: 119 us
  matrix products  45.3 us (38%)
  waiting for transfers between devices  28.1 us (24%)
  starting transfers between devices  18.6 us (16%)
  local copies, waits for them, and re-layouts  16.3 us (14%)
  other arithmetic  9.78 us (8%)
    all_to_all x1, waiting for transfers between devices, body(): lax.all_to_all(send_rows.reshape(flat_shape + (width,)), ('row', 'col'),...  14 us
    dot_general x1, matrix products, expert_work(): jnp.dot(cotangent, weight_out.T, preferred_element_type=jnp.float32)  11.2 us
    dot_general x1, matrix products, expert_work(): jnp.dot(hidden.T, cotangent, preferred_element_type=jnp.float32)  10.5 us
    all_to_all x1, starting transfers between devices, body(): lax.all_to_all(send_rows.reshape(flat_shape + (width,)), ('row', 'col'),...  7.3 us
    all_to_all x1, waiting for transfers between devices, body(): lax.all_to_all(send_cot.reshape(flat_shape + (width,)), ('row', 'col'), s...  7.09 us
    all_to_all x1, waiting for transfers between devices, body(): lax.all_to_all(grad_rows.reshape(flat_shape), ('row', 'col'), split_axis=...  6.94 us
    dot_general x1, matrix products, expert_work(): jnp.dot(grad_preact, weight_in.T, preferred_element_type=jnp.float32)  6.59 us
    unnamed x13, local copies, waits for them, and re-layouts  5.9 us
  transfers between devices with their start and end apart: 4, of which 3 were waited for; matrix products, arithmetic and copies ran while one was open for 48% of the time, Pallas kernels for 0%

profile of v1, /device:TPU:0, one launch (start us, length us, event | category | flops | bytes accessed | tf_op | source)
XLA Modules:
  0.0 118.9 jit_solution(9434031818695613202)
XLA Ops:
  0.6 0.8 copy.42
  1.4 0.1 eq.15
  1.6 0.2 convert_reduce_fusion
  1.7 0.1 reshape.91
  1.9 0.1 copy.43
  2.0 0.7 broadcast_select_fusion.2
  2.7 0.7 compare_select_fusion.1
  3.4 0.1 copy.44
  3.5 0.1 reshape.92
  3.6 1.1 copy.45
  4.8 0.1 fusion.26
  4.9 0.1 copy.46
  5.0 0.2 broadcast_in_dim.48
  5.2 0.1 reshape.122
  5.4 2.6 %scatter_custom_fusion = bf16[512,768]{1,0:T(8,128)(2,1)} fusion(s32[256]{0:T(256)S(1)} %bitcast.54, bf16[256,768]{1,0:T(8,128)(2,1)S(1)} %reshape.122, bf16[]{:T(256)} %constant.15.clone.1), kind=kCustom, calls=%fused_computation.40 | custom fusion | bytes 786434 | tf_op jit(solution)/shard_map/scatter | solution.py:39
  8.0 7.3 %all-to-all-start = ((bf16[32,16,768]{2,1,0:T(8,128)(2,1)}), bf16[32,16,768]{2,1,0:T(8,128)(2,1)S(1)}, u32[]{:S(2)}, u32[]{:S(2)}) async-start(bf16[32,16,768]{2,1,0:T(8,128)(2,1)} %bitcast.3), calls=%async_computation | async-start | bytes 1572864 | tf_op jit(solution)/shard_map/all_to_all | solution.py:72
  15.3 0.7 copy.48
  16.0 0.8 copy.49
  16.8 0.7 copy.41
  17.5 0.1 copy.47
  17.6 0.1 reshape.104
  17.8 0.1 mul.98
  17.9 1.0 convert_element_type.82
  18.9 1.1 mul.100
  20.0 0.5 mul.101
  20.6 2.6 %scatter_custom_fusion.1 = bf16[512,768]{1,0:T(8,128)(2,1)} fusion(s32[256]{0:T(256)S(1)} %bitcast.55, f32[256,768]{1,0:T(8,128)S(1)} %mul.101, f32[256]{0:T(256)S(1)} %mul.98, bf16[]{:T(256)} %constant.15.clone.1), kind=kCustom, calls=%fused_computation.37 | custom fusion | flops 393216 | bytes 1573890 | tf_op jit(solution)/shard_map/scatter | solution.py:39
  23.2 14.0 %all-to-all-done = bf16[32,16,768]{2,1,0:T(8,128)(2,1)S(1)} async-done(((bf16[32,16,768]{2,1,0:T(8,128)(2,1)}), bf16[32,16,768]{2,1,0:T(8,128)(2,1)S(1)}, u32[]{:S(2)}, u32[]{:S(2)}) %all-to-all-start) | async-done | bytes 786464 | tf_op jit(solution)/shard_map/all_to_all | solution.py:72
  37.3 2.6 %all-to-all-start.2 = ((bf16[32,16,768]{2,1,0:T(8,128)(2,1)}), bf16[32,16,768]{2,1,0:T(8,128)(2,1)S(1)}, u32[]{:S(2)}, u32[]{:S(2)}) async-start(bf16[32,16,768]{2,1,0:T(8,128)(2,1)} %bitcast.9), calls=%async_computation.2 | async-start | bytes 1572864 | tf_op jit(solution)/shard_map/all_to_all | solution.py:79
  39.9 0.0 slice-start
  39.9 0.0 slice-start.1
  39.9 5.7 %fusion.13 = f32[512,4096]{1,0:T(8,128)S(1)} fusion(bf16[512,768]{1,0:T(8,128)(2,1)S(1)} %bitcast.49, bf16[1,768,4096]{2,1,0:T(8,128)(2,1)} %param.11), kind=kOutput, calls=%fused_computation.22 | convolution fusion | flops 3221225472 | bytes 15466496 | tf_op jit(solution)/shard_map/dot_general | solution.py:19
  45.7 0.0 copy-start
  45.7 3.2 %copy-done = f32[512,4096]{1,0:T(8,128)} copy-done((f32[512,4096]{1,0:T(8,128)}, f32[512,4096]{1,0:T(8,128)S(1)}, u32[]{:S(2)}) %copy-start) | copy-done | bytes 8388632
  48.9 0.0 slice-done
  48.9 0.0 slice-done.1
  48.9 5.9 %fusion.22 = bf16[512,768]{1,0:T(8,128)(2,1)} fusion(bf16[1,4096,768]{2,1,0:T(8,128)(2,1)S(1)} %bitcast.57, f32[512,4096]{1,0:T(8,128)S(1)} %fusion.13), kind=kOutput, calls=%fused_computation.27 | convolution fusion | flops 3240493056 | bytes 15466496 | tf_op jit(solution)/shard_map/dot_general | solution.py:22
  54.8 7.1 %all-to-all-done.2 = bf16[32,16,768]{2,1,0:T(8,128)(2,1)S(1)} async-done(((bf16[32,16,768]{2,1,0:T(8,128)(2,1)}), bf16[32,16,768]{2,1,0:T(8,128)(2,1)S(1)}, u32[]{:S(2)}, u32[]{:S(2)}) %all-to-all-start.2) | async-done | bytes 786464 | tf_op jit(solution)/shard_map/all_to_all | solution.py:79
  61.9 2.8 %all-to-all-start.1 = ((bf16[32,16,768]{2,1,0:T(8,128)(2,1)}), bf16[32,16,768]{2,1,0:T(8,128)(2,1)S(1)}, u32[]{:S(2)}, u32[]{:S(2)}) async-start(bf16[32,16,768]{2,1,0:T(8,128)(2,1)} %bitcast.7), calls=%async_computation.1 | async-start | bytes 1572864 | tf_op jit(solution)/shard_map/all_to_all | solution.py:95
  64.7 11.2 %fusion.6 = bf16[512,4096]{1,0:T(8,128)(2,1)S(1)} fusion(f32[512,4096]{1,0:T(8,128)} %copy-done, bf16[512,768]{1,0:T(8,128)(2,1)S(1)} %bitcast.52, bf16[1,4096,768]{2,1,0:T(8,128)(2,1)} %param.12), kind=kOutput, calls=%fused_computation.12 | convolution fusion | flops 3263168512 | bytes 19660800 | tf_op jit(solution)/shard_map/dot_general | solution.py:26
  75.9 5.4 %fusion.15 = bf16[1,768,4096]{2,1,0:T(8,128)(2,1)} fusion(bf16[512,768]{1,0:T(8,128)(2,1)S(1)} %bitcast.50, bf16[512,4096]{1,0:T(8,128)(2,1)S(1)} %fusion.6), kind=kOutput, calls=%fused_computation.24 | convolution fusion | flops 3224371200 | bytes 11272192 | tf_op jit(solution)/shard_map/dot_general | solution.py:28
  81.3 6.6 %fusion.19 = bf16[512,768]{1,0:T(8,128)(2,1)} fusion(bf16[512,4096]{1,0:T(8,128)(2,1)S(1)} %fusion.6, bf16[1,768,4096]{2,1,0:T(8,128)(2,1)} %param.11), kind=kOutput, calls=%fused_computation.26 | convolution fusion | flops 3221618688 | bytes 11272192 | tf_op jit(solution)/shard_map/dot_general | solution.py:31
  87.9 0.0 all-to-all-done.1
  87.9 5.9 %all-to-all-start.3 = ((bf16[32,16,768]{2,1,0:T(8,128)(2,1)}), bf16[32,16,768]{2,1,0:T(8,128)(2,1)S(1)}, u32[]{:S(2)}, u32[]{:S(2)}) async-start(bf16[32,16,768]{2,1,0:T(8,128)(2,1)} %bitcast.11), calls=%async_computation.3 | async-start | bytes 1572864 | tf_op jit(solution)/shard_map/all_to_all | solution.py:98
  93.7 0.0 copy-start.1
  93.8 10.5 %fusion.16 = bf16[1,4096,768]{2,1,0:T(8,128)(2,1)} fusion(bf16[512,768]{1,0:T(8,128)(2,1)S(1)} %bitcast.53, f32[512,4096]{1,0:T(8,128)} %copy-done), kind=kOutput, calls=%fused_computation.25 | convolution fusion | flops 3243245568 | bytes 15466496 | tf_op jit(solution)/shard_map/dot_general | solution.py:23
  104.2 0.0 copy-start.2
  104.2 1.2 gather_fusion
  105.4 0.4 reshape.138
  105.8 0.0 copy-done.1
  105.8 2.1 %multiply_reduce_fusion = (f32[128,2]{1,0:T(8,128)S(1)}, bf16[128,768]{1,0:T(8,128)(2,1)}) fusion(f32[128,2,768]{2,1,0:T(2,128)S(1)} %reshape.138, f32[128,768]{1,0:T(8,128)S(1)} %convert_element_type.82, f32[128,2]{1,0:T(8,128)S(1)} %copy-done.1), kind=kLoop, calls=%fused_computation.28 | loop fusion | flops 687872 | bytes 1378304 | tf_op jit(solution)/shard_map/reduce_sum | solution.py:107
  107.9 0.1 copy.50
  108.0 0.6 broadcast_select_fusion.1
  108.6 6.9 %all-to-all-done.3 = bf16[32,16,768]{2,1,0:T(8,128)(2,1)S(1)} async-done(((bf16[32,16,768]{2,1,0:T(8,128)(2,1)}), bf16[32,16,768]{2,1,0:T(8,128)(2,1)S(1)}, u32[]{:S(2)}, u32[]{:S(2)}) %all-to-all-start.3) | async-done | bytes 786464 | tf_op jit(solution)/shard_map/all_to_all | solution.py:98
  115.5 1.2 gather_fusion.1
  116.7 0.4 reshape.139
  117.1 0.0 copy-done.2
  117.1 1.8 %select_reduce_fusion = bf16[128,768]{1,0:T(8,128)(2,1)} fusion(f32[128,2,768]{2,1,0:T(2,128)S(1)} %reshape.139, pred[128,2]{1,0:T(8,128)(4,1)S(1)} %copy-done.2), kind=kLoop, calls=%fused_computation.29 | loop fusion | flops 294912 | bytes 983296 | tf_op jit(solution)/shard_map/reduce_sum | solution.py:110
  (6 shorter events, 0.1 us)
Async XLA Ops:
  8.0 29.3 %all-to-all-start = ((bf16[32,16,768]{2,1,0:T(8,128)(2,1)}), bf16[32,16,768]{2,1,0:T(8,128)(2,1)S(1)}, u32[]{:S(2)}, u32[]{:S(2)}) async-start(bf16[32,16,768]{2,1,0:T(8,128)(2,1)} %bitcast.3), calls=%async_computation | async-start | bytes 1572864 | tf_op jit(solution)/shard_map/all_to_all | solution.py:72
  37.3 24.6 %all-to-all-start.2 = ((bf16[32,16,768]{2,1,0:T(8,128)(2,1)}), bf16[32,16,768]{2,1,0:T(8,128)(2,1)S(1)}, u32[]{:S(2)}, u32[]{:S(2)}) async-start(bf16[32,16,768]{2,1,0:T(8,128)(2,1)} %bitcast.9), calls=%async_computation.2 | async-start | bytes 1572864 | tf_op jit(solution)/shard_map/all_to_all | solution.py:79
  39.9 9.0 %slice-start = ((s8[6291456]{0:T(1024)(128)(4,1)}), s8[4194304]{0:T(1024)(128)(4,1)S(1)}, s32[]{:S(2)}) async-start(s8[6291456]{0:T(1024)(128)(4,1)} %bitcast.56), calls=%async_computation.4 | async-start | bytes 8388608
  39.9 9.0 %slice-start.1 = ((s8[6291456]{0:T(1024)(128)(4,1)}), s8[2097152]{0:T(1024)(128)(4,1)S(1)}, s32[]{:S(2)}) async-start(s8[6291456]{0:T(1024)(128)(4,1)} %bitcast.56), calls=%async_computation.5 | async-start | bytes 4194304
  45.7 3.2 %copy-start = (f32[512,4096]{1,0:T(8,128)}, f32[512,4096]{1,0:T(8,128)S(1)}, u32[]{:S(2)}) copy-start(f32[512,4096]{1,0:T(8,128)S(1)} %fusion.13) | copy-start | bytes 25165828
  61.9 26.0 %all-to-all-start.1 = ((bf16[32,16,768]{2,1,0:T(8,128)(2,1)}), bf16[32,16,768]{2,1,0:T(8,128)(2,1)S(1)}, u32[]{:S(2)}, u32[]{:S(2)}) async-start(bf16[32,16,768]{2,1,0:T(8,128)(2,1)} %bitcast.7), calls=%async_computation.1 | async-start | bytes 1572864 | tf_op jit(solution)/shard_map/all_to_all | solution.py:95
  87.9 27.6 %all-to-all-start.3 = ((bf16[32,16,768]{2,1,0:T(8,128)(2,1)}), bf16[32,16,768]{2,1,0:T(8,128)(2,1)S(1)}, u32[]{:S(2)}, u32[]{:S(2)}) async-start(bf16[32,16,768]{2,1,0:T(8,128)(2,1)} %bitcast.11), calls=%async_computation.3 | async-start | bytes 1572864 | tf_op jit(solution)/shard_map/all_to_all | solution.py:98
  93.7 12.1 %copy-start.1 = (f32[128,2]{1,0:T(8,128)S(1)}, f32[128,2]{1,0:T(8,128)}, u32[]{:S(2)}) copy-start(f32[128,2]{1,0:T(8,128)} %copy.41) | copy-start | bytes 3076
  104.2 12.8 %copy-start.2 = (pred[128,2]{1,0:T(8,128)(4,1)S(1)}, pred[128,2]{1,0:T(8,128)(4,1)}, u32[]{:S(2)}) copy-start(pred[128,2]{1,0:T(8,128)(4,1)} %copy.48) | copy-start | bytes 772

commit v2 on v1

v2 whole, which is shorter than its diff:
```python
import functools

import jax
import jax.numpy as jnp
from jax import lax
from jax.experimental import pallas as pl
from jax.experimental.pallas import tpu as pltpu
from jax.sharding import Mesh
from jax.sharding import PartitionSpec as P

BLOCK = 128
BF16 = jnp.bfloat16
F32 = jnp.float32
GROUP = ("row", "rest")
VMEM_LIMIT = 56 * 1024 * 1024


def dot(a, b, contract_a, contract_b):
    return lax.dot_general(
        a, b, (((contract_a,), (contract_b,)), ((), ())), preferred_element_type=F32
    )


def column(row):
    count = row.shape[1]
    return jnp.transpose(jnp.broadcast_to(row, (count, count)))


def route_kernel(rest_bits, capacity, half_ref, ids_ref, keep_ref, gates_ref, mine_ref, other_ref):
    token_rows = ids_ref.shape[1]
    ids = ids_ref[...].astype(F32)
    earlier = lax.broadcasted_iota(jnp.int32, (token_rows, token_rows), 0) < lax.broadcasted_iota(
        jnp.int32, (token_rows, token_rows), 1
    )
    columns = (column(ids[0:1]), column(ids[1:2]))
    half = half_ref[0]
    for k in range(2):
        count = jnp.zeros((token_rows, token_rows), F32)
        for other_choice in columns:
            count = count + jnp.where(earlier & (other_choice == ids[k : k + 1]), 1.0, 0.0)
        slot = jnp.sum(count, axis=0, keepdims=True).astype(jnp.int32)
        expert = ids_ref[k : k + 1, :]
        kept = keep_ref[k : k + 1, :] > 0
        side = (expert >> rest_bits) & 1
        local = ((expert >> (rest_bits + 1)) << rest_bits) + (expert & ((1 << rest_bits) - 1))
        base = local * (2 * capacity) + slot
        here = kept & (side == half)
        there = kept & (side != half)
        mine_ref[k : k + 1, :] = jnp.where(here, base, -1).astype(F32)
        other_ref[k : k + 1, :] = jnp.where(there, base + capacity, -1).astype(F32)
        mine_ref[k + 2 : k + 3, :] = gates_ref[k : k + 1, :]
        other_ref[k + 2 : k + 3, :] = gates_ref[k : k + 1, :]
    mine_ref[4:8, :] = jnp.zeros((4, token_rows), F32)
    other_ref[4:8, :] = jnp.zeros((4, token_rows), F32)


def hits(slot_total, meta_ref, k):
    rows = meta_ref[k : k + 1, :].astype(jnp.int32)
    index = lax.broadcasted_iota(jnp.int32, (slot_total, rows.shape[1]), 0)
    return index == rows


def one_hot(mask):
    return jnp.where(mask, 1.0, 0.0).astype(BF16)


def restore(tokens_ref):
    pieces = []
    for b in range(tokens_ref.shape[1] // BLOCK):
        x = tokens_ref[:, b * BLOCK : (b + 1) * BLOCK].astype(F32)
        scale = (jnp.max(jnp.abs(x), axis=1, keepdims=True) + 1e-06).astype(BF16).astype(F32)
        quantized = (x / scale).astype(BF16)
        pieces.append((quantized.astype(F32) * scale).astype(BF16))
    return jnp.concatenate(pieces, axis=1)


def place_tokens_kernel(own_ref, partner_ref, own_meta, partner_meta, out_ref):
    slot_total = out_ref.shape[0]
    total = None
    for tokens_ref, meta in ((own_ref, own_meta), (partner_ref, partner_meta)):
        mask = hits(slot_total, meta, 0) | hits(slot_total, meta, 1)
        part = dot(one_hot(mask), restore(tokens_ref), 1, 0)
        total = part if total is None else total + part
    out_ref[...] = total.astype(BF16)


def scaled_rows(gate_row, grad_ref):
    gate = column(gate_row)
    pieces = [
        gate * grad_ref[:, b * BLOCK : (b + 1) * BLOCK].astype(F32)
        for b in range(grad_ref.shape[1] // BLOCK)
    ]
    return jnp.concatenate(pieces, axis=1)


def place_cotangents_kernel(own_ref, partner_ref, own_meta, partner_meta, out_ref):
    slot_total = out_ref.shape[0]
    total = None
    for grad_ref, meta in ((own_ref, own_meta), (partner_ref, partner_meta)):
        for k in range(2):
            rows = scaled_rows(meta[k + 2 : k + 3, :], grad_ref).astype(BF16)
            part = dot(one_hot(hits(slot_total, meta, k)), rows, 1, 0)
            total = part if total is None else total + part
    out_ref[...] = total.astype(BF16)


def forward_kernel(x_ref, w_in_ref, w_out_ref, hidden_ref, slope_ref, out_ref, total):
    step = pl.program_id(0)
    v = dot(x_ref[...], w_in_ref[...], 1, 0)
    c = 0.7978845608028654
    square = v * v
    t = jnp.tanh(v * (c + (c * 0.044715) * square))
    half = 0.5 + 0.5 * t
    hidden = (v * half).astype(BF16)
    slope_ref[...] = half + (0.5 * v) * (1.0 - t * t) * (c + (3 * c * 0.044715) * square)
    hidden_ref[...] = hidden

    @pl.when(step == 0)
    def _():
        total[...] = jnp.zeros_like(total)

    total[...] += dot(hidden, w_out_ref[...], 1, 0)

    @pl.when(step == pl.num_programs(0) - 1)
    def _():
        out_ref[...] = total[...].astype(BF16)


def backward_kernel(cot_ref, w_in_ref, w_out_ref, slope_ref, grad_pre_ref, out_ref, total):
    step = pl.program_id(0)
    grad_hidden = dot(cot_ref[...], w_out_ref[...], 1, 1)
    grad_pre = (grad_hidden * slope_ref[...]).astype(BF16)
    grad_pre_ref[...] = grad_pre

    @pl.when(step == 0)
    def _():
        total[...] = jnp.zeros_like(total)

    total[...] += dot(grad_pre, w_in_ref[...], 1, 1)

    @pl.when(step == pl.num_programs(0) - 1)
    def _():
        out_ref[...] = total[...].astype(BF16)


def weights_kernel(x_ref, cot_ref, hidden_ref, grad_pre_ref, grad_in_ref, grad_out_ref):
    grad_in_ref[...] = dot(x_ref[...], grad_pre_ref[...], 0, 0).astype(BF16)
    grad_out_ref[...] = dot(hidden_ref[...], cot_ref[...], 0, 0).astype(BF16)


def pick_outputs_kernel(
    back_ref, own_grad, partner_grad, own_meta, partner_meta, own_out, partner_out, own_gates, partner_gates
):
    slot_total = back_ref.shape[0]
    for grad_ref, meta, out_ref, gates_ref in (
        (own_grad, own_meta, own_out, own_gates),
        (partner_grad, partner_meta, partner_out, partner_gates),
    ):
        total = None
        for k in range(2):
            picked = dot(one_hot(hits(slot_total, meta, k)), back_ref[...], 0, 0)
            gate = column(meta[k + 2 : k + 3, :])
            pieces = [
                gate * picked[:, b * BLOCK : (b + 1) * BLOCK]
                for b in range(picked.shape[1] // BLOCK)
            ]
            weighted = jnp.concatenate(pieces, axis=1)
            total = weighted if total is None else total + weighted
            sums = jnp.sum(picked * grad_ref[...].astype(F32), axis=1, keepdims=True)
            rows = jnp.transpose(jnp.broadcast_to(sums, (sums.shape[0], sums.shape[0])))
            gates_ref[k : k + 1, :] = rows[0:1, :]
        out_ref[...] = total.astype(out_ref.dtype)


def pick_gradients_kernel(back_ref, own_meta, partner_meta, own_out, partner_out):
    slot_total = back_ref.shape[0]
    for meta, out_ref in ((own_meta, own_out), (partner_meta, partner_out)):
        mask = hits(slot_total, meta, 0) | hits(slot_total, meta, 1)
        out_ref[...] = dot(one_hot(mask), back_ref[...], 0, 0).astype(out_ref.dtype)


def call(kernel, outs, flops=0, traffic=0, **options):
    shapes = [jax.ShapeDtypeStruct(shape, dtype) for shape, dtype in outs]
    return pl.pallas_call(
        kernel,
        out_shape=shapes if len(shapes) > 1 else shapes[0],
        compiler_params=pltpu.CompilerParams(vmem_limit_bytes=VMEM_LIMIT),
        cost_estimate=pl.CostEstimate(flops=flops, bytes_accessed=traffic, transcendentals=0),
        **options,
    )


def body(tokens, expert_ids, keep_mask, gate_weights, weight_in, weight_out, grad_output):
    token_rows, width = tokens.shape
    hidden_width = weight_in.shape[2]
    rest_count = lax.axis_size("rest")
    members = lax.axis_size("row") * rest_count
    experts = 2 * members
    capacity = 2 * expert_ids.shape[1] * token_rows // experts
    slot_total = experts * capacity
    swap = ((0, 1), (1, 0))

    def exchange(values):
        return lax.ppermute(values, "half", swap)

    def shuffle(rows):
        shaped = rows.reshape(members, 2 * capacity, width)
        return lax.all_to_all(shaped, GROUP, split_axis=0, concat_axis=0, tiled=True).reshape(
            slot_total, width
        )

    partner_tokens = exchange(tokens)
    partner_grad = exchange(grad_output)
    half = lax.axis_index("half").astype(jnp.int32).reshape(1)
    meta_shape = ((8, token_rows), F32)
    vmem = pl.BlockSpec(memory_space=pltpu.VMEM)
    own_meta, sent_meta = call(
        functools.partial(route_kernel, rest_count.bit_length() - 1, capacity),
        [meta_shape, meta_shape],
        in_specs=[pl.BlockSpec(memory_space=pltpu.SMEM), vmem, vmem, vmem],
        traffic=8 * token_rows * 8,
    )(half, expert_ids.T, keep_mask.T, gate_weights.T)
    partner_meta = exchange(sent_meta)

    slot_shape = ((slot_total, width), BF16)
    slot_bytes = slot_total * width * 2
    token_bytes = token_rows * width * 2
    place_flops = 2 * slot_total * 2 * token_rows * width
    sent = call(place_tokens_kernel, [slot_shape], place_flops, 2 * token_bytes + slot_bytes)(
        tokens, partner_tokens, own_meta, partner_meta
    )
    x = shuffle(sent)
    sent_cot = call(
        place_cotangents_kernel, [slot_shape], 2 * place_flops, 2 * token_bytes + slot_bytes
    )(grad_output, partner_grad, own_meta, partner_meta)
    cot = shuffle(sent_cot)

    chunk = 512
    steps = hidden_width // chunk
    whole = pl.BlockSpec((slot_total, width), lambda i: (0, 0))
    in_spec = pl.BlockSpec((None, width, chunk), lambda i: (0, 0, i))
    out_spec = pl.BlockSpec((None, chunk, width), lambda i: (0, i, 0))
    mid_spec = pl.BlockSpec((slot_total, chunk), lambda i: (0, i))
    mid = (slot_total, hidden_width)
    product = 2 * slot_total * width * hidden_width
    weight_bytes = 2 * 2 * width * hidden_width
    mid_count = slot_total * hidden_width
    hidden, slope, outputs = call(
        forward_kernel,
        [(mid, BF16), (mid, F32), slot_shape],
        2 * product,
        2 * slot_bytes + weight_bytes + 6 * mid_count,
        grid=(steps,),
        in_specs=[whole, in_spec, out_spec],
        out_specs=[mid_spec, mid_spec, whole],
        scratch_shapes=[pltpu.VMEM((slot_total, width), F32)],
    )(x, weight_in, weight_out)
    back_out = shuffle(outputs)
    grad_pre, grad_rows = call(
        backward_kernel,
        [(mid, BF16), slot_shape],
        2 * product,
        2 * slot_bytes + weight_bytes + 6 * mid_count,
        grid=(steps,),
        in_specs=[whole, in_spec, out_spec, mid_spec],
        out_specs=[mid_spec, whole],
        scratch_shapes=[pltpu.VMEM((slot_total, width), F32)],
    )(cot, weight_in, weight_out, slope)
    back_grad = shuffle(grad_rows)
    own_shape, partner_shape = ((token_rows, width), F32), ((token_rows, width), BF16)
    gates_shape = ((2, token_rows), F32)
    own_out, partner_out, own_gates, partner_gates = call(
        pick_outputs_kernel,
        [own_shape, partner_shape, gates_shape, gates_shape],
        2 * place_flops,
        2 * token_bytes + slot_bytes,
    )(back_out, grad_output, partner_grad, own_meta, partner_meta)
    grad_in_w, grad_out_w = call(
        weights_kernel,
        [(weight_in.shape, BF16), (weight_out.shape, BF16)],
        2 * product,
        2 * slot_bytes + weight_bytes + 4 * mid_count,
        grid=(steps,),
        in_specs=[whole, whole, mid_spec, mid_spec],
        out_specs=[in_spec, out_spec],
    )(x, cot, hidden, grad_pre)
    combined = (own_out + exchange(partner_out).astype(F32)).astype(BF16)
    grad_gates = (own_gates + exchange(partner_gates)).T
    own_back, partner_back = call(
        pick_gradients_kernel, [own_shape, partner_shape], place_flops, slot_bytes + 3 * token_bytes
    )(back_grad, own_meta, partner_meta)
    grad_tokens = (own_back + exchange(partner_back).astype(F32)).astype(BF16)
    return (combined, grad_tokens, grad_gates, grad_in_w, grad_out_w)


def solution(mesh):
    row_count, col_count = mesh.devices.shape
    split = Mesh(
        mesh.devices.reshape(row_count, 2, col_count // 2), ("row", "half", "rest")
    )
    axes = ("row", "half", "rest")
    flat = P(axes, None)
    deep = P(axes, None, None)
    return jax.shard_map(
        body,
        mesh=split,
        in_specs=(flat, flat, flat, flat, deep, deep, flat),
        out_specs=(flat, flat, flat, deep, deep),
        check_vma=False,
    )
```

time: 119 us -> 132 us (1.11); the launches traced: 119 us -> 130 us
  Pallas kernels: 0 us -> 59.1 us
  matrix products: 45.3 us -> 0 us
  starting transfers between devices: 18.6 us -> 33.3 us
  local copies, waits for them, and re-layouts: 16.3 us -> 2.26 us
  other arithmetic: 9.78 us -> 4.66 us
  waiting for transfers between devices: 28.1 us -> 30.4 us
    pallas_call x0 -> x8, Pallas kernels: none -> 59.1 us  [the longest x1 17.6 us: body(): call(forward_kernel, [(mid, BF16), (mid, F32), slot_shape], 2 * product,...]
    dot_general x6 -> x0, matrix products: 45.3 us -> none  [the longest x1 11.2 us: expert_work(): jnp.dot(cotangent, weight_out.T, preferred_element_type=jnp.float32)]
    ppermute x0 -> x6, waiting for transfers between devices: none -> 30.4 us  [exchange(): return lax.ppermute(values, 'half', swap)]
    all_to_all x4, waiting for transfers between devices: 28.1 us -> 0.01 us  [shuffle(): lax.all_to_all(shaped, GROUP, split_axis=0, concat_axis=0, tiled=True)]
    ppermute x0 -> x6, starting transfers between devices: none -> 10.5 us  [exchange(): return lax.ppermute(values, 'half', swap)]
    all_to_all x4, starting transfers between devices: 18.6 us -> 22.8 us  [shuffle(): lax.all_to_all(shaped, GROUP, split_axis=0, concat_axis=0, tiled=True)]
    reduce_sum x3 -> x0, other arithmetic: 4.04 us -> none  [the longest x1 2.09 us: body(): jnp.sum(grad_output.astype(jnp.float32)[:, None, :] * picked_out, axis=2)]
    unnamed x13 -> x14, local copies, waits for them, and re-layouts: 5.9 us -> 2.26 us
  transfers between devices with their start and end apart: 4 -> 10, of which waited for: 3 -> 4; matrix products, arithmetic and copies ran while one was open for 48% -> 2% of each run, Pallas kernels for 0% -> 43%
where the time goes in v2:
time: 132 us; the launch traced here: 130 us
  Pallas kernels  59.1 us (45%)
  starting transfers between devices  33.3 us (25%)
  waiting for transfers between devices  30.4 us (23%)
  other arithmetic  4.66 us (4%)
  local copies, waits for them, and re-layouts  2.26 us (2%)
    ppermute x6, waiting for transfers between devices, exchange(): return lax.ppermute(values, 'half', swap)  30.4 us
    all_to_all x4, starting transfers between devices, shuffle(): lax.all_to_all(shaped, GROUP, split_axis=0, concat_axis=0, tiled=True)  22.8 us
    pallas_call x1, Pallas kernels, body(): call(forward_kernel, [(mid, BF16), (mid, F32), slot_shape], 2 * product,...  17.6 us
    pallas_call x1, Pallas kernels, body(): call(backward_kernel, [(mid, BF16), slot_shape], 2 * product, 2 * slot_by...  16.8 us
    pallas_call x1, Pallas kernels, body(): call(weights_kernel, [(weight_in.shape, BF16), (weight_out.shape, BF16)],...  12.5 us
    ppermute x6, starting transfers between devices, exchange(): return lax.ppermute(values, 'half', swap)  10.5 us
    pallas_call x1, Pallas kernels, body(): call(place_cotangents_kernel, [slot_shape], 2 * place_flops, 2 * token_by...  2.97 us
    pallas_call x1, Pallas kernels, body(): call(pick_outputs_kernel, [own_shape, partner_shape, gates_shape, gates_s...  2.72 us
  transfers between devices with their start and end apart: 10, of which 4 were waited for; matrix products, arithmetic and copies ran while one was open for 2% of the time, Pallas kernels for 43%

profile of v2, /device:TPU:0, one launch (start us, length us, event | category | flops | bytes accessed | tf_op | source)
XLA Modules:
  0.0 130.4 jit_solution(7780722322009205730)
XLA Ops:
  0.6 4.1 %collective-permute-start = (bf16[128,768]{1,0:T(8,128)(2,1)}, bf16[128,768]{1,0:T(8,128)(2,1)S(1)}, u32[]{:S(2)}, u32[]{:S(2)}) collective-permute-start(bf16[128,768]{1,0:T(8,128)(2,1)} %own_ref.2), channel_id=1, source_target_pairs={{0,4},{4,0},{1,5},{5,1},{2,6},{6,2},{3,7},{7,3},{8,12},{12,8},{9,1... | collective-permute-start | bytes 589832 | tf_op jit(solution)/shard_map/ppermute | solution.py:204
  4.7 1.4 %shard_map.110 = (f32[8,128]{1,0:T(8,128)}, f32[8,128]{1,0:T(8,128)}) custom-call(s32[1]{0:T(128)} %bitcast.half_ref, s32[2,128]{1,0:T(2,128)} %bitcast.24, s32[2,128]{1,0:T(2,128)} %bitcast.25, f32[2,128]{1,0:T(2,128)} %bitcast.26), custom_call_target="tpu_custom_call" | custom-call | bytes 8192 | tf_op jit(solution)/shard_map/pallas_call | solution.py:217
  6.2 0.0 collective-permute-start.1
  6.2 8.1 %collective-permute-done.1.partner_meta = f32[8,128]{1,0:T(8,128)S(1)} collective-permute-done((f32[8,128]{1,0:T(8,128)}, f32[8,128]{1,0:T(8,128)S(1)}, u32[]{:S(2)}, u32[]{:S(2)}) %collective-permute-start.1) | collective-permute-done | bytes 4128 | tf_op jit(solution)/shard_map/ppermute | solution.py:204
  14.2 0.0 copy-start.5
  14.2 0.0 collective-permute-done.partner_ref
  14.2 0.0 copy-start.4
  14.2 0.6 copy-done.5
  14.8 0.1 copy-done.4
  14.9 2.7 %shard_map.111 = bf16[512,768]{1,0:T(8,128)(2,1)} custom-call(bf16[128,768]{1,0:T(8,128)(2,1)} %own_ref.2, bf16[128,768]{1,0:T(8,128)(2,1)} %copy-done.4, f32[8,128]{1,0:T(8,128)} %get-tuple-element.20.own_meta, f32[8,128]{1,0:T(8,128)} %copy-done.5), custom_call_target="tpu_custom_call" | custom-call | flops 201326592 | bytes 1179648 | tf_op jit(solution)/shard_map/pallas_call | solution.py:229
  17.6 4.0 %all-to-all-start = ((bf16[16,32,768]{2,1,0:T(8,128)(2,1)}), bf16[16,32,768]{2,1,0:T(8,128)(2,1)S(1)}, u32[]{:S(2)}, u32[]{:S(2)}) async-start(bf16[16,32,768]{2,1,0:T(8,128)(2,1)} %bitcast.15), calls=%async_computation | async-start | bytes 1572864 | tf_op jit(solution)/shard_map/all_to_all | solution.py:208
  21.6 3.4 %collective-permute-start.2 = (bf16[128,768]{1,0:T(8,128)(2,1)}, bf16[128,768]{1,0:T(8,128)(2,1)S(1)}, u32[]{:S(2)}, u32[]{:S(2)}) collective-permute-start(bf16[128,768]{1,0:T(8,128)(2,1)} %own_ref.3), channel_id=1, source_target_pairs={{0,4},{4,0},{1,5},{5,1},{2,6},{6,2},{3,7},{7,3},{8,12},{12,8},{9,1... | collective-permute-start | bytes 589832 | tf_op jit(solution)/shard_map/ppermute | solution.py:204
  25.0 10.4 %collective-permute-done.2.partner_grad.partner_ref = bf16[128,768]{1,0:T(8,128)(2,1)S(1)} collective-permute-done((bf16[128,768]{1,0:T(8,128)(2,1)}, bf16[128,768]{1,0:T(8,128)(2,1)S(1)}, u32[]{:S(2)}, u32[]{:S(2)}) %collective-permute-start.2) | collective-permute-done | bytes 196640 | tf_op jit(solution)/shard_map/ppermute | solution.py:204
  35.4 0.0 copy-start.6
  35.4 0.7 copy-done.6
  36.1 3.0 %shard_map.114 = bf16[512,768]{1,0:T(8,128)(2,1)} custom-call(bf16[128,768]{1,0:T(8,128)(2,1)} %own_ref.3, bf16[128,768]{1,0:T(8,128)(2,1)} %copy-done.6, f32[8,128]{1,0:T(8,128)} %get-tuple-element.20.own_meta, f32[8,128]{1,0:T(8,128)} %copy-done.5), custom_call_target="tpu_custom_call" | custom-call | flops 402653184 | bytes 1179648 | tf_op jit(solution)/shard_map/pallas_call | solution.py:233
  39.1 0.0 all-to-all-done
  39.1 0.0 copy-start.1
  39.1 8.5 %all-to-all-start.2 = ((bf16[16,32,768]{2,1,0:T(8,128)(2,1)}), bf16[16,32,768]{2,1,0:T(8,128)(2,1)S(1)}, u32[]{:S(2)}, u32[]{:S(2)}) async-start(bf16[16,32,768]{2,1,0:T(8,128)(2,1)} %bitcast.23), calls=%async_computation.2 | async-start | bytes 1572864 | tf_op jit(solution)/shard_map/all_to_all | solution.py:208
  47.6 0.0 copy-done.1
  47.6 17.6 %shard_map.112 = (bf16[512,4096]{1,0:T(8,128)(2,1)}, f32[512,4096]{1,0:T(8,128)}, bf16[512,768]{1,0:T(8,128)(2,1)}) custom-call(bf16[512,768]{1,0:T(8,128)(2,1)} %bitcast.16, bf16[1,768,4096]{2,1,0:T(8,128)(2,1)} %w_in_ref.3, bf16[1,4096,768]{2,1,0:T(8,128)(2,1)} %w_out_ref.3), custom_call_target="tpu_custom_call" | custom-call | flops 6442450944 | bytes 26738688 | tf_op jit(solution)/shard_map/pallas_call | solution.py:248
  65.3 0.0 all-to-all-done.2
  65.3 0.0 copy-start.2
  65.3 5.1 %all-to-all-start.1 = ((bf16[16,32,768]{2,1,0:T(8,128)(2,1)}), bf16[16,32,768]{2,1,0:T(8,128)(2,1)S(1)}, u32[]{:S(2)}, u32[]{:S(2)}) async-start(bf16[16,32,768]{2,1,0:T(8,128)(2,1)} %bitcast.22), calls=%async_computation.1 | async-start | bytes 1572864 | tf_op jit(solution)/shard_map/all_to_all | solution.py:208
  70.4 0.0 copy-done.2
  70.4 16.8 %shard_map.115 = (bf16[512,4096]{1,0:T(8,128)(2,1)}, bf16[512,768]{1,0:T(8,128)(2,1)}) custom-call(bf16[512,768]{1,0:T(8,128)(2,1)} %bitcast.18, bf16[1,768,4096]{2,1,0:T(8,128)(2,1)} %w_in_ref.3, bf16[1,4096,768]{2,1,0:T(8,128)(2,1)} %w_out_ref.3, f32[512,4096]{1,0:T(8,128)} %get-tuple-element.25.slope_ref), custom_call_target="tpu_custom_call" | custom-call | flops 6442450944 | bytes 26738688 | tf_op jit(solution)/shard_map/pallas_call | solution.py:259
  87.3 0.0 all-to-all-done.1
  87.3 0.0 copy-start.3
  87.3 5.1 %all-to-all-start.3 = ((bf16[16,32,768]{2,1,0:T(8,128)(2,1)}), bf16[16,32,768]{2,1,0:T(8,128)(2,1)S(1)}, u32[]{:S(2)}, u32[]{:S(2)}) async-start(bf16[16,32,768]{2,1,0:T(8,128)(2,1)} %bitcast.20), calls=%async_computation.3 | async-start | bytes 1572864 | tf_op jit(solution)/shard_map/all_to_all | solution.py:208
  92.4 12.5 %shard_map.117 = (bf16[1,768,4096]{2,1,0:T(8,128)(2,1)}, bf16[1,4096,768]{2,1,0:T(8,128)(2,1)}) custom-call(bf16[512,768]{1,0:T(8,128)(2,1)} %bitcast.17, bf16[512,768]{1,0:T(8,128)(2,1)} %bitcast.19, bf16[512,4096]{1,0:T(8,128)(2,1)} %get-tuple-element.31.hidden_ref, bf16[512,4096]{1,0:T(8,128)(2,1)} %get-tuple-element.32.grad_pre_ref), custom_call_target="tpu_custom_call" | custom-call | flops 6442450944 | bytes 22544384 | tf_op jit(solution)/shard_map/pallas_call | solution.py:278
  105.0 0.0 copy-done.3
  105.0 2.7 %shard_map.113 = (f32[128,768]{1,0:T(8,128)}, bf16[128,768]{1,0:T(8,128)(2,1)}, f32[2,128]{1,0:T(2,128)}, f32[2,128]{1,0:T(2,128)}) custom-call(bf16[512,768]{1,0:T(8,128)(2,1)} %bitcast.21, bf16[128,768]{1,0:T(8,128)(2,1)} %own_ref.3, bf16[128,768]{1,0:T(8,128)(2,1)} %copy-done.6, f32[8,128]{1,0:T(8,128)} %get-tuple-element.20.own_meta, f32[8,128]{1,0:T(8,128)} %copy-done.5), custom_call_target="tpu_custom_call" | custom-call | flops 402653184 | bytes 1179648 | tf_op jit(solution)/shard_map/pallas_call | solution.py:272
  107.7 0.0 collective-permute-start.5
  107.7 2.9 %collective-permute-start.3 = (bf16[128,768]{1,0:T(8,128)(2,1)}, bf16[128,768]{1,0:T(8,128)(2,1)S(1)}, u32[]{:S(2)}, u32[]{:S(2)}) collective-permute-start(bf16[128,768]{1,0:T(8,128)(2,1)} %get-tuple-element.24), channel_id=1, source_target_pairs={{0,4},{4,0},{1,5},{5,1},{2,6},{6,2},{3,7},{7,3},{8,12},{12,8},{9,1... | collective-permute-start | bytes 589832 | tf_op jit(solution)/shard_map/ppermute | solution.py:204
  110.6 0.0 all-to-all-done.3
  110.6 0.0 copy-start
  110.6 0.9 copy-done
  111.5 2.3 %shard_map.116 = (f32[128,768]{1,0:T(8,128)}, bf16[128,768]{1,0:T(8,128)(2,1)}) custom-call(bf16[512,768]{1,0:T(8,128)(2,1)} %bitcast.14, f32[8,128]{1,0:T(8,128)} %get-tuple-element.20.own_meta, f32[8,128]{1,0:T(8,128)} %copy-done.5), custom_call_target="tpu_custom_call" | custom-call | flops 201326592 | bytes 1376256 | tf_op jit(solution)/shard_map/pallas_call | solution.py:289
  113.8 0.0 collective-permute-start.4
  113.8 0.0 collective-permute-done.5
  113.8 1.2 add_bitcast_fusion
  115.1 9.9 %collective-permute-done.3 = bf16[128,768]{1,0:T(8,128)(2,1)S(1)} collective-permute-done((bf16[128,768]{1,0:T(8,128)(2,1)}, bf16[128,768]{1,0:T(8,128)(2,1)S(1)}, u32[]{:S(2)}, u32[]{:S(2)}) %collective-permute-start.3) | collective-permute-done | bytes 196640 | tf_op jit(solution)/shard_map/ppermute | solution.py:204
  125.0 1.7 %add_convert_fusion.1 = bf16[128,768]{1,0:T(8,128)(2,1)} fusion(f32[128,768]{1,0:T(8,128)} %get-tuple-element.23, bf16[128,768]{1,0:T(8,128)(2,1)S(1)} %collective-permute-done.3), kind=kLoop, calls=%fused_computation.1 | loop fusion | flops 294912 | bytes 786432 | tf_op jit(solution)/shard_map/convert_element_type | solution.py:287
  126.7 2.1 %collective-permute-done.4 = bf16[128,768]{1,0:T(8,128)(2,1)S(1)} collective-permute-done((bf16[128,768]{1,0:T(8,128)(2,1)}, bf16[128,768]{1,0:T(8,128)(2,1)S(1)}, u32[]{:S(2)}, u32[]{:S(2)}) %collective-permute-start.4) | collective-permute-done | bytes 196640 | tf_op jit(solution)/shard_map/ppermute | solution.py:204
  128.7 1.7 %add_convert_fusion = bf16[128,768]{1,0:T(8,128)(2,1)} fusion(f32[128,768]{1,0:T(8,128)} %get-tuple-element.27, bf16[128,768]{1,0:T(8,128)(2,1)S(1)} %collective-permute-done.4), kind=kLoop, calls=%fused_computation | loop fusion | flops 294912 | bytes 786432 | tf_op jit(solution)/shard_map/convert_element_type | solution.py:292
Async XLA Ops:
  0.6 13.6 %collective-permute-start = (bf16[128,768]{1,0:T(8,128)(2,1)}, bf16[128,768]{1,0:T(8,128)(2,1)S(1)}, u32[]{:S(2)}, u32[]{:S(2)}) collective-permute-start(bf16[128,768]{1,0:T(8,128)(2,1)} %own_ref.2), channel_id=1, source_target_pairs={{0,4},{4,0},{1,5},{5,1},{2,6},{6,2},{3,7},{7,3},{8,12},{12,8},{9,1... | collective-permute-start | bytes 589832 | tf_op jit(solution)/shard_map/ppermute | solution.py:204
  6.2 8.1 %collective-permute-start.1 = (f32[8,128]{1,0:T(8,128)}, f32[8,128]{1,0:T(8,128)S(1)}, u32[]{:S(2)}, u32[]{:S(2)}) collective-permute-start(f32[8,128]{1,0:T(8,128)} %get-tuple-element.21), channel_id=1, source_target_pairs={{0,4},{4,0},{1,5},{5,1},{2,6},{6,2},{3,7},{7,3},{8,12},{12,8},{9,1... | collective-permute-start | bytes 12296 | tf_op jit(solution)/shard_map/ppermute | solution.py:204
  14.2 0.6 copy-start.5
  14.2 0.7 copy-start.4
  17.6 21.5 %all-to-all-start = ((bf16[16,32,768]{2,1,0:T(8,128)(2,1)}), bf16[16,32,768]{2,1,0:T(8,128)(2,1)S(1)}, u32[]{:S(2)}, u32[]{:S(2)}) async-start(bf16[16,32,768]{2,1,0:T(8,128)(2,1)} %bitcast.15), calls=%async_computation | async-start | bytes 1572864 | tf_op jit(solution)/shard_map/all_to_all | solution.py:208
  21.6 13.8 %collective-permute-start.2 = (bf16[128,768]{1,0:T(8,128)(2,1)}, bf16[128,768]{1,0:T(8,128)(2,1)S(1)}, u32[]{:S(2)}, u32[]{:S(2)}) collective-permute-start(bf16[128,768]{1,0:T(8,128)(2,1)} %own_ref.3), channel_id=1, source_target_pairs={{0,4},{4,0},{1,5},{5,1},{2,6},{6,2},{3,7},{7,3},{8,12},{12,8},{9,1... | collective-permute-start | bytes 589832 | tf_op jit(solution)/shard_map/ppermute | solution.py:204
  35.4 0.7 copy-start.6
  39.1 8.5 %copy-start.1 = (bf16[16,32,768]{2,1,0:T(8,128)(2,1)}, bf16[16,32,768]{2,1,0:T(8,128)(2,1)S(1)}, u32[]{:S(2)}) copy-start(bf16[16,32,768]{2,1,0:T(8,128)(2,1)S(1)} %all-to-all-done) | copy-start | bytes 2359300
  39.1 26.2 %all-to-all-start.2 = ((bf16[16,32,768]{2,1,0:T(8,128)(2,1)}), bf16[16,32,768]{2,1,0:T(8,128)(2,1)S(1)}, u32[]{:S(2)}, u32[]{:S(2)}) async-start(bf16[16,32,768]{2,1,0:T(8,128)(2,1)} %bitcast.23), calls=%async_computation.2 | async-start | bytes 1572864 | tf_op jit(solution)/shard_map/all_to_all | solution.py:208
  65.3 5.1 %copy-start.2 = (bf16[16,32,768]{2,1,0:T(8,128)(2,1)}, bf16[16,32,768]{2,1,0:T(8,128)(2,1)S(1)}, u32[]{:S(2)}) copy-start(bf16[16,32,768]{2,1,0:T(8,128)(2,1)S(1)} %all-to-all-done.2) | copy-start | bytes 2359300
  65.3 22.0 %all-to-all-start.1 = ((bf16[16,32,768]{2,1,0:T(8,128)(2,1)}), bf16[16,32,768]{2,1,0:T(8,128)(2,1)S(1)}, u32[]{:S(2)}, u32[]{:S(2)}) async-start(bf16[16,32,768]{2,1,0:T(8,128)(2,1)} %bitcast.22), calls=%async_computation.1 | async-start | bytes 1572864 | tf_op jit(solution)/shard_map/all_to_all | solution.py:208
  87.3 17.7 %copy-start.3 = (bf16[16,32,768]{2,1,0:T(8,128)(2,1)}, bf16[16,32,768]{2,1,0:T(8,128)(2,1)S(1)}, u32[]{:S(2)}) copy-start(bf16[16,32,768]{2,1,0:T(8,128)(2,1)S(1)} %all-to-all-done.1) | copy-start | bytes 2359300
  87.3 23.3 %all-to-all-start.3 = ((bf16[16,32,768]{2,1,0:T(8,128)(2,1)}), bf16[16,32,768]{2,1,0:T(8,128)(2,1)S(1)}, u32[]{:S(2)}, u32[]{:S(2)}) async-start(bf16[16,32,768]{2,1,0:T(8,128)(2,1)} %bitcast.20), calls=%async_computation.3 | async-start | bytes 1572864 | tf_op jit(solution)/shard_map/all_to_all | solution.py:208
  107.7 6.1 %collective-permute-start.5 = (f32[2,128]{1,0:T(2,128)}, f32[2,128]{1,0:T(2,128)S(1)}, u32[]{:S(2)}, u32[]{:S(2)}) collective-permute-start(f32[2,128]{1,0:T(2,128)} %get-tuple-element.30), channel_id=1, source_target_pairs={{0,4},{4,0},{1,5},{5,1},{2,6},{6,2},{3,7},{7,3},{8,12},{12,8},{9,1... | collective-permute-start | bytes 3080 | tf_op jit(solution)/shard_map/ppermute | solution.py:204
  107.7 17.3 %collective-permute-start.3 = (bf16[128,768]{1,0:T(8,128)(2,1)}, bf16[128,768]{1,0:T(8,128)(2,1)S(1)}, u32[]{:S(2)}, u32[]{:S(2)}) collective-permute-start(bf16[128,768]{1,0:T(8,128)(2,1)} %get-tuple-element.24), channel_id=1, source_target_pairs={{0,4},{4,0},{1,5},{5,1},{2,6},{6,2},{3,7},{7,3},{8,12},{12,8},{9,1... | collective-permute-start | bytes 589832 | tf_op jit(solution)/shard_map/ppermute | solution.py:204
  110.6 0.9 copy-start
  113.8 14.9 %collective-permute-start.4 = (bf16[128,768]{1,0:T(8,128)(2,1)}, bf16[128,768]{1,0:T(8,128)(2,1)S(1)}, u32[]{:S(2)}, u32[]{:S(2)}) collective-permute-start(bf16[128,768]{1,0:T(8,128)(2,1)} %get-tuple-element.28), channel_id=1, source_target_pairs={{0,4},{4,0},{1,5},{5,1},{2,6},{6,2},{3,7},{7,3},{8,12},{12,8},{9,1... | collective-permute-start | bytes 589832 | tf_op jit(solution)/shard_map/ppermute | solution.py:204

commit v3 on v2

--- a/solution.py
+++ b/solution.py
@@ -12,7 +12,8 @@
 BF16 = jnp.bfloat16
 F32 = jnp.float32
 GROUP = ("row", "rest")
-VMEM_LIMIT = 56 * 1024 * 1024
+MIB = 1024 * 1024
+SUB = 256
 
 
 def dot(a, b, contract_a, contract_b):
@@ -104,22 +105,34 @@
     out_ref[...] = total.astype(BF16)
 
 
+def gelu_parts(v):
+    c = 0.7978845608028654
+    inner = c + (c * 0.044715) * (v * v)
+    s = 0.5 + 0.5 * jnp.tanh(v * inner)
+    hidden = v * s
+    slope = s + (hidden * (1.0 - s)) * (6.0 * inner - 4.0 * c)
+    return hidden.astype(BF16), slope.astype(BF16)
+
+
 def forward_kernel(x_ref, w_in_ref, w_out_ref, hidden_ref, slope_ref, out_ref, total):
     step = pl.program_id(0)
-    v = dot(x_ref[...], w_in_ref[...], 1, 0)
-    c = 0.7978845608028654
-    square = v * v
-    t = jnp.tanh(v * (c + (c * 0.044715) * square))
-    half = 0.5 + 0.5 * t
-    hidden = (v * half).astype(BF16)
-    slope_ref[...] = half + (0.5 * v) * (1.0 - t * t) * (c + (3 * c * 0.044715) * square)
-    hidden_ref[...] = hidden
 
     @pl.when(step == 0)
     def _():
         total[...] = jnp.zeros_like(total)
 
-    total[...] += dot(hidden, w_out_ref[...], 1, 0)
+    parts = hidden_ref.shape[1] // SUB
+    v = dot(x_ref[...], w_in_ref[:, :SUB], 1, 0)
+    pieces = []
+    for j in range(parts):
+        if j + 1 < parts:
+            after = dot(x_ref[...], w_in_ref[:, (j + 1) * SUB : (j + 2) * SUB], 1, 0)
+        hidden, slope = gelu_parts(v)
+        hidden_ref[:, j * SUB : (j + 1) * SUB] = hidden
+        slope_ref[:, j * SUB : (j + 1) * SUB] = slope
+        pieces.append(hidden)
+        v = after
+    total[...] += dot(jnp.concatenate(pieces, axis=1), w_out_ref[...], 1, 0)
 
     @pl.when(step == pl.num_programs(0) - 1)
     def _():
@@ -128,15 +141,20 @@
 
 def backward_kernel(cot_ref, w_in_ref, w_out_ref, slope_ref, grad_pre_ref, out_ref, total):
     step = pl.program_id(0)
-    grad_hidden = dot(cot_ref[...], w_out_ref[...], 1, 1)
-    grad_pre = (grad_hidden * slope_ref[...]).astype(BF16)
-    grad_pre_ref[...] = grad_pre
 
     @pl.when(step == 0)
     def _():
         total[...] = jnp.zeros_like(total)
 
-    total[...] += dot(grad_pre, w_in_ref[...], 1, 1)
+    parts = grad_pre_ref.shape[1] // SUB
+    pieces = []
+    for j in range(parts):
+        grad_hidden = dot(cot_ref[...], w_out_ref[j * SUB : (j + 1) * SUB, :], 1, 1)
+        slope = slope_ref[:, j * SUB : (j + 1) * SUB].astype(F32)
+        grad_pre = (grad_hidden * slope).astype(BF16)
+        grad_pre_ref[:, j * SUB : (j + 1) * SUB] = grad_pre
+        pieces.append(grad_pre)
+    total[...] += dot(jnp.concatenate(pieces, axis=1), w_in_ref[...], 1, 1)
 
     @pl.when(step == pl.num_programs(0) - 1)
     def _():
@@ -179,12 +197,20 @@
         out_ref[...] = dot(one_hot(mask), back_ref[...], 0, 0).astype(out_ref.dtype)
 
 
-def call(kernel, outs, flops=0, traffic=0, **options):
+def finish_kernel(
+    own_out, got_out, own_back, got_back, own_gates, got_gates, combined, grad_tokens, grad_gates
+):
+    combined[...] = (own_out[...] + got_out[...].astype(F32)).astype(BF16)
+    grad_tokens[...] = (own_back[...] + got_back[...].astype(F32)).astype(BF16)
+    grad_gates[...] = own_gates[...] + got_gates[...]
+
+
+def call(kernel, outs, flops=0, traffic=0, limit=12, **options):
     shapes = [jax.ShapeDtypeStruct(shape, dtype) for shape, dtype in outs]
     return pl.pallas_call(
         kernel,
         out_shape=shapes if len(shapes) > 1 else shapes[0],
-        compiler_params=pltpu.CompilerParams(vmem_limit_bytes=VMEM_LIMIT),
+        compiler_params=pltpu.CompilerParams(vmem_limit_bytes=limit * MIB),
         cost_estimate=pl.CostEstimate(flops=flops, bytes_accessed=traffic, transcendentals=0),
         **options,
     )
@@ -231,11 +257,11 @@
     )
     x = shuffle(sent)
     sent_cot = call(
-        place_cotangents_kernel, [slot_shape], 2 * place_flops, 2 * token_bytes + slot_bytes
+        place_cotangents_kernel, [slot_shape], 40 * place_flops, 2 * token_bytes + slot_bytes
     )(grad_output, partner_grad, own_meta, partner_meta)
     cot = shuffle(sent_cot)
 
-    chunk = 512
+    chunk = 1024
     steps = hidden_width // chunk
     whole = pl.BlockSpec((slot_total, width), lambda i: (0, 0))
     in_spec = pl.BlockSpec((None, width, chunk), lambda i: (0, 0, i))
@@ -247,9 +273,10 @@
     mid_count = slot_total * hidden_width
     hidden, slope, outputs = call(
         forward_kernel,
-        [(mid, BF16), (mid, F32), slot_shape],
+        [(mid, BF16), (mid, BF16), slot_shape],
         2 * product,
-        2 * slot_bytes + weight_bytes + 6 * mid_count,
+        2 * slot_bytes + weight_bytes + 4 * mid_count,
+        32,
         grid=(steps,),
         in_specs=[whole, in_spec, out_spec],
         out_specs=[mid_spec, mid_spec, whole],
@@ -260,7 +287,8 @@
         backward_kernel,
         [(mid, BF16), slot_shape],
         2 * product,
-        2 * slot_bytes + weight_bytes + 6 * mid_count,
+        2 * slot_bytes + weight_bytes + 4 * mid_count,
+        32,
         grid=(steps,),
         in_specs=[whole, in_spec, out_spec, mid_spec],
         out_specs=[mid_spec, whole],
@@ -275,22 +303,28 @@
         2 * place_flops,
         2 * token_bytes + slot_bytes,
     )(back_out, grad_output, partner_grad, own_meta, partner_meta)
+    grad_pre, partner_out, partner_gates = lax.optimization_barrier(
+        (grad_pre, partner_out, partner_gates)
+    )
     grad_in_w, grad_out_w = call(
         weights_kernel,
         [(weight_in.shape, BF16), (weight_out.shape, BF16)],
         2 * product,
         2 * slot_bytes + weight_bytes + 4 * mid_count,
+        32,
         grid=(steps,),
         in_specs=[whole, whole, mid_spec, mid_spec],
         out_specs=[in_spec, out_spec],
     )(x, cot, hidden, grad_pre)
-    combined = (own_out + exchange(partner_out).astype(F32)).astype(BF16)
-    grad_gates = (own_gates + exchange(partner_gates)).T
+    got_out, got_gates = exchange(partner_out), exchange(partner_gates)
     own_back, partner_back = call(
         pick_gradients_kernel, [own_shape, partner_shape], place_flops, slot_bytes + 3 * token_bytes
     )(back_grad, own_meta, partner_meta)
-    grad_tokens = (own_back + exchange(partner_back).astype(F32)).astype(BF16)
-    return (combined, grad_tokens, grad_gates, grad_in_w, grad_out_w)
+    got_back = exchange(partner_back)
+    combined, grad_tokens, grad_gates = call(
+        finish_kernel, [partner_shape, partner_shape, gates_shape], 0, 8 * token_bytes
+    )(own_out, got_out, own_back, got_back, own_gates, got_gates)
+    return (combined, grad_tokens, grad_gates.T, grad_in_w, grad_out_w)
 
 
 def solution(mesh):

time: 132 us -> 132 us (level)
  local copies, waits for them, and re-layouts: 2.26 us -> 31 us
  Pallas kernels: 59.1 us -> 35.6 us
  other arithmetic: 4.66 us -> 0 us
    unnamed x14 -> x40, local copies, waits for them, and re-layouts: 2.26 us -> 31 us
    ppermute x6, waiting for transfers between devices: 30.4 us -> 21.1 us  [exchange(): return lax.ppermute(values, 'half', swap)]
    all_to_all x4, waiting for transfers between devices: 0.01 us -> 8.79 us  [shuffle(): lax.all_to_all(shaped, GROUP, split_axis=0, concat_axis=0, tiled=True)]
    pallas_call x1, Pallas kernels: 16.8 us -> 9.13 us  [body(): call(backward_kernel, [(mid, BF16), slot_shape], 2 * product, 2 * slot_by...]
    pallas_call x2 -> x3, Pallas kernels: 20.6 us -> 14.4 us  [the longest x1 11.6 us: body(): call(forward_kernel, [(mid, BF16), (mid, BF16), slot_shape], 2 * product,...]
    convert_element_type x2 -> x0, other arithmetic: 3.42 us -> none  [the longest x1 1.72 us: body(): grad_tokens = (own_back + exchange(partner_back).astype(F32)).astype(BF16)]
    pallas_call x1, Pallas kernels: 12.5 us -> 9.16 us  [body(): call(weights_kernel, [(weight_in.shape, BF16), (weight_out.shape, BF16)],...]
    pallas_call x1, Pallas kernels: 2.72 us -> 0.81 us  [body(): call(pick_outputs_kernel, [own_shape, partner_shape, gates_shape, gates_s...]
  transfers between devices with their start and end apart: 10 -> 10, of which waited for: 4 -> 5; matrix products, arithmetic and copies ran while one was open for 2% -> 0% of each run, Pallas kernels for 43% -> 25%
where the time goes in v3:
time: 132 us; the launch traced here: 131 us
  Pallas kernels  35.6 us (27%)
  starting transfers between devices  33.3 us (25%)
  local copies, waits for them, and re-layouts  31 us (23%)
  waiting for transfers between devices  29.9 us (23%)
    unnamed x40, local copies, waits for them, and re-layouts  31 us
    all_to_all x4, starting transfers between devices, shuffle(): lax.all_to_all(shaped, GROUP, split_axis=0, concat_axis=0, tiled=True)  22.8 us
    ppermute x6, waiting for transfers between devices, exchange(): return lax.ppermute(values, 'half', swap)  21.1 us
    pallas_call x1, Pallas kernels, body(): call(forward_kernel, [(mid, BF16), (mid, BF16), slot_shape], 2 * product,...  11.6 us
    ppermute x6, starting transfers between devices, exchange(): return lax.ppermute(values, 'half', swap)  10.6 us
    pallas_call x1, Pallas kernels, body(): call(weights_kernel, [(weight_in.shape, BF16), (weight_out.shape, BF16)],...  9.16 us
    pallas_call x1, Pallas kernels, body(): call(backward_kernel, [(mid, BF16), slot_shape], 2 * product, 2 * slot_by...  9.13 us
    all_to_all x4, waiting for transfers between devices, shuffle(): lax.all_to_all(shaped, GROUP, split_axis=0, concat_axis=0, tiled=True)  8.79 us
  transfers between devices with their start and end apart: 10, of which 5 were waited for; matrix products, arithmetic and copies ran while one was open for 0% of the time, Pallas kernels for 25%

profile of v3, /device:TPU:0, one launch (start us, length us, event | category | flops | bytes accessed | tf_op | source)
XLA Modules:
  0.0 130.6 jit_solution(6321148123256219030)
XLA Ops:
  0.6 4.1 %collective-permute-start = (bf16[128,768]{1,0:T(8,128)(2,1)}, bf16[128,768]{1,0:T(8,128)(2,1)S(1)}, u32[]{:S(2)}, u32[]{:S(2)}) collective-permute-start(bf16[128,768]{1,0:T(8,128)(2,1)} %own_ref.2), channel_id=1, source_target_pairs={{0,4},{4,0},{1,5},{5,1},{2,6},{6,2},{3,7},{7,3},{8,12},{12,8},{9,1... | collective-permute-start | bytes 589832 | tf_op jit(solution)/shard_map/ppermute | solution.py:230
  4.7 0.0 copy-start.2
  4.7 0.7 copy-done.2
  5.4 0.0 copy-start.3
  5.4 0.7 copy-done.3
  6.1 0.0 copy-start.4
  6.1 0.7 copy-done.4
  6.8 0.1 shard_map.110
  6.9 0.1 collective-permute-start.1
  7.0 7.3 %collective-permute-done.1.partner_meta = f32[8,128]{1,0:T(8,128)S(1)} collective-permute-done((f32[8,128]{1,0:T(8,128)S(1)}, f32[8,128]{1,0:T(8,128)S(1)}, u32[]{:S(2)}, u32[]{:S(2)}) %collective-permute-start.1) | collective-permute-done | bytes 4128 | tf_op jit(solution)/shard_map/ppermute | solution.py:230
  14.2 0.0 collective-permute-done.partner_ref
  14.2 0.0 copy-start.1
  14.2 0.9 copy-done.1
  15.2 1.6 %shard_map.111 = bf16[512,768]{1,0:T(8,128)(2,1)} custom-call(bf16[128,768]{1,0:T(8,128)(2,1)S(1)} %copy-done.1, bf16[128,768]{1,0:T(8,128)(2,1)S(1)} %collective-permute-done.partner_ref, f32[8,128]{1,0:T(8,128)S(1)} %get-tuple-element.26.own_meta, f32[8,128]{1,0:T(8,128)S(1)} %collective-permute-done.1.partner_meta), custom_call_target="tpu_custom_call" | custom-call | flops 201326592 | bytes 1179648 | tf_op jit(solution)/shard_map/pallas_call | solution.py:255
  16.8 4.0 %all-to-all-start = ((bf16[16,32,768]{2,1,0:T(8,128)(2,1)}), bf16[16,32,768]{2,1,0:T(8,128)(2,1)S(1)}, u32[]{:S(2)}, u32[]{:S(2)}) async-start(bf16[16,32,768]{2,1,0:T(8,128)(2,1)} %bitcast.4), calls=%async_computation | async-start | bytes 1572864 | tf_op jit(solution)/shard_map/all_to_all | solution.py:234
  20.9 3.4 %collective-permute-start.2 = (bf16[128,768]{1,0:T(8,128)(2,1)}, bf16[128,768]{1,0:T(8,128)(2,1)S(1)}, u32[]{:S(2)}, u32[]{:S(2)}) collective-permute-start(bf16[128,768]{1,0:T(8,128)(2,1)} %own_ref.3), channel_id=1, source_target_pairs={{0,4},{4,0},{1,5},{5,1},{2,6},{6,2},{3,7},{7,3},{8,12},{12,8},{9,1... | collective-permute-start | bytes 589832 | tf_op jit(solution)/shard_map/ppermute | solution.py:230
  24.2 10.4 %collective-permute-done.2.partner_grad.partner_ref = bf16[128,768]{1,0:T(8,128)(2,1)S(1)} collective-permute-done((bf16[128,768]{1,0:T(8,128)(2,1)}, bf16[128,768]{1,0:T(8,128)(2,1)S(1)}, u32[]{:S(2)}, u32[]{:S(2)}) %collective-permute-start.2) | collective-permute-done | bytes 196640 | tf_op jit(solution)/shard_map/ppermute | solution.py:230
  34.7 0.0 copy-start.9
  34.7 0.9 copy-done.9
  35.6 0.0 copy-start.11
  35.6 2.0 %shard_map.114 = bf16[512,768]{1,0:T(8,128)(2,1)} custom-call(bf16[128,768]{1,0:T(8,128)(2,1)S(1)} %copy-done.9, bf16[128,768]{1,0:T(8,128)(2,1)S(1)} %collective-permute-done.2.partner_grad.partner_ref, f32[8,128]{1,0:T(8,128)S(1)} %get-tuple-element.26.own_meta, f32[8,128]{1,0:T(8,128)S(1)} %collective-permute-done.1.partner_meta), custom_call_target="tpu_custom_call" | custom-call | flops 8053063680 | bytes 1179648 | tf_op jit(solution)/shard_map/pallas_call | solution.py:259
  37.6 0.0 copy-done.11
  37.6 0.0 all-to-all-done
  37.6 8.5 %all-to-all-start.2 = ((bf16[16,32,768]{2,1,0:T(8,128)(2,1)}), bf16[16,32,768]{2,1,0:T(8,128)(2,1)S(1)}, u32[]{:S(2)}, u32[]{:S(2)}) async-start(bf16[16,32,768]{2,1,0:T(8,128)(2,1)} %bitcast.8), calls=%async_computation.2 | async-start | bytes 1572864 | tf_op jit(solution)/shard_map/all_to_all | solution.py:234
  46.1 0.0 copy-start.5
  46.1 2.8 %copy-done.5 = bf16[1,768,4096]{2,1,0:T(8,128)(2,1)S(1)} copy-done((bf16[1,768,4096]{2,1,0:T(8,128)(2,1)S(1)}, bf16[1,768,4096]{2,1,0:T(8,128)(2,1)}, u32[]{:S(2)}) %copy-start.5) | copy-done | bytes 6291480
  48.9 0.0 copy-start.7
  48.9 2.8 %copy-done.7 = bf16[1,4096,768]{2,1,0:T(8,128)(2,1)S(1)} copy-done((bf16[1,4096,768]{2,1,0:T(8,128)(2,1)S(1)}, bf16[1,4096,768]{2,1,0:T(8,128)(2,1)}, u32[]{:S(2)}) %copy-start.7) | copy-done | bytes 6291480
  51.7 11.6 %shard_map.112 = (bf16[512,4096]{1,0:T(8,128)(2,1)S(1)}, bf16[512,4096]{1,0:T(8,128)(2,1)S(1)}, bf16[512,768]{1,0:T(8,128)(2,1)}) custom-call(bf16[512,768]{1,0:T(8,128)(2,1)S(1)} %bitcast.14, bf16[1,768,4096]{2,1,0:T(8,128)(2,1)S(1)} %copy-done.5, bf16[1,4096,768]{2,1,0:T(8,128)(2,1)S(1)} %copy-done.7), custom_call_target="tpu_custom_call" | custom-call | flops 6442450944 | bytes 22544384 | tf_op jit(solution)/shard_map/pallas_call | solution.py:274
  63.2 0.0 copy-start.16
  63.3 2.0 %copy-done.16 = bf16[512,4096]{1,0:T(8,128)(2,1)} copy-done((bf16[512,4096]{1,0:T(8,128)(2,1)}, bf16[512,4096]{1,0:T(8,128)(2,1)S(1)}, u32[]{:S(2)}) %copy-start.16) | copy-done | bytes 4194328
  65.3 0.0 copy-start.18
  65.3 2.0 %copy-done.18 = bf16[512,4096]{1,0:T(8,128)(2,1)} copy-done((bf16[512,4096]{1,0:T(8,128)(2,1)}, bf16[512,4096]{1,0:T(8,128)(2,1)S(1)}, u32[]{:S(2)}) %copy-start.18) | copy-done | bytes 4194328
  67.3 0.0 all-to-all-done.2
  67.3 5.1 %all-to-all-start.1 = ((bf16[16,32,768]{2,1,0:T(8,128)(2,1)}), bf16[16,32,768]{2,1,0:T(8,128)(2,1)S(1)}, u32[]{:S(2)}, u32[]{:S(2)}) async-start(bf16[16,32,768]{2,1,0:T(8,128)(2,1)} %bitcast.6), calls=%async_computation.1 | async-start | bytes 1572864 | tf_op jit(solution)/shard_map/all_to_all | solution.py:234
  72.4 0.0 copy-start.6
  72.4 2.8 %copy-done.6 = bf16[1,768,4096]{2,1,0:T(8,128)(2,1)S(1)} copy-done((bf16[1,768,4096]{2,1,0:T(8,128)(2,1)S(1)}, bf16[1,768,4096]{2,1,0:T(8,128)(2,1)}, u32[]{:S(2)}) %copy-start.6) | copy-done | bytes 6291480
  75.2 0.0 copy-start.8
  75.2 2.8 %copy-done.8 = bf16[1,4096,768]{2,1,0:T(8,128)(2,1)S(1)} copy-done((bf16[1,4096,768]{2,1,0:T(8,128)(2,1)S(1)}, bf16[1,4096,768]{2,1,0:T(8,128)(2,1)}, u32[]{:S(2)}) %copy-start.8) | copy-done | bytes 6291480
  78.0 2.2 %copy-done.17 = bf16[512,4096]{1,0:T(8,128)(2,1)S(1)} copy-done((bf16[512,4096]{1,0:T(8,128)(2,1)S(1)}, bf16[512,4096]{1,0:T(8,128)(2,1)}, u32[]{:S(2)}) %copy-start.17) | copy-done | bytes 4194328
  80.2 9.1 %shard_map.115 = (bf16[512,4096]{1,0:T(8,128)(2,1)S(1)}, bf16[512,768]{1,0:T(8,128)(2,1)S(1)}) custom-call(bf16[512,768]{1,0:T(8,128)(2,1)S(1)} %bitcast.16, bf16[1,768,4096]{2,1,0:T(8,128)(2,1)S(1)} %copy-done.6, bf16[1,4096,768]{2,1,0:T(8,128)(2,1)S(1)} %copy-done.8, bf16[512,4096]{1,0:T(8,128)(2,1)S(1)} %copy-done.17), custom_call_target="tpu_custom_call" | custom-call | flops 6442450944 | bytes 22544384 | tf_op jit(solution)/shard_map/pallas_call | solution.py:286
  89.3 0.0 copy-start
  89.3 0.9 copy-done
  90.2 2.0 %copy-done.14 = bf16[512,4096]{1,0:T(8,128)(2,1)} copy-done((bf16[512,4096]{1,0:T(8,128)(2,1)}, bf16[512,4096]{1,0:T(8,128)(2,1)S(1)}, u32[]{:S(2)}) %copy-start.14) | copy-done | bytes 4194328
  92.2 0.0 all-to-all-done.1
  92.2 5.1 %all-to-all-start.3 = ((bf16[16,32,768]{2,1,0:T(8,128)(2,1)}), bf16[16,32,768]{2,1,0:T(8,128)(2,1)S(1)}, u32[]{:S(2)}, u32[]{:S(2)}) async-start(bf16[16,32,768]{2,1,0:T(8,128)(2,1)} %bitcast.19), calls=%async_computation.3 | async-start | bytes 1572864 | tf_op jit(solution)/shard_map/all_to_all | solution.py:234
  97.3 0.0 copy-start.10
  97.3 0.9 copy-done.10
  98.3 0.9 copy-done.12
  99.2 0.8 shard_map.113
  100.0 0.0 copy-start.13
  100.0 0.7 copy-done.13
  100.7 0.0 collective-permute-start.5
  100.7 8.8 %all-to-all-done.3 = bf16[16,32,768]{2,1,0:T(8,128)(2,1)S(1)} async-done(((bf16[16,32,768]{2,1,0:T(8,128)(2,1)}), bf16[16,32,768]{2,1,0:T(8,128)(2,1)S(1)}, u32[]{:S(2)}, u32[]{:S(2)}) %all-to-all-start.3) | async-done | bytes 786464 | tf_op jit(solution)/shard_map/all_to_all | solution.py:234
  109.5 0.4 shard_map.116
  109.9 0.1 collective-permute-start.4
  109.9 2.9 %collective-permute-start.3 = (bf16[128,768]{1,0:T(8,128)(2,1)}, bf16[128,768]{1,0:T(8,128)(2,1)S(1)}, u32[]{:S(2)}, u32[]{:S(2)}) collective-permute-start(bf16[128,768]{1,0:T(8,128)(2,1)} %copy-done.13), channel_id=1, source_target_pairs={{0,4},{4,0},{1,5},{5,1},{2,6},{6,2},{3,7},{7,3},{8,12},{12,8},{9,1... | collective-permute-start | bytes 589832 | tf_op jit(solution)/shard_map/ppermute | solution.py:230
  112.9 2.2 %copy-done.15 = bf16[512,4096]{1,0:T(8,128)(2,1)S(1)} copy-done((bf16[512,4096]{1,0:T(8,128)(2,1)S(1)}, bf16[512,4096]{1,0:T(8,128)(2,1)}, u32[]{:S(2)}) %copy-start.15) | copy-done | bytes 4194328
  115.0 2.2 %copy-done.19 = bf16[512,4096]{1,0:T(8,128)(2,1)S(1)} copy-done((bf16[512,4096]{1,0:T(8,128)(2,1)S(1)}, bf16[512,4096]{1,0:T(8,128)(2,1)}, u32[]{:S(2)}) %copy-start.19) | copy-done | bytes 4194328
  117.2 9.2 %shard_map.118 = (bf16[1,768,4096]{2,1,0:T(8,128)(2,1)}, bf16[1,4096,768]{2,1,0:T(8,128)(2,1)}) custom-call(bf16[512,768]{1,0:T(8,128)(2,1)S(1)} %bitcast.15, bf16[512,768]{1,0:T(8,128)(2,1)S(1)} %bitcast.17, bf16[512,4096]{1,0:T(8,128)(2,1)S(1)} %copy-done.19, bf16[512,4096]{1,0:T(8,128)(2,1)S(1)} %copy-done.15), custom_call_target="tpu_custom_call" | custom-call | flops 6442450944 | bytes 22544384 | tf_op jit(solution)/shard_map/pallas_call | solution.py:309
  126.4 0.0 collective-permute-done.5.got_gates
  126.4 0.3 collective-permute-done.4.got_back
  126.7 3.1 %collective-permute-done.3.got_out = bf16[128,768]{1,0:T(8,128)(2,1)S(1)} collective-permute-done((bf16[128,768]{1,0:T(8,128)(2,1)}, bf16[128,768]{1,0:T(8,128)(2,1)S(1)}, u32[]{:S(2)}, u32[]{:S(2)}) %collective-permute-start.3) | collective-permute-done | bytes 196640 | tf_op jit(solution)/shard_map/ppermute | solution.py:230
  129.8 0.8 shard_map.117
  (5 shorter events, 0.0 us)
Async XLA Ops:
  0.6 13.6 %collective-permute-start = (bf16[128,768]{1,0:T(8,128)(2,1)}, bf16[128,768]{1,0:T(8,128)(2,1)S(1)}, u32[]{:S(2)}, u32[]{:S(2)}) collective-permute-start(bf16[128,768]{1,0:T(8,128)(2,1)} %own_ref.2), channel_id=1, source_target_pairs={{0,4},{4,0},{1,5},{5,1},{2,6},{6,2},{3,7},{7,3},{8,12},{12,8},{9,1... | collective-permute-start | bytes 589832 | tf_op jit(solution)/shard_map/ppermute | solution.py:230
  4.7 0.7 copy-start.2
  5.4 0.7 copy-start.3
  6.1 0.7 copy-start.4
  6.9 7.3 %collective-permute-start.1 = (f32[8,128]{1,0:T(8,128)S(1)}, f32[8,128]{1,0:T(8,128)S(1)}, u32[]{:S(2)}, u32[]{:S(2)}) collective-permute-start(f32[8,128]{1,0:T(8,128)S(1)} %get-tuple-element.27), channel_id=1, source_target_pairs={{0,4},{4,0},{1,5},{5,1},{2,6},{6,2},{3,7},{7,3},{8,12},{12,8},{9,1... | collective-permute-start | bytes 12296 | tf_op jit(solution)/shard_map/ppermute | solution.py:230
  14.2 0.9 copy-start.1
  16.8 20.8 %all-to-all-start = ((bf16[16,32,768]{2,1,0:T(8,128)(2,1)}), bf16[16,32,768]{2,1,0:T(8,128)(2,1)S(1)}, u32[]{:S(2)}, u32[]{:S(2)}) async-start(bf16[16,32,768]{2,1,0:T(8,128)(2,1)} %bitcast.4), calls=%async_computation | async-start | bytes 1572864 | tf_op jit(solution)/shard_map/all_to_all | solution.py:234
  20.9 13.8 %collective-permute-start.2 = (bf16[128,768]{1,0:T(8,128)(2,1)}, bf16[128,768]{1,0:T(8,128)(2,1)S(1)}, u32[]{:S(2)}, u32[]{:S(2)}) collective-permute-start(bf16[128,768]{1,0:T(8,128)(2,1)} %own_ref.3), channel_id=1, source_target_pairs={{0,4},{4,0},{1,5},{5,1},{2,6},{6,2},{3,7},{7,3},{8,12},{12,8},{9,1... | collective-permute-start | bytes 589832 | tf_op jit(solution)/shard_map/ppermute | solution.py:230
  34.7 0.9 copy-start.9
  35.6 2.0 %copy-start.11 = (bf16[128,768]{1,0:T(8,128)(2,1)}, bf16[128,768]{1,0:T(8,128)(2,1)S(1)}, u32[]{:S(2)}) copy-start(bf16[128,768]{1,0:T(8,128)(2,1)S(1)} %collective-permute-done.2.partner_grad.partner_ref) | copy-start | bytes 589828
  37.6 29.7 %all-to-all-start.2 = ((bf16[16,32,768]{2,1,0:T(8,128)(2,1)}), bf16[16,32,768]{2,1,0:T(8,128)(2,1)S(1)}, u32[]{:S(2)}, u32[]{:S(2)}) async-start(bf16[16,32,768]{2,1,0:T(8,128)(2,1)} %bitcast.8), calls=%async_computation.2 | async-start | bytes 1572864 | tf_op jit(solution)/shard_map/all_to_all | solution.py:234
  46.1 2.8 %copy-start.5 = (bf16[1,768,4096]{2,1,0:T(8,128)(2,1)S(1)}, bf16[1,768,4096]{2,1,0:T(8,128)(2,1)}, u32[]{:S(2)}) copy-start(bf16[1,768,4096]{2,1,0:T(8,128)(2,1)} %w_in_ref.3) | copy-start | bytes 18874372
  48.9 2.8 %copy-start.7 = (bf16[1,4096,768]{2,1,0:T(8,128)(2,1)S(1)}, bf16[1,4096,768]{2,1,0:T(8,128)(2,1)}, u32[]{:S(2)}) copy-start(bf16[1,4096,768]{2,1,0:T(8,128)(2,1)} %w_out_ref.3) | copy-start | bytes 18874372
  63.2 2.0 %copy-start.16 = (bf16[512,4096]{1,0:T(8,128)(2,1)}, bf16[512,4096]{1,0:T(8,128)(2,1)S(1)}, u32[]{:S(2)}) copy-start(bf16[512,4096]{1,0:T(8,128)(2,1)S(1)} %get-tuple-element.30.slope_ref) | copy-start | bytes 12582916
  65.3 2.0 %copy-start.18 = (bf16[512,4096]{1,0:T(8,128)(2,1)}, bf16[512,4096]{1,0:T(8,128)(2,1)S(1)}, u32[]{:S(2)}) copy-start(bf16[512,4096]{1,0:T(8,128)(2,1)S(1)} %get-tuple-element.43.hidden_ref) | copy-start | bytes 12582916
  67.3 24.9 %all-to-all-start.1 = ((bf16[16,32,768]{2,1,0:T(8,128)(2,1)}), bf16[16,32,768]{2,1,0:T(8,128)(2,1)S(1)}, u32[]{:S(2)}, u32[]{:S(2)}) async-start(bf16[16,32,768]{2,1,0:T(8,128)(2,1)} %bitcast.6), calls=%async_computation.1 | async-start | bytes 1572864 | tf_op jit(solution)/shard_map/all_to_all | solution.py:234
  72.4 2.8 %copy-start.6 = (bf16[1,768,4096]{2,1,0:T(8,128)(2,1)S(1)}, bf16[1,768,4096]{2,1,0:T(8,128)(2,1)}, u32[]{:S(2)}) copy-start(bf16[1,768,4096]{2,1,0:T(8,128)(2,1)} %w_in_ref.3) | copy-start | bytes 18874372
  75.2 2.8 %copy-start.8 = (bf16[1,4096,768]{2,1,0:T(8,128)(2,1)S(1)}, bf16[1,4096,768]{2,1,0:T(8,128)(2,1)}, u32[]{:S(2)}) copy-start(bf16[1,4096,768]{2,1,0:T(8,128)(2,1)} %w_out_ref.3) | copy-start | bytes 18874372
  78.0 2.2 %copy-start.17 = (bf16[512,4096]{1,0:T(8,128)(2,1)S(1)}, bf16[512,4096]{1,0:T(8,128)(2,1)}, u32[]{:S(2)}) copy-start(bf16[512,4096]{1,0:T(8,128)(2,1)} %copy-done.16) | copy-start | bytes 12582916
  89.3 0.9 copy-start
  90.2 2.0 %copy-start.14 = (bf16[512,4096]{1,0:T(8,128)(2,1)}, bf16[512,4096]{1,0:T(8,128)(2,1)S(1)}, u32[]{:S(2)}) copy-start(bf16[512,4096]{1,0:T(8,128)(2,1)S(1)} %get-tuple-element.44.grad_pre_ref) | copy-start | bytes 12582916
  92.2 17.2 %all-to-all-start.3 = ((bf16[16,32,768]{2,1,0:T(8,128)(2,1)}), bf16[16,32,768]{2,1,0:T(8,128)(2,1)S(1)}, u32[]{:S(2)}, u32[]{:S(2)}) async-start(bf16[16,32,768]{2,1,0:T(8,128)(2,1)} %bitcast.19), calls=%async_computation.3 | async-start | bytes 1572864 | tf_op jit(solution)/shard_map/all_to_all | solution.py:234
  97.3 0.9 copy-start.10
  98.2 0.9 copy-start.12
  100.0 0.7 copy-start.13
  100.7 25.7 %collective-permute-start.5 = (f32[2,128]{1,0:T(2,128)S(1)}, f32[2,128]{1,0:T(2,128)S(1)}, u32[]{:S(2)}, u32[]{:S(2)}) collective-permute-start(f32[2,128]{1,0:T(2,128)S(1)} %get-tuple-element.39), channel_id=1, source_target_pairs={{0,4},{4,0},{1,5},{5,1},{2,6},{6,2},{3,7},{7,3},{8,12},{12,8},{9,1... | collective-permute-start | bytes 3080 | tf_op jit(solution)/shard_map/ppermute | solution.py:230
  109.9 16.9 %collective-permute-start.4 = (bf16[128,768]{1,0:T(8,128)(2,1)S(1)}, bf16[128,768]{1,0:T(8,128)(2,1)S(1)}, u32[]{:S(2)}, u32[]{:S(2)}) collective-permute-start(bf16[128,768]{1,0:T(8,128)(2,1)S(1)} %get-tuple-element.37), channel_id=1, source_target_pairs={{0,4},{4,0},{1,5},{5,1},{2,6},{6,2},{3,7},{7,3},{8,12},{12,8},{9,1... | collective-permute-start | bytes 589832 | tf_op jit(solution)/shard_map/ppermute | solution.py:230
  109.9 19.9 %collective-permute-start.3 = (bf16[128,768]{1,0:T(8,128)(2,1)}, bf16[128,768]{1,0:T(8,128)(2,1)S(1)}, u32[]{:S(2)}, u32[]{:S(2)}) collective-permute-start(bf16[128,768]{1,0:T(8,128)(2,1)} %copy-done.13), channel_id=1, source_target_pairs={{0,4},{4,0},{1,5},{5,1},{2,6},{6,2},{3,7},{7,3},{8,12},{12,8},{9,1... | collective-permute-start | bytes 589832 | tf_op jit(solution)/shard_map/ppermute | solution.py:230
  112.9 2.2 %copy-start.15 = (bf16[512,4096]{1,0:T(8,128)(2,1)S(1)}, bf16[512,4096]{1,0:T(8,128)(2,1)}, u32[]{:S(2)}) copy-start(bf16[512,4096]{1,0:T(8,128)(2,1)} %copy-done.14) | copy-start | bytes 12582916
  115.0 2.2 %copy-start.19 = (bf16[512,4096]{1,0:T(8,128)(2,1)S(1)}, bf16[512,4096]{1,0:T(8,128)(2,1)}, u32[]{:S(2)}) copy-start(bf16[512,4096]{1,0:T(8,128)(2,1)} %copy-done.18) | copy-start | bytes 12582916

commit v4 on v3

v4 whole, which is shorter than its diff:
```python
import functools

import jax
import jax.numpy as jnp
from jax import lax
from jax.experimental import pallas as pl
from jax.experimental.pallas import tpu as pltpu
from jax.sharding import Mesh
from jax.sharding import PartitionSpec as P

BLOCK = 128
BF16 = jnp.bfloat16
F32 = jnp.float32
GROUP = ("row", "rest")
MIB = 1024 * 1024
SUB = 256


def dot(a, b, contract_a, contract_b):
    return lax.dot_general(
        a, b, (((contract_a,), (contract_b,)), ((), ())), preferred_element_type=F32
    )


def column(row):
    count = row.shape[1]
    return jnp.transpose(jnp.broadcast_to(row, (count, count)))


def route_kernel(rest_bits, capacity, place_ref, ids_ref, keep_ref, gates_ref, mine_ref, other_ref):
    token_rows = ids_ref.shape[1]
    ids = ids_ref[...].astype(F32)
    earlier = lax.broadcasted_iota(jnp.int32, (token_rows, token_rows), 0) < lax.broadcasted_iota(
        jnp.int32, (token_rows, token_rows), 1
    )
    columns = (column(ids[0:1]), column(ids[1:2]))
    half, member = place_ref[0], place_ref[1]
    for k in range(2):
        count = jnp.zeros((token_rows, token_rows), F32)
        for other_choice in columns:
            count = count + jnp.where(earlier & (other_choice == ids[k : k + 1]), 1.0, 0.0)
        slot = jnp.sum(count, axis=0, keepdims=True).astype(jnp.int32)
        expert = ids_ref[k : k + 1, :]
        kept = keep_ref[k : k + 1, :] > 0
        side = (expert >> rest_bits) & 1
        local = ((expert >> (rest_bits + 1)) << rest_bits) + (expert & ((1 << rest_bits) - 1))
        base = (local ^ member) * (2 * capacity) + slot
        here = kept & (side == half)
        there = kept & (side != half)
        mine_ref[k : k + 1, :] = jnp.where(here, base, -1).astype(F32)
        other_ref[k : k + 1, :] = jnp.where(there, base + capacity, -1).astype(F32)
        mine_ref[k + 2 : k + 3, :] = gates_ref[k : k + 1, :]
        other_ref[k + 2 : k + 3, :] = gates_ref[k : k + 1, :]
    mine_ref[4:8, :] = jnp.zeros((4, token_rows), F32)
    other_ref[4:8, :] = jnp.zeros((4, token_rows), F32)


def hits(slot_total, meta_ref, k):
    rows = meta_ref[k : k + 1, :].astype(jnp.int32)
    index = lax.broadcasted_iota(jnp.int32, (slot_total, rows.shape[1]), 0)
    return index == rows


def one_hot(mask):
    return jnp.where(mask, 1.0, 0.0).astype(BF16)


def restore(tokens_ref):
    pieces = []
    for b in range(tokens_ref.shape[1] // BLOCK):
        x = tokens_ref[:, b * BLOCK : (b + 1) * BLOCK].astype(F32)
        scale = (jnp.max(jnp.abs(x), axis=1, keepdims=True) + 1e-06).astype(BF16).astype(F32)
        quantized = (x / scale).astype(BF16)
        pieces.append((quantized.astype(F32) * scale).astype(BF16))
    return jnp.concatenate(pieces, axis=1)


def split(values, out_refs):
    rows = out_refs[0].shape[0]
    for d, out_ref in enumerate(out_refs):
        out_ref[...] = values[d * rows : (d + 1) * rows, :]


def join(refs):
    return jnp.concatenate([ref[...] for ref in refs], axis=0)


def place_tokens_kernel(own_ref, partner_ref, own_meta, partner_meta, *out_refs):
    slot_total = len(out_refs) * out_refs[0].shape[0]
    total = None
    for tokens_ref, meta in ((own_ref, own_meta), (partner_ref, partner_meta)):
        mask = hits(slot_total, meta, 0) | hits(slot_total, meta, 1)
        part = dot(one_hot(mask), restore(tokens_ref), 1, 0)
        total = part if total is None else total + part
    split(total.astype(BF16), out_refs)


def scaled_rows(gate_row, grad_ref):
    gate = column(gate_row)
    pieces = [
        gate * grad_ref[:, b * BLOCK : (b + 1) * BLOCK].astype(F32)
        for b in range(grad_ref.shape[1] // BLOCK)
    ]
    return jnp.concatenate(pieces, axis=1)


def place_cotangents_kernel(own_ref, partner_ref, own_meta, partner_meta, *out_refs):
    slot_total = len(out_refs) * out_refs[0].shape[0]
    total = None
    for grad_ref, meta in ((own_ref, own_meta), (partner_ref, partner_meta)):
        for k in range(2):
            rows = scaled_rows(meta[k + 2 : k + 3, :], grad_ref).astype(BF16)
            part = dot(one_hot(hits(slot_total, meta, k)), rows, 1, 0)
            total = part if total is None else total + part
    split(total.astype(BF16), out_refs)


def gelu_parts(v):
    c = 0.7978845608028654
    inner = c + (c * 0.044715) * (v * v)
    s = 0.5 + 0.5 * jnp.tanh(v * inner)
    hidden = v * s
    slope = s + (hidden * (1.0 - s)) * (6.0 * inner - 4.0 * c)
    return hidden.astype(BF16), slope.astype(BF16)


def stream(step, chunk, width, slots, refs, kinds):
    specs = {
        "wide": pl.BlockSpec((None, width, chunk), lambda i: (0, 0, i)),
        "tall": pl.BlockSpec((None, chunk, width), lambda i: (0, i, 0)),
        "middle": pl.BlockSpec((slots, chunk), lambda i: (0, i)),
    }
    ins, outs = kinds
    steps = refs[0].shape[2] // chunk
    pltpu.emit_pipeline(
        step,
        grid=(steps,),
        in_specs=[specs[kind] for kind in ins],
        out_specs=[specs[kind] for kind in outs],
    )(*refs)


def forward_kernel(pieces, chunk, *refs):
    x_pieces, (w_in, w_out) = refs[:pieces], refs[pieces : pieces + 2]
    out_pieces = refs[pieces + 2 : 2 * pieces + 2]
    x, hidden_all, slope_all, total = refs[2 * pieces + 2 :]
    x[...] = join(x_pieces)
    total[...] = jnp.zeros_like(total)

    def step(w_in_ref, w_out_ref, hidden_ref, slope_ref):
        parts = chunk // SUB
        v = dot(x[...], w_in_ref[:, :SUB], 1, 0)
        done = []
        for j in range(parts):
            if j + 1 < parts:
                after = dot(x[...], w_in_ref[:, (j + 1) * SUB : (j + 2) * SUB], 1, 0)
            hidden, slope = gelu_parts(v)
            hidden_ref[:, j * SUB : (j + 1) * SUB] = hidden
            slope_ref[:, j * SUB : (j + 1) * SUB] = slope
            done.append(hidden)
            v = after
        total[...] += dot(jnp.concatenate(done, axis=1), w_out_ref[...], 1, 0)

    stream(
        step,
        chunk,
        x.shape[1],
        x.shape[0],
        (w_in, w_out, hidden_all, slope_all),
        (("wide", "tall"), ("middle", "middle")),
    )
    split(total[...].astype(BF16), out_pieces)


def backward_kernel(pieces, chunk, *refs):
    cot_pieces, (w_in, w_out, slope_all) = refs[:pieces], refs[pieces : pieces + 3]
    out_pieces = refs[pieces + 3 : 2 * pieces + 3]
    cot, grad_pre_all, total = refs[2 * pieces + 3 :]
    cot[...] = join(cot_pieces)
    total[...] = jnp.zeros_like(total)

    def step(w_in_ref, w_out_ref, slope_ref, grad_pre_ref):
        done = []
        for j in range(chunk // SUB):
            grad_hidden = dot(cot[...], w_out_ref[j * SUB : (j + 1) * SUB, :], 1, 1)
            slope = slope_ref[:, j * SUB : (j + 1) * SUB].astype(F32)
            grad_pre = (grad_hidden * slope).astype(BF16)
            grad_pre_ref[:, j * SUB : (j + 1) * SUB] = grad_pre
            done.append(grad_pre)
        total[...] += dot(jnp.concatenate(done, axis=1), w_in_ref[...], 1, 1)

    stream(
        step,
        chunk,
        cot.shape[1],
        cot.shape[0],
        (w_in, w_out, slope_all, grad_pre_all),
        (("wide", "tall", "middle"), ("middle",)),
    )
    split(total[...].astype(BF16), out_pieces)


def weights_kernel(chunk, x, cot, hidden_all, grad_pre_all, grad_in_all, grad_out_all):
    def step(hidden_ref, grad_pre_ref, grad_in_ref, grad_out_ref):
        grad_in_ref[...] = dot(x[...], grad_pre_ref[...], 0, 0).astype(BF16)
        grad_out_ref[...] = dot(hidden_ref[...], cot[...], 0, 0).astype(BF16)

    slots, width = x.shape
    pltpu.emit_pipeline(
        step,
        grid=(hidden_all.shape[1] // chunk,),
        in_specs=[pl.BlockSpec((slots, chunk), lambda i: (0, i))] * 2,
        out_specs=[
            pl.BlockSpec((None, width, chunk), lambda i: (0, 0, i)),
            pl.BlockSpec((None, chunk, width), lambda i: (0, i, 0)),
        ],
    )(hidden_all, grad_pre_all, grad_in_all, grad_out_all)


def pick_outputs_kernel(pieces, *refs):
    back = join(refs[:pieces])
    own_grad, partner_grad, own_meta, partner_meta = refs[pieces : pieces + 4]
    own_out, partner_out, own_gates, partner_gates = refs[pieces + 4 :]
    slot_total = back.shape[0]
    for grad_ref, meta, out_ref, gates_ref in (
        (own_grad, own_meta, own_out, own_gates),
        (partner_grad, partner_meta, partner_out, partner_gates),
    ):
        total = None
        for k in range(2):
            picked = dot(one_hot(hits(slot_total, meta, k)), back, 0, 0)
            gate = column(meta[k + 2 : k + 3, :])
            weighted = jnp.concatenate(
                [
                    gate * picked[:, b * BLOCK : (b + 1) * BLOCK]
                    for b in range(picked.shape[1] // BLOCK)
                ],
                axis=1,
            )
            total = weighted if total is None else total + weighted
            sums = jnp.sum(picked * grad_ref[...].astype(F32), axis=1, keepdims=True)
            rows = jnp.transpose(jnp.broadcast_to(sums, (sums.shape[0], sums.shape[0])))
            gates_ref[k : k + 1, :] = rows[0:1, :]
        out_ref[...] = total.astype(out_ref.dtype)


def pick_gradients_kernel(pieces, *refs):
    back = join(refs[:pieces])
    own_meta, partner_meta, own_out, partner_out = refs[pieces:]
    for meta, out_ref in ((own_meta, own_out), (partner_meta, partner_out)):
        mask = hits(back.shape[0], meta, 0) | hits(back.shape[0], meta, 1)
        out_ref[...] = dot(one_hot(mask), back, 0, 0).astype(out_ref.dtype)


def finish_kernel(
    own_out, got_out, own_back, got_back, own_gates, got_gates, combined, grad_tokens, grad_gates
):
    combined[...] = (own_out[...] + got_out[...].astype(F32)).astype(BF16)
    grad_tokens[...] = (own_back[...] + got_back[...].astype(F32)).astype(BF16)
    grad_gates[...] = own_gates[...] + got_gates[...]


def call(kernel, outs, flops=0, traffic=0, limit=12, **options):
    shapes = [jax.ShapeDtypeStruct(shape, dtype) for shape, dtype in outs]
    return pl.pallas_call(
        kernel,
        out_shape=shapes,
        compiler_params=pltpu.CompilerParams(vmem_limit_bytes=limit * MIB),
        cost_estimate=pl.CostEstimate(flops=flops, bytes_accessed=traffic, transcendentals=0),
        **options,
    )


def body(tokens, expert_ids, keep_mask, gate_weights, weight_in, weight_out, grad_output):
    token_rows, width = tokens.shape
    hidden_width = weight_in.shape[2]
    rest_count = lax.axis_size("rest")
    members = lax.axis_size("row") * rest_count
    experts = 2 * members
    capacity = 2 * expert_ids.shape[1] * token_rows // experts
    slot_total = experts * capacity
    swap = ((0, 1), (1, 0))

    def exchange(values):
        return lax.ppermute(values, "half", swap)

    member = lax.axis_index("row") * rest_count + lax.axis_index("rest")
    swaps = members if 2 * capacity % 16 == 0 else 1

    def shuffle(pieces):
        if swaps > 1:
            moved = [
                lax.ppermute(piece, GROUP, [(m, m ^ d) for m in range(members)])
                for d, piece in enumerate(pieces)
                if d > 0
            ]
            return [pieces[0]] + moved
        order = jnp.arange(members) ^ member
        shaped = pieces[0].reshape(members, 2 * capacity, width)[order]
        moved = lax.all_to_all(shaped, GROUP, split_axis=0, concat_axis=0, tiled=True)
        return [moved[order].reshape(slot_total, width)]

    partner_tokens = exchange(tokens)
    partner_grad = exchange(grad_output)
    position = jnp.stack([lax.axis_index("half"), member]).astype(jnp.int32)
    meta_shape = ((8, token_rows), F32)
    vmem = pl.BlockSpec(memory_space=pltpu.VMEM)
    hbm = pl.BlockSpec(memory_space=pltpu.HBM)
    own_meta, sent_meta = call(
        functools.partial(route_kernel, rest_count.bit_length() - 1, capacity),
        [meta_shape, meta_shape],
        in_specs=[pl.BlockSpec(memory_space=pltpu.SMEM), vmem, vmem, vmem],
        traffic=8 * token_rows * 8,
    )(position, expert_ids.T, keep_mask.T, gate_weights.T)
    partner_meta = exchange(sent_meta)

    piece_shape = ((slot_total // swaps, width), BF16)
    slot_shape = ((slot_total, width), BF16)
    slot_bytes = slot_total * width * 2
    token_bytes = token_rows * width * 2
    place_flops = 2 * slot_total * 2 * token_rows * width
    sent = call(
        place_tokens_kernel, [piece_shape] * swaps, place_flops, 2 * token_bytes + slot_bytes
    )(tokens, partner_tokens, own_meta, partner_meta)
    x_pieces = shuffle(sent)
    sent_cot = call(
        place_cotangents_kernel,
        [piece_shape] * swaps,
        2 * place_flops,
        2 * token_bytes + slot_bytes,
    )(grad_output, partner_grad, own_meta, partner_meta)
    cot_pieces = shuffle(sent_cot)

    chunk = 512
    mid = (slot_total, hidden_width)
    product = 2 * slot_total * width * hidden_width
    weight_bytes = 2 * 2 * width * hidden_width
    mid_count = slot_total * hidden_width
    *out_pieces, x, hidden, slope = call(
        functools.partial(forward_kernel, swaps, chunk),
        [piece_shape] * swaps + [slot_shape, (mid, BF16), (mid, BF16)],
        2 * product,
        2 * slot_bytes + weight_bytes + 4 * mid_count,
        32,
        in_specs=[vmem] * swaps + [hbm] * 2,
        out_specs=[vmem] * (swaps + 1) + [hbm] * 2,
        scratch_shapes=[pltpu.VMEM((slot_total, width), F32)],
    )(*x_pieces, weight_in, weight_out)
    back_out = shuffle(out_pieces)
    *grad_pieces, cot, grad_pre = call(
        functools.partial(backward_kernel, swaps, chunk),
        [piece_shape] * swaps + [slot_shape, (mid, BF16)],
        2 * product,
        2 * slot_bytes + weight_bytes + 4 * mid_count,
        32,
        in_specs=[vmem] * swaps + [hbm] * 3,
        out_specs=[vmem] * (swaps + 1) + [hbm],
        scratch_shapes=[pltpu.VMEM((slot_total, width), F32)],
    )(*cot_pieces, weight_in, weight_out, slope)
    back_grad = shuffle(grad_pieces)
    own_shape, partner_shape = ((token_rows, width), F32), ((token_rows, width), BF16)
    gates_shape = ((2, token_rows), F32)
    own_out, partner_out, own_gates, partner_gates = call(
        functools.partial(pick_outputs_kernel, swaps),
        [own_shape, partner_shape, gates_shape, gates_shape],
        2 * place_flops,
        2 * token_bytes + slot_bytes,
    )(*back_out, grad_output, partner_grad, own_meta, partner_meta)
    grad_pre, partner_out, partner_gates = lax.optimization_barrier(
        (grad_pre, partner_out, partner_gates)
    )
    grad_in_w, grad_out_w = call(
        functools.partial(weights_kernel, chunk),
        [(weight_in.shape, BF16), (weight_out.shape, BF16)],
        2 * product,
        2 * slot_bytes + weight_bytes + 4 * mid_count,
        32,
        in_specs=[vmem] * 2 + [hbm] * 2,
        out_specs=[hbm] * 2,
    )(x, cot, hidden, grad_pre)
    got_out, got_gates = exchange(partner_out), exchange(partner_gates)
    own_back, partner_back = call(
        functools.partial(pick_gradients_kernel, swaps),
        [own_shape, partner_shape],
        place_flops,
        slot_bytes + 3 * token_bytes,
    )(*back_grad, own_meta, partner_meta)
    got_back = exchange(partner_back)
    combined, grad_tokens, grad_gates = call(
        finish_kernel, [partner_shape, partner_shape, gates_shape], 0, 8 * token_bytes
    )(own_out, got_out, own_back, got_back, own_gates, got_gates)
    return (combined, grad_tokens, grad_gates.T, grad_in_w, grad_out_w)


def solution(mesh):
    row_count, col_count = mesh.devices.shape
    split = Mesh(
        mesh.devices.reshape(row_count, 2, col_count // 2), ("row", "half", "rest")
    )
    axes = ("row", "half", "rest")
    flat = P(axes, None)
    deep = P(axes, None, None)
    return jax.shard_map(
        body,
        mesh=split,
        in_specs=(flat, flat, flat, flat, deep, deep, flat),
        out_specs=(flat, flat, flat, deep, deep),
        check_vma=False,
    )
```

time: 132 us -> 159 us (1.20)
  starting transfers between devices: 33.3 us -> 84.6 us
  local copies, waits for them, and re-layouts: 31 us -> 8.69 us
  waiting for transfers between devices: 29.9 us -> 21.7 us
  Pallas kernels: 35.6 us -> 43 us
    ppermute x0 -> x60, starting transfers between devices: none -> 70.9 us  [shuffle(): lax.ppermute(piece, GROUP, [(m, m ^ d) for m in range(members)])]
    all_to_all x4 -> x0, starting transfers between devices: 22.8 us -> none  [shuffle(): lax.all_to_all(shaped, GROUP, split_axis=0, concat_axis=0, tiled=True)]
    unnamed x40 -> x20, local copies, waits for them, and re-layouts: 31 us -> 8.69 us
    all_to_all x4 -> x0, waiting for transfers between devices: 8.79 us -> none  [shuffle(): lax.all_to_all(shaped, GROUP, split_axis=0, concat_axis=0, tiled=True)]
    pallas_call x7, Pallas kernels: 34.7 us -> 41.6 us  [the longest x1 14.4 us: body(): call(functools.partial(forward_kernel, swaps, chunk), [piece_shape] * swa...]
    ppermute x6, starting transfers between devices: 10.6 us -> 13.7 us  [exchange(): return lax.ppermute(values, 'half', swap)]
    ppermute x0 -> x60, waiting for transfers between devices: none -> 2.39 us  [shuffle(): lax.ppermute(piece, GROUP, [(m, m ^ d) for m in range(members)])]
    ppermute x6, waiting for transfers between devices: 21.1 us -> 19.3 us  [exchange(): return lax.ppermute(values, 'half', swap)]
  transfers between devices with their start and end apart: 10 -> 66, of which waited for: 5 -> 9; matrix products, arithmetic and copies ran while one was open for 0% -> 0% of each run, Pallas kernels for 25% -> 27%
where the time goes in v4:
time: 159 us
  starting transfers between devices  84.6 us (53%)
  Pallas kernels  43 us (27%)
  waiting for transfers between devices  21.7 us (14%)
  local copies, waits for them, and re-layouts  8.69 us (5%)
    ppermute x60, starting transfers between devices, shuffle(): lax.ppermute(piece, GROUP, [(m, m ^ d) for m in range(members)])  70.9 us
    ppermute x6, waiting for transfers between devices, exchange(): return lax.ppermute(values, 'half', swap)  19.3 us
    pallas_call x1, Pallas kernels, body(): call(functools.partial(forward_kernel, swaps, chunk), [piece_shape] * swa...  14.4 us
    ppermute x6, starting transfers between devices, exchange(): return lax.ppermute(values, 'half', swap)  13.7 us
    pallas_call x1, Pallas kernels, body(): call(functools.partial(backward_kernel, swaps, chunk), [piece_shape] * sw...  13 us
    pallas_call x1, Pallas kernels, body(): call(functools.partial(weights_kernel, chunk), [(weight_in.shape, BF16),...  11.1 us
    unnamed x20, local copies, waits for them, and re-layouts  8.69 us
  transfers between devices with their start and end apart: 66, of which 9 were waited for; matrix products, arithmetic and copies ran while one was open for 0% of the time, Pallas kernels for 27%

profile of v4, /device:TPU:0, one launch (start us, length us, event | category | flops | bytes accessed | tf_op | source)
XLA Modules:
  0.0 158.9 jit_solution(14270862828086551754)
XLA Ops:
  0.6 4.1 %collective-permute-start = (bf16[128,768]{1,0:T(8,128)(2,1)}, bf16[128,768]{1,0:T(8,128)(2,1)S(1)}, u32[]{:S(2)}, u32[]{:S(2)}) collective-permute-start(bf16[128,768]{1,0:T(8,128)(2,1)} %own_ref.2), channel_id=1, source_target_pairs={{0,4},{4,0},{1,5},{5,1},{2,6},{6,2},{3,7},{7,3},{8,12},{12,8},{9,1... | collective-permute-start | bytes 589832 | tf_op jit(solution)/shard_map/ppermute | solution.py:285
  4.9 0.7 copy-done
  7.6 2.9 %collective-permute-start.1 = (f32[8,128]{1,0:T(8,128)S(1)}, f32[8,128]{1,0:T(8,128)S(1)}, u32[]{:S(2)}, u32[]{:S(2)}) collective-permute-start(f32[8,128]{1,0:T(8,128)S(1)} %get-tuple-element.91), channel_id=1, source_target_pairs={{0,4},{4,0},{1,5},{5,1},{2,6},{6,2},{3,7},{7,3},{8,12},{12,8},{9,1... | collective-permute-start | bytes 12296 | tf_op jit(solution)/shard_map/ppermute | solution.py:285
  10.5 12.2 %collective-permute-done.1.partner_meta.refs_19_.refs_17_ = f32[8,128]{1,0:T(8,128)S(1)} collective-permute-done((f32[8,128]{1,0:T(8,128)S(1)}, f32[8,128]{1,0:T(8,128)S(1)}, u32[]{:S(2)}, u32[]{:S(2)}) %collective-permute-start.1) | collective-permute-done | bytes 4128 | tf_op jit(solution)/shard_map/ppermute | solution.py:285
  22.7 0.9 copy-done.5
  23.6 0.7 shard_map.111
  24.3 1.6 %collective-permute-start.2 = (bf16[32,768]{1,0:T(8,128)(2,1)S(1)}, bf16[32,768]{1,0:T(8,128)(2,1)S(1)}, u32[]{:S(2)}, u32[]{:S(2)}) collective-permute-start(bf16[32,768]{1,0:T(8,128)(2,1)S(1)} %get-tuple-element.93), channel_id=1, source_target_pairs={{0,1},{1,0},{2,3},{3,2},{8,9},{9,8},{10,11},{11,10},{16,17},{17,16... | collective-permute-start | bytes 147464 | tf_op jit(solution)/shard_map/ppermute | solution.py:293
  26.0 0.7 collective-permute-start.3
  26.7 1.2 collective-permute-start.4
  27.9 1.7 %collective-permute-start.6 = (bf16[32,768]{1,0:T(8,128)(2,1)S(1)}, bf16[32,768]{1,0:T(8,128)(2,1)S(1)}, u32[]{:S(2)}, u32[]{:S(2)}) collective-permute-start(bf16[32,768]{1,0:T(8,128)(2,1)S(1)} %get-tuple-element.97), channel_id=1, source_target_pairs={{0,9},{1,8},{2,11},{3,10},{8,1},{9,0},{10,3},{11,2},{16,25},{17,24... | collective-permute-start | bytes 147464 | tf_op jit(solution)/shard_map/ppermute | solution.py:293
  30.0 1.2 collective-permute-start.8
  31.8 1.5 collective-permute-start.9
  33.3 0.9 collective-permute-start.10
  34.3 1.7 %collective-permute-start.11 = (bf16[32,768]{1,0:T(8,128)(2,1)S(1)}, bf16[32,768]{1,0:T(8,128)(2,1)S(1)}, u32[]{:S(2)}, u32[]{:S(2)}) collective-permute-start(bf16[32,768]{1,0:T(8,128)(2,1)S(1)} %get-tuple-element.102), channel_id=1, source_target_pairs={{0,18},{1,19},{2,16},{3,17},{8,26},{9,27},{10,24},{11,25},{16,2},{... | collective-permute-start | bytes 147464 | tf_op jit(solution)/shard_map/ppermute | solution.py:293
  36.0 1.7 %collective-permute-start.12 = (bf16[32,768]{1,0:T(8,128)(2,1)S(1)}, bf16[32,768]{1,0:T(8,128)(2,1)S(1)}, u32[]{:S(2)}, u32[]{:S(2)}) collective-permute-start(bf16[32,768]{1,0:T(8,128)(2,1)S(1)} %get-tuple-element.103), channel_id=1, source_target_pairs={{0,19},{1,18},{2,17},{3,16},{8,27},{9,26},{10,25},{11,24},{16,3},{... | collective-permute-start | bytes 147464 | tf_op jit(solution)/shard_map/ppermute | solution.py:293
  37.7 2.2 %collective-permute-start.14 = (bf16[32,768]{1,0:T(8,128)(2,1)S(1)}, bf16[32,768]{1,0:T(8,128)(2,1)S(1)}, u32[]{:S(2)}, u32[]{:S(2)}) collective-permute-start(bf16[32,768]{1,0:T(8,128)(2,1)S(1)} %get-tuple-element.105), channel_id=1, source_target_pairs={{0,25},{1,24},{2,27},{3,26},{8,17},{9,16},{10,19},{11,18},{16,9},{... | collective-permute-start | bytes 147464 | tf_op jit(solution)/shard_map/ppermute | solution.py:293
  40.2 2.7 %collective-permute-start.16 = (bf16[32,768]{1,0:T(8,128)(2,1)S(1)}, bf16[32,768]{1,0:T(8,128)(2,1)S(1)}, u32[]{:S(2)}, u32[]{:S(2)}) collective-permute-start(bf16[32,768]{1,0:T(8,128)(2,1)S(1)} %get-tuple-element.107), channel_id=1, source_target_pairs={{0,27},{1,26},{2,25},{3,24},{8,19},{9,18},{10,17},{11,16},{16,11},... | collective-permute-start | bytes 147464 | tf_op jit(solution)/shard_map/ppermute | solution.py:293
  43.0 0.9 copy-done.6
  43.9 1.1 shard_map.114
  45.0 1.1 collective-permute-start.33
  46.0 0.7 collective-permute-start.34
  46.8 1.7 %collective-permute-start.35 = (bf16[32,768]{1,0:T(8,128)(2,1)S(1)}, bf16[32,768]{1,0:T(8,128)(2,1)S(1)}, u32[]{:S(2)}, u32[]{:S(2)}) collective-permute-start(bf16[32,768]{1,0:T(8,128)(2,1)S(1)} %get-tuple-element.128), channel_id=1, source_target_pairs={{0,3},{1,2},{2,1},{3,0},{8,11},{9,10},{10,9},{11,8},{16,19},{17,18... | collective-permute-start | bytes 147464 | tf_op jit(solution)/shard_map/ppermute | solution.py:293
  48.5 1.1 collective-permute-start.37
  50.5 1.4 collective-permute-start.39
  51.9 1.5 collective-permute-start.40
  53.4 1.5 collective-permute-start.41
  54.9 1.7 %collective-permute-start.42 = (bf16[32,768]{1,0:T(8,128)(2,1)S(1)}, bf16[32,768]{1,0:T(8,128)(2,1)S(1)}, u32[]{:S(2)}, u32[]{:S(2)}) collective-permute-start(bf16[32,768]{1,0:T(8,128)(2,1)S(1)} %get-tuple-element.135), channel_id=1, source_target_pairs={{0,18},{1,19},{2,16},{3,17},{8,26},{9,27},{10,24},{11,25},{16,2},{... | collective-permute-start | bytes 147464 | tf_op jit(solution)/shard_map/ppermute | solution.py:293
  56.6 1.1 collective-permute-start.43
  57.9 2.6 %collective-permute-start.45 = (bf16[32,768]{1,0:T(8,128)(2,1)S(1)}, bf16[32,768]{1,0:T(8,128)(2,1)S(1)}, u32[]{:S(2)}, u32[]{:S(2)}) collective-permute-start(bf16[32,768]{1,0:T(8,128)(2,1)S(1)} %get-tuple-element.138), channel_id=1, source_target_pairs={{0,25},{1,24},{2,27},{3,26},{8,17},{9,16},{10,19},{11,18},{16,9},{... | collective-permute-start | bytes 147464 | tf_op jit(solution)/shard_map/ppermute | solution.py:293
  60.8 2.3 %collective-permute-start.47 = (bf16[32,768]{1,0:T(8,128)(2,1)S(1)}, bf16[32,768]{1,0:T(8,128)(2,1)S(1)}, u32[]{:S(2)}, u32[]{:S(2)}) collective-permute-start(bf16[32,768]{1,0:T(8,128)(2,1)S(1)} %get-tuple-element.140), channel_id=1, source_target_pairs={{0,27},{1,26},{2,25},{3,24},{8,19},{9,18},{10,17},{11,16},{16,11},... | collective-permute-start | bytes 147464 | tf_op jit(solution)/shard_map/ppermute | solution.py:293
  63.1 2.8 %copy-done.3 = bf16[1,768,4096]{2,1,0:T(8,128)(2,1)S(1)} copy-done((bf16[1,768,4096]{2,1,0:T(8,128)(2,1)S(1)}, bf16[1,768,4096]{2,1,0:T(8,128)(2,1)}, u32[]{:S(2)}) %copy-start.3) | copy-done | bytes 6291480
  65.8 14.4 %shard_map.112 = (bf16[32,768]{1,0:T(8,128)(2,1)S(1)}, bf16[32,768]{1,0:T(8,128)(2,1)S(1)}, bf16[32,768]{1,0:T(8,128)(2,1)S(1)}, bf16[32,768]{1,0:T(8,128)(2,1)S...) custom-call(bf16[32,768]{1,0:T(8,128)(2,1)S(1)} %get-tuple-element.9, ...), custom_call_target="tpu_custom_call" | custom-call | flops 6442450944 | bytes 22544384 | tf_op jit(solution)/shard_map/pallas_call | solution.py:339
  80.3 2.0 %copy-done.8 = bf16[512,4096]{1,0:T(8,128)(2,1)} copy-done((bf16[512,4096]{1,0:T(8,128)(2,1)}, bf16[512,4096]{1,0:T(8,128)(2,1)S(1)}, u32[]{:S(2)}) %copy-start.8) | copy-done | bytes 4194328
  82.3 1.6 collective-permute-start.17
  83.9 0.7 collective-permute-start.18
  84.6 1.2 collective-permute-start.19
  85.8 1.7 %collective-permute-start.21 = (bf16[32,768]{1,0:T(8,128)(2,1)S(1)}, bf16[32,768]{1,0:T(8,128)(2,1)S(1)}, u32[]{:S(2)}, u32[]{:S(2)}) collective-permute-start(bf16[32,768]{1,0:T(8,128)(2,1)S(1)} %get-tuple-element.113), channel_id=1, source_target_pairs={{0,9},{1,8},{2,11},{3,10},{8,1},{9,0},{10,3},{11,2},{16,25},{17,24... | collective-permute-start | bytes 147464 | tf_op jit(solution)/shard_map/ppermute | solution.py:293
  88.1 1.1 collective-permute-start.23
  89.7 1.5 collective-permute-start.24
  91.2 0.9 collective-permute-start.25
  92.2 1.7 %collective-permute-start.26 = (bf16[32,768]{1,0:T(8,128)(2,1)S(1)}, bf16[32,768]{1,0:T(8,128)(2,1)S(1)}, u32[]{:S(2)}, u32[]{:S(2)}) collective-permute-start(bf16[32,768]{1,0:T(8,128)(2,1)S(1)} %get-tuple-element.118), channel_id=1, source_target_pairs={{0,18},{1,19},{2,16},{3,17},{8,26},{9,27},{10,24},{11,25},{16,2},{... | collective-permute-start | bytes 147464 | tf_op jit(solution)/shard_map/ppermute | solution.py:293
  93.9 1.7 %collective-permute-start.27 = (bf16[32,768]{1,0:T(8,128)(2,1)S(1)}, bf16[32,768]{1,0:T(8,128)(2,1)S(1)}, u32[]{:S(2)}, u32[]{:S(2)}) collective-permute-start(bf16[32,768]{1,0:T(8,128)(2,1)S(1)} %get-tuple-element.119), channel_id=1, source_target_pairs={{0,19},{1,18},{2,17},{3,16},{8,27},{9,26},{10,25},{11,24},{16,3},{... | collective-permute-start | bytes 147464 | tf_op jit(solution)/shard_map/ppermute | solution.py:293
  95.6 2.2 %collective-permute-start.29 = (bf16[32,768]{1,0:T(8,128)(2,1)S(1)}, bf16[32,768]{1,0:T(8,128)(2,1)S(1)}, u32[]{:S(2)}, u32[]{:S(2)}) collective-permute-start(bf16[32,768]{1,0:T(8,128)(2,1)S(1)} %get-tuple-element.121), channel_id=1, source_target_pairs={{0,25},{1,24},{2,27},{3,26},{8,17},{9,16},{10,19},{11,18},{16,9},{... | collective-permute-start | bytes 147464 | tf_op jit(solution)/shard_map/ppermute | solution.py:293
  98.1 2.7 %collective-permute-start.31 = (bf16[32,768]{1,0:T(8,128)(2,1)S(1)}, bf16[32,768]{1,0:T(8,128)(2,1)S(1)}, u32[]{:S(2)}, u32[]{:S(2)}) collective-permute-start(bf16[32,768]{1,0:T(8,128)(2,1)S(1)} %get-tuple-element.123), channel_id=1, source_target_pairs={{0,27},{1,26},{2,25},{3,24},{8,19},{9,18},{10,17},{11,16},{16,11},... | collective-permute-start | bytes 147464 | tf_op jit(solution)/shard_map/ppermute | solution.py:293
  100.9 13.0 %shard_map.115 = (bf16[32,768]{1,0:T(8,128)(2,1)S(1)}, bf16[32,768]{1,0:T(8,128)(2,1)S(1)}, bf16[32,768]{1,0:T(8,128)(2,1)S(1)}, bf16[32,768]{1,0:T(8,128)(2,1)S...) custom-call(bf16[32,768]{1,0:T(8,128)(2,1)S(1)} %get-tuple-element.1, ...), custom_call_target="tpu_custom_call" | custom-call | flops 6442450944 | bytes 22544384 | tf_op jit(solution)/shard_map/pallas_call | solution.py:350
  113.9 1.1 collective-permute-start.49
  115.0 0.7 collective-permute-start.50
  115.8 1.7 %collective-permute-start.51 = (bf16[32,768]{1,0:T(8,128)(2,1)S(1)}, bf16[32,768]{1,0:T(8,128)(2,1)S(1)}, u32[]{:S(2)}, u32[]{:S(2)}) collective-permute-start(bf16[32,768]{1,0:T(8,128)(2,1)S(1)} %get-tuple-element.149), channel_id=1, source_target_pairs={{0,3},{1,2},{2,1},{3,0},{8,11},{9,10},{10,9},{11,8},{16,19},{17,18... | collective-permute-start | bytes 147464 | tf_op jit(solution)/shard_map/ppermute | solution.py:293
  117.5 1.1 collective-permute-start.53
  119.5 1.4 collective-permute-start.55
  120.8 1.5 collective-permute-start.56
  122.4 1.5 collective-permute-start.57
  123.9 1.7 %collective-permute-start.58 = (bf16[32,768]{1,0:T(8,128)(2,1)S(1)}, bf16[32,768]{1,0:T(8,128)(2,1)S(1)}, u32[]{:S(2)}, u32[]{:S(2)}) collective-permute-start(bf16[32,768]{1,0:T(8,128)(2,1)S(1)} %get-tuple-element.156), channel_id=1, source_target_pairs={{0,18},{1,19},{2,16},{3,17},{8,26},{9,27},{10,24},{11,25},{16,2},{... | collective-permute-start | bytes 147464 | tf_op jit(solution)/shard_map/ppermute | solution.py:293
  125.6 1.1 collective-permute-start.59
  126.9 2.6 %collective-permute-start.61 = (bf16[32,768]{1,0:T(8,128)(2,1)S(1)}, bf16[32,768]{1,0:T(8,128)(2,1)S(1)}, u32[]{:S(2)}, u32[]{:S(2)}) collective-permute-start(bf16[32,768]{1,0:T(8,128)(2,1)S(1)} %get-tuple-element.159), channel_id=1, source_target_pairs={{0,25},{1,24},{2,27},{3,26},{8,17},{9,16},{10,19},{11,18},{16,9},{... | collective-permute-start | bytes 147464 | tf_op jit(solution)/shard_map/ppermute | solution.py:293
  129.7 2.3 %collective-permute-start.63 = (bf16[32,768]{1,0:T(8,128)(2,1)S(1)}, bf16[32,768]{1,0:T(8,128)(2,1)S(1)}, u32[]{:S(2)}, u32[]{:S(2)}) collective-permute-start(bf16[32,768]{1,0:T(8,128)(2,1)S(1)} %get-tuple-element.161), channel_id=1, source_target_pairs={{0,27},{1,26},{2,25},{3,24},{8,19},{9,18},{10,17},{11,16},{16,11},... | collective-permute-start | bytes 147464 | tf_op jit(solution)/shard_map/ppermute | solution.py:293
  132.0 0.8 shard_map.113
  132.8 3.6 %collective-permute-start.65 = (f32[2,128]{1,0:T(2,128)S(1)}, f32[2,128]{1,0:T(2,128)S(1)}, u32[]{:S(2)}, u32[]{:S(2)}) collective-permute-start(f32[2,128]{1,0:T(2,128)S(1)} %get-tuple-element.165), channel_id=1, source_target_pairs={{0,4},{4,0},{1,5},{5,1},{2,6},{6,2},{3,7},{7,3},{8,12},{12,8},{9,1... | collective-permute-start | bytes 3080 | tf_op jit(solution)/shard_map/ppermute | solution.py:285
  136.9 2.2 %collective-permute-start.64 = (bf16[128,768]{1,0:T(8,128)(2,1)S(1)}, bf16[128,768]{1,0:T(8,128)(2,1)S(1)}, u32[]{:S(2)}, u32[]{:S(2)}) collective-permute-start(bf16[128,768]{1,0:T(8,128)(2,1)S(1)} %get-tuple-element.163), channel_id=1, source_target_pairs={{0,4},{4,0},{1,5},{5,1},{2,6},{6,2},{3,7},{7,3},{8,12},{12,8},{9,1... | collective-permute-start | bytes 589832 | tf_op jit(solution)/shard_map/ppermute | solution.py:285
  139.1 0.8 collective-permute-start.48
  139.9 11.1 %shard_map.118 = (bf16[1,768,4096]{2,1,0:T(8,128)(2,1)}, bf16[1,4096,768]{2,1,0:T(8,128)(2,1)}) custom-call(bf16[512,768]{1,0:T(8,128)(2,1)S(1)} %get-tuple-element.169.x, bf16[512,768]{1,0:T(8,128)(2,1)S(1)} %get-tuple-element.170.cot, bf16[512,4096]{1,0:T(8,128)(2,1)S(1)} %copy-done.9, bf16[512,4096]{1,0:T(8,128)(2,1)S(1)} %get-tuple-element.172.grad_pre_all), custom_call_target="tpu_custom_call" | custom-call | flops 6442450944 | bytes 22544384 | tf_op jit(solution)/shard_map/pallas_call | solution.py:372
  151.0 2.9 %collective-permute-done.64.got_back = bf16[128,768]{1,0:T(8,128)(2,1)S(1)} collective-permute-done((bf16[128,768]{1,0:T(8,128)(2,1)S(1)}, bf16[128,768]{1,0:T(8,128)(2,1)S(1)}, u32[]{:S(2)}, u32[]{:S(2)}) %collective-permute-start.64) | collective-permute-done | bytes 196640 | tf_op jit(solution)/shard_map/ppermute | solution.py:285
  153.9 4.2 %collective-permute-done.48.got_out = bf16[128,768]{1,0:T(8,128)(2,1)S(1)} collective-permute-done((bf16[128,768]{1,0:T(8,128)(2,1)S(1)}, bf16[128,768]{1,0:T(8,128)(2,1)S(1)}, u32[]{:S(2)}, u32[]{:S(2)}) %collective-permute-start.48) | collective-permute-done | bytes 196640 | tf_op jit(solution)/shard_map/ppermute | solution.py:285
  158.1 0.8 shard_map.117
  (98 shorter events, 8.1 us)
Async XLA Ops:
  0.6 22.0 %collective-permute-start = (bf16[128,768]{1,0:T(8,128)(2,1)}, bf16[128,768]{1,0:T(8,128)(2,1)S(1)}, u32[]{:S(2)}, u32[]{:S(2)}) collective-permute-start(bf16[128,768]{1,0:T(8,128)(2,1)} %own_ref.2), channel_id=1, source_target_pairs={{0,4},{4,0},{1,5},{5,1},{2,6},{6,2},{3,7},{7,3},{8,12},{12,8},{9,1... | collective-permute-start | bytes 589832 | tf_op jit(solution)/shard_map/ppermute | solution.py:285
  4.7 23.2 %collective-permute-start.32 = (bf16[128,768]{1,0:T(8,128)(2,1)}, bf16[128,768]{1,0:T(8,128)(2,1)S(1)}, u32[]{:S(2)}, u32[]{:S(2)}) collective-permute-start(bf16[128,768]{1,0:T(8,128)(2,1)} %own_ref.3), channel_id=1, source_target_pairs={{0,4},{4,0},{1,5},{5,1},{2,6},{6,2},{3,7},{7,3},{8,12},{12,8},{9,1... | collective-permute-start | bytes 589832 | tf_op jit(solution)/shard_map/ppermute | solution.py:285
  7.6 15.1 %collective-permute-start.1 = (f32[8,128]{1,0:T(8,128)S(1)}, f32[8,128]{1,0:T(8,128)S(1)}, u32[]{:S(2)}, u32[]{:S(2)}) collective-permute-start(f32[8,128]{1,0:T(8,128)S(1)} %get-tuple-element.91), channel_id=1, source_target_pairs={{0,4},{4,0},{1,5},{5,1},{2,6},{6,2},{3,7},{7,3},{8,12},{12,8},{9,1... | collective-permute-start | bytes 12296 | tf_op jit(solution)/shard_map/ppermute | solution.py:285
  24.3 5.2 %collective-permute-start.2 = (bf16[32,768]{1,0:T(8,128)(2,1)S(1)}, bf16[32,768]{1,0:T(8,128)(2,1)S(1)}, u32[]{:S(2)}, u32[]{:S(2)}) collective-permute-start(bf16[32,768]{1,0:T(8,128)(2,1)S(1)} %get-tuple-element.93), channel_id=1, source_target_pairs={{0,1},{1,0},{2,3},{3,2},{8,9},{9,8},{10,11},{11,10},{16,17},{17,16... | collective-permute-start | bytes 147464 | tf_op jit(solution)/shard_map/ppermute | solution.py:293
  26.7 5.1 %collective-permute-start.4 = (bf16[32,768]{1,0:T(8,128)(2,1)S(1)}, bf16[32,768]{1,0:T(8,128)(2,1)S(1)}, u32[]{:S(2)}, u32[]{:S(2)}) collective-permute-start(bf16[32,768]{1,0:T(8,128)(2,1)S(1)} %get-tuple-element.95), channel_id=1, source_target_pairs={{0,3},{1,2},{2,1},{3,0},{8,11},{9,10},{10,9},{11,8},{16,19},{17,18... | collective-permute-start | bytes 147464 | tf_op jit(solution)/shard_map/ppermute | solution.py:293
  27.9 5.4 %collective-permute-start.5 = (bf16[32,768]{1,0:T(8,128)(2,1)S(1)}, bf16[32,768]{1,0:T(8,128)(2,1)S(1)}, u32[]{:S(2)}, u32[]{:S(2)}) collective-permute-start(bf16[32,768]{1,0:T(8,128)(2,1)S(1)} %get-tuple-element.96), channel_id=1, source_target_pairs={{0,8},{1,9},{2,10},{3,11},{8,0},{9,1},{10,2},{11,3},{16,24},{17,25... | collective-permute-start | bytes 147464 | tf_op jit(solution)/shard_map/ppermute | solution.py:293
  27.9 6.3 %collective-permute-start.6 = (bf16[32,768]{1,0:T(8,128)(2,1)S(1)}, bf16[32,768]{1,0:T(8,128)(2,1)S(1)}, u32[]{:S(2)}, u32[]{:S(2)}) collective-permute-start(bf16[32,768]{1,0:T(8,128)(2,1)S(1)} %get-tuple-element.97), channel_id=1, source_target_pairs={{0,9},{1,8},{2,11},{3,10},{8,1},{9,0},{10,3},{11,2},{16,25},{17,24... | collective-permute-start | bytes 147464 | tf_op jit(solution)/shard_map/ppermute | solution.py:293
  29.6 6.4 %collective-permute-start.7 = (bf16[32,768]{1,0:T(8,128)(2,1)S(1)}, bf16[32,768]{1,0:T(8,128)(2,1)S(1)}, u32[]{:S(2)}, u32[]{:S(2)}) collective-permute-start(bf16[32,768]{1,0:T(8,128)(2,1)S(1)} %get-tuple-element.98), channel_id=1, source_target_pairs={{0,10},{1,11},{2,8},{3,9},{8,2},{9,3},{10,0},{11,1},{16,26},{17,27... | collective-permute-start | bytes 147464 | tf_op jit(solution)/shard_map/ppermute | solution.py:293
  30.0 7.6 %collective-permute-start.8 = (bf16[32,768]{1,0:T(8,128)(2,1)S(1)}, bf16[32,768]{1,0:T(8,128)(2,1)S(1)}, u32[]{:S(2)}, u32[]{:S(2)}) collective-permute-start(bf16[32,768]{1,0:T(8,128)(2,1)S(1)} %get-tuple-element.99), channel_id=1, source_target_pairs={{0,11},{1,10},{2,9},{3,8},{8,3},{9,2},{10,1},{11,0},{16,27},{17,26... | collective-permute-start | bytes 147464 | tf_op jit(solution)/shard_map/ppermute | solution.py:293
  31.8 5.9 %collective-permute-start.9 = (bf16[32,768]{1,0:T(8,128)(2,1)S(1)}, bf16[32,768]{1,0:T(8,128)(2,1)S(1)}, u32[]{:S(2)}, u32[]{:S(2)}) collective-permute-start(bf16[32,768]{1,0:T(8,128)(2,1)S(1)} %get-tuple-element.100), channel_id=1, source_target_pairs={{0,16},{1,17},{2,18},{3,19},{8,24},{9,25},{10,26},{11,27},{16,0},{... | collective-permute-start | bytes 147464 | tf_op jit(solution)/shard_map/ppermute | solution.py:293
  33.3 6.5 %collective-permute-start.10 = (bf16[32,768]{1,0:T(8,128)(2,1)S(1)}, bf16[32,768]{1,0:T(8,128)(2,1)S(1)}, u32[]{:S(2)}, u32[]{:S(2)}) collective-permute-start(bf16[32,768]{1,0:T(8,128)(2,1)S(1)} %get-tuple-element.101), channel_id=1, source_target_pairs={{0,17},{1,16},{2,19},{3,18},{8,25},{9,24},{10,27},{11,26},{16,1},{... | collective-permute-start | bytes 147464 | tf_op jit(solution)/shard_map/ppermute | solution.py:293
  34.3 6.0 %collective-permute-start.11 = (bf16[32,768]{1,0:T(8,128)(2,1)S(1)}, bf16[32,768]{1,0:T(8,128)(2,1)S(1)}, u32[]{:S(2)}, u32[]{:S(2)}) collective-permute-start(bf16[32,768]{1,0:T(8,128)(2,1)S(1)} %get-tuple-element.102), channel_id=1, source_target_pairs={{0,18},{1,19},{2,16},{3,17},{8,26},{9,27},{10,24},{11,25},{16,2},{... | collective-permute-start | bytes 147464 | tf_op jit(solution)/shard_map/ppermute | solution.py:293
  36.0 9.0 %collective-permute-start.12 = (bf16[32,768]{1,0:T(8,128)(2,1)S(1)}, bf16[32,768]{1,0:T(8,128)(2,1)S(1)}, u32[]{:S(2)}, u32[]{:S(2)}) collective-permute-start(bf16[32,768]{1,0:T(8,128)(2,1)S(1)} %get-tuple-element.103), channel_id=1, source_target_pairs={{0,19},{1,18},{2,17},{3,16},{8,27},{9,26},{10,25},{11,24},{16,3},{... | collective-permute-start | bytes 147464 | tf_op jit(solution)/shard_map/ppermute | solution.py:293
  37.6 8.4 %collective-permute-start.13 = (bf16[32,768]{1,0:T(8,128)(2,1)S(1)}, bf16[32,768]{1,0:T(8,128)(2,1)S(1)}, u32[]{:S(2)}, u32[]{:S(2)}) collective-permute-start(bf16[32,768]{1,0:T(8,128)(2,1)S(1)} %get-tuple-element.104), channel_id=1, source_target_pairs={{0,24},{1,25},{2,26},{3,27},{8,16},{9,17},{10,18},{11,19},{16,8},{... | collective-permute-start | bytes 147464 | tf_op jit(solution)/shard_map/ppermute | solution.py:293
  37.7 9.1 %collective-permute-start.14 = (bf16[32,768]{1,0:T(8,128)(2,1)S(1)}, bf16[32,768]{1,0:T(8,128)(2,1)S(1)}, u32[]{:S(2)}, u32[]{:S(2)}) collective-permute-start(bf16[32,768]{1,0:T(8,128)(2,1)S(1)} %get-tuple-element.105), channel_id=1, source_target_pairs={{0,25},{1,24},{2,27},{3,26},{8,17},{9,16},{10,19},{11,18},{16,9},{... | collective-permute-start | bytes 147464 | tf_op jit(solution)/shard_map/ppermute | solution.py:293
  39.8 8.7 %collective-permute-start.15 = (bf16[32,768]{1,0:T(8,128)(2,1)S(1)}, bf16[32,768]{1,0:T(8,128)(2,1)S(1)}, u32[]{:S(2)}, u32[]{:S(2)}) collective-permute-start(bf16[32,768]{1,0:T(8,128)(2,1)S(1)} %get-tuple-element.106), channel_id=1, source_target_pairs={{0,26},{1,27},{2,24},{3,25},{8,18},{9,19},{10,16},{11,17},{16,10},... | collective-permute-start | bytes 147464 | tf_op jit(solution)/shard_map/ppermute | solution.py:293
  40.2 8.3 %collective-permute-start.16 = (bf16[32,768]{1,0:T(8,128)(2,1)S(1)}, bf16[32,768]{1,0:T(8,128)(2,1)S(1)}, u32[]{:S(2)}, u32[]{:S(2)}) collective-permute-start(bf16[32,768]{1,0:T(8,128)(2,1)S(1)} %get-tuple-element.107), channel_id=1, source_target_pairs={{0,27},{1,26},{2,25},{3,24},{8,19},{9,18},{10,17},{11,16},{16,11},... | collective-permute-start | bytes 147464 | tf_op jit(solution)/shard_map/ppermute | solution.py:293
  45.0 4.7 %collective-permute-start.33 = (bf16[32,768]{1,0:T(8,128)(2,1)S(1)}, bf16[32,768]{1,0:T(8,128)(2,1)S(1)}, u32[]{:S(2)}, u32[]{:S(2)}) collective-permute-start(bf16[32,768]{1,0:T(8,128)(2,1)S(1)} %get-tuple-element.126), channel_id=1, source_target_pairs={{0,1},{1,0},{2,3},{3,2},{8,9},{9,8},{10,11},{11,10},{16,17},{17,16... | collective-permute-start | bytes 147464 | tf_op jit(solution)/shard_map/ppermute | solution.py:293
  46.0 4.4 %collective-permute-start.34 = (bf16[32,768]{1,0:T(8,128)(2,1)S(1)}, bf16[32,768]{1,0:T(8,128)(2,1)S(1)}, u32[]{:S(2)}, u32[]{:S(2)}) collective-permute-start(bf16[32,768]{1,0:T(8,128)(2,1)S(1)} %get-tuple-element.127), channel_id=1, source_target_pairs={{0,2},{1,3},{2,0},{3,1},{8,10},{9,11},{10,8},{11,9},{16,18},{17,19... | collective-permute-start | bytes 147464 | tf_op jit(solution)/shard_map/ppermute | solution.py:293
  46.8 5.1 %collective-permute-start.35 = (bf16[32,768]{1,0:T(8,128)(2,1)S(1)}, bf16[32,768]{1,0:T(8,128)(2,1)S(1)}, u32[]{:S(2)}, u32[]{:S(2)}) collective-permute-start(bf16[32,768]{1,0:T(8,128)(2,1)S(1)} %get-tuple-element.128), channel_id=1, source_target_pairs={{0,3},{1,2},{2,1},{3,0},{8,11},{9,10},{10,9},{11,8},{16,19},{17,18... | collective-permute-start | bytes 147464 | tf_op jit(solution)/shard_map/ppermute | solution.py:293
  48.5 4.9 %collective-permute-start.36 = (bf16[32,768]{1,0:T(8,128)(2,1)S(1)}, bf16[32,768]{1,0:T(8,128)(2,1)S(1)}, u32[]{:S(2)}, u32[]{:S(2)}) collective-permute-start(bf16[32,768]{1,0:T(8,128)(2,1)S(1)} %get-tuple-element.129), channel_id=1, source_target_pairs={{0,8},{1,9},{2,10},{3,11},{8,0},{9,1},{10,2},{11,3},{16,24},{17,25... | collective-permute-start | bytes 147464 | tf_op jit(solution)/shard_map/ppermute | solution.py:293
  48.5 6.4 %collective-permute-start.37 = (bf16[32,768]{1,0:T(8,128)(2,1)S(1)}, bf16[32,768]{1,0:T(8,128)(2,1)S(1)}, u32[]{:S(2)}, u32[]{:S(2)}) collective-permute-start(bf16[32,768]{1,0:T(8,128)(2,1)S(1)} %get-tuple-element.130), channel_id=1, source_target_pairs={{0,9},{1,8},{2,11},{3,10},{8,1},{9,0},{10,3},{11,2},{16,25},{17,24... | collective-permute-start | bytes 147464 | tf_op jit(solution)/shard_map/ppermute | solution.py:293
  49.7 7.0 %collective-permute-start.38 = (bf16[32,768]{1,0:T(8,128)(2,1)S(1)}, bf16[32,768]{1,0:T(8,128)(2,1)S(1)}, u32[]{:S(2)}, u32[]{:S(2)}) collective-permute-start(bf16[32,768]{1,0:T(8,128)(2,1)S(1)} %get-tuple-element.131), channel_id=1, source_target_pairs={{0,10},{1,11},{2,8},{3,9},{8,2},{9,3},{10,0},{11,1},{16,26},{17,27... | collective-permute-start | bytes 147464 | tf_op jit(solution)/shard_map/ppermute | solution.py:293
  50.5 7.3 %collective-permute-start.39 = (bf16[32,768]{1,0:T(8,128)(2,1)S(1)}, bf16[32,768]{1,0:T(8,128)(2,1)S(1)}, u32[]{:S(2)}, u32[]{:S(2)}) collective-permute-start(bf16[32,768]{1,0:T(8,128)(2,1)S(1)} %get-tuple-element.132), channel_id=1, source_target_pairs={{0,11},{1,10},{2,9},{3,8},{8,3},{9,2},{10,1},{11,0},{16,27},{17,26... | collective-permute-start | bytes 147464 | tf_op jit(solution)/shard_map/ppermute | solution.py:293
  51.9 6.0 %collective-permute-start.40 = (bf16[32,768]{1,0:T(8,128)(2,1)S(1)}, bf16[32,768]{1,0:T(8,128)(2,1)S(1)}, u32[]{:S(2)}, u32[]{:S(2)}) collective-permute-start(bf16[32,768]{1,0:T(8,128)(2,1)S(1)} %get-tuple-element.133), channel_id=1, source_target_pairs={{0,16},{1,17},{2,18},{3,19},{8,24},{9,25},{10,26},{11,27},{16,0},{... | collective-permute-start | bytes 147464 | tf_op jit(solution)/shard_map/ppermute | solution.py:293
  53.4 7.1 %collective-permute-start.41 = (bf16[32,768]{1,0:T(8,128)(2,1)S(1)}, bf16[32,768]{1,0:T(8,128)(2,1)S(1)}, u32[]{:S(2)}, u32[]{:S(2)}) collective-permute-start(bf16[32,768]{1,0:T(8,128)(2,1)S(1)} %get-tuple-element.134), channel_id=1, source_target_pairs={{0,17},{1,16},{2,19},{3,18},{8,25},{9,24},{10,27},{11,26},{16,1},{... | collective-permute-start | bytes 147464 | tf_op jit(solution)/shard_map/ppermute | solution.py:293
  54.9 5.8 %collective-permute-start.42 = (bf16[32,768]{1,0:T(8,128)(2,1)S(1)}, bf16[32,768]{1,0:T(8,128)(2,1)S(1)}, u32[]{:S(2)}, u32[]{:S(2)}) collective-permute-start(bf16[32,768]{1,0:T(8,128)(2,1)S(1)} %get-tuple-element.135), channel_id=1, source_target_pairs={{0,18},{1,19},{2,16},{3,17},{8,26},{9,27},{10,24},{11,25},{16,2},{... | collective-permute-start | bytes 147464 | tf_op jit(solution)/shard_map/ppermute | solution.py:293
  56.6 25.7 %collective-permute-start.43 = (bf16[32,768]{1,0:T(8,128)(2,1)S(1)}, bf16[32,768]{1,0:T(8,128)(2,1)S(1)}, u32[]{:S(2)}, u32[]{:S(2)}) collective-permute-start(bf16[32,768]{1,0:T(8,128)(2,1)S(1)} %get-tuple-element.136), channel_id=1, source_target_pairs={{0,19},{1,18},{2,17},{3,16},{8,27},{9,26},{10,25},{11,24},{16,3},{... | collective-permute-start | bytes 147464 | tf_op jit(solution)/shard_map/ppermute | solution.py:293
  57.7 26.1 %collective-permute-start.44 = (bf16[32,768]{1,0:T(8,128)(2,1)S(1)}, bf16[32,768]{1,0:T(8,128)(2,1)S(1)}, u32[]{:S(2)}, u32[]{:S(2)}) collective-permute-start(bf16[32,768]{1,0:T(8,128)(2,1)S(1)} %get-tuple-element.137), channel_id=1, source_target_pairs={{0,24},{1,25},{2,26},{3,27},{8,16},{9,17},{10,18},{11,19},{16,8},{... | collective-permute-start | bytes 147464 | tf_op jit(solution)/shard_map/ppermute | solution.py:293
  57.9 26.7 %collective-permute-start.45 = (bf16[32,768]{1,0:T(8,128)(2,1)S(1)}, bf16[32,768]{1,0:T(8,128)(2,1)S(1)}, u32[]{:S(2)}, u32[]{:S(2)}) collective-permute-start(bf16[32,768]{1,0:T(8,128)(2,1)S(1)} %get-tuple-element.138), channel_id=1, source_target_pairs={{0,25},{1,24},{2,27},{3,26},{8,17},{9,16},{10,19},{11,18},{16,9},{... | collective-permute-start | bytes 147464 | tf_op jit(solution)/shard_map/ppermute | solution.py:293
  60.5 25.3 %collective-permute-start.46 = (bf16[32,768]{1,0:T(8,128)(2,1)S(1)}, bf16[32,768]{1,0:T(8,128)(2,1)S(1)}, u32[]{:S(2)}, u32[]{:S(2)}) collective-permute-start(bf16[32,768]{1,0:T(8,128)(2,1)S(1)} %get-tuple-element.139), channel_id=1, source_target_pairs={{0,26},{1,27},{2,24},{3,25},{8,18},{9,19},{10,16},{11,17},{16,10},... | collective-permute-start | bytes 147464 | tf_op jit(solution)/shard_map/ppermute | solution.py:293
  60.8 25.0 %collective-permute-start.47 = (bf16[32,768]{1,0:T(8,128)(2,1)S(1)}, bf16[32,768]{1,0:T(8,128)(2,1)S(1)}, u32[]{:S(2)}, u32[]{:S(2)}) collective-permute-start(bf16[32,768]{1,0:T(8,128)(2,1)S(1)} %get-tuple-element.140), channel_id=1, source_target_pairs={{0,27},{1,26},{2,25},{3,24},{8,19},{9,18},{10,17},{11,16},{16,11},... | collective-permute-start | bytes 147464 | tf_op jit(solution)/shard_map/ppermute | solution.py:293
  82.3 5.2 %collective-permute-start.17 = (bf16[32,768]{1,0:T(8,128)(2,1)S(1)}, bf16[32,768]{1,0:T(8,128)(2,1)S(1)}, u32[]{:S(2)}, u32[]{:S(2)}) collective-permute-start(bf16[32,768]{1,0:T(8,128)(2,1)S(1)} %get-tuple-element.109), channel_id=1, source_target_pairs={{0,1},{1,0},{2,3},{3,2},{8,9},{9,8},{10,11},{11,10},{16,17},{17,16... | collective-permute-start | bytes 147464 | tf_op jit(solution)/shard_map/ppermute | solution.py:293
  84.6 5.1 %collective-permute-start.19 = (bf16[32,768]{1,0:T(8,128)(2,1)S(1)}, bf16[32,768]{1,0:T(8,128)(2,1)S(1)}, u32[]{:S(2)}, u32[]{:S(2)}) collective-permute-start(bf16[32,768]{1,0:T(8,128)(2,1)S(1)} %get-tuple-element.111), channel_id=1, source_target_pairs={{0,3},{1,2},{2,1},{3,0},{8,11},{9,10},{10,9},{11,8},{16,19},{17,18... | collective-permute-start | bytes 147464 | tf_op jit(solution)/shard_map/ppermute | solution.py:293
  85.8 5.4 %collective-permute-start.20 = (bf16[32,768]{1,0:T(8,128)(2,1)S(1)}, bf16[32,768]{1,0:T(8,128)(2,1)S(1)}, u32[]{:S(2)}, u32[]{:S(2)}) collective-permute-start(bf16[32,768]{1,0:T(8,128)(2,1)S(1)} %get-tuple-element.112), channel_id=1, source_target_pairs={{0,8},{1,9},{2,10},{3,11},{8,0},{9,1},{10,2},{11,3},{16,24},{17,25... | collective-permute-start | bytes 147464 | tf_op jit(solution)/shard_map/ppermute | solution.py:293
  85.8 6.4 %collective-permute-start.21 = (bf16[32,768]{1,0:T(8,128)(2,1)S(1)}, bf16[32,768]{1,0:T(8,128)(2,1)S(1)}, u32[]{:S(2)}, u32[]{:S(2)}) collective-permute-start(bf16[32,768]{1,0:T(8,128)(2,1)S(1)} %get-tuple-element.113), channel_id=1, source_target_pairs={{0,9},{1,8},{2,11},{3,10},{8,1},{9,0},{10,3},{11,2},{16,25},{17,24... | collective-permute-start | bytes 147464 | tf_op jit(solution)/shard_map/ppermute | solution.py:293
  87.5 6.4 %collective-permute-start.22 = (bf16[32,768]{1,0:T(8,128)(2,1)S(1)}, bf16[32,768]{1,0:T(8,128)(2,1)S(1)}, u32[]{:S(2)}, u32[]{:S(2)}) collective-permute-start(bf16[32,768]{1,0:T(8,128)(2,1)S(1)} %get-tuple-element.114), channel_id=1, source_target_pairs={{0,10},{1,11},{2,8},{3,9},{8,2},{9,3},{10,0},{11,1},{16,26},{17,27... | collective-permute-start | bytes 147464 | tf_op jit(solution)/shard_map/ppermute | solution.py:293
  88.1 7.5 %collective-permute-start.23 = (bf16[32,768]{1,0:T(8,128)(2,1)S(1)}, bf16[32,768]{1,0:T(8,128)(2,1)S(1)}, u32[]{:S(2)}, u32[]{:S(2)}) collective-permute-start(bf16[32,768]{1,0:T(8,128)(2,1)S(1)} %get-tuple-element.115), channel_id=1, source_target_pairs={{0,11},{1,10},{2,9},{3,8},{8,3},{9,2},{10,1},{11,0},{16,27},{17,26... | collective-permute-start | bytes 147464 | tf_op jit(solution)/shard_map/ppermute | solution.py:293
  89.7 5.9 %collective-permute-start.24 = (bf16[32,768]{1,0:T(8,128)(2,1)S(1)}, bf16[32,768]{1,0:T(8,128)(2,1)S(1)}, u32[]{:S(2)}, u32[]{:S(2)}) collective-permute-start(bf16[32,768]{1,0:T(8,128)(2,1)S(1)} %get-tuple-element.116), channel_id=1, source_target_pairs={{0,16},{1,17},{2,18},{3,19},{8,24},{9,25},{10,26},{11,27},{16,0},{... | collective-permute-start | bytes 147464 | tf_op jit(solution)/shard_map/ppermute | solution.py:293
  91.2 6.5 %collective-permute-start.25 = (bf16[32,768]{1,0:T(8,128)(2,1)S(1)}, bf16[32,768]{1,0:T(8,128)(2,1)S(1)}, u32[]{:S(2)}, u32[]{:S(2)}) collective-permute-start(bf16[32,768]{1,0:T(8,128)(2,1)S(1)} %get-tuple-element.117), channel_id=1, source_target_pairs={{0,17},{1,16},{2,19},{3,18},{8,25},{9,24},{10,27},{11,26},{16,1},{... | collective-permute-start | bytes 147464 | tf_op jit(solution)/shard_map/ppermute | solution.py:293
  92.2 6.0 %collective-permute-start.26 = (bf16[32,768]{1,0:T(8,128)(2,1)S(1)}, bf16[32,768]{1,0:T(8,128)(2,1)S(1)}, u32[]{:S(2)}, u32[]{:S(2)}) collective-permute-start(bf16[32,768]{1,0:T(8,128)(2,1)S(1)} %get-tuple-element.118), channel_id=1, source_target_pairs={{0,18},{1,19},{2,16},{3,17},{8,26},{9,27},{10,24},{11,25},{16,2},{... | collective-permute-start | bytes 147464 | tf_op jit(solution)/shard_map/ppermute | solution.py:293
  93.9 20.1 %collective-permute-start.27 = (bf16[32,768]{1,0:T(8,128)(2,1)S(1)}, bf16[32,768]{1,0:T(8,128)(2,1)S(1)}, u32[]{:S(2)}, u32[]{:S(2)}) collective-permute-start(bf16[32,768]{1,0:T(8,128)(2,1)S(1)} %get-tuple-element.119), channel_id=1, source_target_pairs={{0,19},{1,18},{2,17},{3,16},{8,27},{9,26},{10,25},{11,24},{16,3},{... | collective-permute-start | bytes 147464 | tf_op jit(solution)/shard_map/ppermute | solution.py:293
  95.6 19.5 %collective-permute-start.28 = (bf16[32,768]{1,0:T(8,128)(2,1)S(1)}, bf16[32,768]{1,0:T(8,128)(2,1)S(1)}, u32[]{:S(2)}, u32[]{:S(2)}) collective-permute-start(bf16[32,768]{1,0:T(8,128)(2,1)S(1)} %get-tuple-element.120), channel_id=1, source_target_pairs={{0,24},{1,25},{2,26},{3,27},{8,16},{9,17},{10,18},{11,19},{16,8},{... | collective-permute-start | bytes 147464 | tf_op jit(solution)/shard_map/ppermute | solution.py:293
  95.6 20.2 %collective-permute-start.29 = (bf16[32,768]{1,0:T(8,128)(2,1)S(1)}, bf16[32,768]{1,0:T(8,128)(2,1)S(1)}, u32[]{:S(2)}, u32[]{:S(2)}) collective-permute-start(bf16[32,768]{1,0:T(8,128)(2,1)S(1)} %get-tuple-element.121), channel_id=1, source_target_pairs={{0,25},{1,24},{2,27},{3,26},{8,17},{9,16},{10,19},{11,18},{16,9},{... | collective-permute-start | bytes 147464 | tf_op jit(solution)/shard_map/ppermute | solution.py:293
  97.8 19.7 %collective-permute-start.30 = (bf16[32,768]{1,0:T(8,128)(2,1)S(1)}, bf16[32,768]{1,0:T(8,128)(2,1)S(1)}, u32[]{:S(2)}, u32[]{:S(2)}) collective-permute-start(bf16[32,768]{1,0:T(8,128)(2,1)S(1)} %get-tuple-element.122), channel_id=1, source_target_pairs={{0,26},{1,27},{2,24},{3,25},{8,18},{9,19},{10,16},{11,17},{16,10},... | collective-permute-start | bytes 147464 | tf_op jit(solution)/shard_map/ppermute | solution.py:293
  98.1 19.4 %collective-permute-start.31 = (bf16[32,768]{1,0:T(8,128)(2,1)S(1)}, bf16[32,768]{1,0:T(8,128)(2,1)S(1)}, u32[]{:S(2)}, u32[]{:S(2)}) collective-permute-start(bf16[32,768]{1,0:T(8,128)(2,1)S(1)} %get-tuple-element.123), channel_id=1, source_target_pairs={{0,27},{1,26},{2,25},{3,24},{8,19},{9,18},{10,17},{11,16},{16,11},... | collective-permute-start | bytes 147464 | tf_op jit(solution)/shard_map/ppermute | solution.py:293
  113.9 4.7 %collective-permute-start.49 = (bf16[32,768]{1,0:T(8,128)(2,1)S(1)}, bf16[32,768]{1,0:T(8,128)(2,1)S(1)}, u32[]{:S(2)}, u32[]{:S(2)}) collective-permute-start(bf16[32,768]{1,0:T(8,128)(2,1)S(1)} %get-tuple-element.147), channel_id=1, source_target_pairs={{0,1},{1,0},{2,3},{3,2},{8,9},{9,8},{10,11},{11,10},{16,17},{17,16... | collective-permute-start | bytes 147464 | tf_op jit(solution)/shard_map/ppermute | solution.py:293
  115.0 4.5 %collective-permute-start.50 = (bf16[32,768]{1,0:T(8,128)(2,1)S(1)}, bf16[32,768]{1,0:T(8,128)(2,1)S(1)}, u32[]{:S(2)}, u32[]{:S(2)}) collective-permute-start(bf16[32,768]{1,0:T(8,128)(2,1)S(1)} %get-tuple-element.148), channel_id=1, source_target_pairs={{0,2},{1,3},{2,0},{3,1},{8,10},{9,11},{10,8},{11,9},{16,18},{17,19... | collective-permute-start | bytes 147464 | tf_op jit(solution)/shard_map/ppermute | solution.py:293
  115.8 5.1 %collective-permute-start.51 = (bf16[32,768]{1,0:T(8,128)(2,1)S(1)}, bf16[32,768]{1,0:T(8,128)(2,1)S(1)}, u32[]{:S(2)}, u32[]{:S(2)}) collective-permute-start(bf16[32,768]{1,0:T(8,128)(2,1)S(1)} %get-tuple-element.149), channel_id=1, source_target_pairs={{0,3},{1,2},{2,1},{3,0},{8,11},{9,10},{10,9},{11,8},{16,19},{17,18... | collective-permute-start | bytes 147464 | tf_op jit(solution)/shard_map/ppermute | solution.py:293
  117.5 4.9 %collective-permute-start.52 = (bf16[32,768]{1,0:T(8,128)(2,1)S(1)}, bf16[32,768]{1,0:T(8,128)(2,1)S(1)}, u32[]{:S(2)}, u32[]{:S(2)}) collective-permute-start(bf16[32,768]{1,0:T(8,128)(2,1)S(1)} %get-tuple-element.150), channel_id=1, source_target_pairs={{0,8},{1,9},{2,10},{3,11},{8,0},{9,1},{10,2},{11,3},{16,24},{17,25... | collective-permute-start | bytes 147464 | tf_op jit(solution)/shard_map/ppermute | solution.py:293
  117.5 6.4 %collective-permute-start.53 = (bf16[32,768]{1,0:T(8,128)(2,1)S(1)}, bf16[32,768]{1,0:T(8,128)(2,1)S(1)}, u32[]{:S(2)}, u32[]{:S(2)}) collective-permute-start(bf16[32,768]{1,0:T(8,128)(2,1)S(1)} %get-tuple-element.151), channel_id=1, source_target_pairs={{0,9},{1,8},{2,11},{3,10},{8,1},{9,0},{10,3},{11,2},{16,25},{17,24... | collective-permute-start | bytes 147464 | tf_op jit(solution)/shard_map/ppermute | solution.py:293
  118.6 6.9 %collective-permute-start.54 = (bf16[32,768]{1,0:T(8,128)(2,1)S(1)}, bf16[32,768]{1,0:T(8,128)(2,1)S(1)}, u32[]{:S(2)}, u32[]{:S(2)}) collective-permute-start(bf16[32,768]{1,0:T(8,128)(2,1)S(1)} %get-tuple-element.152), channel_id=1, source_target_pairs={{0,10},{1,11},{2,8},{3,9},{8,2},{9,3},{10,0},{11,1},{16,26},{17,27... | collective-permute-start | bytes 147464 | tf_op jit(solution)/shard_map/ppermute | solution.py:293
  119.5 7.2 %collective-permute-start.55 = (bf16[32,768]{1,0:T(8,128)(2,1)S(1)}, bf16[32,768]{1,0:T(8,128)(2,1)S(1)}, u32[]{:S(2)}, u32[]{:S(2)}) collective-permute-start(bf16[32,768]{1,0:T(8,128)(2,1)S(1)} %get-tuple-element.153), channel_id=1, source_target_pairs={{0,11},{1,10},{2,9},{3,8},{8,3},{9,2},{10,1},{11,0},{16,27},{17,26... | collective-permute-start | bytes 147464 | tf_op jit(solution)/shard_map/ppermute | solution.py:293
  120.8 6.0 %collective-permute-start.56 = (bf16[32,768]{1,0:T(8,128)(2,1)S(1)}, bf16[32,768]{1,0:T(8,128)(2,1)S(1)}, u32[]{:S(2)}, u32[]{:S(2)}) collective-permute-start(bf16[32,768]{1,0:T(8,128)(2,1)S(1)} %get-tuple-element.154), channel_id=1, source_target_pairs={{0,16},{1,17},{2,18},{3,19},{8,24},{9,25},{10,26},{11,27},{16,0},{... | collective-permute-start | bytes 147464 | tf_op jit(solution)/shard_map/ppermute | solution.py:293
  122.4 7.1 %collective-permute-start.57 = (bf16[32,768]{1,0:T(8,128)(2,1)S(1)}, bf16[32,768]{1,0:T(8,128)(2,1)S(1)}, u32[]{:S(2)}, u32[]{:S(2)}) collective-permute-start(bf16[32,768]{1,0:T(8,128)(2,1)S(1)} %get-tuple-element.155), channel_id=1, source_target_pairs={{0,17},{1,16},{2,19},{3,18},{8,25},{9,24},{10,27},{11,26},{16,1},{... | collective-permute-start | bytes 147464 | tf_op jit(solution)/shard_map/ppermute | solution.py:293
  123.9 5.8 %collective-permute-start.58 = (bf16[32,768]{1,0:T(8,128)(2,1)S(1)}, bf16[32,768]{1,0:T(8,128)(2,1)S(1)}, u32[]{:S(2)}, u32[]{:S(2)}) collective-permute-start(bf16[32,768]{1,0:T(8,128)(2,1)S(1)} %get-tuple-element.156), channel_id=1, source_target_pairs={{0,18},{1,19},{2,16},{3,17},{8,26},{9,27},{10,24},{11,25},{16,2},{... | collective-permute-start | bytes 147464 | tf_op jit(solution)/shard_map/ppermute | solution.py:293
  125.6 7.3 %collective-permute-start.59 = (bf16[32,768]{1,0:T(8,128)(2,1)S(1)}, bf16[32,768]{1,0:T(8,128)(2,1)S(1)}, u32[]{:S(2)}, u32[]{:S(2)}) collective-permute-start(bf16[32,768]{1,0:T(8,128)(2,1)S(1)} %get-tuple-element.157), channel_id=1, source_target_pairs={{0,19},{1,18},{2,17},{3,16},{8,27},{9,26},{10,25},{11,24},{16,3},{... | collective-permute-start | bytes 147464 | tf_op jit(solution)/shard_map/ppermute | solution.py:293
  126.7 9.8 %collective-permute-start.60 = (bf16[32,768]{1,0:T(8,128)(2,1)S(1)}, bf16[32,768]{1,0:T(8,128)(2,1)S(1)}, u32[]{:S(2)}, u32[]{:S(2)}) collective-permute-start(bf16[32,768]{1,0:T(8,128)(2,1)S(1)} %get-tuple-element.158), channel_id=1, source_target_pairs={{0,24},{1,25},{2,26},{3,27},{8,16},{9,17},{10,18},{11,19},{16,8},{... | collective-permute-start | bytes 147464 | tf_op jit(solution)/shard_map/ppermute | solution.py:293
  126.9 9.6 %collective-permute-start.61 = (bf16[32,768]{1,0:T(8,128)(2,1)S(1)}, bf16[32,768]{1,0:T(8,128)(2,1)S(1)}, u32[]{:S(2)}, u32[]{:S(2)}) collective-permute-start(bf16[32,768]{1,0:T(8,128)(2,1)S(1)} %get-tuple-element.159), channel_id=1, source_target_pairs={{0,25},{1,24},{2,27},{3,26},{8,17},{9,16},{10,19},{11,18},{16,9},{... | collective-permute-start | bytes 147464 | tf_op jit(solution)/shard_map/ppermute | solution.py:293
  129.5 7.0 %collective-permute-start.62 = (bf16[32,768]{1,0:T(8,128)(2,1)S(1)}, bf16[32,768]{1,0:T(8,128)(2,1)S(1)}, u32[]{:S(2)}, u32[]{:S(2)}) collective-permute-start(bf16[32,768]{1,0:T(8,128)(2,1)S(1)} %get-tuple-element.160), channel_id=1, source_target_pairs={{0,26},{1,27},{2,24},{3,25},{8,18},{9,19},{10,16},{11,17},{16,10},... | collective-permute-start | bytes 147464 | tf_op jit(solution)/shard_map/ppermute | solution.py:293
  129.7 6.7 %collective-permute-start.63 = (bf16[32,768]{1,0:T(8,128)(2,1)S(1)}, bf16[32,768]{1,0:T(8,128)(2,1)S(1)}, u32[]{:S(2)}, u32[]{:S(2)}) collective-permute-start(bf16[32,768]{1,0:T(8,128)(2,1)S(1)} %get-tuple-element.161), channel_id=1, source_target_pairs={{0,27},{1,26},{2,25},{3,24},{8,19},{9,18},{10,17},{11,16},{16,11},... | collective-permute-start | bytes 147464 | tf_op jit(solution)/shard_map/ppermute | solution.py:293
  132.8 18.1 %collective-permute-start.65 = (f32[2,128]{1,0:T(2,128)S(1)}, f32[2,128]{1,0:T(2,128)S(1)}, u32[]{:S(2)}, u32[]{:S(2)}) collective-permute-start(f32[2,128]{1,0:T(2,128)S(1)} %get-tuple-element.165), channel_id=1, source_target_pairs={{0,4},{4,0},{1,5},{5,1},{2,6},{6,2},{3,7},{7,3},{8,12},{12,8},{9,1... | collective-permute-start | bytes 3080 | tf_op jit(solution)/shard_map/ppermute | solution.py:285
  136.9 17.0 %collective-permute-start.64 = (bf16[128,768]{1,0:T(8,128)(2,1)S(1)}, bf16[128,768]{1,0:T(8,128)(2,1)S(1)}, u32[]{:S(2)}, u32[]{:S(2)}) collective-permute-start(bf16[128,768]{1,0:T(8,128)(2,1)S(1)} %get-tuple-element.163), channel_id=1, source_target_pairs={{0,4},{4,0},{1,5},{5,1},{2,6},{6,2},{3,7},{7,3},{8,12},{12,8},{9,1... | collective-permute-start | bytes 589832 | tf_op jit(solution)/shard_map/ppermute | solution.py:285
  139.1 19.1 %collective-permute-start.48 = (bf16[128,768]{1,0:T(8,128)(2,1)S(1)}, bf16[128,768]{1,0:T(8,128)(2,1)S(1)}, u32[]{:S(2)}, u32[]{:S(2)}) collective-permute-start(bf16[128,768]{1,0:T(8,128)(2,1)S(1)} %get-tuple-element.145), channel_id=1, source_target_pairs={{0,4},{4,0},{1,5},{5,1},{2,6},{6,2},{3,7},{7,3},{8,12},{12,8},{9,1... | collective-permute-start | bytes 589832 | tf_op jit(solution)/shard_map/ppermute | solution.py:285
  (12 other events, 122.2 us)

commit v5 on v3

v5 whole, which is shorter than its diff:
```python
import functools

import jax
import jax.numpy as jnp
from jax import lax
from jax.experimental import pallas as pl
from jax.experimental.pallas import tpu as pltpu
from jax.sharding import PartitionSpec as P

BLOCK = 128
BF16 = jnp.bfloat16
F32 = jnp.float32
MIB = 1024 * 1024
SUB = 256


def dot(a, b, contract_a, contract_b):
    return lax.dot_general(
        a, b, (((contract_a,), (contract_b,)), ((), ())), preferred_element_type=F32
    )


def column(row):
    count = row.shape[1]
    return jnp.transpose(jnp.broadcast_to(row, (count, count)))


def route(ids_ref, keep_ref, gates_ref, meta_ref, capacity):
    token_rows = ids_ref.shape[1]
    ids = ids_ref[...].astype(F32)
    earlier = lax.broadcasted_iota(jnp.int32, (token_rows, token_rows), 0) < lax.broadcasted_iota(
        jnp.int32, (token_rows, token_rows), 1
    )
    columns = (column(ids[0:1]), column(ids[1:2]))
    for k in range(2):
        count = jnp.zeros((token_rows, token_rows), F32)
        for other_choice in columns:
            count = count + jnp.where(earlier & (other_choice == ids[k : k + 1]), 1.0, 0.0)
        slot = jnp.sum(count, axis=0, keepdims=True).astype(jnp.int32)
        row = ids_ref[k : k + 1, :] * capacity + slot
        meta_ref[k : k + 1, :] = jnp.where(keep_ref[k : k + 1, :] > 0, row, -1).astype(F32)
        meta_ref[k + 2 : k + 3, :] = gates_ref[k : k + 1, :]
    meta_ref[4:8, :] = jnp.zeros((4, token_rows), F32)


def hits(slot_total, meta_ref, k):
    rows = meta_ref[k : k + 1, :].astype(jnp.int32)
    index = lax.broadcasted_iota(jnp.int32, (slot_total, rows.shape[1]), 0)
    return index == rows


def one_hot(mask):
    return jnp.where(mask, 1.0, 0.0).astype(BF16)


def restore(tokens_ref):
    pieces = []
    for b in range(tokens_ref.shape[1] // BLOCK):
        x = tokens_ref[:, b * BLOCK : (b + 1) * BLOCK].astype(F32)
        scale = (jnp.max(jnp.abs(x), axis=1, keepdims=True) + 1e-06).astype(BF16).astype(F32)
        quantized = (x / scale).astype(BF16)
        pieces.append((quantized.astype(F32) * scale).astype(BF16))
    return jnp.concatenate(pieces, axis=1)


def place_tokens_kernel(capacity, tokens_ref, ids_ref, keep_ref, gates_ref, meta_ref, out_ref):
    route(ids_ref, keep_ref, gates_ref, meta_ref, capacity)
    slot_total = out_ref.shape[0]
    mask = hits(slot_total, meta_ref, 0) | hits(slot_total, meta_ref, 1)
    out_ref[...] = dot(one_hot(mask), restore(tokens_ref), 1, 0).astype(BF16)


def scaled_rows(gate_row, grad_ref):
    gate = column(gate_row)
    pieces = [
        gate * grad_ref[:, b * BLOCK : (b + 1) * BLOCK].astype(F32)
        for b in range(grad_ref.shape[1] // BLOCK)
    ]
    return jnp.concatenate(pieces, axis=1)


def place_cotangents_kernel(grad_ref, meta_ref, out_ref):
    slot_total = out_ref.shape[0]
    parts = [
        dot(
            one_hot(hits(slot_total, meta_ref, k)),
            scaled_rows(meta_ref[k + 2 : k + 3, :], grad_ref).astype(BF16),
            1,
            0,
        )
        for k in range(2)
    ]
    out_ref[...] = (parts[0] + parts[1]).astype(BF16)


def gelu_parts(v):
    c = 0.7978845608028654
    inner = c + (c * 0.044715) * (v * v)
    s = 0.5 + 0.5 * jnp.tanh(v * inner)
    hidden = v * s
    slope = s + (hidden * (1.0 - s)) * (6.0 * inner - 4.0 * c)
    return hidden.astype(BF16), slope.astype(BF16)


def forward_kernel(x_ref, w_in_ref, w_out_ref, hidden_ref, slope_ref, out_ref, total):
    step = pl.program_id(0)

    @pl.when(step == 0)
    def _():
        total[...] = jnp.zeros_like(total)

    parts = hidden_ref.shape[1] // SUB
    v = dot(x_ref[...], w_in_ref[:, :SUB], 1, 0)
    pieces = []
    for j in range(parts):
        if j + 1 < parts:
            after = dot(x_ref[...], w_in_ref[:, (j + 1) * SUB : (j + 2) * SUB], 1, 0)
        hidden, slope = gelu_parts(v)
        hidden_ref[:, j * SUB : (j + 1) * SUB] = hidden
        slope_ref[:, j * SUB : (j + 1) * SUB] = slope
        pieces.append(hidden)
        v = after
    total[...] += dot(jnp.concatenate(pieces, axis=1), w_out_ref[...], 1, 0)

    @pl.when(step == pl.num_programs(0) - 1)
    def _():
        out_ref[...] = total[...].astype(BF16)


def backward_kernel(cot_ref, w_in_ref, w_out_ref, slope_ref, grad_pre_ref, out_ref, total):
    step = pl.program_id(0)

    @pl.when(step == 0)
    def _():
        total[...] = jnp.zeros_like(total)

    parts = grad_pre_ref.shape[1] // SUB
    pieces = []
    for j in range(parts):
        grad_hidden = dot(cot_ref[...], w_out_ref[j * SUB : (j + 1) * SUB, :], 1, 1)
        slope = slope_ref[:, j * SUB : (j + 1) * SUB].astype(F32)
        grad_pre = (grad_hidden * slope).astype(BF16)
        grad_pre_ref[:, j * SUB : (j + 1) * SUB] = grad_pre
        pieces.append(grad_pre)
    total[...] += dot(jnp.concatenate(pieces, axis=1), w_in_ref[...], 1, 1)

    @pl.when(step == pl.num_programs(0) - 1)
    def _():
        out_ref[...] = total[...].astype(BF16)


def weights_kernel(x_ref, cot_ref, hidden_ref, grad_pre_ref, grad_in_ref, grad_out_ref):
    grad_in_ref[...] = dot(x_ref[...], grad_pre_ref[...], 0, 0).astype(BF16)
    grad_out_ref[...] = dot(hidden_ref[...], cot_ref[...], 0, 0).astype(BF16)


def pick_outputs_kernel(back_ref, grad_ref, meta_ref, out_ref, gates_ref):
    slot_total = back_ref.shape[0]
    total = None
    for k in range(2):
        picked = dot(one_hot(hits(slot_total, meta_ref, k)), back_ref[...], 0, 0)
        gate = column(meta_ref[k + 2 : k + 3, :])
        weighted = jnp.concatenate(
            [
                gate * picked[:, b * BLOCK : (b + 1) * BLOCK]
                for b in range(picked.shape[1] // BLOCK)
            ],
            axis=1,
        )
        total = weighted if total is None else total + weighted
        sums = jnp.sum(picked * grad_ref[...].astype(F32), axis=1, keepdims=True)
        rows = jnp.transpose(jnp.broadcast_to(sums, (sums.shape[0], sums.shape[0])))
        gates_ref[k : k + 1, :] = rows[0:1, :]
    out_ref[...] = total.astype(BF16)


def pick_gradients_kernel(back_ref, meta_ref, out_ref):
    slot_total = back_ref.shape[0]
    mask = hits(slot_total, meta_ref, 0) | hits(slot_total, meta_ref, 1)
    out_ref[...] = dot(one_hot(mask), back_ref[...], 0, 0).astype(BF16)


def call(kernel, outs, flops=0, traffic=0, limit=12, **options):
    return pl.pallas_call(
        kernel,
        out_shape=outs,
        compiler_params=pltpu.CompilerParams(vmem_limit_bytes=limit * MIB),
        cost_estimate=pl.CostEstimate(flops=flops, bytes_accessed=traffic, transcendentals=0),
        **options,
    )


def in_hbm(values):
    return pltpu.with_memory_space_constraint(values, pltpu.HBM)


def body(tokens, expert_ids, keep_mask, gate_weights, weight_in, weight_out, grad_output):
    token_rows, width = tokens.shape
    hidden_width = weight_in.shape[2]
    experts = lax.axis_size("row") * lax.axis_size("col")
    capacity = 2 * expert_ids.shape[1] * token_rows // experts
    slot_total = experts * capacity

    def shuffle(rows):
        shaped = rows.reshape(experts, capacity, width)
        return lax.all_to_all(
            shaped, ("row", "col"), split_axis=0, concat_axis=0, tiled=True
        ).reshape(slot_total, width)

    slots = jax.ShapeDtypeStruct((slot_total, width), BF16)
    slot_bytes = slot_total * width * 2
    token_bytes = token_rows * width * 2
    place_flops = 2 * slot_total * token_rows * width
    meta, sent = call(
        functools.partial(place_tokens_kernel, capacity),
        [jax.ShapeDtypeStruct((8, token_rows), F32), slots],
        place_flops,
        token_bytes + slot_bytes,
    )(in_hbm(tokens), in_hbm(expert_ids.T), in_hbm(keep_mask.T), in_hbm(gate_weights.T))
    x = shuffle(sent)
    sent_cot = call(
        place_cotangents_kernel, slots, 2 * place_flops, token_bytes + slot_bytes
    )(in_hbm(grad_output), meta)
    cot = shuffle(sent_cot)

    chunk = 1024
    whole = pl.BlockSpec((slot_total, width), lambda i: (0, 0))
    in_spec = pl.BlockSpec((None, width, chunk), lambda i: (0, 0, i))
    out_spec = pl.BlockSpec((None, chunk, width), lambda i: (0, i, 0))
    mid_spec = pl.BlockSpec((slot_total, chunk), lambda i: (0, i))
    mid = pltpu.HBM((slot_total, hidden_width), BF16)
    product = 2 * slot_total * width * hidden_width
    traffic = 2 * slot_bytes + 4 * width * hidden_width + 4 * slot_total * hidden_width
    grid = (hidden_width // chunk,)
    total = pltpu.VMEM((slot_total, width), F32)
    weight_in, weight_out = in_hbm(weight_in), in_hbm(weight_out)
    hidden, slope, outputs = call(
        forward_kernel,
        [mid, mid, slots],
        2 * product,
        traffic,
        32,
        grid=grid,
        in_specs=[whole, in_spec, out_spec],
        out_specs=[mid_spec, mid_spec, whole],
        scratch_shapes=[total],
    )(x, weight_in, weight_out)
    back_out = shuffle(outputs)
    grad_pre, grad_rows = call(
        backward_kernel,
        [mid, slots],
        2 * product,
        traffic,
        32,
        grid=grid,
        in_specs=[whole, in_spec, out_spec, mid_spec],
        out_specs=[mid_spec, whole],
        scratch_shapes=[total],
    )(cot, weight_in, weight_out, in_hbm(slope))
    back_grad = shuffle(grad_rows)
    combined, grad_gates = call(
        pick_outputs_kernel,
        [
            jax.ShapeDtypeStruct((token_rows, width), BF16),
            jax.ShapeDtypeStruct((2, token_rows), F32),
        ],
        2 * place_flops,
        2 * token_bytes + slot_bytes,
    )(back_out, in_hbm(grad_output), meta)
    grad_in_w, grad_out_w = call(
        weights_kernel,
        [pltpu.HBM(weight_in.shape, BF16), pltpu.HBM(weight_out.shape, BF16)],
        2 * product,
        traffic,
        32,
        grid=grid,
        in_specs=[whole, whole, mid_spec, mid_spec],
        out_specs=[in_spec, out_spec],
    )(x, cot, in_hbm(hidden), in_hbm(grad_pre))
    grad_tokens = call(
        pick_gradients_kernel,
        jax.ShapeDtypeStruct((token_rows, width), BF16),
        place_flops,
        slot_bytes + token_bytes,
    )(back_grad, meta)
    return (combined, grad_tokens, grad_gates.T, grad_in_w, grad_out_w)


def solution(mesh):
    flat = P(("row", "col"), None)
    deep = P(("row", "col"), None, None)
    return jax.shard_map(
        body,
        mesh=mesh,
        in_specs=(flat, flat, flat, flat, deep, deep, flat),
        out_specs=(flat, flat, flat, deep, deep),
        check_vma=False,
    )
```

time: 132 us -> 108 us (0.82)
  local copies, waits for them, and re-layouts: 31 us -> 0.96 us
  starting transfers between devices: 33.3 us -> 15.2 us
  waiting for transfers between devices: 29.9 us -> 46.3 us
  Pallas kernels: 35.6 us -> 44.1 us
    all_to_all x4, waiting for transfers between devices: 8.79 us -> 46.3 us  [shuffle(): lax.all_to_all(shaped, ('row', 'col'), split_axis=0, concat_axis=0, tiled...]
    unnamed x40 -> x2, local copies, waits for them, and re-layouts: 31 us -> 0.96 us
    ppermute x6 -> x0, waiting for transfers between devices: 21.1 us -> none  [exchange(): return lax.ppermute(values, 'half', swap)]
    ppermute x6 -> x0, starting transfers between devices: 10.6 us -> none  [exchange(): return lax.ppermute(values, 'half', swap)]
    pallas_call x9 -> x7, Pallas kernels: 35.6 us -> 44.1 us  [the longest x1 13.4 us: body(): call(forward_kernel, [mid, mid, slots], 2 * product, traffic, 32, grid=gr...]
    all_to_all x4, starting transfers between devices: 22.8 us -> 15.2 us  [shuffle(): lax.all_to_all(shaped, ('row', 'col'), split_axis=0, concat_axis=0, tiled...]
  transfers between devices with their start and end apart: 10 -> 4, of which waited for: 5 -> 4; matrix products, arithmetic and copies ran while one was open for 0% -> 0% of each run, Pallas kernels for 25% -> 38%
where the time goes in v5:
time: 108 us; the launch traced here: 107 us
  waiting for transfers between devices  46.3 us (43%)
  Pallas kernels  44.1 us (41%)
  starting transfers between devices  15.2 us (14%)
    all_to_all x4, waiting for transfers between devices, shuffle(): lax.all_to_all(shaped, ('row', 'col'), split_axis=0, concat_axis=0, tiled...  46.3 us
    all_to_all x4, starting transfers between devices, shuffle(): lax.all_to_all(shaped, ('row', 'col'), split_axis=0, concat_axis=0, tiled...  15.2 us
    pallas_call x1, Pallas kernels, body(): call(forward_kernel, [mid, mid, slots], 2 * product, traffic, 32, grid=gr...  13.4 us
    pallas_call x1, Pallas kernels, body(): call(backward_kernel, [mid, slots], 2 * product, traffic, 32, grid=grid,...  12 us
    pallas_call x1, Pallas kernels, body(): call(weights_kernel, [pltpu.HBM(weight_in.shape, BF16), pltpu.HBM(weight_...  10.7 us
    pallas_call x1, Pallas kernels, body(): call(place_cotangents_kernel, slots, 2 * place_flops, token_bytes + slot_...  2.46 us
    pallas_call x1, Pallas kernels, body(): call(functools.partial(place_tokens_kernel, capacity), [jax.ShapeDtypeStr...  2.41 us
  transfers between devices with their start and end apart: 4, of which 4 were waited for; matrix products, arithmetic and copies ran while one was open for 0% of the time, Pallas kernels for 38%

profile of v5, /device:TPU:0, one launch (start us, length us, event | category | flops | bytes accessed | tf_op | source)
XLA Modules:
  0.0 107.1 jit_solution(9741431489957156710)
XLA Ops:
  0.6 2.4 %shard_map.110 = (f32[8,128]{1,0:T(8,128)S(1)}, bf16[512,768]{1,0:T(8,128)(2,1)}) custom-call(bf16[128,768]{1,0:T(8,128)(2,1)} %tokens_ref.1, s32[2,128]{1,0:T(2,128)} %bitcast.19, s32[2,128]{1,0:T(2,128)} %bitcast.20, f32[2,128]{1,0:T(2,128)} %bitcast.21), custom_call_target="tpu_custom_call" | custom-call | flops 100663296 | bytes 983040 | tf_op jit(solution)/shard_map/pallas_call | solution.py:214
  3.0 7.3 %all-to-all-start = ((bf16[32,16,768]{2,1,0:T(8,128)(2,1)}), bf16[32,16,768]{2,1,0:T(8,128)(2,1)S(1)}, u32[]{:S(2)}, u32[]{:S(2)}) async-start(bf16[32,16,768]{2,1,0:T(8,128)(2,1)} %bitcast.3), calls=%async_computation | async-start | bytes 1572864 | tf_op jit(solution)/shard_map/all_to_all | solution.py:206
  10.4 2.5 %shard_map.113 = bf16[512,768]{1,0:T(8,128)(2,1)} custom-call(bf16[128,768]{1,0:T(8,128)(2,1)} %grad_ref.3, f32[8,128]{1,0:T(8,128)S(1)} %get-tuple-element.18.meta_ref), custom_call_target="tpu_custom_call" | custom-call | flops 201326592 | bytes 983040 | tf_op jit(solution)/shard_map/pallas_call | solution.py:221
  12.8 19.5 %all-to-all-done = bf16[32,16,768]{2,1,0:T(8,128)(2,1)S(1)} async-done(((bf16[32,16,768]{2,1,0:T(8,128)(2,1)}), bf16[32,16,768]{2,1,0:T(8,128)(2,1)S(1)}, u32[]{:S(2)}, u32[]{:S(2)}) %all-to-all-start) | async-done | bytes 786464 | tf_op jit(solution)/shard_map/all_to_all | solution.py:206
  32.3 2.6 %all-to-all-start.2 = ((bf16[32,16,768]{2,1,0:T(8,128)(2,1)}), bf16[32,16,768]{2,1,0:T(8,128)(2,1)S(1)}, u32[]{:S(2)}, u32[]{:S(2)}) async-start(bf16[32,16,768]{2,1,0:T(8,128)(2,1)} %bitcast.7), calls=%async_computation.2 | async-start | bytes 1572864 | tf_op jit(solution)/shard_map/all_to_all | solution.py:206
  35.0 13.4 %shard_map.111 = (bf16[512,4096]{1,0:T(8,128)(2,1)}, bf16[512,4096]{1,0:T(8,128)(2,1)}, bf16[512,768]{1,0:T(8,128)(2,1)}) custom-call(bf16[512,768]{1,0:T(8,128)(2,1)S(1)} %bitcast.14, bf16[1,768,4096]{2,1,0:T(8,128)(2,1)} %w_in_ref.3, bf16[1,4096,768]{2,1,0:T(8,128)(2,1)} %w_out_ref.3), custom_call_target="tpu_custom_call" | custom-call | flops 6442450944 | bytes 22544384 | tf_op jit(solution)/shard_map/pallas_call | solution.py:237
  48.3 8.6 %all-to-all-done.2 = bf16[32,16,768]{2,1,0:T(8,128)(2,1)S(1)} async-done(((bf16[32,16,768]{2,1,0:T(8,128)(2,1)}), bf16[32,16,768]{2,1,0:T(8,128)(2,1)S(1)}, u32[]{:S(2)}, u32[]{:S(2)}) %all-to-all-start.2) | async-done | bytes 786464 | tf_op jit(solution)/shard_map/all_to_all | solution.py:206
  56.9 2.6 %all-to-all-start.1 = ((bf16[32,16,768]{2,1,0:T(8,128)(2,1)}), bf16[32,16,768]{2,1,0:T(8,128)(2,1)S(1)}, u32[]{:S(2)}, u32[]{:S(2)}) async-start(bf16[32,16,768]{2,1,0:T(8,128)(2,1)} %bitcast.5), calls=%async_computation.1 | async-start | bytes 1572864 | tf_op jit(solution)/shard_map/all_to_all | solution.py:206
  59.6 12.0 %shard_map.114 = (bf16[512,4096]{1,0:T(8,128)(2,1)}, bf16[512,768]{1,0:T(8,128)(2,1)S(1)}) custom-call(bf16[512,768]{1,0:T(8,128)(2,1)S(1)} %bitcast.16, bf16[1,768,4096]{2,1,0:T(8,128)(2,1)} %w_in_ref.3, bf16[1,4096,768]{2,1,0:T(8,128)(2,1)} %w_out_ref.3, bf16[512,4096]{1,0:T(8,128)(2,1)} %get-tuple-element.20.slope_ref), custom_call_target="tpu_custom_call" | custom-call | flops 6442450944 | bytes 22544384 | tf_op jit(solution)/shard_map/pallas_call | solution.py:249
  71.6 0.0 copy-start
  71.6 1.0 copy-done
  72.5 9.0 %all-to-all-done.1 = bf16[32,16,768]{2,1,0:T(8,128)(2,1)S(1)} async-done(((bf16[32,16,768]{2,1,0:T(8,128)(2,1)}), bf16[32,16,768]{2,1,0:T(8,128)(2,1)S(1)}, u32[]{:S(2)}, u32[]{:S(2)}) %all-to-all-start.1) | async-done | bytes 786464 | tf_op jit(solution)/shard_map/all_to_all | solution.py:206
  81.5 2.6 %all-to-all-start.3 = ((bf16[32,16,768]{2,1,0:T(8,128)(2,1)}), bf16[32,16,768]{2,1,0:T(8,128)(2,1)S(1)}, u32[]{:S(2)}, u32[]{:S(2)}) async-start(bf16[32,16,768]{2,1,0:T(8,128)(2,1)} %bitcast.18), calls=%async_computation.3 | async-start | bytes 1572864 | tf_op jit(solution)/shard_map/all_to_all | solution.py:206
  84.2 10.7 %shard_map.116 = (bf16[1,768,4096]{2,1,0:T(8,128)(2,1)}, bf16[1,4096,768]{2,1,0:T(8,128)(2,1)}) custom-call(bf16[512,768]{1,0:T(8,128)(2,1)S(1)} %bitcast.15, bf16[512,768]{1,0:T(8,128)(2,1)S(1)} %bitcast.17, bf16[512,4096]{1,0:T(8,128)(2,1)} %get-tuple-element.23.hidden_ref, bf16[512,4096]{1,0:T(8,128)(2,1)} %get-tuple-element.24.grad_pre_ref), custom_call_target="tpu_custom_call" | custom-call | flops 6442450944 | bytes 22544384 | tf_op jit(solution)/shard_map/pallas_call | solution.py:270
  94.9 2.1 %shard_map.112 = (bf16[128,768]{1,0:T(8,128)(2,1)}, f32[2,128]{1,0:T(2,128)}) custom-call(bf16[512,768]{1,0:T(8,128)(2,1)S(1)} %bitcast.12, bf16[128,768]{1,0:T(8,128)(2,1)} %grad_ref.3, f32[8,128]{1,0:T(8,128)S(1)} %get-tuple-element.18.meta_ref), custom_call_target="tpu_custom_call" | custom-call | flops 201326592 | bytes 1179648 | tf_op jit(solution)/shard_map/pallas_call | solution.py:261
  97.0 9.2 %all-to-all-done.3 = bf16[32,16,768]{2,1,0:T(8,128)(2,1)S(1)} async-done(((bf16[32,16,768]{2,1,0:T(8,128)(2,1)}), bf16[32,16,768]{2,1,0:T(8,128)(2,1)S(1)}, u32[]{:S(2)}, u32[]{:S(2)}) %all-to-all-start.3) | async-done | bytes 786464 | tf_op jit(solution)/shard_map/all_to_all | solution.py:206
  106.1 1.0 shard_map.115
Async XLA Ops:
  3.0 29.3 %all-to-all-start = ((bf16[32,16,768]{2,1,0:T(8,128)(2,1)}), bf16[32,16,768]{2,1,0:T(8,128)(2,1)S(1)}, u32[]{:S(2)}, u32[]{:S(2)}) async-start(bf16[32,16,768]{2,1,0:T(8,128)(2,1)} %bitcast.3), calls=%async_computation | async-start | bytes 1572864 | tf_op jit(solution)/shard_map/all_to_all | solution.py:206
  32.3 24.6 %all-to-all-start.2 = ((bf16[32,16,768]{2,1,0:T(8,128)(2,1)}), bf16[32,16,768]{2,1,0:T(8,128)(2,1)S(1)}, u32[]{:S(2)}, u32[]{:S(2)}) async-start(bf16[32,16,768]{2,1,0:T(8,128)(2,1)} %bitcast.7), calls=%async_computation.2 | async-start | bytes 1572864 | tf_op jit(solution)/shard_map/all_to_all | solution.py:206
  56.9 24.6 %all-to-all-start.1 = ((bf16[32,16,768]{2,1,0:T(8,128)(2,1)}), bf16[32,16,768]{2,1,0:T(8,128)(2,1)S(1)}, u32[]{:S(2)}, u32[]{:S(2)}) async-start(bf16[32,16,768]{2,1,0:T(8,128)(2,1)} %bitcast.5), calls=%async_computation.1 | async-start | bytes 1572864 | tf_op jit(solution)/shard_map/all_to_all | solution.py:206
  71.6 1.0 copy-start
  81.5 24.6 %all-to-all-start.3 = ((bf16[32,16,768]{2,1,0:T(8,128)(2,1)}), bf16[32,16,768]{2,1,0:T(8,128)(2,1)S(1)}, u32[]{:S(2)}, u32[]{:S(2)}) async-start(bf16[32,16,768]{2,1,0:T(8,128)(2,1)} %bitcast.18), calls=%async_computation.3 | async-start | bytes 1572864 | tf_op jit(solution)/shard_map/all_to_all | solution.py:206

commit v6 on v5

v6 whole, which is shorter than its diff:
```python
import functools

import jax
import jax.numpy as jnp
from jax import lax
from jax.experimental import pallas as pl
from jax.experimental.pallas import tpu as pltpu
from jax.sharding import Mesh
from jax.sharding import PartitionSpec as P

BLOCK = 128
BF16 = jnp.bfloat16
F32 = jnp.float32
MIB = 1024 * 1024
SUB = 256
GROUP = ("row", "rest")


def dot(a, b, contract_a, contract_b):
    return lax.dot_general(
        a, b, (((contract_a,), (contract_b,)), ((), ())), preferred_element_type=F32
    )


def column(row):
    count = row.shape[1]
    return jnp.transpose(jnp.broadcast_to(row, (count, count)))


def route(rest_bits, capacity, half, ids_ref, keep_ref, gates_ref, mine_ref, other_ref):
    token_rows = ids_ref.shape[1]
    ids = ids_ref[...].astype(F32)
    earlier = lax.broadcasted_iota(jnp.int32, (token_rows, token_rows), 0) < lax.broadcasted_iota(
        jnp.int32, (token_rows, token_rows), 1
    )
    columns = (column(ids[0:1]), column(ids[1:2]))
    for k in range(2):
        count = jnp.zeros((token_rows, token_rows), F32)
        for other_choice in columns:
            count = count + jnp.where(earlier & (other_choice == ids[k : k + 1]), 1.0, 0.0)
        slot = jnp.sum(count, axis=0, keepdims=True).astype(jnp.int32)
        expert = ids_ref[k : k + 1, :]
        kept = keep_ref[k : k + 1, :] > 0
        side = (expert >> rest_bits) & 1
        local = ((expert >> (rest_bits + 1)) << rest_bits) + (expert & ((1 << rest_bits) - 1))
        for ref, there, offset in (
            (mine_ref, kept & (side == half), 0),
            (other_ref, kept & (side != half), capacity),
        ):
            ref[k : k + 1, :] = jnp.where(there, local * capacity + slot, -1).astype(F32)
            joint = local * (2 * capacity) + offset + slot
            ref[k + 4 : k + 5, :] = jnp.where(there, joint, -1).astype(F32)
            ref[k + 2 : k + 3, :] = gates_ref[k : k + 1, :]
    for ref in (mine_ref, other_ref):
        ref[6:8, :] = jnp.zeros((2, token_rows), F32)


def hits(slot_total, meta_ref, k):
    rows = meta_ref[k : k + 1, :].astype(jnp.int32)
    index = lax.broadcasted_iota(jnp.int32, (slot_total, rows.shape[1]), 0)
    return index == rows


def one_hot(mask):
    return jnp.where(mask, 1.0, 0.0).astype(BF16)


def restore(tokens_ref):
    pieces = []
    for b in range(tokens_ref.shape[1] // BLOCK):
        x = tokens_ref[:, b * BLOCK : (b + 1) * BLOCK].astype(F32)
        scale = (jnp.max(jnp.abs(x), axis=1, keepdims=True) + 1e-06).astype(BF16).astype(F32)
        quantized = (x / scale).astype(BF16)
        pieces.append((quantized.astype(F32) * scale).astype(BF16))
    return jnp.concatenate(pieces, axis=1)


def place_own_kernel(
    rest_bits, capacity, half_ref, tokens_ref, ids_ref, keep_ref, gates_ref, mine_ref, other_ref, out_ref
):
    route(rest_bits, capacity, half_ref[0], ids_ref, keep_ref, gates_ref, mine_ref, other_ref)
    slot_total = out_ref.shape[0]
    mask = hits(slot_total, mine_ref, 0) | hits(slot_total, mine_ref, 1)
    out_ref[...] = dot(one_hot(mask), restore(tokens_ref), 1, 0).astype(BF16)


def place_partner_kernel(tokens_ref, meta_ref, grad_ref, out_ref, grad_copy_ref):
    slot_total = out_ref.shape[0]
    mask = hits(slot_total, meta_ref, 0) | hits(slot_total, meta_ref, 1)
    out_ref[...] = dot(one_hot(mask), restore(tokens_ref), 1, 0).astype(BF16)
    grad_copy_ref[...] = grad_ref[...]


def scaled_rows(gate_row, grad_ref):
    gate = column(gate_row)
    pieces = [
        gate * grad_ref[:, b * BLOCK : (b + 1) * BLOCK].astype(F32)
        for b in range(grad_ref.shape[1] // BLOCK)
    ]
    return jnp.concatenate(pieces, axis=1)


def place_cotangents_kernel(own_grad, partner_grad, own_meta, partner_meta, out_ref):
    slot_total = out_ref.shape[0]
    total = None
    for grad_ref, meta_ref in ((own_grad, own_meta), (partner_grad, partner_meta)):
        for k in range(2):
            rows = scaled_rows(meta_ref[k + 2 : k + 3, :], grad_ref).astype(BF16)
            part = dot(one_hot(hits(slot_total, meta_ref, k + 4)), rows, 1, 0)
            total = part if total is None else total + part
    out_ref[...] = total.astype(BF16)


def gelu_parts(v):
    c = 0.7978845608028654
    inner = c + (c * 0.044715) * (v * v)
    s = 0.5 + 0.5 * jnp.tanh(v * inner)
    hidden = v * s
    slope = s + (hidden * (1.0 - s)) * (6.0 * inner - 4.0 * c)
    return hidden.astype(BF16), slope.astype(BF16)


def interleave(block, own, partner):
    pieces = []
    for at in range(0, own.shape[0], block):
        pieces += [own[at : at + block, :], partner[at : at + block, :]]
    return jnp.concatenate(pieces, axis=0)


def separate(block, values):
    pieces = [values[at : at + block, :] for at in range(0, values.shape[0], block)]
    return jnp.concatenate(pieces[0::2], axis=0), jnp.concatenate(pieces[1::2], axis=0)


def at_chunk(j, size):
    return pl.ds(pl.multiple_of(j * size, size), size)


def run_chunks(count, fetches, sends, work):
    ahead = min(2, count)
    for j in range(ahead):
        for copy in fetches(j):
            copy.start()

    def each(j, carry):
        @pl.when(j + ahead < count)
        def _():
            for copy in fetches(j + ahead):
                copy.start()

        work(j, [copy.wait for copy in fetches(j)])
        for copy in sends(j):
            copy.start()
        return carry

    lax.fori_loop(0, count, each, 0)

    def drain(j, carry):
        for copy in sends(j):
            copy.wait()
        return carry

    lax.fori_loop(0, count, drain, 0)


def forward_kernel(
    block, own, partner, w_in, w_out, out_ref, x, hidden, slope, w_in_buf, w_out_buf, hidden_buf, slope_buf, total, in_sem, out_sem
):
    count, _, chunk = hidden.shape
    parts = chunk // SUB
    x[...] = interleave(block, own, partner)
    total[...] = jnp.zeros_like(total)

    def fetches(j):
        copies = [
            pltpu.make_async_copy(
                w_in.at[0, :, at_chunk(j * parts + p, SUB)],
                w_in_buf.at[j * parts + p],
                in_sem.at[j, p],
            )
            for p in range(parts)
        ]
        rows = w_out.at[0, at_chunk(j, chunk), :]
        return copies + [pltpu.make_async_copy(rows, w_out_buf.at[j], in_sem.at[j, parts])]

    def sends(j):
        return [
            pltpu.make_async_copy(hidden_buf.at[j], hidden.at[j], out_sem.at[j, 0]),
            pltpu.make_async_copy(slope_buf.at[j], slope.at[j], out_sem.at[j, 1]),
        ]

    def work(j, waits):
        waits[0]()
        v = dot(x[...], w_in_buf[j * parts], 1, 0)
        done = []
        for p in range(parts):
            if p + 1 < parts:
                waits[p + 1]()
                after = dot(x[...], w_in_buf[j * parts + p + 1], 1, 0)
            else:
                waits[parts]()
            hidden_part, slope_part = gelu_parts(v)
            hidden_buf[j, :, p * SUB : (p + 1) * SUB] = hidden_part
            slope_buf[j, :, p * SUB : (p + 1) * SUB] = slope_part
            done.append(hidden_part)
            v = after
        total[...] += dot(jnp.concatenate(done, axis=1), w_out_buf[j], 1, 0)

    run_chunks(count, fetches, sends, work)
    out_ref[...] = total[...].astype(BF16)


def backward_kernel(
    block, cot, w_in, w_out, slope, own_out, partner_out, grad_pre, w_in_buf, w_out_buf, slope_buf, grad_buf, total, in_sem, out_sem
):
    count, _, chunk = grad_pre.shape
    parts = chunk // SUB
    total[...] = jnp.zeros_like(total)

    def fetches(j):
        copies = [
            pltpu.make_async_copy(
                w_out.at[0, at_chunk(j * parts + p, SUB), :],
                w_out_buf.at[j * parts + p],
                in_sem.at[j, p],
            )
            for p in range(parts)
        ]
        return copies + [
            pltpu.make_async_copy(slope.at[j], slope_buf.at[j], in_sem.at[j, parts]),
            pltpu.make_async_copy(
                w_in.at[0, :, at_chunk(j, chunk)], w_in_buf.at[j], in_sem.at[j, parts + 1]
            ),
        ]

    def sends(j):
        return [pltpu.make_async_copy(grad_buf.at[j], grad_pre.at[j], out_sem.at[j, 0])]

    def work(j, waits):
        done = []
        for p in range(parts):
            waits[p]()
            grad_hidden = dot(cot[...], w_out_buf[j * parts + p], 1, 1)
            if p == 0:
                waits[parts]()
            slope_part = slope_buf[j, :, p * SUB : (p + 1) * SUB].astype(F32)
            part = (grad_hidden * slope_part).astype(BF16)
            grad_buf[j, :, p * SUB : (p + 1) * SUB] = part
            done.append(part)
        waits[parts + 1]()
        total[...] += dot(jnp.concatenate(done, axis=1), w_in_buf[j], 1, 1)

    run_chunks(count, fetches, sends, work)
    own_out[...], partner_out[...] = separate(block, total[...].astype(BF16))


def weights_kernel(
    x, cot, hidden, grad_pre, grad_in, grad_out, hidden_buf, grad_buf, in_buf, out_buf, in_sem, out_sem
):
    count, _, chunk = hidden.shape

    def fetches(j):
        return [
            pltpu.make_async_copy(hidden.at[j], hidden_buf.at[j], in_sem.at[j, 0]),
            pltpu.make_async_copy(grad_pre.at[j], grad_buf.at[j], in_sem.at[j, 1]),
        ]

    def sends(j):
        return [
            pltpu.make_async_copy(in_buf.at[j], grad_in.at[0, :, at_chunk(j, chunk)], out_sem.at[j, 0]),
            pltpu.make_async_copy(out_buf.at[j], grad_out.at[0, at_chunk(j, chunk), :], out_sem.at[j, 1]),
        ]

    def work(j, waits):
        waits[0]()
        waits[1]()
        in_buf[j] = dot(x[...], grad_buf[j], 0, 0).astype(BF16)
        out_buf[j] = dot(hidden_buf[j], cot[...], 0, 0).astype(BF16)

    run_chunks(count, fetches, sends, work)


def pick_outputs_kernel(
    back_ref, own_grad, partner_grad, own_meta, partner_meta, own_out, partner_out, own_gates, partner_gates
):
    slot_total = back_ref.shape[0]
    for grad_ref, meta_ref, out_ref, gates_ref in (
        (own_grad, own_meta, own_out, own_gates),
        (partner_grad, partner_meta, partner_out, partner_gates),
    ):
        total = None
        for k in range(2):
            picked = dot(one_hot(hits(slot_total, meta_ref, k + 4)), back_ref[...], 0, 0)
            gate = column(meta_ref[k + 2 : k + 3, :])
            weighted = jnp.concatenate(
                [
                    gate * picked[:, b * BLOCK : (b + 1) * BLOCK]
                    for b in range(picked.shape[1] // BLOCK)
                ],
                axis=1,
            )
            total = weighted if total is None else total + weighted
            sums = jnp.sum(picked * grad_ref[...].astype(F32), axis=1, keepdims=True)
            rows = jnp.transpose(jnp.broadcast_to(sums, (sums.shape[0], sums.shape[0])))
            gates_ref[k : k + 1, :] = rows[0:1, :]
        out_ref[...] = total.astype(out_ref.dtype)


def pick_partner_kernel(back_ref, meta_ref, out_ref):
    slot_total = back_ref.shape[0]
    mask = hits(slot_total, meta_ref, 0) | hits(slot_total, meta_ref, 1)
    out_ref[...] = dot(one_hot(mask), back_ref[...], 0, 0).astype(BF16)


def finish_kernel(
    back_ref, meta_ref, got_back, own_out, got_out, own_gates, got_gates, combined, grad_tokens, grad_gates
):
    slot_total = back_ref.shape[0]
    mask = hits(slot_total, meta_ref, 0) | hits(slot_total, meta_ref, 1)
    own = dot(one_hot(mask), back_ref[...], 0, 0)
    grad_tokens[...] = (own + got_back[...].astype(F32)).astype(BF16)
    combined[...] = (own_out[...] + got_out[...].astype(F32)).astype(BF16)
    grad_gates[...] = own_gates[...] + got_gates[...]


def call(kernel, outs, flops=0, traffic=0, limit=12, **options):
    return pl.pallas_call(
        kernel,
        out_shape=outs,
        compiler_params=pltpu.CompilerParams(vmem_limit_bytes=limit * MIB),
        cost_estimate=pl.CostEstimate(flops=flops, bytes_accessed=traffic, transcendentals=0),
        **options,
    )


def in_hbm(values):
    return pltpu.with_memory_space_constraint(values, pltpu.HBM)


def body(tokens, expert_ids, keep_mask, gate_weights, weight_in, weight_out, grad_output):
    token_rows, width = tokens.shape
    hidden_width = weight_in.shape[2]
    rest_count = lax.axis_size("rest")
    members = lax.axis_size("row") * rest_count
    capacity = expert_ids.shape[1] * token_rows // members
    slot_total = 2 * members * capacity
    set_total = members * capacity
    aligned = capacity % 16 == 0
    block = capacity if aligned else set_total

    def exchange(values):
        return lax.ppermute(values, "half", ((0, 1), (1, 0)))

    def shuffle(rows):
        shaped = rows.reshape(members, rows.shape[0] // members, width)
        return lax.all_to_all(shaped, GROUP, split_axis=0, concat_axis=0, tiled=True).reshape(
            rows.shape
        )

    def shape(*dims, dtype=BF16):
        return jax.ShapeDtypeStruct(dims, dtype)

    vmem = pl.BlockSpec(memory_space=pltpu.VMEM)
    hbm = pl.BlockSpec(memory_space=pl.ANY)
    meta_shape = shape(8, token_rows, dtype=F32)
    set_bytes, token_bytes = set_total * width * 2, token_rows * width * 2
    place_flops = 2 * set_total * token_rows * width
    far = 200 * 10**9

    partner_tokens = exchange(tokens)
    half = lax.axis_index("half").astype(jnp.int32).reshape(1)
    own_meta, sent_meta, sent_own = call(
        functools.partial(place_own_kernel, rest_count.bit_length() - 1, capacity),
        [meta_shape, meta_shape, shape(set_total, width)],
        place_flops,
        token_bytes + set_bytes,
        in_specs=[pl.BlockSpec(memory_space=pltpu.SMEM)] + [vmem] * 4,
    )(
        half,
        in_hbm(tokens),
        in_hbm(expert_ids.T),
        in_hbm(keep_mask.T),
        in_hbm(gate_weights.T),
    )
    x_own = shuffle(sent_own)
    partner_meta = exchange(sent_meta)
    sent_partner, grad_copy = call(
        place_partner_kernel,
        [shape(set_total, width), shape(token_rows, width)],
        place_flops,
        token_bytes + set_bytes,
    )(partner_tokens, partner_meta, in_hbm(grad_output))
    partner_grad = exchange(grad_copy)
    x_partner = shuffle(sent_partner)
    sent_cot = call(
        place_cotangents_kernel, shape(slot_total, width), far, 2 * (token_bytes + set_bytes)
    )(in_hbm(grad_output), partner_grad, own_meta, partner_meta)
    cot = shuffle(sent_cot)

    if not aligned:
        rows = jnp.stack([x_own, x_partner]).reshape(2, members, capacity, width)
        rows = rows.transpose(1, 0, 2, 3).reshape(slot_total, width)
        x_own, x_partner = rows[:set_total], rows[set_total:]
    chunk = 1024
    count, parts = hidden_width // chunk, chunk // SUB
    mid = pltpu.HBM((count, slot_total, chunk), BF16)
    mid_buf = pltpu.VMEM((count, slot_total, chunk), BF16)
    total = pltpu.VMEM((slot_total, width), F32)
    product = 2 * slot_total * width * hidden_width
    traffic = 4 * set_bytes + 4 * width * hidden_width + 4 * slot_total * hidden_width
    weight_in, weight_out = in_hbm(weight_in), in_hbm(weight_out)
    outputs, x, hidden, slope = call(
        functools.partial(forward_kernel, block),
        [shape(slot_total, width), shape(slot_total, width), mid, mid],
        2 * product,
        traffic,
        40,
        in_specs=[vmem, vmem, hbm, hbm],
        out_specs=[vmem, vmem, hbm, hbm],
        scratch_shapes=[
            pltpu.VMEM((count * parts, width, SUB), BF16),
            pltpu.VMEM((count, chunk, width), BF16),
            mid_buf,
            mid_buf,
            total,
            pltpu.SemaphoreType.DMA((count, parts + 1)),
            pltpu.SemaphoreType.DMA((count, 2)),
        ],
    )(x_own, x_partner, weight_in, weight_out)
    back_out = shuffle(outputs)
    rows_own, rows_partner, grad_pre = call(
        functools.partial(backward_kernel, block),
        [shape(set_total, width), shape(set_total, width), mid],
        2 * product,
        traffic,
        40,
        in_specs=[vmem, hbm, hbm, hbm],
        out_specs=[vmem, vmem, hbm],
        scratch_shapes=[
            pltpu.VMEM((count, width, chunk), BF16),
            pltpu.VMEM((count * parts, SUB, width), BF16),
            mid_buf,
            mid_buf,
            total,
            pltpu.SemaphoreType.DMA((count, parts + 2)),
            pltpu.SemaphoreType.DMA((count, 1)),
        ],
    )(cot, weight_in, weight_out, in_hbm(slope))
    if not aligned:
        rows = jnp.concatenate([rows_own, rows_partner]).reshape(members, 2, capacity, width)
        rows_own = rows[:, 0].reshape(set_total, width)
        rows_partner = rows[:, 1].reshape(set_total, width)
    back_partner = shuffle(rows_partner)
    tokens_f32, gates_shape = shape(token_rows, width, dtype=F32), shape(2, token_rows, dtype=F32)
    own_out, partner_out, own_gates, partner_gates = call(
        pick_outputs_kernel,
        [tokens_f32, shape(token_rows, width), gates_shape, gates_shape],
        8 * place_flops,
        2 * (token_bytes + set_bytes),
    )(back_out, in_hbm(grad_output), partner_grad, own_meta, partner_meta)
    got_out, got_gates = exchange(partner_out), exchange(partner_gates)
    partner_back = call(
        pick_partner_kernel, shape(token_rows, width), place_flops, set_bytes + token_bytes
    )(back_partner, partner_meta)
    back_own = shuffle(rows_own)
    grad_pre, partner_back = lax.optimization_barrier((grad_pre, partner_back))
    got_back = exchange(partner_back)
    grad_in_w, grad_out_w = call(
        weights_kernel,
        [pltpu.HBM(weight_in.shape, BF16), pltpu.HBM(weight_out.shape, BF16)],
        2 * product,
        traffic,
        40,
        in_specs=[vmem, vmem, hbm, hbm],
        out_specs=[hbm, hbm],
        scratch_shapes=[
            mid_buf,
            mid_buf,
            pltpu.VMEM((count, width, chunk), BF16),
            pltpu.VMEM((count, chunk, width), BF16),
            pltpu.SemaphoreType.DMA((count, 2)),
            pltpu.SemaphoreType.DMA((count, 2)),
        ],
    )(x, cot, in_hbm(hidden), in_hbm(grad_pre))
    combined, grad_tokens, grad_gates = call(
        finish_kernel,
        [shape(token_rows, width), shape(token_rows, width), gates_shape],
        place_flops,
        set_bytes + 4 * token_bytes,
    )(back_own, own_meta, got_back, own_out, got_out, own_gates, got_gates)
    return (combined, grad_tokens, grad_gates.T, grad_in_w, grad_out_w)


def solution(mesh):
    rows, cols = mesh.devices.shape
    axes = ("row", "half", "rest")
    halves = Mesh(mesh.devices.reshape(rows, 2, cols // 2), axes)
    flat, deep = P(axes, None), P(axes, None, None)
    return jax.shard_map(
        body,
        mesh=halves,
        in_specs=(flat, flat, flat, flat, deep, deep, flat),
        out_specs=(flat, flat, flat, deep, deep),
        check_vma=False,
    )
```

time: 108 us -> 129 us (1.19)
  waiting for transfers between devices: 46.3 us -> 17.6 us
  starting transfers between devices: 15.2 us -> 37.1 us
  Pallas kernels: 44.1 us -> 58.2 us
  blocking collectives: 0 us -> 12.9 us
    all_to_all x4 -> x5, waiting for transfers between devices: 46.3 us -> 3.29 us  [shuffle(): lax.all_to_all(shaped, GROUP, split_axis=0, concat_axis=0, tiled=True)]
    pallas_call x6 -> x8, Pallas kernels: 33.4 us -> 47.9 us  [the longest x1 21.2 us: body(): call(functools.partial(forward_kernel, block), [shape(slot_total, width),...]
    ppermute x0 -> x6, waiting for transfers between devices: none -> 14.3 us  [exchange(): return lax.ppermute(values, 'half', ((0, 1), (1, 0)))]
    all_to_all x0 -> x1, blocking collectives: none -> 12.9 us  [shuffle(): lax.all_to_all(shaped, GROUP, split_axis=0, concat_axis=0, tiled=True)]
    ppermute x0 -> x6, starting transfers between devices: none -> 11.2 us  [exchange(): return lax.ppermute(values, 'half', ((0, 1), (1, 0)))]
    all_to_all x4 -> x5, starting transfers between devices: 15.2 us -> 25.9 us  [shuffle(): lax.all_to_all(shaped, GROUP, split_axis=0, concat_axis=0, tiled=True)]
  transfers between devices with their start and end apart: 4 -> 11, of which waited for: 4 -> 5; matrix products, arithmetic and copies ran while one was open for 0% -> 0% of each run, Pallas kernels for 38% -> 43%
where the time goes in v6:
time: 129 us
  Pallas kernels  58.2 us (45%)
  starting transfers between devices  37.1 us (29%)
  waiting for transfers between devices  17.6 us (14%)
  blocking collectives  12.9 us (10%)
  local copies, waits for them, and re-layouts  2 us (2%)
    all_to_all x5, starting transfers between devices, shuffle(): lax.all_to_all(shaped, GROUP, split_axis=0, concat_axis=0, tiled=True)  25.9 us
    pallas_call x1, Pallas kernels, body(): call(functools.partial(forward_kernel, block), [shape(slot_total, width),...  21.2 us
    pallas_call x1, Pallas kernels, body(): call(functools.partial(backward_kernel, block), [shape(set_total, width),...  16.6 us
    ppermute x6, waiting for transfers between devices, exchange(): return lax.ppermute(values, 'half', ((0, 1), (1, 0)))  14.3 us
    all_to_all x1, blocking collectives, shuffle(): lax.all_to_all(shaped, GROUP, split_axis=0, concat_axis=0, tiled=True)  12.9 us
    ppermute x6, starting transfers between devices, exchange(): return lax.ppermute(values, 'half', ((0, 1), (1, 0)))  11.2 us
    pallas_call x1, Pallas kernels, body(): call(weights_kernel, [pltpu.HBM(weight_in.shape, BF16), pltpu.HBM(weight_...  10.2 us
    all_to_all x5, waiting for transfers between devices, shuffle(): lax.all_to_all(shaped, GROUP, split_axis=0, concat_axis=0, tiled=True)  3.29 us
  transfers between devices with their start and end apart: 11, of which 5 were waited for; matrix products, arithmetic and copies ran while one was open for 0% of the time, Pallas kernels for 43%

profile of v6, /device:TPU:0, one launch (start us, length us, event | category | flops | bytes accessed | tf_op | source)
XLA Modules:
  0.0 128.6 jit_solution(17594542970039962105)
XLA Ops:
  0.6 2.2 %shard_map.110 = (f32[8,128]{1,0:T(8,128)S(1)}, f32[8,128]{1,0:T(8,128)S(1)}, bf16[256,768]{1,0:T(8,128)(2,1)}) custom-call(s32[1]{0:T(128)} %bitcast.half_ref, bf16[128,768]{1,0:T(8,128)(2,1)} %tokens_ref.1, s32[2,128]{1,0:T(2,128)} %bitcast.24, s32[2,128]{1,0:T(2,128)} %bitcast.25, f32[2,128]{1,0:T(2,128)} %bitcast.26), custom_call_target="tpu_custom_call" | custom-call | flops 50331648 | bytes 589824 | tf_op jit(solution)/shard_map/pallas_call | solution.py:372
  2.8 6.3 %all-to-all-start.1 = ((bf16[16,16,768]{2,1,0:T(8,128)(2,1)}), bf16[16,16,768]{2,1,0:T(8,128)(2,1)S(1)}, u32[]{:S(2)}, u32[]{:S(2)}) async-start(bf16[16,16,768]{2,1,0:T(8,128)(2,1)} %bitcast.6), calls=%async_computation.1 | async-start | bytes 786432 | tf_op jit(solution)/shard_map/all_to_all | solution.py:356
  9.1 2.6 %collective-permute-start = (bf16[128,768]{1,0:T(8,128)(2,1)}, bf16[128,768]{1,0:T(8,128)(2,1)S(1)}, u32[]{:S(2)}, u32[]{:S(2)}) collective-permute-start(bf16[128,768]{1,0:T(8,128)(2,1)} %tokens_ref.1), channel_id=1, source_target_pairs={{0,4},{4,0},{1,5},{5,1},{2,6},{6,2},{3,7},{7,3},{8,12},{12,8},{9,1... | collective-permute-start | bytes 589832 | tf_op jit(solution)/shard_map/ppermute | solution.py:352
  11.8 0.3 collective-permute-start.1
  12.1 6.7 %collective-permute-done.1.meta_ref.partner_meta = f32[8,128]{1,0:T(8,128)S(1)} collective-permute-done((f32[8,128]{1,0:T(8,128)S(1)}, f32[8,128]{1,0:T(8,128)S(1)}, u32[]{:S(2)}, u32[]{:S(2)}) %collective-permute-start.1) | collective-permute-done | bytes 4128 | tf_op jit(solution)/shard_map/ppermute | solution.py:352
  18.8 0.0 collective-permute-done.tokens_ref
  18.8 2.1 %shard_map.111 = (bf16[256,768]{1,0:T(8,128)(2,1)}, bf16[128,768]{1,0:T(8,128)(2,1)S(1)}) custom-call(bf16[128,768]{1,0:T(8,128)(2,1)S(1)} %collective-permute-done.tokens_ref, f32[8,128]{1,0:T(8,128)S(1)} %collective-permute-done.1.meta_ref.partner_meta, bf16[128,768]{1,0:T(8,128)(2,1)} %own_grad.3), custom_call_target="tpu_custom_call" | custom-call | flops 50331648 | bytes 589824 | tf_op jit(solution)/shard_map/pallas_call | solution.py:387
  20.9 3.4 %collective-permute-start.2 = (bf16[128,768]{1,0:T(8,128)(2,1)S(1)}, bf16[128,768]{1,0:T(8,128)(2,1)S(1)}, u32[]{:S(2)}, u32[]{:S(2)}) collective-permute-start(bf16[128,768]{1,0:T(8,128)(2,1)S(1)} %get-tuple-element.29), channel_id=1, source_target_pairs={{0,4},{4,0},{1,5},{5,1},{2,6},{6,2},{3,7},{7,3},{8,12},{12,8},{9,1... | collective-permute-start | bytes 589832 | tf_op jit(solution)/shard_map/ppermute | solution.py:352
  24.3 0.0 all-to-all-done.1
  24.3 7.2 %all-to-all-start.2 = ((bf16[16,16,768]{2,1,0:T(8,128)(2,1)}), bf16[16,16,768]{2,1,0:T(8,128)(2,1)}, u32[]{:S(2)}, u32[]{:S(2)}) async-start(bf16[16,16,768]{2,1,0:T(8,128)(2,1)} %bitcast.8), calls=%async_computation.2 | async-start | bytes 786432 | tf_op jit(solution)/shard_map/all_to_all | solution.py:356
  31.5 1.9 %collective-permute-done.2.partner_grad = bf16[128,768]{1,0:T(8,128)(2,1)S(1)} collective-permute-done((bf16[128,768]{1,0:T(8,128)(2,1)S(1)}, bf16[128,768]{1,0:T(8,128)(2,1)S(1)}, u32[]{:S(2)}, u32[]{:S(2)}) %collective-permute-start.2) | collective-permute-done | bytes 196640 | tf_op jit(solution)/shard_map/ppermute | solution.py:352
  33.4 2.9 %shard_map.112 = bf16[512,768]{1,0:T(8,128)(2,1)} custom-call(bf16[128,768]{1,0:T(8,128)(2,1)} %own_grad.3, bf16[128,768]{1,0:T(8,128)(2,1)S(1)} %collective-permute-done.2.partner_grad, f32[8,128]{1,0:T(8,128)S(1)} %get-tuple-element.30.own_meta.meta_ref, f32[8,128]{1,0:T(8,128)S(1)} %collective-permute-done.1.meta_ref.partner_meta), custom_call_target="tpu_custom_call" | custom-call | flops 199999995904 | bytes 1179648 | tf_op jit(solution)/shard_map/pallas_call | solution.py:395
  36.3 3.3 %all-to-all-done.2 = bf16[16,16,768]{2,1,0:T(8,128)(2,1)} async-done(((bf16[16,16,768]{2,1,0:T(8,128)(2,1)}), bf16[16,16,768]{2,1,0:T(8,128)(2,1)}, u32[]{:S(2)}, u32[]{:S(2)}) %all-to-all-start.2) | async-done | bytes 393248 | tf_op jit(solution)/shard_map/all_to_all | solution.py:356
  39.6 3.6 %all-to-all-start = ((bf16[16,32,768]{2,1,0:T(8,128)(2,1)}), bf16[16,32,768]{2,1,0:T(8,128)(2,1)S(1)}, u32[]{:S(2)}, u32[]{:S(2)}) async-start(bf16[16,32,768]{2,1,0:T(8,128)(2,1)} %bitcast.4), calls=%async_computation | async-start | bytes 1572864 | tf_op jit(solution)/shard_map/all_to_all | solution.py:356
  43.2 21.2 %shard_map.113 = (bf16[512,768]{1,0:T(8,128)(2,1)}, bf16[512,768]{1,0:T(8,128)(2,1)S(1)}, bf16[4,512,1024]{2,1,0:T(8,128)(2,1)}, bf16[4,512,1024]{2,1,0:T(8,128)(2,1)}) custom-call(bf16[256,768]{1,0:T(8,128)(2,1)S(1)} %bitcast.22, bf16[256,768]{1,0:T(8,128)(2,1)} %bitcast.9.partner, bf16[1,768,4096]{2,1,0:T(8,128)(2,1)} %w_in.3, bf16[1,4096,768]{2,1,0:T(8,128)(2,1)} %w_out.3), custom_call_target="tpu_custom_call" | custom-call | flops 6442450944 | bytes 22544384 | tf_op jit(solution)/shard_map/pallas_call | solution.py:412
  64.4 0.0 copy-start
  64.4 0.9 copy-done
  65.3 0.0 all-to-all-done
  65.3 5.1 %all-to-all-start.5 = ((bf16[16,32,768]{2,1,0:T(8,128)(2,1)}), bf16[16,32,768]{2,1,0:T(8,128)(2,1)S(1)}, u32[]{:S(2)}, u32[]{:S(2)}) async-start(bf16[16,32,768]{2,1,0:T(8,128)(2,1)} %bitcast.14), calls=%async_computation.5 | async-start | bytes 1572864 | tf_op jit(solution)/shard_map/all_to_all | solution.py:356
  70.3 16.6 %shard_map.114 = (bf16[256,768]{1,0:T(8,128)(2,1)}, bf16[256,768]{1,0:T(8,128)(2,1)S(1)}, bf16[4,512,1024]{2,1,0:T(8,128)(2,1)}) custom-call(bf16[512,768]{1,0:T(8,128)(2,1)S(1)} %bitcast.19, bf16[1,768,4096]{2,1,0:T(8,128)(2,1)} %w_in.3, bf16[1,4096,768]{2,1,0:T(8,128)(2,1)} %w_out.3, bf16[4,512,1024]{2,1,0:T(8,128)(2,1)} %get-tuple-element.33.slope), custom_call_target="tpu_custom_call" | custom-call | flops 6442450944 | bytes 22544384 | tf_op jit(solution)/shard_map/pallas_call | solution.py:431
  87.0 0.0 all-to-all-done.5
  87.0 12.9 %all_to_all.30 = bf16[16,16,768]{2,1,0:T(8,128)(2,1)S(1)} all-to-all(bf16[16,16,768]{2,1,0:T(8,128)(2,1)S(1)} %bitcast.23), channel_id=1, replica_groups=mesh['row'=4,'half'=2,'rest'=4] {'row','rest'}, dimensions={0} | all-to-all | bytes 786432 | tf_op jit(solution)/shard_map/all_to_all | solution.py:356
  99.9 3.7 %all-to-all-start.3 = ((bf16[16,16,768]{2,1,0:T(8,128)(2,1)}), bf16[16,16,768]{2,1,0:T(8,128)(2,1)S(1)}, u32[]{:S(2)}, u32[]{:S(2)}) async-start(bf16[16,16,768]{2,1,0:T(8,128)(2,1)} %bitcast.10), calls=%async_computation.3 | async-start | bytes 786432 | tf_op jit(solution)/shard_map/all_to_all | solution.py:356
  103.7 1.7 %shard_map.116 = (f32[128,768]{1,0:T(8,128)S(1)}, bf16[128,768]{1,0:T(8,128)(2,1)S(1)}, f32[2,128]{1,0:T(2,128)S(1)}, f32[2,128]{1,0:T(2,128)S(1)}) custom-call(bf16[512,768]{1,0:T(8,128)(2,1)S(1)} %bitcast.21, bf16[128,768]{1,0:T(8,128)(2,1)} %own_grad.3, bf16[128,768]{1,0:T(8,128)(2,1)S(1)} %collective-permute-done.2.partner_grad, ...), custom_call_target="tpu_custom_call" | custom-call | flops 402653184 | bytes 1179648 | tf_op jit(solution)/shard_map/pallas_call | solution.py:455
  105.4 1.9 %collective-permute-start.5 = (f32[2,128]{1,0:T(2,128)S(1)}, f32[2,128]{1,0:T(2,128)S(1)}, u32[]{:S(2)}, u32[]{:S(2)}) collective-permute-start(f32[2,128]{1,0:T(2,128)S(1)} %get-tuple-element.42), channel_id=1, source_target_pairs={{0,4},{4,0},{1,5},{5,1},{2,6},{6,2},{3,7},{7,3},{8,12},{12,8},{9,1... | collective-permute-start | bytes 3080 | tf_op jit(solution)/shard_map/ppermute | solution.py:352
  107.3 1.1 collective-permute-start.4
  108.4 0.2 shard_map.115
  108.6 1.9 %collective-permute-start.3 = (bf16[128,768]{1,0:T(8,128)(2,1)S(1)}, bf16[128,768]{1,0:T(8,128)(2,1)S(1)}, u32[]{:S(2)}, u32[]{:S(2)}) collective-permute-start(bf16[128,768]{1,0:T(8,128)(2,1)S(1)} %shard_map.115), channel_id=1, source_target_pairs={{0,4},{4,0},{1,5},{5,1},{2,6},{6,2},{3,7},{7,3},{8,12},{12,8},{9,1... | collective-permute-start | bytes 589832 | tf_op jit(solution)/shard_map/ppermute | solution.py:352
  110.5 0.0 copy-start.1
  110.5 1.1 copy-done.1
  111.6 10.2 %shard_map.118 = (bf16[1,768,4096]{2,1,0:T(8,128)(2,1)}, bf16[1,4096,768]{2,1,0:T(8,128)(2,1)}) custom-call(bf16[512,768]{1,0:T(8,128)(2,1)S(1)} %copy-done.1, bf16[512,768]{1,0:T(8,128)(2,1)S(1)} %bitcast.20, bf16[4,512,1024]{2,1,0:T(8,128)(2,1)} %get-tuple-element.47.hidden, bf16[4,512,1024]{2,1,0:T(8,128)(2,1)} %get-tuple-element.48.grad_pre), custom_call_target="tpu_custom_call" | custom-call | flops 6442450944 | bytes 22544384 | tf_op jit(solution)/shard_map/pallas_call | solution.py:468
  121.9 0.0 collective-permute-done.5.got_gates
  121.9 2.5 %collective-permute-done.4.got_out = bf16[128,768]{1,0:T(8,128)(2,1)S(1)} collective-permute-done((bf16[128,768]{1,0:T(8,128)(2,1)S(1)}, bf16[128,768]{1,0:T(8,128)(2,1)S(1)}, u32[]{:S(2)}, u32[]{:S(2)}) %collective-permute-start.4) | collective-permute-done | bytes 196640 | tf_op jit(solution)/shard_map/ppermute | solution.py:352
  124.4 0.0 all-to-all-done.3
  124.4 3.2 %collective-permute-done.3.got_back = bf16[128,768]{1,0:T(8,128)(2,1)S(1)} collective-permute-done((bf16[128,768]{1,0:T(8,128)(2,1)S(1)}, bf16[128,768]{1,0:T(8,128)(2,1)S(1)}, u32[]{:S(2)}, u32[]{:S(2)}) %collective-permute-start.3) | collective-permute-done | bytes 196640 | tf_op jit(solution)/shard_map/ppermute | solution.py:352
  127.6 1.0 shard_map.117
Async XLA Ops:
  2.8 21.5 %all-to-all-start.1 = ((bf16[16,16,768]{2,1,0:T(8,128)(2,1)}), bf16[16,16,768]{2,1,0:T(8,128)(2,1)S(1)}, u32[]{:S(2)}, u32[]{:S(2)}) async-start(bf16[16,16,768]{2,1,0:T(8,128)(2,1)} %bitcast.6), calls=%async_computation.1 | async-start | bytes 786432 | tf_op jit(solution)/shard_map/all_to_all | solution.py:356
  9.1 9.7 %collective-permute-start = (bf16[128,768]{1,0:T(8,128)(2,1)}, bf16[128,768]{1,0:T(8,128)(2,1)S(1)}, u32[]{:S(2)}, u32[]{:S(2)}) collective-permute-start(bf16[128,768]{1,0:T(8,128)(2,1)} %tokens_ref.1), channel_id=1, source_target_pairs={{0,4},{4,0},{1,5},{5,1},{2,6},{6,2},{3,7},{7,3},{8,12},{12,8},{9,1... | collective-permute-start | bytes 589832 | tf_op jit(solution)/shard_map/ppermute | solution.py:352
  11.8 7.0 %collective-permute-start.1 = (f32[8,128]{1,0:T(8,128)S(1)}, f32[8,128]{1,0:T(8,128)S(1)}, u32[]{:S(2)}, u32[]{:S(2)}) collective-permute-start(f32[8,128]{1,0:T(8,128)S(1)} %get-tuple-element.28), channel_id=1, source_target_pairs={{0,4},{4,0},{1,5},{5,1},{2,6},{6,2},{3,7},{7,3},{8,12},{12,8},{9,1... | collective-permute-start | bytes 12296 | tf_op jit(solution)/shard_map/ppermute | solution.py:352
  20.9 12.5 %collective-permute-start.2 = (bf16[128,768]{1,0:T(8,128)(2,1)S(1)}, bf16[128,768]{1,0:T(8,128)(2,1)S(1)}, u32[]{:S(2)}, u32[]{:S(2)}) collective-permute-start(bf16[128,768]{1,0:T(8,128)(2,1)S(1)} %get-tuple-element.29), channel_id=1, source_target_pairs={{0,4},{4,0},{1,5},{5,1},{2,6},{6,2},{3,7},{7,3},{8,12},{12,8},{9,1... | collective-permute-start | bytes 589832 | tf_op jit(solution)/shard_map/ppermute | solution.py:352
  24.3 15.3 %all-to-all-start.2 = ((bf16[16,16,768]{2,1,0:T(8,128)(2,1)}), bf16[16,16,768]{2,1,0:T(8,128)(2,1)}, u32[]{:S(2)}, u32[]{:S(2)}) async-start(bf16[16,16,768]{2,1,0:T(8,128)(2,1)} %bitcast.8), calls=%async_computation.2 | async-start | bytes 786432 | tf_op jit(solution)/shard_map/all_to_all | solution.py:356
  39.6 25.7 %all-to-all-start = ((bf16[16,32,768]{2,1,0:T(8,128)(2,1)}), bf16[16,32,768]{2,1,0:T(8,128)(2,1)S(1)}, u32[]{:S(2)}, u32[]{:S(2)}) async-start(bf16[16,32,768]{2,1,0:T(8,128)(2,1)} %bitcast.4), calls=%async_computation | async-start | bytes 1572864 | tf_op jit(solution)/shard_map/all_to_all | solution.py:356
  64.4 0.9 copy-start
  65.3 21.7 %all-to-all-start.5 = ((bf16[16,32,768]{2,1,0:T(8,128)(2,1)}), bf16[16,32,768]{2,1,0:T(8,128)(2,1)S(1)}, u32[]{:S(2)}, u32[]{:S(2)}) async-start(bf16[16,32,768]{2,1,0:T(8,128)(2,1)} %bitcast.14), calls=%async_computation.5 | async-start | bytes 1572864 | tf_op jit(solution)/shard_map/all_to_all | solution.py:356
  99.9 24.4 %all-to-all-start.3 = ((bf16[16,16,768]{2,1,0:T(8,128)(2,1)}), bf16[16,16,768]{2,1,0:T(8,128)(2,1)S(1)}, u32[]{:S(2)}, u32[]{:S(2)}) async-start(bf16[16,16,768]{2,1,0:T(8,128)(2,1)} %bitcast.10), calls=%async_computation.3 | async-start | bytes 786432 | tf_op jit(solution)/shard_map/all_to_all | solution.py:356
  105.4 16.5 %collective-permute-start.5 = (f32[2,128]{1,0:T(2,128)S(1)}, f32[2,128]{1,0:T(2,128)S(1)}, u32[]{:S(2)}, u32[]{:S(2)}) collective-permute-start(f32[2,128]{1,0:T(2,128)S(1)} %get-tuple-element.42), channel_id=1, source_target_pairs={{0,4},{4,0},{1,5},{5,1},{2,6},{6,2},{3,7},{7,3},{8,12},{12,8},{9,1... | collective-permute-start | bytes 3080 | tf_op jit(solution)/shard_map/ppermute | solution.py:352
  107.3 17.1 %collective-permute-start.4 = (bf16[128,768]{1,0:T(8,128)(2,1)S(1)}, bf16[128,768]{1,0:T(8,128)(2,1)S(1)}, u32[]{:S(2)}, u32[]{:S(2)}) collective-permute-start(bf16[128,768]{1,0:T(8,128)(2,1)S(1)} %get-tuple-element.40), channel_id=1, source_target_pairs={{0,4},{4,0},{1,5},{5,1},{2,6},{6,2},{3,7},{7,3},{8,12},{12,8},{9,1... | collective-permute-start | bytes 589832 | tf_op jit(solution)/shard_map/ppermute | solution.py:352
  108.6 19.0 %collective-permute-start.3 = (bf16[128,768]{1,0:T(8,128)(2,1)S(1)}, bf16[128,768]{1,0:T(8,128)(2,1)S(1)}, u32[]{:S(2)}, u32[]{:S(2)}) collective-permute-start(bf16[128,768]{1,0:T(8,128)(2,1)S(1)} %shard_map.115), channel_id=1, source_target_pairs={{0,4},{4,0},{1,5},{5,1},{2,6},{6,2},{3,7},{7,3},{8,12},{12,8},{9,1... | collective-permute-start | bytes 589832 | tf_op jit(solution)/shard_map/ppermute | solution.py:352
  110.5 1.1 copy-start.1

commit v7 on v5

--- a/solution.py
+++ b/solution.py
@@ -5,6 +5,7 @@
 from jax import lax
 from jax.experimental import pallas as pl
 from jax.experimental.pallas import tpu as pltpu
+from jax.sharding import Mesh
 from jax.sharding import PartitionSpec as P
 
 BLOCK = 128
@@ -12,6 +13,8 @@
 F32 = jnp.float32
 MIB = 1024 * 1024
 SUB = 256
+AXES = ("row", "outer", "inner")
+GROUP = ("row", "inner", "outer")
 
 
 def dot(a, b, contract_a, contract_b):
@@ -25,7 +28,7 @@
     return jnp.transpose(jnp.broadcast_to(row, (count, count)))
 
 
-def route(ids_ref, keep_ref, gates_ref, meta_ref, capacity):
+def route(ids_ref, keep_ref, gates_ref, meta_ref, capacity, place_of):
     token_rows = ids_ref.shape[1]
     ids = ids_ref[...].astype(F32)
     earlier = lax.broadcasted_iota(jnp.int32, (token_rows, token_rows), 0) < lax.broadcasted_iota(
@@ -37,7 +40,7 @@
         for other_choice in columns:
             count = count + jnp.where(earlier & (other_choice == ids[k : k + 1]), 1.0, 0.0)
         slot = jnp.sum(count, axis=0, keepdims=True).astype(jnp.int32)
-        row = ids_ref[k : k + 1, :] * capacity + slot
+        row = place_of(ids_ref[k : k + 1, :]) * capacity + slot
         meta_ref[k : k + 1, :] = jnp.where(keep_ref[k : k + 1, :] > 0, row, -1).astype(F32)
         meta_ref[k + 2 : k + 3, :] = gates_ref[k : k + 1, :]
     meta_ref[4:8, :] = jnp.zeros((4, token_rows), F32)
@@ -63,8 +66,8 @@
     return jnp.concatenate(pieces, axis=1)
 
 
-def place_tokens_kernel(capacity, tokens_ref, ids_ref, keep_ref, gates_ref, meta_ref, out_ref):
-    route(ids_ref, keep_ref, gates_ref, meta_ref, capacity)
+def place_tokens_kernel(capacity, place_of, tokens_ref, ids_ref, keep_ref, gates_ref, meta_ref, out_ref):
+    route(ids_ref, keep_ref, gates_ref, meta_ref, capacity, place_of)
     slot_total = out_ref.shape[0]
     mask = hits(slot_total, meta_ref, 0) | hits(slot_total, meta_ref, 1)
     out_ref[...] = dot(one_hot(mask), restore(tokens_ref), 1, 0).astype(BF16)
@@ -197,14 +200,23 @@
 def body(tokens, expert_ids, keep_mask, gate_weights, weight_in, weight_out, grad_output):
     token_rows, width = tokens.shape
     hidden_width = weight_in.shape[2]
-    experts = lax.axis_size("row") * lax.axis_size("col")
+    row_count, outer = lax.axis_size("row"), lax.axis_size("outer")
+    experts = row_count * outer * lax.axis_size("inner")
+    bits = outer.bit_length() - 1
+
+    def place_of(expert):
+        inner_at = expert & 1
+        outer_at = (expert >> 1) & (outer - 1)
+        row_at = expert >> (bits + 1)
+        return ((row_at * 2 + inner_at) << bits) + outer_at
+
     capacity = 2 * expert_ids.shape[1] * token_rows // experts
     slot_total = experts * capacity
 
     def shuffle(rows):
         shaped = rows.reshape(experts, capacity, width)
         return lax.all_to_all(
-            shaped, ("row", "col"), split_axis=0, concat_axis=0, tiled=True
+            shaped, GROUP, split_axis=0, concat_axis=0, tiled=True
         ).reshape(slot_total, width)
 
     slots = jax.ShapeDtypeStruct((slot_total, width), BF16)
@@ -212,7 +224,7 @@
     token_bytes = token_rows * width * 2
     place_flops = 2 * slot_total * token_rows * width
     meta, sent = call(
-        functools.partial(place_tokens_kernel, capacity),
+        functools.partial(place_tokens_kernel, capacity, place_of),
         [jax.ShapeDtypeStruct((8, token_rows), F32), slots],
         place_flops,
         token_bytes + slot_bytes,
@@ -287,11 +299,12 @@
 
 
 def solution(mesh):
-    flat = P(("row", "col"), None)
-    deep = P(("row", "col"), None, None)
+    rows, cols = mesh.devices.shape
+    split = Mesh(mesh.devices.reshape(rows, cols // 2, 2), AXES)
+    flat, deep = P(AXES, None), P(AXES, None, None)
     return jax.shard_map(
         body,
-        mesh=mesh,
+        mesh=split,
         in_specs=(flat, flat, flat, flat, deep, deep, flat),
         out_specs=(flat, flat, flat, deep, deep),
         check_vma=False,

time: 108 us -> 105 us (0.972)
  waiting for transfers between devices: 46.3 us -> 43.4 us
    all_to_all x4, waiting for transfers between devices: 46.3 us -> 43.4 us  [shuffle(): lax.all_to_all(shaped, GROUP, split_axis=0, concat_axis=0, tiled=True)]
  transfers between devices with their start and end apart: 4 -> 4, of which waited for: 4 -> 4; matrix products, arithmetic and copies ran while one was open for 0% -> 0% of each run, Pallas kernels for 38% -> 39%
where the time goes in v7:
time: 105 us; the launch traced here: 104 us
  Pallas kernels  44.1 us (42%)
  waiting for transfers between devices  43.4 us (41%)
  starting transfers between devices  15.2 us (14%)
    all_to_all x4, waiting for transfers between devices, shuffle(): lax.all_to_all(shaped, GROUP, split_axis=0, concat_axis=0, tiled=True)  43.4 us
    all_to_all x4, starting transfers between devices, shuffle(): lax.all_to_all(shaped, GROUP, split_axis=0, concat_axis=0, tiled=True)  15.2 us
    pallas_call x1, Pallas kernels, body(): call(forward_kernel, [mid, mid, slots], 2 * product, traffic, 32, grid=gr...  13.4 us
    pallas_call x1, Pallas kernels, body(): call(backward_kernel, [mid, slots], 2 * product, traffic, 32, grid=grid,...  12 us
    pallas_call x1, Pallas kernels, body(): call(weights_kernel, [pltpu.HBM(weight_in.shape, BF16), pltpu.HBM(weight_...  10.7 us
    pallas_call x1, Pallas kernels, body(): call(place_cotangents_kernel, slots, 2 * place_flops, token_bytes + slot_...  2.46 us
    pallas_call x1, Pallas kernels, body(): call(functools.partial(place_tokens_kernel, capacity, place_of), [jax.Sha...  2.41 us
  transfers between devices with their start and end apart: 4, of which 4 were waited for; matrix products, arithmetic and copies ran while one was open for 0% of the time, Pallas kernels for 39%

profile of v7, /device:TPU:0, one launch (start us, length us, event | category | flops | bytes accessed | tf_op | source)
XLA Modules:
  0.0 104.3 jit_solution(8009364882722304542)
XLA Ops:
  0.6 2.4 %shard_map.110 = (f32[8,128]{1,0:T(8,128)S(1)}, bf16[512,768]{1,0:T(8,128)(2,1)}) custom-call(bf16[128,768]{1,0:T(8,128)(2,1)} %tokens_ref.1, s32[2,128]{1,0:T(2,128)} %bitcast.19, s32[2,128]{1,0:T(2,128)} %bitcast.20, f32[2,128]{1,0:T(2,128)} %bitcast.21), custom_call_target="tpu_custom_call" | custom-call | flops 100663296 | bytes 983040 | tf_op jit(solution)/shard_map/pallas_call | solution.py:226
  3.0 7.3 %all-to-all-start = ((bf16[32,16,768]{2,1,0:T(8,128)(2,1)}), bf16[32,16,768]{2,1,0:T(8,128)(2,1)S(1)}, u32[]{:S(2)}, u32[]{:S(2)}) async-start(bf16[32,16,768]{2,1,0:T(8,128)(2,1)} %bitcast.3), calls=%async_computation | async-start | bytes 1572864 | tf_op jit(solution)/shard_map/all_to_all | solution.py:218
  10.4 2.5 %shard_map.113 = bf16[512,768]{1,0:T(8,128)(2,1)} custom-call(bf16[128,768]{1,0:T(8,128)(2,1)} %grad_ref.3, f32[8,128]{1,0:T(8,128)S(1)} %get-tuple-element.18.meta_ref), custom_call_target="tpu_custom_call" | custom-call | flops 201326592 | bytes 983040 | tf_op jit(solution)/shard_map/pallas_call | solution.py:233
  12.8 18.8 %all-to-all-done = bf16[32,16,768]{2,1,0:T(8,128)(2,1)S(1)} async-done(((bf16[32,16,768]{2,1,0:T(8,128)(2,1)}), bf16[32,16,768]{2,1,0:T(8,128)(2,1)S(1)}, u32[]{:S(2)}, u32[]{:S(2)}) %all-to-all-start) | async-done | bytes 786464 | tf_op jit(solution)/shard_map/all_to_all | solution.py:218
  31.6 2.6 %all-to-all-start.2 = ((bf16[32,16,768]{2,1,0:T(8,128)(2,1)}), bf16[32,16,768]{2,1,0:T(8,128)(2,1)S(1)}, u32[]{:S(2)}, u32[]{:S(2)}) async-start(bf16[32,16,768]{2,1,0:T(8,128)(2,1)} %bitcast.7), calls=%async_computation.2 | async-start | bytes 1572864 | tf_op jit(solution)/shard_map/all_to_all | solution.py:218
  34.2 13.4 %shard_map.111 = (bf16[512,4096]{1,0:T(8,128)(2,1)}, bf16[512,4096]{1,0:T(8,128)(2,1)}, bf16[512,768]{1,0:T(8,128)(2,1)}) custom-call(bf16[512,768]{1,0:T(8,128)(2,1)S(1)} %bitcast.14, bf16[1,768,4096]{2,1,0:T(8,128)(2,1)} %w_in_ref.3, bf16[1,4096,768]{2,1,0:T(8,128)(2,1)} %w_out_ref.3), custom_call_target="tpu_custom_call" | custom-call | flops 6442450944 | bytes 22544384 | tf_op jit(solution)/shard_map/pallas_call | solution.py:249
  47.6 7.9 %all-to-all-done.2 = bf16[32,16,768]{2,1,0:T(8,128)(2,1)S(1)} async-done(((bf16[32,16,768]{2,1,0:T(8,128)(2,1)}), bf16[32,16,768]{2,1,0:T(8,128)(2,1)S(1)}, u32[]{:S(2)}, u32[]{:S(2)}) %all-to-all-start.2) | async-done | bytes 786464 | tf_op jit(solution)/shard_map/all_to_all | solution.py:218
  55.5 2.6 %all-to-all-start.1 = ((bf16[32,16,768]{2,1,0:T(8,128)(2,1)}), bf16[32,16,768]{2,1,0:T(8,128)(2,1)S(1)}, u32[]{:S(2)}, u32[]{:S(2)}) async-start(bf16[32,16,768]{2,1,0:T(8,128)(2,1)} %bitcast.5), calls=%async_computation.1 | async-start | bytes 1572864 | tf_op jit(solution)/shard_map/all_to_all | solution.py:218
  58.1 12.0 %shard_map.114 = (bf16[512,4096]{1,0:T(8,128)(2,1)}, bf16[512,768]{1,0:T(8,128)(2,1)S(1)}) custom-call(bf16[512,768]{1,0:T(8,128)(2,1)S(1)} %bitcast.16, bf16[1,768,4096]{2,1,0:T(8,128)(2,1)} %w_in_ref.3, bf16[1,4096,768]{2,1,0:T(8,128)(2,1)} %w_out_ref.3, bf16[512,4096]{1,0:T(8,128)(2,1)} %get-tuple-element.20.slope_ref), custom_call_target="tpu_custom_call" | custom-call | flops 6442450944 | bytes 22544384 | tf_op jit(solution)/shard_map/pallas_call | solution.py:261
  70.2 0.0 copy-start
  70.2 1.0 copy-done
  71.1 8.3 %all-to-all-done.1 = bf16[32,16,768]{2,1,0:T(8,128)(2,1)S(1)} async-done(((bf16[32,16,768]{2,1,0:T(8,128)(2,1)}), bf16[32,16,768]{2,1,0:T(8,128)(2,1)S(1)}, u32[]{:S(2)}, u32[]{:S(2)}) %all-to-all-start.1) | async-done | bytes 786464 | tf_op jit(solution)/shard_map/all_to_all | solution.py:218
  79.4 2.6 %all-to-all-start.3 = ((bf16[32,16,768]{2,1,0:T(8,128)(2,1)}), bf16[32,16,768]{2,1,0:T(8,128)(2,1)S(1)}, u32[]{:S(2)}, u32[]{:S(2)}) async-start(bf16[32,16,768]{2,1,0:T(8,128)(2,1)} %bitcast.18), calls=%async_computation.3 | async-start | bytes 1572864 | tf_op jit(solution)/shard_map/all_to_all | solution.py:218
  82.0 10.7 %shard_map.116 = (bf16[1,768,4096]{2,1,0:T(8,128)(2,1)}, bf16[1,4096,768]{2,1,0:T(8,128)(2,1)}) custom-call(bf16[512,768]{1,0:T(8,128)(2,1)S(1)} %bitcast.15, bf16[512,768]{1,0:T(8,128)(2,1)S(1)} %bitcast.17, bf16[512,4096]{1,0:T(8,128)(2,1)} %get-tuple-element.23.hidden_ref, bf16[512,4096]{1,0:T(8,128)(2,1)} %get-tuple-element.24.grad_pre_ref), custom_call_target="tpu_custom_call" | custom-call | flops 6442450944 | bytes 22544384 | tf_op jit(solution)/shard_map/pallas_call | solution.py:282
  92.7 2.1 %shard_map.112 = (bf16[128,768]{1,0:T(8,128)(2,1)}, f32[2,128]{1,0:T(2,128)}) custom-call(bf16[512,768]{1,0:T(8,128)(2,1)S(1)} %bitcast.12, bf16[128,768]{1,0:T(8,128)(2,1)} %grad_ref.3, f32[8,128]{1,0:T(8,128)S(1)} %get-tuple-element.18.meta_ref), custom_call_target="tpu_custom_call" | custom-call | flops 201326592 | bytes 1179648 | tf_op jit(solution)/shard_map/pallas_call | solution.py:273
  94.8 8.4 %all-to-all-done.3 = bf16[32,16,768]{2,1,0:T(8,128)(2,1)S(1)} async-done(((bf16[32,16,768]{2,1,0:T(8,128)(2,1)}), bf16[32,16,768]{2,1,0:T(8,128)(2,1)S(1)}, u32[]{:S(2)}, u32[]{:S(2)}) %all-to-all-start.3) | async-done | bytes 786464 | tf_op jit(solution)/shard_map/all_to_all | solution.py:218
  103.3 1.0 shard_map.115
Async XLA Ops:
  3.0 28.6 %all-to-all-start = ((bf16[32,16,768]{2,1,0:T(8,128)(2,1)}), bf16[32,16,768]{2,1,0:T(8,128)(2,1)S(1)}, u32[]{:S(2)}, u32[]{:S(2)}) async-start(bf16[32,16,768]{2,1,0:T(8,128)(2,1)} %bitcast.3), calls=%async_computation | async-start | bytes 1572864 | tf_op jit(solution)/shard_map/all_to_all | solution.py:218
  31.6 23.9 %all-to-all-start.2 = ((bf16[32,16,768]{2,1,0:T(8,128)(2,1)}), bf16[32,16,768]{2,1,0:T(8,128)(2,1)S(1)}, u32[]{:S(2)}, u32[]{:S(2)}) async-start(bf16[32,16,768]{2,1,0:T(8,128)(2,1)} %bitcast.7), calls=%async_computation.2 | async-start | bytes 1572864 | tf_op jit(solution)/shard_map/all_to_all | solution.py:218
  55.5 23.9 %all-to-all-start.1 = ((bf16[32,16,768]{2,1,0:T(8,128)(2,1)}), bf16[32,16,768]{2,1,0:T(8,128)(2,1)S(1)}, u32[]{:S(2)}, u32[]{:S(2)}) async-start(bf16[32,16,768]{2,1,0:T(8,128)(2,1)} %bitcast.5), calls=%async_computation.1 | async-start | bytes 1572864 | tf_op jit(solution)/shard_map/all_to_all | solution.py:218
  70.2 1.0 copy-start
  79.4 23.9 %all-to-all-start.3 = ((bf16[32,16,768]{2,1,0:T(8,128)(2,1)}), bf16[32,16,768]{2,1,0:T(8,128)(2,1)S(1)}, u32[]{:S(2)}, u32[]{:S(2)}) async-start(bf16[32,16,768]{2,1,0:T(8,128)(2,1)} %bitcast.18), calls=%async_computation.3 | async-start | bytes 1572864 | tf_op jit(solution)/shard_map/all_to_all | solution.py:218

commit v8 on v3

v8 whole, which is shorter than its diff:
```python
import functools

import jax
import jax.numpy as jnp
from jax import lax
from jax.experimental import pallas as pl
from jax.experimental.pallas import tpu as pltpu
from jax.sharding import Mesh
from jax.sharding import PartitionSpec as P

BLOCK = 128
BF16 = jnp.bfloat16
F32 = jnp.float32
MIB = 1024 * 1024
SUB = 256
CHUNK = 1024
WIDE = 512
GROUP = ("row", "rest")


def dot(a, b, contract_a, contract_b):
    return lax.dot_general(
        a, b, (((contract_a,), (contract_b,)), ((), ())), preferred_element_type=F32
    )


def column(row):
    count = row.shape[1]
    return jnp.transpose(jnp.broadcast_to(row, (count, count)))


def route_kernel(rest_bits, capacity, half_ref, ids_ref, keep_ref, gates_ref, mine_ref, other_ref):
    token_rows = ids_ref.shape[1]
    ids = ids_ref[...].astype(F32)
    earlier = lax.broadcasted_iota(jnp.int32, (token_rows, token_rows), 0) < lax.broadcasted_iota(
        jnp.int32, (token_rows, token_rows), 1
    )
    columns = (column(ids[0:1]), column(ids[1:2]))
    for k in range(2):
        count = jnp.zeros((token_rows, token_rows), F32)
        for other_choice in columns:
            count = count + jnp.where(earlier & (other_choice == ids[k : k + 1]), 1.0, 0.0)
        slot = jnp.sum(count, axis=0, keepdims=True).astype(jnp.int32)
        expert = ids_ref[k : k + 1, :]
        kept = keep_ref[k : k + 1, :] > 0
        side = (expert >> rest_bits) & 1
        local = ((expert >> (rest_bits + 1)) << rest_bits) + (expert & ((1 << rest_bits) - 1))
        base = local * (2 * capacity) + slot
        for ref, there, offset in (
            (mine_ref, kept & (side == half_ref[0]), 0),
            (other_ref, kept & (side != half_ref[0]), capacity),
        ):
            ref[k : k + 1, :] = jnp.where(there, base + offset, -1).astype(F32)
            ref[k + 2 : k + 3, :] = gates_ref[k : k + 1, :]
    for ref in (mine_ref, other_ref):
        ref[4:8, :] = jnp.zeros((4, token_rows), F32)


def hits(slot_total, meta_ref, k):
    rows = meta_ref[k : k + 1, :].astype(jnp.int32)
    index = lax.broadcasted_iota(jnp.int32, (slot_total, rows.shape[1]), 0)
    return index == rows


def one_hot(mask):
    return jnp.where(mask, 1.0, 0.0).astype(BF16)


def restore(tokens_ref):
    pieces = []
    for b in range(tokens_ref.shape[1] // BLOCK):
        x = tokens_ref[:, b * BLOCK : (b + 1) * BLOCK].astype(F32)
        scale = (jnp.max(jnp.abs(x), axis=1, keepdims=True) + 1e-06).astype(BF16).astype(F32)
        quantized = (x / scale).astype(BF16)
        pieces.append((quantized.astype(F32) * scale).astype(BF16))
    return jnp.concatenate(pieces, axis=1)


def place_tokens_kernel(own_ref, partner_ref, own_meta, partner_meta, grad_ref, out_ref, grad_copy):
    slot_total = out_ref.shape[0]
    total = None
    for tokens_ref, meta_ref in ((own_ref, own_meta), (partner_ref, partner_meta)):
        mask = hits(slot_total, meta_ref, 0) | hits(slot_total, meta_ref, 1)
        part = dot(one_hot(mask), restore(tokens_ref), 1, 0)
        total = part if total is None else total + part
    out_ref[...] = total.astype(BF16)
    grad_copy[...] = grad_ref[...]


def scaled_rows(gate_row, grad_ref):
    gate = column(gate_row)
    pieces = [
        gate * grad_ref[:, b * BLOCK : (b + 1) * BLOCK].astype(F32)
        for b in range(grad_ref.shape[1] // BLOCK)
    ]
    return jnp.concatenate(pieces, axis=1)


def place_cotangents_kernel(own_grad, partner_grad, own_meta, partner_meta, out_ref):
    slot_total = out_ref.shape[0]
    total = None
    for grad_ref, meta_ref in ((own_grad, own_meta), (partner_grad, partner_meta)):
        for k in range(2):
            rows = scaled_rows(meta_ref[k + 2 : k + 3, :], grad_ref).astype(BF16)
            part = dot(one_hot(hits(slot_total, meta_ref, k)), rows, 1, 0)
            total = part if total is None else total + part
    out_ref[...] = total.astype(BF16)


def gelu_parts(v):
    c = 0.7978845608028654
    inner = c + (c * 0.044715) * (v * v)
    s = 0.5 + 0.5 * jnp.tanh(v * inner)
    hidden = v * s
    slope = s + (hidden * (1.0 - s)) * (6.0 * inner - 4.0 * c)
    return hidden.astype(BF16), slope.astype(BF16)


def load_kernel(w_in, w_out, w_in_buf, w_out_buf, sems):
    copies = [
        pltpu.make_async_copy(w_in.at[0], w_in_buf, sems.at[0]),
        pltpu.make_async_copy(w_out.at[0], w_out_buf, sems.at[1]),
    ]
    for copy in copies:
        copy.start()
    for copy in copies:
        copy.wait()


def chunk_loop(ref, work):
    def each(j, carry):
        work(pl.multiple_of(j * CHUNK, CHUNK))
        return carry

    lax.fori_loop(0, ref.shape[1] // CHUNK, each, 0)


def part_at(start, p):
    return pl.ds(pl.multiple_of(start + p * SUB, SUB), SUB)


def forward_kernel(x, w_in, w_out, hidden, slope, out_ref, total):
    total[...] = jnp.zeros_like(total)
    parts = CHUNK // SUB

    def work(start):
        v = dot(x[...], w_in[:, part_at(start, 0)], 1, 0)
        done = []
        for p in range(parts):
            if p + 1 < parts:
                after = dot(x[...], w_in[:, part_at(start, p + 1)], 1, 0)
            hidden_part, slope_part = gelu_parts(v)
            hidden[:, part_at(start, p)] = hidden_part
            slope[:, part_at(start, p)] = slope_part
            done.append(hidden_part)
            v = after
        total[...] += dot(jnp.concatenate(done, axis=1), w_out[pl.ds(start, CHUNK), :], 1, 0)

    chunk_loop(w_in, work)
    out_ref[...] = total[...].astype(BF16)


def backward_kernel(cot, w_in, w_out, slope, grad_pre, out_ref, total):
    total[...] = jnp.zeros_like(total)

    def work(start):
        done = []
        for p in range(CHUNK // SUB):
            grad_hidden = dot(cot[...], w_out[part_at(start, p), :], 1, 1)
            part = (grad_hidden * slope[:, part_at(start, p)].astype(F32)).astype(BF16)
            grad_pre[:, part_at(start, p)] = part
            done.append(part)
        total[...] += dot(jnp.concatenate(done, axis=1), w_in[:, pl.ds(start, CHUNK)], 1, 1)

    chunk_loop(w_in, work)
    out_ref[...] = total[...].astype(BF16)


def weights_kernel(x_ref, cot_ref, hidden_ref, grad_pre_ref, grad_in_ref, grad_out_ref):
    columns = pl.ds(pl.multiple_of(pl.program_id(0) * WIDE, WIDE), WIDE)
    grad_in_ref[...] = dot(x_ref[...], grad_pre_ref[:, columns], 0, 0).astype(BF16)
    grad_out_ref[...] = dot(hidden_ref[:, columns], cot_ref[...], 0, 0).astype(BF16)


def pick_outputs_kernel(
    back_ref, own_grad, partner_grad, own_meta, partner_meta, own_out, partner_out, own_gates, partner_gates
):
    slot_total = back_ref.shape[0]
    for grad_ref, meta_ref, out_ref, gates_ref in (
        (own_grad, own_meta, own_out, own_gates),
        (partner_grad, partner_meta, partner_out, partner_gates),
    ):
        total = None
        for k in range(2):
            picked = dot(one_hot(hits(slot_total, meta_ref, k)), back_ref[...], 0, 0)
            gate = column(meta_ref[k + 2 : k + 3, :])
            weighted = jnp.concatenate(
                [
                    gate * picked[:, b * BLOCK : (b + 1) * BLOCK]
                    for b in range(picked.shape[1] // BLOCK)
                ],
                axis=1,
            )
            total = weighted if total is None else total + weighted
            sums = jnp.sum(picked * grad_ref[...].astype(F32), axis=1, keepdims=True)
            rows = jnp.transpose(jnp.broadcast_to(sums, (sums.shape[0], sums.shape[0])))
            gates_ref[k : k + 1, :] = rows[0:1, :]
        out_ref[...] = total.astype(out_ref.dtype)


def pick_partner_kernel(back_ref, meta_ref, out_ref):
    slot_total = back_ref.shape[0]
    mask = hits(slot_total, meta_ref, 0) | hits(slot_total, meta_ref, 1)
    out_ref[...] = dot(one_hot(mask), back_ref[...], 0, 0).astype(BF16)


def finish_kernel(
    back_ref, meta_ref, got_back, own_out, got_out, own_gates, got_gates, combined, grad_tokens, grad_gates
):
    slot_total = back_ref.shape[0]
    mask = hits(slot_total, meta_ref, 0) | hits(slot_total, meta_ref, 1)
    own = dot(one_hot(mask), back_ref[...], 0, 0)
    grad_tokens[...] = (own + got_back[...].astype(F32)).astype(BF16)
    combined[...] = (own_out[...] + got_out[...].astype(F32)).astype(BF16)
    grad_gates[...] = own_gates[...] + got_gates[...]


def call(kernel, outs, flops=0, traffic=0, limit=12, **options):
    return pl.pallas_call(
        kernel,
        out_shape=outs,
        compiler_params=pltpu.CompilerParams(vmem_limit_bytes=limit * MIB),
        cost_estimate=pl.CostEstimate(flops=flops, bytes_accessed=traffic, transcendentals=0),
        **options,
    )


def in_hbm(values):
    return pltpu.with_memory_space_constraint(values, pltpu.HBM)


def in_vmem(values):
    return pltpu.with_memory_space_constraint(values, pltpu.VMEM)


def body(tokens, expert_ids, keep_mask, gate_weights, weight_in, weight_out, grad_output):
    token_rows, width = tokens.shape
    hidden_width = weight_in.shape[2]
    rest_count = lax.axis_size("rest")
    members = lax.axis_size("row") * rest_count
    capacity = expert_ids.shape[1] * token_rows // members
    slot_total = 2 * members * capacity

    def exchange(values):
        return lax.ppermute(values, "half", ((0, 1), (1, 0)))

    def shuffle(rows):
        shaped = rows.reshape(members, 2 * capacity, width)
        return lax.all_to_all(shaped, GROUP, split_axis=0, concat_axis=0, tiled=True).reshape(
            rows.shape
        )

    def shape(*dims, dtype=BF16):
        return jax.ShapeDtypeStruct(dims, dtype)

    vmem = pl.BlockSpec(memory_space=pltpu.VMEM)
    hbm = pl.BlockSpec(memory_space=pl.ANY)
    meta_shape = shape(8, token_rows, dtype=F32)
    slots, token_shape = shape(slot_total, width), shape(token_rows, width)
    slot_bytes, token_bytes = slot_total * width * 2, token_rows * width * 2
    place_flops = 4 * slot_total * token_rows * width
    far = 200 * 10**9

    partner_tokens = exchange(tokens)
    half = lax.axis_index("half").astype(jnp.int32).reshape(1)
    own_meta, sent_meta = call(
        functools.partial(route_kernel, rest_count.bit_length() - 1, capacity),
        [meta_shape, meta_shape],
        traffic=64 * token_rows,
        in_specs=[pl.BlockSpec(memory_space=pltpu.SMEM)] + [vmem] * 3,
    )(half, in_hbm(expert_ids.T), in_hbm(keep_mask.T), in_hbm(gate_weights.T))
    partner_meta = exchange(sent_meta)
    sent, grad_copy = call(
        place_tokens_kernel, [slots, token_shape], place_flops, 4 * token_bytes + slot_bytes
    )(in_hbm(tokens), partner_tokens, own_meta, partner_meta, in_hbm(grad_output))
    partner_grad = exchange(grad_copy)
    x = shuffle(sent)
    sent_cot = call(place_cotangents_kernel, slots, far, 2 * token_bytes + slot_bytes)(
        in_hbm(grad_output), partner_grad, own_meta, partner_meta
    )
    cot = shuffle(sent_cot)

    w_in, w_out = call(
        load_kernel,
        [
            pltpu.VMEM((width, hidden_width), BF16),
            pltpu.VMEM((hidden_width, width), BF16),
        ],
        0,
        4 * width * hidden_width,
        in_specs=[hbm] * 2,
        out_specs=[vmem] * 2,
        scratch_shapes=[pltpu.SemaphoreType.DMA((2,))],
    )(in_hbm(weight_in), in_hbm(weight_out))
    mid = pltpu.VMEM((slot_total, hidden_width), BF16)
    total = pltpu.VMEM((slot_total, width), F32)
    product = 2 * slot_total * width * hidden_width
    hidden, slope, outputs = call(
        forward_kernel,
        [mid, mid, slots],
        2 * product,
        2 * slot_bytes,
        16,
        in_specs=[vmem] * 3,
        out_specs=[vmem] * 3,
        scratch_shapes=[total],
    )(x, in_vmem(w_in), in_vmem(w_out))
    back_out = shuffle(outputs)
    grad_pre, grad_rows = call(
        backward_kernel,
        [mid, slots],
        2 * product,
        2 * slot_bytes,
        16,
        in_specs=[vmem] * 4,
        out_specs=[vmem] * 2,
        scratch_shapes=[total],
    )(cot, in_vmem(w_in), in_vmem(w_out), in_vmem(slope))
    back_grad = shuffle(grad_rows)
    tokens_f32, gates_shape = shape(token_rows, width, dtype=F32), shape(2, token_rows, dtype=F32)
    own_out, partner_out, own_gates, partner_gates = call(
        pick_outputs_kernel,
        [tokens_f32, token_shape, gates_shape, gates_shape],
        2 * place_flops,
        4 * token_bytes + slot_bytes,
    )(back_out, in_hbm(grad_output), partner_grad, own_meta, partner_meta)
    got_out, got_gates = exchange(partner_out), exchange(partner_gates)
    partner_back = call(
        pick_partner_kernel, token_shape, place_flops, slot_bytes + token_bytes
    )(back_grad, partner_meta)
    got_back = exchange(partner_back)
    grad_pre, partner_back = lax.optimization_barrier((grad_pre, partner_back))
    grad_in_w, grad_out_w = call(
        weights_kernel,
        [pltpu.HBM(weight_in.shape, BF16), pltpu.HBM(weight_out.shape, BF16)],
        2 * product,
        2 * slot_bytes + 4 * width * hidden_width,
        16,
        grid=(hidden_width // WIDE,),
        in_specs=[vmem] * 4,
        out_specs=[
            pl.BlockSpec((None, width, WIDE), lambda i: (0, 0, i)),
            pl.BlockSpec((None, WIDE, width), lambda i: (0, i, 0)),
        ],
    )(x, cot, in_vmem(hidden), in_vmem(grad_pre))
    combined, grad_tokens, grad_gates = call(
        finish_kernel,
        [token_shape, token_shape, gates_shape],
        place_flops,
        slot_bytes + 6 * token_bytes,
    )(back_grad, own_meta, got_back, own_out, got_out, own_gates, got_gates)
    return (combined, grad_tokens, grad_gates.T, grad_in_w, grad_out_w)


def solution(mesh):
    rows, cols = mesh.devices.shape
    axes = ("row", "half", "rest")
    halves = Mesh(mesh.devices.reshape(rows, 2, cols // 2), axes)
    flat, deep = P(axes, None), P(axes, None, None)
    return jax.shard_map(
        body,
        mesh=halves,
        in_specs=(flat, flat, flat, flat, deep, deep, flat),
        out_specs=(flat, flat, flat, deep, deep),
        check_vma=False,
    )
```

time: 132 us -> 129 us (0.977)
  Pallas kernels: 35.6 us -> 45.2 us
  local copies, waits for them, and re-layouts: 31 us -> 23.5 us
  starting transfers between devices: 33.3 us -> 28.4 us
    all_to_all x4, waiting for transfers between devices: 8.79 us -> 17.8 us  [shuffle(): lax.all_to_all(shaped, GROUP, split_axis=0, concat_axis=0, tiled=True)]
    pallas_call x8 -> x9, Pallas kernels: 35.5 us -> 44.4 us  [the longest x1 11.6 us: body(): call(forward_kernel, [mid, mid, slots], 2 * product, 2 * slot_bytes, 16,...]
    ppermute x6, waiting for transfers between devices: 21.1 us -> 12.5 us  [exchange(): return lax.ppermute(values, 'half', ((0, 1), (1, 0)))]
    unnamed x40 -> x20, local copies, waits for them, and re-layouts: 31 us -> 23.5 us
    ppermute x6, starting transfers between devices: 10.6 us -> 7.25 us  [exchange(): return lax.ppermute(values, 'half', ((0, 1), (1, 0)))]
    all_to_all x4, starting transfers between devices: 22.8 us -> 21.2 us  [shuffle(): lax.all_to_all(shaped, GROUP, split_axis=0, concat_axis=0, tiled=True)]
  transfers between devices with their start and end apart: 10 -> 10, of which waited for: 5 -> 4; matrix products, arithmetic and copies ran while one was open for 0% -> 0% of each run, Pallas kernels for 25% -> 32%
where the time goes in v8:
time: 129 us; the launch traced here: 128 us
  Pallas kernels  45.2 us (35%)
  waiting for transfers between devices  30.3 us (23%)
  starting transfers between devices  28.4 us (22%)
  local copies, waits for them, and re-layouts  23.5 us (18%)
    unnamed x20, local copies, waits for them, and re-layouts  23.5 us
    all_to_all x4, starting transfers between devices, shuffle(): lax.all_to_all(shaped, GROUP, split_axis=0, concat_axis=0, tiled=True)  21.2 us
    all_to_all x4, waiting for transfers between devices, shuffle(): lax.all_to_all(shaped, GROUP, split_axis=0, concat_axis=0, tiled=True)  17.8 us
    ppermute x6, waiting for transfers between devices, exchange(): return lax.ppermute(values, 'half', ((0, 1), (1, 0)))  12.5 us
    pallas_call x1, Pallas kernels, body(): call(forward_kernel, [mid, mid, slots], 2 * product, 2 * slot_bytes, 16,...  11.6 us
    pallas_call x1, Pallas kernels, body(): call(weights_kernel, [pltpu.HBM(weight_in.shape, BF16), pltpu.HBM(weight_...  10.4 us
    pallas_call x1, Pallas kernels, body(): call(backward_kernel, [mid, slots], 2 * product, 2 * slot_bytes, 16, in_s...  9.06 us
    ppermute x6, starting transfers between devices, exchange(): return lax.ppermute(values, 'half', ((0, 1), (1, 0)))  7.25 us
  transfers between devices with their start and end apart: 10, of which 4 were waited for; matrix products, arithmetic and copies ran while one was open for 0% of the time, Pallas kernels for 32%

profile of v8, /device:TPU:0, one launch (start us, length us, event | category | flops | bytes accessed | tf_op | source)
XLA Modules:
  0.0 128.2 jit_solution(5806442797834380618)
XLA Ops:
  0.6 4.1 %collective-permute-start = (bf16[128,768]{1,0:T(8,128)(2,1)}, bf16[128,768]{1,0:T(8,128)(2,1)S(1)}, u32[]{:S(2)}, u32[]{:S(2)}) collective-permute-start(bf16[128,768]{1,0:T(8,128)(2,1)} %own_ref.1), channel_id=1, source_target_pairs={{0,4},{4,0},{1,5},{5,1},{2,6},{6,2},{3,7},{7,3},{8,12},{12,8},{9,1... | collective-permute-start | bytes 589832 | tf_op jit(solution)/shard_map/ppermute | solution.py:255
  4.7 0.8 shard_map.110
  5.6 0.1 collective-permute-start.1
  5.7 8.6 %collective-permute-done.1.partner_meta.meta_ref = f32[8,128]{1,0:T(8,128)S(1)} collective-permute-done((f32[8,128]{1,0:T(8,128)S(1)}, f32[8,128]{1,0:T(8,128)S(1)}, u32[]{:S(2)}, u32[]{:S(2)}) %collective-permute-start.1) | collective-permute-done | bytes 4128 | tf_op jit(solution)/shard_map/ppermute | solution.py:255
  14.2 0.0 collective-permute-done.partner_ref
  14.2 2.7 %shard_map.111 = (bf16[512,768]{1,0:T(8,128)(2,1)}, bf16[128,768]{1,0:T(8,128)(2,1)S(1)}) custom-call(bf16[128,768]{1,0:T(8,128)(2,1)} %own_ref.1, bf16[128,768]{1,0:T(8,128)(2,1)S(1)} %collective-permute-done.partner_ref, f32[8,128]{1,0:T(8,128)S(1)} %get-tuple-element.26.own_meta.meta_ref, f32[8,128]{1,0:T(8,128)S(1)} %collective-permute-done.1.partner_meta.meta_ref, ...), custom_call_target="tpu_custom_call" | custom-call | flops 201326592 | bytes 1572864 | tf_op jit(solution)/shard_map/pallas_call | solution.py:283
  16.9 0.0 collective-permute-start.2
  16.9 7.4 %all-to-all-start.1 = ((bf16[16,32,768]{2,1,0:T(8,128)(2,1)}), bf16[16,32,768]{2,1,0:T(8,128)(2,1)}, u32[]{:S(2)}, u32[]{:S(2)}) async-start(bf16[16,32,768]{2,1,0:T(8,128)(2,1)} %bitcast.6), calls=%async_computation.1 | async-start | bytes 1572864 | tf_op jit(solution)/shard_map/all_to_all | solution.py:259
  24.3 3.9 %collective-permute-done.2.partner_grad = bf16[128,768]{1,0:T(8,128)(2,1)S(1)} collective-permute-done((bf16[128,768]{1,0:T(8,128)(2,1)S(1)}, bf16[128,768]{1,0:T(8,128)(2,1)S(1)}, u32[]{:S(2)}, u32[]{:S(2)}) %collective-permute-start.2) | collective-permute-done | bytes 196640 | tf_op jit(solution)/shard_map/ppermute | solution.py:255
  28.2 2.9 %shard_map.112 = bf16[512,768]{1,0:T(8,128)(2,1)} custom-call(bf16[128,768]{1,0:T(8,128)(2,1)} %own_grad.3, bf16[128,768]{1,0:T(8,128)(2,1)S(1)} %collective-permute-done.2.partner_grad, f32[8,128]{1,0:T(8,128)S(1)} %get-tuple-element.26.own_meta.meta_ref, f32[8,128]{1,0:T(8,128)S(1)} %collective-permute-done.1.partner_meta.meta_ref), custom_call_target="tpu_custom_call" | custom-call | flops 199999995904 | bytes 1179648 | tf_op jit(solution)/shard_map/pallas_call | solution.py:288
  31.1 6.3 %all-to-all-done.1 = bf16[16,32,768]{2,1,0:T(8,128)(2,1)} async-done(((bf16[16,32,768]{2,1,0:T(8,128)(2,1)}), bf16[16,32,768]{2,1,0:T(8,128)(2,1)}, u32[]{:S(2)}, u32[]{:S(2)}) %all-to-all-start.1) | async-done | bytes 786464 | tf_op jit(solution)/shard_map/all_to_all | solution.py:259
  37.4 3.6 %all-to-all-start = ((bf16[16,32,768]{2,1,0:T(8,128)(2,1)}), bf16[16,32,768]{2,1,0:T(8,128)(2,1)S(1)}, u32[]{:S(2)}, u32[]{:S(2)}) async-start(bf16[16,32,768]{2,1,0:T(8,128)(2,1)} %bitcast.4), calls=%async_computation | async-start | bytes 1572864 | tf_op jit(solution)/shard_map/all_to_all | solution.py:259
  41.0 4.6 %shard_map.113 = (bf16[768,4096]{1,0:T(8,128)(2,1)S(1)}, bf16[4096,768]{1,0:T(8,128)(2,1)S(1)}) custom-call(bf16[1,768,4096]{2,1,0:T(8,128)(2,1)} %w_in.1, bf16[1,4096,768]{2,1,0:T(8,128)(2,1)} %w_out.1), custom_call_target="tpu_custom_call" | custom-call | bytes 12582912 | tf_op jit(solution)/shard_map/pallas_call | solution.py:293
  45.6 11.6 %shard_map.114 = (bf16[512,4096]{1,0:T(8,128)(2,1)S(1)}, bf16[512,4096]{1,0:T(8,128)(2,1)S(1)}, bf16[512,768]{1,0:T(8,128)(2,1)}) custom-call(bf16[512,768]{1,0:T(8,128)(2,1)} %bitcast.7.x.x_ref, bf16[768,4096]{1,0:T(8,128)(2,1)S(1)} %get-tuple-element.29.w_in, bf16[4096,768]{1,0:T(8,128)(2,1)S(1)} %get-tuple-element.30.w_out), custom_call_target="tpu_custom_call" | custom-call | flops 6442450944 | bytes 1572864 | tf_op jit(solution)/shard_map/pallas_call | solution.py:308
  57.3 0.0 copy-start
  57.3 2.7 %copy-done = bf16[768,4096]{1,0:T(8,128)(2,1)} copy-done((bf16[768,4096]{1,0:T(8,128)(2,1)}, bf16[768,4096]{1,0:T(8,128)(2,1)S(1)}, u32[]{:S(2)}) %copy-start) | copy-done | bytes 6291480
  60.0 0.0 copy-start.2
  60.0 2.7 %copy-done.2 = bf16[4096,768]{1,0:T(8,128)(2,1)} copy-done((bf16[4096,768]{1,0:T(8,128)(2,1)}, bf16[4096,768]{1,0:T(8,128)(2,1)S(1)}, u32[]{:S(2)}) %copy-start.2) | copy-done | bytes 6291480
  62.7 0.0 copy-start.6
  62.7 2.0 %copy-done.6 = bf16[512,4096]{1,0:T(8,128)(2,1)} copy-done((bf16[512,4096]{1,0:T(8,128)(2,1)}, bf16[512,4096]{1,0:T(8,128)(2,1)S(1)}, u32[]{:S(2)}) %copy-start.6) | copy-done | bytes 4194328
  64.7 0.0 copy-start.8
  64.7 2.0 %copy-done.8 = bf16[512,4096]{1,0:T(8,128)(2,1)} copy-done((bf16[512,4096]{1,0:T(8,128)(2,1)}, bf16[512,4096]{1,0:T(8,128)(2,1)S(1)}, u32[]{:S(2)}) %copy-start.8) | copy-done | bytes 4194328
  66.7 0.0 all-to-all-done
  66.7 5.0 %all-to-all-start.3 = ((bf16[16,32,768]{2,1,0:T(8,128)(2,1)}), bf16[16,32,768]{2,1,0:T(8,128)(2,1)S(1)}, u32[]{:S(2)}, u32[]{:S(2)}) async-start(bf16[16,32,768]{2,1,0:T(8,128)(2,1)} %bitcast.10), calls=%async_computation.3 | async-start | bytes 1572864 | tf_op jit(solution)/shard_map/all_to_all | solution.py:259
  71.7 0.0 copy-start.1
  71.7 2.8 %copy-done.1 = bf16[768,4096]{1,0:T(8,128)(2,1)S(1)} copy-done((bf16[768,4096]{1,0:T(8,128)(2,1)S(1)}, bf16[768,4096]{1,0:T(8,128)(2,1)}, u32[]{:S(2)}) %copy-start.1) | copy-done | bytes 6291480
  74.5 0.0 copy-start.3
  74.5 2.8 %copy-done.3 = bf16[4096,768]{1,0:T(8,128)(2,1)S(1)} copy-done((bf16[4096,768]{1,0:T(8,128)(2,1)S(1)}, bf16[4096,768]{1,0:T(8,128)(2,1)}, u32[]{:S(2)}) %copy-start.3) | copy-done | bytes 6291480
  77.3 0.0 copy-start.7
  77.3 2.2 %copy-done.7 = bf16[512,4096]{1,0:T(8,128)(2,1)S(1)} copy-done((bf16[512,4096]{1,0:T(8,128)(2,1)S(1)}, bf16[512,4096]{1,0:T(8,128)(2,1)}, u32[]{:S(2)}) %copy-start.7) | copy-done | bytes 4194328
  79.5 9.1 %shard_map.115 = (bf16[512,4096]{1,0:T(8,128)(2,1)S(1)}, bf16[512,768]{1,0:T(8,128)(2,1)}) custom-call(bf16[512,768]{1,0:T(8,128)(2,1)S(1)} %bitcast.15, bf16[768,4096]{1,0:T(8,128)(2,1)S(1)} %copy-done.1, bf16[4096,768]{1,0:T(8,128)(2,1)S(1)} %copy-done.3, bf16[512,4096]{1,0:T(8,128)(2,1)S(1)} %copy-done.7), custom_call_target="tpu_custom_call" | custom-call | flops 6442450944 | bytes 1572864 | tf_op jit(solution)/shard_map/pallas_call | solution.py:319
  88.5 0.0 copy-start.4
  88.5 2.0 %copy-done.4 = bf16[512,4096]{1,0:T(8,128)(2,1)} copy-done((bf16[512,4096]{1,0:T(8,128)(2,1)}, bf16[512,4096]{1,0:T(8,128)(2,1)S(1)}, u32[]{:S(2)}) %copy-start.4) | copy-done | bytes 4194328
  90.6 0.0 all-to-all-done.3
  90.6 5.1 %all-to-all-start.2 = ((bf16[16,32,768]{2,1,0:T(8,128)(2,1)}), bf16[16,32,768]{2,1,0:T(8,128)(2,1)S(1)}, u32[]{:S(2)}, u32[]{:S(2)}) async-start(bf16[16,32,768]{2,1,0:T(8,128)(2,1)} %bitcast.8), calls=%async_computation.2 | async-start | bytes 1572864 | tf_op jit(solution)/shard_map/all_to_all | solution.py:259
  95.7 1.7 %shard_map.117 = (f32[128,768]{1,0:T(8,128)S(1)}, bf16[128,768]{1,0:T(8,128)(2,1)S(1)}, f32[2,128]{1,0:T(2,128)S(1)}, f32[2,128]{1,0:T(2,128)S(1)}) custom-call(bf16[512,768]{1,0:T(8,128)(2,1)S(1)} %bitcast.17, bf16[128,768]{1,0:T(8,128)(2,1)} %own_grad.3, bf16[128,768]{1,0:T(8,128)(2,1)S(1)} %collective-permute-done.2.partner_grad, ...), custom_call_target="tpu_custom_call" | custom-call | flops 402653184 | bytes 1572864 | tf_op jit(solution)/shard_map/pallas_call | solution.py:331
  97.4 0.6 collective-permute-start.5
  98.0 2.4 %collective-permute-start.4 = (bf16[128,768]{1,0:T(8,128)(2,1)S(1)}, bf16[128,768]{1,0:T(8,128)(2,1)S(1)}, u32[]{:S(2)}, u32[]{:S(2)}) collective-permute-start(bf16[128,768]{1,0:T(8,128)(2,1)S(1)} %get-tuple-element.36), channel_id=1, source_target_pairs={{0,4},{4,0},{1,5},{5,1},{2,6},{6,2},{3,7},{7,3},{8,12},{12,8},{9,1... | collective-permute-start | bytes 589832 | tf_op jit(solution)/shard_map/ppermute | solution.py:255
  100.4 11.5 %all-to-all-done.2 = bf16[16,32,768]{2,1,0:T(8,128)(2,1)S(1)} async-done(((bf16[16,32,768]{2,1,0:T(8,128)(2,1)}), bf16[16,32,768]{2,1,0:T(8,128)(2,1)S(1)}, u32[]{:S(2)}, u32[]{:S(2)}) %all-to-all-start.2) | async-done | bytes 786464 | tf_op jit(solution)/shard_map/all_to_all | solution.py:259
  111.9 0.3 shard_map.116
  112.2 0.1 collective-permute-start.3
  112.3 0.0 copy-start.5
  112.3 2.2 %copy-done.5 = bf16[512,4096]{1,0:T(8,128)(2,1)S(1)} copy-done((bf16[512,4096]{1,0:T(8,128)(2,1)S(1)}, bf16[512,4096]{1,0:T(8,128)(2,1)}, u32[]{:S(2)}) %copy-start.5) | copy-done | bytes 4194328
  114.5 0.0 copy-start.9
  114.5 2.2 %copy-done.9 = bf16[512,4096]{1,0:T(8,128)(2,1)S(1)} copy-done((bf16[512,4096]{1,0:T(8,128)(2,1)S(1)}, bf16[512,4096]{1,0:T(8,128)(2,1)}, u32[]{:S(2)}) %copy-start.9) | copy-done | bytes 4194328
  116.7 10.4 %shard_map.119 = (bf16[1,768,4096]{2,1,0:T(8,128)(2,1)}, bf16[1,4096,768]{2,1,0:T(8,128)(2,1)}) custom-call(bf16[512,768]{1,0:T(8,128)(2,1)} %bitcast.7.x.x_ref, bf16[512,768]{1,0:T(8,128)(2,1)S(1)} %bitcast.16, bf16[512,4096]{1,0:T(8,128)(2,1)S(1)} %copy-done.9, bf16[512,4096]{1,0:T(8,128)(2,1)S(1)} %copy-done.5), custom_call_target="tpu_custom_call" | custom-call | flops 6442450944 | bytes 14155776 | tf_op jit(solution)/shard_map/pallas_call | solution.py:343
  127.1 0.0 collective-permute-done.5.got_gates
  127.1 0.0 collective-permute-done.4.got_out
  127.1 0.0 collective-permute-done.3.got_back
  127.1 1.1 shard_map.118
Async XLA Ops:
  0.6 13.6 %collective-permute-start = (bf16[128,768]{1,0:T(8,128)(2,1)}, bf16[128,768]{1,0:T(8,128)(2,1)S(1)}, u32[]{:S(2)}, u32[]{:S(2)}) collective-permute-start(bf16[128,768]{1,0:T(8,128)(2,1)} %own_ref.1), channel_id=1, source_target_pairs={{0,4},{4,0},{1,5},{5,1},{2,6},{6,2},{3,7},{7,3},{8,12},{12,8},{9,1... | collective-permute-start | bytes 589832 | tf_op jit(solution)/shard_map/ppermute | solution.py:255
  5.6 8.7 %collective-permute-start.1 = (f32[8,128]{1,0:T(8,128)S(1)}, f32[8,128]{1,0:T(8,128)S(1)}, u32[]{:S(2)}, u32[]{:S(2)}) collective-permute-start(f32[8,128]{1,0:T(8,128)S(1)} %get-tuple-element.27), channel_id=1, source_target_pairs={{0,4},{4,0},{1,5},{5,1},{2,6},{6,2},{3,7},{7,3},{8,12},{12,8},{9,1... | collective-permute-start | bytes 12296 | tf_op jit(solution)/shard_map/ppermute | solution.py:255
  16.9 11.3 %collective-permute-start.2 = (bf16[128,768]{1,0:T(8,128)(2,1)S(1)}, bf16[128,768]{1,0:T(8,128)(2,1)S(1)}, u32[]{:S(2)}, u32[]{:S(2)}) collective-permute-start(bf16[128,768]{1,0:T(8,128)(2,1)S(1)} %get-tuple-element.28), channel_id=1, source_target_pairs={{0,4},{4,0},{1,5},{5,1},{2,6},{6,2},{3,7},{7,3},{8,12},{12,8},{9,1... | collective-permute-start | bytes 589832 | tf_op jit(solution)/shard_map/ppermute | solution.py:255
  16.9 20.5 %all-to-all-start.1 = ((bf16[16,32,768]{2,1,0:T(8,128)(2,1)}), bf16[16,32,768]{2,1,0:T(8,128)(2,1)}, u32[]{:S(2)}, u32[]{:S(2)}) async-start(bf16[16,32,768]{2,1,0:T(8,128)(2,1)} %bitcast.6), calls=%async_computation.1 | async-start | bytes 1572864 | tf_op jit(solution)/shard_map/all_to_all | solution.py:259
  37.4 29.3 %all-to-all-start = ((bf16[16,32,768]{2,1,0:T(8,128)(2,1)}), bf16[16,32,768]{2,1,0:T(8,128)(2,1)S(1)}, u32[]{:S(2)}, u32[]{:S(2)}) async-start(bf16[16,32,768]{2,1,0:T(8,128)(2,1)} %bitcast.4), calls=%async_computation | async-start | bytes 1572864 | tf_op jit(solution)/shard_map/all_to_all | solution.py:259
  57.3 2.7 %copy-start = (bf16[768,4096]{1,0:T(8,128)(2,1)}, bf16[768,4096]{1,0:T(8,128)(2,1)S(1)}, u32[]{:S(2)}) copy-start(bf16[768,4096]{1,0:T(8,128)(2,1)S(1)} %get-tuple-element.29.w_in) | copy-start | bytes 18874372
  60.0 2.7 %copy-start.2 = (bf16[4096,768]{1,0:T(8,128)(2,1)}, bf16[4096,768]{1,0:T(8,128)(2,1)S(1)}, u32[]{:S(2)}) copy-start(bf16[4096,768]{1,0:T(8,128)(2,1)S(1)} %get-tuple-element.30.w_out) | copy-start | bytes 18874372
  62.7 2.0 %copy-start.6 = (bf16[512,4096]{1,0:T(8,128)(2,1)}, bf16[512,4096]{1,0:T(8,128)(2,1)S(1)}, u32[]{:S(2)}) copy-start(bf16[512,4096]{1,0:T(8,128)(2,1)S(1)} %get-tuple-element.32.slope) | copy-start | bytes 12582916
  64.7 2.0 %copy-start.8 = (bf16[512,4096]{1,0:T(8,128)(2,1)}, bf16[512,4096]{1,0:T(8,128)(2,1)S(1)}, u32[]{:S(2)}) copy-start(bf16[512,4096]{1,0:T(8,128)(2,1)S(1)} %get-tuple-element.42.hidden_ref) | copy-start | bytes 12582916
  66.7 23.9 %all-to-all-start.3 = ((bf16[16,32,768]{2,1,0:T(8,128)(2,1)}), bf16[16,32,768]{2,1,0:T(8,128)(2,1)S(1)}, u32[]{:S(2)}, u32[]{:S(2)}) async-start(bf16[16,32,768]{2,1,0:T(8,128)(2,1)} %bitcast.10), calls=%async_computation.3 | async-start | bytes 1572864 | tf_op jit(solution)/shard_map/all_to_all | solution.py:259
  71.7 2.8 %copy-start.1 = (bf16[768,4096]{1,0:T(8,128)(2,1)S(1)}, bf16[768,4096]{1,0:T(8,128)(2,1)}, u32[]{:S(2)}) copy-start(bf16[768,4096]{1,0:T(8,128)(2,1)} %copy-done) | copy-start | bytes 18874372
  74.5 2.8 %copy-start.3 = (bf16[4096,768]{1,0:T(8,128)(2,1)S(1)}, bf16[4096,768]{1,0:T(8,128)(2,1)}, u32[]{:S(2)}) copy-start(bf16[4096,768]{1,0:T(8,128)(2,1)} %copy-done.2) | copy-start | bytes 18874372
  77.3 2.2 %copy-start.7 = (bf16[512,4096]{1,0:T(8,128)(2,1)S(1)}, bf16[512,4096]{1,0:T(8,128)(2,1)}, u32[]{:S(2)}) copy-start(bf16[512,4096]{1,0:T(8,128)(2,1)} %copy-done.6) | copy-start | bytes 12582916
  88.5 2.0 %copy-start.4 = (bf16[512,4096]{1,0:T(8,128)(2,1)}, bf16[512,4096]{1,0:T(8,128)(2,1)S(1)}, u32[]{:S(2)}) copy-start(bf16[512,4096]{1,0:T(8,128)(2,1)S(1)} %get-tuple-element.44.grad_pre_ref) | copy-start | bytes 12582916
  90.6 21.3 %all-to-all-start.2 = ((bf16[16,32,768]{2,1,0:T(8,128)(2,1)}), bf16[16,32,768]{2,1,0:T(8,128)(2,1)S(1)}, u32[]{:S(2)}, u32[]{:S(2)}) async-start(bf16[16,32,768]{2,1,0:T(8,128)(2,1)} %bitcast.8), calls=%async_computation.2 | async-start | bytes 1572864 | tf_op jit(solution)/shard_map/all_to_all | solution.py:259
  97.4 29.7 %collective-permute-start.5 = (f32[2,128]{1,0:T(2,128)S(1)}, f32[2,128]{1,0:T(2,128)S(1)}, u32[]{:S(2)}, u32[]{:S(2)}) collective-permute-start(f32[2,128]{1,0:T(2,128)S(1)} %get-tuple-element.38), channel_id=1, source_target_pairs={{0,4},{4,0},{1,5},{5,1},{2,6},{6,2},{3,7},{7,3},{8,12},{12,8},{9,1... | collective-permute-start | bytes 3080 | tf_op jit(solution)/shard_map/ppermute | solution.py:255
  98.0 29.2 %collective-permute-start.4 = (bf16[128,768]{1,0:T(8,128)(2,1)S(1)}, bf16[128,768]{1,0:T(8,128)(2,1)S(1)}, u32[]{:S(2)}, u32[]{:S(2)}) collective-permute-start(bf16[128,768]{1,0:T(8,128)(2,1)S(1)} %get-tuple-element.36), channel_id=1, source_target_pairs={{0,4},{4,0},{1,5},{5,1},{2,6},{6,2},{3,7},{7,3},{8,12},{12,8},{9,1... | collective-permute-start | bytes 589832 | tf_op jit(solution)/shard_map/ppermute | solution.py:255
  112.2 14.9 %collective-permute-start.3 = (bf16[128,768]{1,0:T(8,128)(2,1)S(1)}, bf16[128,768]{1,0:T(8,128)(2,1)S(1)}, u32[]{:S(2)}, u32[]{:S(2)}) collective-permute-start(bf16[128,768]{1,0:T(8,128)(2,1)S(1)} %shard_map.116), channel_id=1, source_target_pairs={{0,4},{4,0},{1,5},{5,1},{2,6},{6,2},{3,7},{7,3},{8,12},{12,8},{9,1... | collective-permute-start | bytes 589832 | tf_op jit(solution)/shard_map/ppermute | solution.py:255
  112.3 2.2 %copy-start.5 = (bf16[512,4096]{1,0:T(8,128)(2,1)S(1)}, bf16[512,4096]{1,0:T(8,128)(2,1)}, u32[]{:S(2)}) copy-start(bf16[512,4096]{1,0:T(8,128)(2,1)} %copy-done.4) | copy-start | bytes 12582916
  114.5 2.2 %copy-start.9 = (bf16[512,4096]{1,0:T(8,128)(2,1)S(1)}, bf16[512,4096]{1,0:T(8,128)(2,1)}, u32[]{:S(2)}) copy-start(bf16[512,4096]{1,0:T(8,128)(2,1)} %copy-done.8) | copy-start | bytes 12582916

commit v9 on v5

--- a/solution.py
+++ b/solution.py
@@ -5,6 +5,7 @@
 from jax import lax
 from jax.experimental import pallas as pl
 from jax.experimental.pallas import tpu as pltpu
+from jax.sharding import Mesh
 from jax.sharding import PartitionSpec as P
 
 BLOCK = 128
@@ -12,6 +13,9 @@
 F32 = jnp.float32
 MIB = 1024 * 1024
 SUB = 256
+AXES = ("row", "half", "rest")
+ALL = ("row", "rest", "half")
+GROUP = ("row", "rest")
 
 
 def dot(a, b, contract_a, contract_b):
@@ -25,7 +29,7 @@
     return jnp.transpose(jnp.broadcast_to(row, (count, count)))
 
 
-def route(ids_ref, keep_ref, gates_ref, meta_ref, capacity):
+def route(rest_bits, capacity, half, ids_ref, keep_ref, gates_ref, mine_ref, other_ref):
     token_rows = ids_ref.shape[1]
     ids = ids_ref[...].astype(F32)
     earlier = lax.broadcasted_iota(jnp.int32, (token_rows, token_rows), 0) < lax.broadcasted_iota(
@@ -37,10 +41,19 @@
         for other_choice in columns:
             count = count + jnp.where(earlier & (other_choice == ids[k : k + 1]), 1.0, 0.0)
         slot = jnp.sum(count, axis=0, keepdims=True).astype(jnp.int32)
-        row = ids_ref[k : k + 1, :] * capacity + slot
-        meta_ref[k : k + 1, :] = jnp.where(keep_ref[k : k + 1, :] > 0, row, -1).astype(F32)
-        meta_ref[k + 2 : k + 3, :] = gates_ref[k : k + 1, :]
-    meta_ref[4:8, :] = jnp.zeros((4, token_rows), F32)
+        expert = ids_ref[k : k + 1, :]
+        kept = keep_ref[k : k + 1, :] > 0
+        side = (expert >> rest_bits) & 1
+        local = ((expert >> (rest_bits + 1)) << rest_bits) + (expert & ((1 << rest_bits) - 1))
+        base = local * (2 * capacity) + slot
+        row = base + half * capacity
+        mine_ref[k : k + 1, :] = jnp.where(kept & (side == half), row, -1).astype(F32)
+        other_ref[k : k + 1, :] = jnp.where(kept & (side != half), row, -1).astype(F32)
+        mine_ref[k + 4 : k + 5, :] = jnp.where(kept, base + side * capacity, -1).astype(F32)
+        for ref in (mine_ref, other_ref):
+            ref[k + 2 : k + 3, :] = gates_ref[k : k + 1, :]
+    mine_ref[6:8, :] = jnp.zeros((2, token_rows), F32)
+    other_ref[4:8, :] = jnp.zeros((4, token_rows), F32)
 
 
 def hits(slot_total, meta_ref, k):
@@ -63,10 +76,12 @@
     return jnp.concatenate(pieces, axis=1)
 
 
-def place_tokens_kernel(capacity, tokens_ref, ids_ref, keep_ref, gates_ref, meta_ref, out_ref):
-    route(ids_ref, keep_ref, gates_ref, meta_ref, capacity)
+def place_tokens_kernel(
+    rest_bits, capacity, half_ref, tokens_ref, ids_ref, keep_ref, gates_ref, mine_ref, other_ref, out_ref
+):
+    route(rest_bits, capacity, half_ref[0], ids_ref, keep_ref, gates_ref, mine_ref, other_ref)
     slot_total = out_ref.shape[0]
-    mask = hits(slot_total, meta_ref, 0) | hits(slot_total, meta_ref, 1)
+    mask = hits(slot_total, mine_ref, 4) | hits(slot_total, mine_ref, 5)
     out_ref[...] = dot(one_hot(mask), restore(tokens_ref), 1, 0).astype(BF16)
 
 
@@ -79,18 +94,15 @@
     return jnp.concatenate(pieces, axis=1)
 
 
-def place_cotangents_kernel(grad_ref, meta_ref, out_ref):
+def place_cotangents_kernel(own_grad, partner_grad, own_meta, partner_meta, out_ref):
     slot_total = out_ref.shape[0]
-    parts = [
-        dot(
-            one_hot(hits(slot_total, meta_ref, k)),
-            scaled_rows(meta_ref[k + 2 : k + 3, :], grad_ref).astype(BF16),
-            1,
-            0,
-        )
-        for k in range(2)
-    ]
-    out_ref[...] = (parts[0] + parts[1]).astype(BF16)
+    total = None
+    for grad_ref, meta_ref in ((own_grad, own_meta), (partner_grad, partner_meta)):
+        for k in range(2):
+            rows = scaled_rows(meta_ref[k + 2 : k + 3, :], grad_ref).astype(BF16)
+            part = dot(one_hot(hits(slot_total, meta_ref, k)), rows, 1, 0)
+            total = part if total is None else total + part
+    out_ref[...] = total.astype(BF16)
 
 
 def gelu_parts(v):
@@ -154,30 +166,47 @@
     grad_out_ref[...] = dot(hidden_ref[...], cot_ref[...], 0, 0).astype(BF16)
 
 
-def pick_outputs_kernel(back_ref, grad_ref, meta_ref, out_ref, gates_ref):
+def pick_outputs_kernel(
+    back_ref, own_grad, partner_grad, own_meta, partner_meta, own_out, partner_out, own_gates, partner_gates
+):
     slot_total = back_ref.shape[0]
-    total = None
-    for k in range(2):
-        picked = dot(one_hot(hits(slot_total, meta_ref, k)), back_ref[...], 0, 0)
-        gate = column(meta_ref[k + 2 : k + 3, :])
-        weighted = jnp.concatenate(
-            [
-                gate * picked[:, b * BLOCK : (b + 1) * BLOCK]
-                for b in range(picked.shape[1] // BLOCK)
-            ],
-            axis=1,
-        )
-        total = weighted if total is None else total + weighted
-        sums = jnp.sum(picked * grad_ref[...].astype(F32), axis=1, keepdims=True)
-        rows = jnp.transpose(jnp.broadcast_to(sums, (sums.shape[0], sums.shape[0])))
-        gates_ref[k : k + 1, :] = rows[0:1, :]
-    out_ref[...] = total.astype(BF16)
-
-
-def pick_gradients_kernel(back_ref, meta_ref, out_ref):
+    for grad_ref, meta_ref, out_ref, gates_ref in (
+        (own_grad, own_meta, own_out, own_gates),
+        (partner_grad, partner_meta, partner_out, partner_gates),
+    ):
+        total = None
+        for k in range(2):
+            picked = dot(one_hot(hits(slot_total, meta_ref, k)), back_ref[...], 0, 0)
+            gate = column(meta_ref[k + 2 : k + 3, :])
+            weighted = jnp.concatenate(
+                [
+                    gate * picked[:, b * BLOCK : (b + 1) * BLOCK]
+                    for b in range(picked.shape[1] // BLOCK)
+                ],
+                axis=1,
+            )
+            total = weighted if total is None else total + weighted
+            sums = jnp.sum(picked * grad_ref[...].astype(F32), axis=1, keepdims=True)
+            rows = jnp.transpose(jnp.broadcast_to(sums, (sums.shape[0], sums.shape[0])))
+            gates_ref[k : k + 1, :] = rows[0:1, :]
+        out_ref[...] = total.astype(out_ref.dtype)
+
+
+def pick_partner_kernel(back_ref, meta_ref, out_ref):
     slot_total = back_ref.shape[0]
     mask = hits(slot_total, meta_ref, 0) | hits(slot_total, meta_ref, 1)
     out_ref[...] = dot(one_hot(mask), back_ref[...], 0, 0).astype(BF16)
+
+
+def finish_kernel(
+    back_ref, meta_ref, got_back, own_out, got_out, own_gates, got_gates, combined, grad_tokens, grad_gates
+):
+    slot_total = back_ref.shape[0]
+    mask = hits(slot_total, meta_ref, 0) | hits(slot_total, meta_ref, 1)
+    own = dot(one_hot(mask), back_ref[...], 0, 0)
+    grad_tokens[...] = (own + got_back[...].astype(F32)).astype(BF16)
+    combined[...] = (own_out[...] + got_out[...].astype(F32)).astype(BF16)
+    grad_gates[...] = own_gates[...] + got_gates[...]
 
 
 def call(kernel, outs, flops=0, traffic=0, limit=12, **options):
@@ -197,31 +226,50 @@
 def body(tokens, expert_ids, keep_mask, gate_weights, weight_in, weight_out, grad_output):
     token_rows, width = tokens.shape
     hidden_width = weight_in.shape[2]
-    experts = lax.axis_size("row") * lax.axis_size("col")
-    capacity = 2 * expert_ids.shape[1] * token_rows // experts
-    slot_total = experts * capacity
-
-    def shuffle(rows):
-        shaped = rows.reshape(experts, capacity, width)
-        return lax.all_to_all(
-            shaped, ("row", "col"), split_axis=0, concat_axis=0, tiled=True
-        ).reshape(slot_total, width)
-
-    slots = jax.ShapeDtypeStruct((slot_total, width), BF16)
-    slot_bytes = slot_total * width * 2
-    token_bytes = token_rows * width * 2
+    rest_count = lax.axis_size("rest")
+    members = lax.axis_size("row") * rest_count
+    capacity = expert_ids.shape[1] * token_rows // members
+    slot_total = 2 * members * capacity
+
+    def exchange(values):
+        return lax.ppermute(values, "half", ((0, 1), (1, 0)))
+
+    def shuffle(rows, group, peers):
+        shaped = rows.reshape(peers, slot_total // peers, width)
+        return lax.all_to_all(shaped, group, split_axis=0, concat_axis=0, tiled=True).reshape(
+            rows.shape
+        )
+
+    def shape(*dims, dtype=BF16):
+        return jax.ShapeDtypeStruct(dims, dtype)
+
+    vmem = pl.BlockSpec(memory_space=pltpu.VMEM)
+    meta_shape = shape(8, token_rows, dtype=F32)
+    slots, token_shape = shape(slot_total, width), shape(token_rows, width)
+    slot_bytes, token_bytes = slot_total * width * 2, token_rows * width * 2
     place_flops = 2 * slot_total * token_rows * width
-    meta, sent = call(
-        functools.partial(place_tokens_kernel, capacity),
-        [jax.ShapeDtypeStruct((8, token_rows), F32), slots],
+
+    partner_grad = exchange(grad_output)
+    half = lax.axis_index("half").astype(jnp.int32).reshape(1)
+    own_meta, sent_meta, sent = call(
+        functools.partial(place_tokens_kernel, rest_count.bit_length() - 1, capacity),
+        [meta_shape, meta_shape, slots],
         place_flops,
         token_bytes + slot_bytes,
-    )(in_hbm(tokens), in_hbm(expert_ids.T), in_hbm(keep_mask.T), in_hbm(gate_weights.T))
-    x = shuffle(sent)
+        in_specs=[pl.BlockSpec(memory_space=pltpu.SMEM)] + [vmem] * 4,
+    )(
+        half,
+        in_hbm(tokens),
+        in_hbm(expert_ids.T),
+        in_hbm(keep_mask.T),
+        in_hbm(gate_weights.T),
+    )
+    x = shuffle(sent, ALL, 2 * members)
+    partner_meta = exchange(sent_meta)
     sent_cot = call(
-        place_cotangents_kernel, slots, 2 * place_flops, token_bytes + slot_bytes
-    )(in_hbm(grad_output), meta)
-    cot = shuffle(sent_cot)
+        place_cotangents_kernel, slots, 4 * place_flops, 2 * token_bytes + slot_bytes
+    )(in_hbm(grad_output), partner_grad, own_meta, partner_meta)
+    cot = shuffle(sent_cot, GROUP, members)
 
     chunk = 1024
     whole = pl.BlockSpec((slot_total, width), lambda i: (0, 0))
@@ -245,7 +293,7 @@
         out_specs=[mid_spec, mid_spec, whole],
         scratch_shapes=[total],
     )(x, weight_in, weight_out)
-    back_out = shuffle(outputs)
+    back_out = shuffle(outputs, GROUP, members)
     grad_pre, grad_rows = call(
         backward_kernel,
         [mid, slots],
@@ -257,16 +305,20 @@
         out_specs=[mid_spec, whole],
         scratch_shapes=[total],
     )(cot, weight_in, weight_out, in_hbm(slope))
-    back_grad = shuffle(grad_rows)
-    combined, grad_gates = call(
+    back_grad = shuffle(grad_rows, GROUP, members)
+    tokens_f32, gates_shape = shape(token_rows, width, dtype=F32), shape(2, token_rows, dtype=F32)
+    own_out, partner_out, own_gates, partner_gates = call(
         pick_outputs_kernel,
-        [
-            jax.ShapeDtypeStruct((token_rows, width), BF16),
-            jax.ShapeDtypeStruct((2, token_rows), F32),
-        ],
-        2 * place_flops,
-        2 * token_bytes + slot_bytes,
-    )(back_out, in_hbm(grad_output), meta)
+        [tokens_f32, token_shape, gates_shape, gates_shape],
+        4 * place_flops,
+        4 * token_bytes + slot_bytes,
+    )(back_out, in_hbm(grad_output), partner_grad, own_meta, partner_meta)
+    got_out, got_gates = exchange(partner_out), exchange(partner_gates)
+    partner_back = call(
+        pick_partner_kernel, token_shape, place_flops, slot_bytes + token_bytes
+    )(back_grad, partner_meta)
+    got_back = exchange(partner_back)
+    grad_pre, partner_back = lax.optimization_barrier((grad_pre, partner_back))
     grad_in_w, grad_out_w = call(
         weights_kernel,
         [pltpu.HBM(weight_in.shape, BF16), pltpu.HBM(weight_out.shape, BF16)],
@@ -277,21 +329,22 @@
         in_specs=[whole, whole, mid_spec, mid_spec],
         out_specs=[in_spec, out_spec],
     )(x, cot, in_hbm(hidden), in_hbm(grad_pre))
-    grad_tokens = call(
-        pick_gradients_kernel,
-        jax.ShapeDtypeStruct((token_rows, width), BF16),
+    combined, grad_tokens, grad_gates = call(
+        finish_kernel,
+        [token_shape, token_shape, gates_shape],
         place_flops,
-        slot_bytes + token_bytes,
-    )(back_grad, meta)
+        slot_bytes + 6 * token_bytes,
+    )(back_grad, own_meta, got_back, own_out, got_out, own_gates, got_gates)
     return (combined, grad_tokens, grad_gates.T, grad_in_w, grad_out_w)
 
 
 def solution(mesh):
-    flat = P(("row", "col"), None)
-    deep = P(("row", "col"), None, None)
+    rows, cols = mesh.devices.shape
+    halves = Mesh(mesh.devices.reshape(rows, 2, cols // 2), AXES)
+    flat, deep = P(AXES, None), P(AXES, None, None)
     return jax.shard_map(
         body,
-        mesh=mesh,
+        mesh=halves,
         in_specs=(flat, flat, flat, flat, deep, deep, flat),
         out_specs=(flat, flat, flat, deep, deep),
         check_vma=False,

time: 108 us -> 111 us (1.028)
  starting transfers between devices: 15.2 us -> 27.3 us
  waiting for transfers between devices: 46.3 us -> 36 us
  Pallas kernels: 44.1 us -> 45.5 us
    all_to_all x4, waiting for transfers between devices: 46.3 us -> 9.77 us  [shuffle(): lax.all_to_all(shaped, group, split_axis=0, concat_axis=0, tiled=True)]
    ppermute x0 -> x5, waiting for transfers between devices: none -> 26.2 us  [exchange(): return lax.ppermute(values, 'half', ((0, 1), (1, 0)))]
    all_to_all x4, starting transfers between devices: 15.2 us -> 21.3 us  [shuffle(): lax.all_to_all(shaped, group, split_axis=0, concat_axis=0, tiled=True)]
    ppermute x0 -> x5, starting transfers between devices: none -> 5.99 us  [exchange(): return lax.ppermute(values, 'half', ((0, 1), (1, 0)))]
    pallas_call x4 -> x5, Pallas kernels: 7.98 us -> 9.11 us  [the longest x1 2.94 us: body(): call(place_cotangents_kernel, slots, 4 * place_flops, 2 * token_bytes + s...]
  transfers between devices with their start and end apart: 4 -> 9, of which waited for: 4 -> 2; matrix products, arithmetic and copies ran while one was open for 0% -> 0% of each run, Pallas kernels for 38% -> 38%
where the time goes in v9:
time: 111 us; the launch traced here: 110 us
  Pallas kernels  45.5 us (41%)
  waiting for transfers between devices  36 us (32%)
  starting transfers between devices  27.3 us (25%)
    ppermute x5, waiting for transfers between devices, exchange(): return lax.ppermute(values, 'half', ((0, 1), (1, 0)))  26.2 us
    all_to_all x4, starting transfers between devices, shuffle(): lax.all_to_all(shaped, group, split_axis=0, concat_axis=0, tiled=True)  21.3 us
    pallas_call x1, Pallas kernels, body(): call(forward_kernel, [mid, mid, slots], 2 * product, traffic, 32, grid=gr...  13.5 us
    pallas_call x1, Pallas kernels, body(): call(backward_kernel, [mid, slots], 2 * product, traffic, 32, grid=grid,...  12.2 us
    pallas_call x1, Pallas kernels, body(): call(weights_kernel, [pltpu.HBM(weight_in.shape, BF16), pltpu.HBM(weight_...  10.7 us
    all_to_all x4, waiting for transfers between devices, shuffle(): lax.all_to_all(shaped, group, split_axis=0, concat_axis=0, tiled=True)  9.77 us
    ppermute x5, starting transfers between devices, exchange(): return lax.ppermute(values, 'half', ((0, 1), (1, 0)))  5.99 us
    pallas_call x1, Pallas kernels, body(): call(place_cotangents_kernel, slots, 4 * place_flops, 2 * token_bytes + s...  2.94 us
  transfers between devices with their start and end apart: 9, of which 2 were waited for; matrix products, arithmetic and copies ran while one was open for 0% of the time, Pallas kernels for 38%

profile of v9, /device:TPU:0, one launch (start us, length us, event | category | flops | bytes accessed | tf_op | source)
XLA Modules:
  0.0 110.4 jit_solution(4829416765658995833)
XLA Ops:
  0.6 2.4 %shard_map.110 = (f32[8,128]{1,0:T(8,128)S(1)}, f32[8,128]{1,0:T(8,128)S(1)}, bf16[512,768]{1,0:T(8,128)(2,1)}) custom-call(s32[1]{0:T(128)} %bitcast.half_ref, bf16[128,768]{1,0:T(8,128)(2,1)} %tokens_ref.1, s32[2,128]{1,0:T(2,128)} %bitcast.20, s32[2,128]{1,0:T(2,128)} %bitcast.21, f32[2,128]{1,0:T(2,128)} %bitcast.22), custom_call_target="tpu_custom_call" | custom-call | flops 100663296 | bytes 983040 | tf_op jit(solution)/shard_map/pallas_call | solution.py:254
  3.1 7.3 %all-to-all-start.1 = ((bf16[32,16,768]{2,1,0:T(8,128)(2,1)}), bf16[32,16,768]{2,1,0:T(8,128)(2,1)S(1)}, u32[]{:S(2)}, u32[]{:S(2)}) async-start(bf16[32,16,768]{2,1,0:T(8,128)(2,1)} %bitcast.6), calls=%async_computation.1 | async-start | bytes 1572864 | tf_op jit(solution)/shard_map/all_to_all | solution.py:239
  10.4 2.7 %collective-permute-start = (bf16[128,768]{1,0:T(8,128)(2,1)}, bf16[128,768]{1,0:T(8,128)(2,1)S(1)}, u32[]{:S(2)}, u32[]{:S(2)}) collective-permute-start(bf16[128,768]{1,0:T(8,128)(2,1)} %own_grad.3), channel_id=1, source_target_pairs={{0,4},{4,0},{1,5},{5,1},{2,6},{6,2},{3,7},{7,3},{8,12},{12,8},{9,1... | collective-permute-start | bytes 589832 | tf_op jit(solution)/shard_map/ppermute | solution.py:235
  13.1 0.3 collective-permute-start.1
  13.3 26.2 %collective-permute-done.1.partner_meta.meta_ref = f32[8,128]{1,0:T(8,128)S(1)} collective-permute-done((f32[8,128]{1,0:T(8,128)S(1)}, f32[8,128]{1,0:T(8,128)S(1)}, u32[]{:S(2)}, u32[]{:S(2)}) %collective-permute-start.1) | collective-permute-done | bytes 4128 | tf_op jit(solution)/shard_map/ppermute | solution.py:235
  39.6 0.0 collective-permute-done.partner_grad
  39.6 0.0 copy-start
  39.6 2.9 %shard_map.111 = bf16[512,768]{1,0:T(8,128)(2,1)} custom-call(bf16[128,768]{1,0:T(8,128)(2,1)} %own_grad.3, bf16[128,768]{1,0:T(8,128)(2,1)S(1)} %collective-permute-done.partner_grad, f32[8,128]{1,0:T(8,128)S(1)} %get-tuple-element.23.own_meta.meta_ref, f32[8,128]{1,0:T(8,128)S(1)} %collective-permute-done.1.partner_meta.meta_ref), custom_call_target="tpu_custom_call" | custom-call | flops 402653184 | bytes 1179648 | tf_op jit(solution)/shard_map/pallas_call | solution.py:269
  42.5 0.0 all-to-all-done.1
  42.5 0.0 copy-done
  42.5 3.8 %all-to-all-start = ((bf16[16,32,768]{2,1,0:T(8,128)(2,1)}), bf16[16,32,768]{2,1,0:T(8,128)(2,1)S(1)}, u32[]{:S(2)}, u32[]{:S(2)}) async-start(bf16[16,32,768]{2,1,0:T(8,128)(2,1)} %bitcast.4), calls=%async_computation | async-start | bytes 1572864 | tf_op jit(solution)/shard_map/all_to_all | solution.py:239
  46.3 13.5 %shard_map.112 = (bf16[512,4096]{1,0:T(8,128)(2,1)}, bf16[512,4096]{1,0:T(8,128)(2,1)}, bf16[512,768]{1,0:T(8,128)(2,1)}) custom-call(bf16[512,768]{1,0:T(8,128)(2,1)S(1)} %bitcast.15, bf16[1,768,4096]{2,1,0:T(8,128)(2,1)} %w_in_ref.3, bf16[1,4096,768]{2,1,0:T(8,128)(2,1)} %w_out_ref.3), custom_call_target="tpu_custom_call" | custom-call | flops 6442450944 | bytes 22544384 | tf_op jit(solution)/shard_map/pallas_call | solution.py:285
  59.8 0.0 all-to-all-done
  59.8 5.1 %all-to-all-start.3 = ((bf16[16,32,768]{2,1,0:T(8,128)(2,1)}), bf16[16,32,768]{2,1,0:T(8,128)(2,1)S(1)}, u32[]{:S(2)}, u32[]{:S(2)}) async-start(bf16[16,32,768]{2,1,0:T(8,128)(2,1)} %bitcast.10), calls=%async_computation.3 | async-start | bytes 1572864 | tf_op jit(solution)/shard_map/all_to_all | solution.py:239
  64.9 12.2 %shard_map.113 = (bf16[512,4096]{1,0:T(8,128)(2,1)}, bf16[512,768]{1,0:T(8,128)(2,1)}) custom-call(bf16[512,768]{1,0:T(8,128)(2,1)S(1)} %bitcast.17, bf16[1,768,4096]{2,1,0:T(8,128)(2,1)} %w_in_ref.3, bf16[1,4096,768]{2,1,0:T(8,128)(2,1)} %w_out_ref.3, bf16[512,4096]{1,0:T(8,128)(2,1)} %get-tuple-element.26.slope_ref), custom_call_target="tpu_custom_call" | custom-call | flops 6442450944 | bytes 22544384 | tf_op jit(solution)/shard_map/pallas_call | solution.py:297
  77.1 0.0 all-to-all-done.3
  77.1 5.1 %all-to-all-start.2 = ((bf16[16,32,768]{2,1,0:T(8,128)(2,1)}), bf16[16,32,768]{2,1,0:T(8,128)(2,1)S(1)}, u32[]{:S(2)}, u32[]{:S(2)}) async-start(bf16[16,32,768]{2,1,0:T(8,128)(2,1)} %bitcast.8), calls=%async_computation.2 | async-start | bytes 1572864 | tf_op jit(solution)/shard_map/all_to_all | solution.py:239
  82.2 0.0 copy-start.1
  82.3 0.9 copy-done.1
  83.2 2.4 %shard_map.115 = (f32[128,768]{1,0:T(8,128)S(1)}, bf16[128,768]{1,0:T(8,128)(2,1)}, f32[2,128]{1,0:T(2,128)S(1)}, f32[2,128]{1,0:T(2,128)S(1)}) custom-call(bf16[512,768]{1,0:T(8,128)(2,1)S(1)} %bitcast.19, bf16[128,768]{1,0:T(8,128)(2,1)} %own_grad.3, bf16[128,768]{1,0:T(8,128)(2,1)S(1)} %copy-done.1, f32[8,128]{1,0:T(8,128)S(1)} %get-tuple-element.23.own_meta.meta_ref, ...), custom_call_target="tpu_custom_call" | custom-call | flops 402653184 | bytes 1572864 | tf_op jit(solution)/shard_map/pallas_call | solution.py:310
  85.6 1.4 %collective-permute-start.4 = (f32[2,128]{1,0:T(2,128)S(1)}, f32[2,128]{1,0:T(2,128)S(1)}, u32[]{:S(2)}, u32[]{:S(2)}) collective-permute-start(f32[2,128]{1,0:T(2,128)S(1)} %get-tuple-element.32), channel_id=1, source_target_pairs={{0,4},{4,0},{1,5},{5,1},{2,6},{6,2},{3,7},{7,3},{8,12},{12,8},{9,1... | collective-permute-start | bytes 3080 | tf_op jit(solution)/shard_map/ppermute | solution.py:235
  87.0 1.5 %collective-permute-start.3 = (bf16[128,768]{1,0:T(8,128)(2,1)}, bf16[128,768]{1,0:T(8,128)(2,1)S(1)}, u32[]{:S(2)}, u32[]{:S(2)}) collective-permute-start(bf16[128,768]{1,0:T(8,128)(2,1)} %get-tuple-element.30), channel_id=1, source_target_pairs={{0,4},{4,0},{1,5},{5,1},{2,6},{6,2},{3,7},{7,3},{8,12},{12,8},{9,1... | collective-permute-start | bytes 589832 | tf_op jit(solution)/shard_map/ppermute | solution.py:235
  88.5 9.8 %all-to-all-done.2 = bf16[16,32,768]{2,1,0:T(8,128)(2,1)S(1)} async-done(((bf16[16,32,768]{2,1,0:T(8,128)(2,1)}), bf16[16,32,768]{2,1,0:T(8,128)(2,1)S(1)}, u32[]{:S(2)}, u32[]{:S(2)}) %all-to-all-start.2) | async-done | bytes 786464 | tf_op jit(solution)/shard_map/all_to_all | solution.py:239
  98.2 0.3 shard_map.114
  98.6 0.1 collective-permute-start.2
  98.6 10.7 %shard_map.117 = (bf16[1,768,4096]{2,1,0:T(8,128)(2,1)}, bf16[1,4096,768]{2,1,0:T(8,128)(2,1)}) custom-call(bf16[512,768]{1,0:T(8,128)(2,1)S(1)} %bitcast.16, bf16[512,768]{1,0:T(8,128)(2,1)S(1)} %bitcast.18, bf16[512,4096]{1,0:T(8,128)(2,1)} %get-tuple-element.36.hidden_ref, bf16[512,4096]{1,0:T(8,128)(2,1)} %get-tuple-element.38.grad_pre_ref), custom_call_target="tpu_custom_call" | custom-call | flops 6442450944 | bytes 22544384 | tf_op jit(solution)/shard_map/pallas_call | solution.py:322
  109.3 0.0 collective-permute-done.4.got_gates
  109.4 0.0 collective-permute-done.3.got_out
  109.4 0.0 collective-permute-done.2.got_back
  109.4 1.1 shard_map.116
Async XLA Ops:
  3.1 39.5 %all-to-all-start.1 = ((bf16[32,16,768]{2,1,0:T(8,128)(2,1)}), bf16[32,16,768]{2,1,0:T(8,128)(2,1)S(1)}, u32[]{:S(2)}, u32[]{:S(2)}) async-start(bf16[32,16,768]{2,1,0:T(8,128)(2,1)} %bitcast.6), calls=%async_computation.1 | async-start | bytes 1572864 | tf_op jit(solution)/shard_map/all_to_all | solution.py:239
  10.4 29.2 %collective-permute-start = (bf16[128,768]{1,0:T(8,128)(2,1)}, bf16[128,768]{1,0:T(8,128)(2,1)S(1)}, u32[]{:S(2)}, u32[]{:S(2)}) collective-permute-start(bf16[128,768]{1,0:T(8,128)(2,1)} %own_grad.3), channel_id=1, source_target_pairs={{0,4},{4,0},{1,5},{5,1},{2,6},{6,2},{3,7},{7,3},{8,12},{12,8},{9,1... | collective-permute-start | bytes 589832 | tf_op jit(solution)/shard_map/ppermute | solution.py:235
  13.1 26.5 %collective-permute-start.1 = (f32[8,128]{1,0:T(8,128)S(1)}, f32[8,128]{1,0:T(8,128)S(1)}, u32[]{:S(2)}, u32[]{:S(2)}) collective-permute-start(f32[8,128]{1,0:T(8,128)S(1)} %get-tuple-element.24), channel_id=1, source_target_pairs={{0,4},{4,0},{1,5},{5,1},{2,6},{6,2},{3,7},{7,3},{8,12},{12,8},{9,1... | collective-permute-start | bytes 12296 | tf_op jit(solution)/shard_map/ppermute | solution.py:235
  39.6 3.0 %copy-start = (bf16[128,768]{1,0:T(8,128)(2,1)}, bf16[128,768]{1,0:T(8,128)(2,1)S(1)}, u32[]{:S(2)}) copy-start(bf16[128,768]{1,0:T(8,128)(2,1)S(1)} %collective-permute-done.partner_grad) | copy-start | bytes 589828
  42.5 17.2 %all-to-all-start = ((bf16[16,32,768]{2,1,0:T(8,128)(2,1)}), bf16[16,32,768]{2,1,0:T(8,128)(2,1)S(1)}, u32[]{:S(2)}, u32[]{:S(2)}) async-start(bf16[16,32,768]{2,1,0:T(8,128)(2,1)} %bitcast.4), calls=%async_computation | async-start | bytes 1572864 | tf_op jit(solution)/shard_map/all_to_all | solution.py:239
  59.8 17.3 %all-to-all-start.3 = ((bf16[16,32,768]{2,1,0:T(8,128)(2,1)}), bf16[16,32,768]{2,1,0:T(8,128)(2,1)S(1)}, u32[]{:S(2)}, u32[]{:S(2)}) async-start(bf16[16,32,768]{2,1,0:T(8,128)(2,1)} %bitcast.10), calls=%async_computation.3 | async-start | bytes 1572864 | tf_op jit(solution)/shard_map/all_to_all | solution.py:239
  77.1 21.1 %all-to-all-start.2 = ((bf16[16,32,768]{2,1,0:T(8,128)(2,1)}), bf16[16,32,768]{2,1,0:T(8,128)(2,1)S(1)}, u32[]{:S(2)}, u32[]{:S(2)}) async-start(bf16[16,32,768]{2,1,0:T(8,128)(2,1)} %bitcast.8), calls=%async_computation.2 | async-start | bytes 1572864 | tf_op jit(solution)/shard_map/all_to_all | solution.py:239
  82.2 0.9 copy-start.1
  85.6 23.8 %collective-permute-start.4 = (f32[2,128]{1,0:T(2,128)S(1)}, f32[2,128]{1,0:T(2,128)S(1)}, u32[]{:S(2)}, u32[]{:S(2)}) collective-permute-start(f32[2,128]{1,0:T(2,128)S(1)} %get-tuple-element.32), channel_id=1, source_target_pairs={{0,4},{4,0},{1,5},{5,1},{2,6},{6,2},{3,7},{7,3},{8,12},{12,8},{9,1... | collective-permute-start | bytes 3080 | tf_op jit(solution)/shard_map/ppermute | solution.py:235
  87.0 22.4 %collective-permute-start.3 = (bf16[128,768]{1,0:T(8,128)(2,1)}, bf16[128,768]{1,0:T(8,128)(2,1)S(1)}, u32[]{:S(2)}, u32[]{:S(2)}) collective-permute-start(bf16[128,768]{1,0:T(8,128)(2,1)} %get-tuple-element.30), channel_id=1, source_target_pairs={{0,4},{4,0},{1,5},{5,1},{2,6},{6,2},{3,7},{7,3},{8,12},{12,8},{9,1... | collective-permute-start | bytes 589832 | tf_op jit(solution)/shard_map/ppermute | solution.py:235
  98.6 10.8 %collective-permute-start.2 = (bf16[128,768]{1,0:T(8,128)(2,1)S(1)}, bf16[128,768]{1,0:T(8,128)(2,1)S(1)}, u32[]{:S(2)}, u32[]{:S(2)}) collective-permute-start(bf16[128,768]{1,0:T(8,128)(2,1)S(1)} %shard_map.114), channel_id=1, source_target_pairs={{0,4},{4,0},{1,5},{5,1},{2,6},{6,2},{3,7},{7,3},{8,12},{12,8},{9,1... | collective-permute-start | bytes 589832 | tf_op jit(solution)/shard_map/ppermute | solution.py:235

commit v10 on v9

--- a/solution.py
+++ b/solution.py
@@ -94,10 +94,14 @@
     return jnp.concatenate(pieces, axis=1)
 
 
-def place_cotangents_kernel(own_grad, partner_grad, own_meta, partner_meta, out_ref):
+def place_cotangents_kernel(half_ref, both_grads, own_meta, partner_meta, out_ref):
     slot_total = out_ref.shape[0]
+    half = half_ref[0]
     total = None
-    for grad_ref, meta_ref in ((own_grad, own_meta), (partner_grad, partner_meta)):
+    for grad_ref, meta_ref in (
+        (both_grads.at[half], own_meta),
+        (both_grads.at[1 - half], partner_meta),
+    ):
         for k in range(2):
             rows = scaled_rows(meta_ref[k + 2 : k + 3, :], grad_ref).astype(BF16)
             part = dot(one_hot(hits(slot_total, meta_ref, k)), rows, 1, 0)
@@ -167,12 +171,13 @@
 
 
 def pick_outputs_kernel(
-    back_ref, own_grad, partner_grad, own_meta, partner_meta, own_out, partner_out, own_gates, partner_gates
+    half_ref, back_ref, both_grads, own_meta, partner_meta, own_out, partner_out, own_gates, partner_gates
 ):
     slot_total = back_ref.shape[0]
+    half = half_ref[0]
     for grad_ref, meta_ref, out_ref, gates_ref in (
-        (own_grad, own_meta, own_out, own_gates),
-        (partner_grad, partner_meta, partner_out, partner_gates),
+        (both_grads.at[half], own_meta, own_out, own_gates),
+        (both_grads.at[1 - half], partner_meta, partner_out, partner_gates),
     ):
         total = None
         for k in range(2):
@@ -192,21 +197,15 @@
         out_ref[...] = total.astype(out_ref.dtype)
 
 
-def pick_partner_kernel(back_ref, meta_ref, out_ref):
-    slot_total = back_ref.shape[0]
-    mask = hits(slot_total, meta_ref, 0) | hits(slot_total, meta_ref, 1)
-    out_ref[...] = dot(one_hot(mask), back_ref[...], 0, 0).astype(BF16)
-
-
-def finish_kernel(
-    back_ref, meta_ref, got_back, own_out, got_out, own_gates, got_gates, combined, grad_tokens, grad_gates
-):
-    slot_total = back_ref.shape[0]
-    mask = hits(slot_total, meta_ref, 0) | hits(slot_total, meta_ref, 1)
-    own = dot(one_hot(mask), back_ref[...], 0, 0)
-    grad_tokens[...] = (own + got_back[...].astype(F32)).astype(BF16)
+def finish_outputs_kernel(own_out, got_out, own_gates, got_gates, combined, grad_gates):
     combined[...] = (own_out[...] + got_out[...].astype(F32)).astype(BF16)
     grad_gates[...] = own_gates[...] + got_gates[...]
+
+
+def pick_gradients_kernel(back_ref, meta_ref, out_ref):
+    slot_total = back_ref.shape[0]
+    mask = hits(slot_total, meta_ref, 4) | hits(slot_total, meta_ref, 5)
+    out_ref[...] = dot(one_hot(mask), back_ref[...], 0, 0).astype(BF16)
 
 
 def call(kernel, outs, flops=0, traffic=0, limit=12, **options):
@@ -249,7 +248,7 @@
     slot_bytes, token_bytes = slot_total * width * 2, token_rows * width * 2
     place_flops = 2 * slot_total * token_rows * width
 
-    partner_grad = exchange(grad_output)
+    both_grads = lax.all_gather(grad_output, "half")
     half = lax.axis_index("half").astype(jnp.int32).reshape(1)
     own_meta, sent_meta, sent = call(
         functools.partial(place_tokens_kernel, rest_count.bit_length() - 1, capacity),
@@ -266,9 +265,14 @@
     )
     x = shuffle(sent, ALL, 2 * members)
     partner_meta = exchange(sent_meta)
+    smem = pl.BlockSpec(memory_space=pltpu.SMEM)
     sent_cot = call(
-        place_cotangents_kernel, slots, 4 * place_flops, 2 * token_bytes + slot_bytes
-    )(in_hbm(grad_output), partner_grad, own_meta, partner_meta)
+        place_cotangents_kernel,
+        slots,
+        4 * place_flops,
+        2 * token_bytes + slot_bytes,
+        in_specs=[smem] + [vmem] * 3,
+    )(half, both_grads, own_meta, partner_meta)
     cot = shuffle(sent_cot, GROUP, members)
 
     chunk = 1024
@@ -289,7 +293,7 @@
         traffic,
         32,
         grid=grid,
-        in_specs=[whole, in_spec, out_spec],
+        in_specs=[vmem, in_spec, out_spec],
         out_specs=[mid_spec, mid_spec, whole],
         scratch_shapes=[total],
     )(x, weight_in, weight_out)
@@ -301,24 +305,21 @@
         traffic,
         32,
         grid=grid,
-        in_specs=[whole, in_spec, out_spec, mid_spec],
+        in_specs=[vmem, in_spec, out_spec, mid_spec],
         out_specs=[mid_spec, whole],
         scratch_shapes=[total],
     )(cot, weight_in, weight_out, in_hbm(slope))
-    back_grad = shuffle(grad_rows, GROUP, members)
+    back_grad = shuffle(grad_rows, ALL, 2 * members)
     tokens_f32, gates_shape = shape(token_rows, width, dtype=F32), shape(2, token_rows, dtype=F32)
     own_out, partner_out, own_gates, partner_gates = call(
         pick_outputs_kernel,
         [tokens_f32, token_shape, gates_shape, gates_shape],
         4 * place_flops,
         4 * token_bytes + slot_bytes,
-    )(back_out, in_hbm(grad_output), partner_grad, own_meta, partner_meta)
+        in_specs=[smem] + [vmem] * 4,
+    )(half, back_out, both_grads, own_meta, partner_meta)
+    grad_pre, partner_out = lax.optimization_barrier((grad_pre, partner_out))
     got_out, got_gates = exchange(partner_out), exchange(partner_gates)
-    partner_back = call(
-        pick_partner_kernel, token_shape, place_flops, slot_bytes + token_bytes
-    )(back_grad, partner_meta)
-    got_back = exchange(partner_back)
-    grad_pre, partner_back = lax.optimization_barrier((grad_pre, partner_back))
     grad_in_w, grad_out_w = call(
         weights_kernel,
         [pltpu.HBM(weight_in.shape, BF16), pltpu.HBM(weight_out.shape, BF16)],
@@ -326,15 +327,15 @@
         traffic,
         32,
         grid=grid,
-        in_specs=[whole, whole, mid_spec, mid_spec],
+        in_specs=[vmem, vmem, mid_spec, mid_spec],
         out_specs=[in_spec, out_spec],
     )(x, cot, in_hbm(hidden), in_hbm(grad_pre))
-    combined, grad_tokens, grad_gates = call(
-        finish_kernel,
-        [token_shape, token_shape, gates_shape],
-        place_flops,
-        slot_bytes + 6 * token_bytes,
-    )(back_grad, own_meta, got_back, own_out, got_out, own_gates, got_gates)
+    combined, grad_gates = call(
+        finish_outputs_kernel, [token_shape, gates_shape], 0, 6 * token_bytes
+    )(own_out, got_out, own_gates, got_gates)
+    grad_tokens = call(
+        pick_gradients_kernel, token_shape, place_flops, slot_bytes + token_bytes
+    )(back_grad, own_meta)
     return (combined, grad_tokens, grad_gates.T, grad_in_w, grad_out_w)
 
 

time: 111 us -> 111 us (level)
  blocking collectives: 0 us -> 26.5 us
  waiting for transfers between devices: 36 us -> 12.2 us
  Pallas kernels: 45.5 us -> 44 us
    all_gather x0 -> x1, blocking collectives: none -> 26.5 us  [body(): both_grads = lax.all_gather(grad_output, 'half')]
    ppermute x5 -> x3, waiting for transfers between devices: 26.2 us -> 2 us  [exchange(): return lax.ppermute(values, 'half', ((0, 1), (1, 0)))]
    ppermute x5 -> x3, starting transfers between devices: 5.99 us -> 5.66 us  [exchange(): return lax.ppermute(values, 'half', ((0, 1), (1, 0)))]
  transfers between devices with their start and end apart: 9 -> 7, of which waited for: 2 -> 2; matrix products, arithmetic and copies ran while one was open for 0% -> 0% of each run, Pallas kernels for 38% -> 37%
where the time goes in v10:
time: 111 us
  Pallas kernels  44 us (40%)
  starting transfers between devices  26.8 us (24%)
  blocking collectives  26.5 us (24%)
  waiting for transfers between devices  12.2 us (11%)
    all_gather x1, blocking collectives, body(): both_grads = lax.all_gather(grad_output, 'half')  26.5 us
    all_to_all x4, starting transfers between devices, shuffle(): lax.all_to_all(shaped, group, split_axis=0, concat_axis=0, tiled=True)  21.1 us
    pallas_call x1, Pallas kernels, body(): call(forward_kernel, [mid, mid, slots], 2 * product, traffic, 32, grid=gr...  13.4 us
    pallas_call x1, Pallas kernels, body(): call(backward_kernel, [mid, slots], 2 * product, traffic, 32, grid=grid,...  12.3 us
    pallas_call x1, Pallas kernels, body(): call(weights_kernel, [pltpu.HBM(weight_in.shape, BF16), pltpu.HBM(weight_...  10.8 us
    all_to_all x4, waiting for transfers between devices, shuffle(): lax.all_to_all(shaped, group, split_axis=0, concat_axis=0, tiled=True)  10.2 us
    ppermute x3, starting transfers between devices, exchange(): return lax.ppermute(values, 'half', ((0, 1), (1, 0)))  5.66 us
    pallas_call x1, Pallas kernels, body(): call(functools.partial(place_tokens_kernel, rest_count.bit_length() - 1,...  2.42 us
  transfers between devices with their start and end apart: 7, of which 2 were waited for; matrix products, arithmetic and copies ran while one was open for 0% of the time, Pallas kernels for 37%

profile of v10, /device:TPU:0, one launch (start us, length us, event | category | flops | bytes accessed | tf_op | source)
XLA Modules:
  0.0 110.9 jit_solution(14374902990665778945)
XLA Ops:
  0.6 2.4 %shard_map.110 = (f32[8,128]{1,0:T(8,128)S(1)}, f32[8,128]{1,0:T(8,128)S(1)}, bf16[512,768]{1,0:T(8,128)(2,1)}) custom-call(s32[1]{0:T(128)} %bitcast.half_ref, bf16[128,768]{1,0:T(8,128)(2,1)} %tokens_ref.1, s32[2,128]{1,0:T(2,128)} %bitcast.22, s32[2,128]{1,0:T(2,128)} %bitcast.23, f32[2,128]{1,0:T(2,128)} %bitcast.24), custom_call_target="tpu_custom_call" | custom-call | flops 100663296 | bytes 983040 | tf_op jit(solution)/shard_map/pallas_call | solution.py:253
  3.1 7.3 %all-to-all-start = ((bf16[32,16,768]{2,1,0:T(8,128)(2,1)}), bf16[32,16,768]{2,1,0:T(8,128)(2,1)S(1)}, u32[]{:S(2)}, u32[]{:S(2)}) async-start(bf16[32,16,768]{2,1,0:T(8,128)(2,1)} %bitcast.4), calls=%async_computation | async-start | bytes 1572864 | tf_op jit(solution)/shard_map/all_to_all | solution.py:238
  10.4 2.7 %collective-permute-start = (f32[8,128]{1,0:T(8,128)S(1)}, f32[8,128]{1,0:T(8,128)S(1)}, u32[]{:S(2)}, u32[]{:S(2)}) collective-permute-start(f32[8,128]{1,0:T(8,128)S(1)} %get-tuple-element.26), channel_id=1, source_target_pairs={{0,4},{4,0},{1,5},{5,1},{2,6},{6,2},{3,7},{7,3},{8,12},{12,8},{9,1... | collective-permute-start | bytes 12296 | tf_op jit(solution)/shard_map/ppermute | solution.py:234
  13.1 26.5 %all-gather = bf16[256,768]{1,0:T(8,128)(2,1)S(1)} all-gather(bf16[128,768]{1,0:T(8,128)(2,1)} %param.13), channel_id=2, replica_groups=mesh['row'=4,'half'=2,'rest'=4] {'half'}, dimensions={0}, use_global_device_ids=true | all-gather | bytes 589824 | tf_op jit(solution)/shard_map/all_gather | solution.py:251
  39.6 0.0 collective-permute-done.partner_meta
  39.6 2.0 %shard_map.113 = bf16[512,768]{1,0:T(8,128)(2,1)} custom-call(s32[1]{0:T(128)} %bitcast.half_ref, bf16[2,128,768]{2,1,0:T(8,128)(2,1)S(1)} %bitcast.20, f32[8,128]{1,0:T(8,128)S(1)} %get-tuple-element.25.own_meta.meta_ref, f32[8,128]{1,0:T(8,128)S(1)} %collective-permute-done.partner_meta), custom_call_target="tpu_custom_call" | custom-call | flops 402653184 | bytes 1179648 | tf_op jit(solution)/shard_map/pallas_call | solution.py:269
  41.6 0.0 all-to-all-done
  41.6 3.8 %all-to-all-start.2 = ((bf16[16,32,768]{2,1,0:T(8,128)(2,1)}), bf16[16,32,768]{2,1,0:T(8,128)(2,1)S(1)}, u32[]{:S(2)}, u32[]{:S(2)}) async-start(bf16[16,32,768]{2,1,0:T(8,128)(2,1)} %bitcast.9), calls=%async_computation.2 | async-start | bytes 1572864 | tf_op jit(solution)/shard_map/all_to_all | solution.py:238
  45.3 13.4 %shard_map.111 = (bf16[512,4096]{1,0:T(8,128)(2,1)}, bf16[512,4096]{1,0:T(8,128)(2,1)}, bf16[512,768]{1,0:T(8,128)(2,1)}) custom-call(bf16[512,768]{1,0:T(8,128)(2,1)S(1)} %bitcast.15, bf16[1,768,4096]{2,1,0:T(8,128)(2,1)} %w_in_ref.3, bf16[1,4096,768]{2,1,0:T(8,128)(2,1)} %w_out_ref.3), custom_call_target="tpu_custom_call" | custom-call | flops 6442450944 | bytes 22544384 | tf_op jit(solution)/shard_map/pallas_call | solution.py:289
  58.7 0.0 all-to-all-done.2
  58.7 5.1 %all-to-all-start.1 = ((bf16[16,32,768]{2,1,0:T(8,128)(2,1)}), bf16[16,32,768]{2,1,0:T(8,128)(2,1)S(1)}, u32[]{:S(2)}, u32[]{:S(2)}) async-start(bf16[16,32,768]{2,1,0:T(8,128)(2,1)} %bitcast.6), calls=%async_computation.1 | async-start | bytes 1572864 | tf_op jit(solution)/shard_map/all_to_all | solution.py:238
  63.8 12.3 %shard_map.114 = (bf16[512,4096]{1,0:T(8,128)(2,1)}, bf16[512,768]{1,0:T(8,128)(2,1)}) custom-call(bf16[512,768]{1,0:T(8,128)(2,1)S(1)} %bitcast.17, bf16[1,768,4096]{2,1,0:T(8,128)(2,1)} %w_in_ref.3, bf16[1,4096,768]{2,1,0:T(8,128)(2,1)} %w_out_ref.3, bf16[512,4096]{1,0:T(8,128)(2,1)} %get-tuple-element.28.slope_ref), custom_call_target="tpu_custom_call" | custom-call | flops 6442450944 | bytes 22544384 | tf_op jit(solution)/shard_map/pallas_call | solution.py:301
  76.1 0.0 all-to-all-done.1
  76.1 5.0 %all-to-all-start.3 = ((bf16[32,16,768]{2,1,0:T(8,128)(2,1)}), bf16[32,16,768]{2,1,0:T(8,128)(2,1)S(1)}, u32[]{:S(2)}, u32[]{:S(2)}) async-start(bf16[32,16,768]{2,1,0:T(8,128)(2,1)} %bitcast.11), calls=%async_computation.3 | async-start | bytes 1572864 | tf_op jit(solution)/shard_map/all_to_all | solution.py:238
  81.1 1.4 %shard_map.112 = (f32[128,768]{1,0:T(8,128)S(1)}, bf16[128,768]{1,0:T(8,128)(2,1)}, f32[2,128]{1,0:T(2,128)S(1)}, f32[2,128]{1,0:T(2,128)S(1)}) custom-call(s32[1]{0:T(128)} %bitcast.half_ref, bf16[512,768]{1,0:T(8,128)(2,1)S(1)} %bitcast.19, bf16[2,128,768]{2,1,0:T(8,128)(2,1)S(1)} %bitcast.21, f32[8,128]{1,0:T(8,128)S(1)} %get-tuple-element.25.own_meta.meta_ref, ...), custom_call_target="tpu_custom_call" | custom-call | flops 402653184 | bytes 1572864 | tf_op jit(solution)/shard_map/pallas_call | solution.py:314
  82.6 0.0 copy-start
  82.6 0.7 copy-done
  83.3 2.7 %collective-permute-start.2 = (f32[2,128]{1,0:T(2,128)S(1)}, f32[2,128]{1,0:T(2,128)S(1)}, u32[]{:S(2)}, u32[]{:S(2)}) collective-permute-start(f32[2,128]{1,0:T(2,128)S(1)} %get-tuple-element.33), channel_id=1, source_target_pairs={{0,4},{4,0},{1,5},{5,1},{2,6},{6,2},{3,7},{7,3},{8,12},{12,8},{9,1... | collective-permute-start | bytes 3080 | tf_op jit(solution)/shard_map/ppermute | solution.py:234
  86.0 0.3 collective-permute-start.1
  86.2 0.0 copy-start.1
  86.2 10.8 %shard_map.117 = (bf16[1,768,4096]{2,1,0:T(8,128)(2,1)}, bf16[1,4096,768]{2,1,0:T(8,128)(2,1)}) custom-call(bf16[512,768]{1,0:T(8,128)(2,1)S(1)} %bitcast.16, bf16[512,768]{1,0:T(8,128)(2,1)S(1)} %bitcast.18, bf16[512,4096]{1,0:T(8,128)(2,1)} %get-tuple-element.37.hidden_ref, bf16[512,4096]{1,0:T(8,128)(2,1)} %get-tuple-element.38.grad_pre_ref), custom_call_target="tpu_custom_call" | custom-call | flops 6442450944 | bytes 22544384 | tf_op jit(solution)/shard_map/pallas_call | solution.py:323
  97.0 10.2 %all-to-all-done.3 = bf16[32,16,768]{2,1,0:T(8,128)(2,1)S(1)} async-done(((bf16[32,16,768]{2,1,0:T(8,128)(2,1)}), bf16[32,16,768]{2,1,0:T(8,128)(2,1)S(1)}, u32[]{:S(2)}, u32[]{:S(2)}) %all-to-all-start.3) | async-done | bytes 786464 | tf_op jit(solution)/shard_map/all_to_all | solution.py:238
  107.2 1.0 shard_map.116
  108.2 0.0 collective-permute-done.2.got_gates
  108.2 2.0 %collective-permute-done.1.got_out = bf16[128,768]{1,0:T(8,128)(2,1)S(1)} collective-permute-done((bf16[128,768]{1,0:T(8,128)(2,1)}, bf16[128,768]{1,0:T(8,128)(2,1)S(1)}, u32[]{:S(2)}, u32[]{:S(2)}) %collective-permute-start.1) | collective-permute-done | bytes 196640 | tf_op jit(solution)/shard_map/ppermute | solution.py:234
  110.2 0.0 copy-done.1
  110.2 0.7 shard_map.115
Async XLA Ops:
  3.1 38.5 %all-to-all-start = ((bf16[32,16,768]{2,1,0:T(8,128)(2,1)}), bf16[32,16,768]{2,1,0:T(8,128)(2,1)S(1)}, u32[]{:S(2)}, u32[]{:S(2)}) async-start(bf16[32,16,768]{2,1,0:T(8,128)(2,1)} %bitcast.4), calls=%async_computation | async-start | bytes 1572864 | tf_op jit(solution)/shard_map/all_to_all | solution.py:238
  10.4 29.2 %collective-permute-start = (f32[8,128]{1,0:T(8,128)S(1)}, f32[8,128]{1,0:T(8,128)S(1)}, u32[]{:S(2)}, u32[]{:S(2)}) collective-permute-start(f32[8,128]{1,0:T(8,128)S(1)} %get-tuple-element.26), channel_id=1, source_target_pairs={{0,4},{4,0},{1,5},{5,1},{2,6},{6,2},{3,7},{7,3},{8,12},{12,8},{9,1... | collective-permute-start | bytes 12296 | tf_op jit(solution)/shard_map/ppermute | solution.py:234
  41.6 17.2 %all-to-all-start.2 = ((bf16[16,32,768]{2,1,0:T(8,128)(2,1)}), bf16[16,32,768]{2,1,0:T(8,128)(2,1)S(1)}, u32[]{:S(2)}, u32[]{:S(2)}) async-start(bf16[16,32,768]{2,1,0:T(8,128)(2,1)} %bitcast.9), calls=%async_computation.2 | async-start | bytes 1572864 | tf_op jit(solution)/shard_map/all_to_all | solution.py:238
  58.7 17.4 %all-to-all-start.1 = ((bf16[16,32,768]{2,1,0:T(8,128)(2,1)}), bf16[16,32,768]{2,1,0:T(8,128)(2,1)S(1)}, u32[]{:S(2)}, u32[]{:S(2)}) async-start(bf16[16,32,768]{2,1,0:T(8,128)(2,1)} %bitcast.6), calls=%async_computation.1 | async-start | bytes 1572864 | tf_op jit(solution)/shard_map/all_to_all | solution.py:238
  76.1 31.1 %all-to-all-start.3 = ((bf16[32,16,768]{2,1,0:T(8,128)(2,1)}), bf16[32,16,768]{2,1,0:T(8,128)(2,1)S(1)}, u32[]{:S(2)}, u32[]{:S(2)}) async-start(bf16[32,16,768]{2,1,0:T(8,128)(2,1)} %bitcast.11), calls=%async_computation.3 | async-start | bytes 1572864 | tf_op jit(solution)/shard_map/all_to_all | solution.py:238
  82.6 0.7 copy-start
  83.3 24.9 %collective-permute-start.2 = (f32[2,128]{1,0:T(2,128)S(1)}, f32[2,128]{1,0:T(2,128)S(1)}, u32[]{:S(2)}, u32[]{:S(2)}) collective-permute-start(f32[2,128]{1,0:T(2,128)S(1)} %get-tuple-element.33), channel_id=1, source_target_pairs={{0,4},{4,0},{1,5},{5,1},{2,6},{6,2},{3,7},{7,3},{8,12},{12,8},{9,1... | collective-permute-start | bytes 3080 | tf_op jit(solution)/shard_map/ppermute | solution.py:234
  86.0 24.2 %collective-permute-start.1 = (bf16[128,768]{1,0:T(8,128)(2,1)}, bf16[128,768]{1,0:T(8,128)(2,1)S(1)}, u32[]{:S(2)}, u32[]{:S(2)}) collective-permute-start(bf16[128,768]{1,0:T(8,128)(2,1)} %get-tuple-element.31), channel_id=1, source_target_pairs={{0,4},{4,0},{1,5},{5,1},{2,6},{6,2},{3,7},{7,3},{8,12},{12,8},{9,1... | collective-permute-start | bytes 589832 | tf_op jit(solution)/shard_map/ppermute | solution.py:234
  86.2 24.0 %copy-start.1 = (f32[128,768]{1,0:T(8,128)S(1)}, f32[128,768]{1,0:T(8,128)}, u32[]{:S(2)}) copy-start(f32[128,768]{1,0:T(8,128)} %copy-done) | copy-start | bytes 1179652

commit v11 on v7

--- a/solution.py
+++ b/solution.py
@@ -13,8 +13,8 @@
 F32 = jnp.float32
 MIB = 1024 * 1024
 SUB = 256
-AXES = ("row", "outer", "inner")
-GROUP = ("row", "inner", "outer")
+AXES = ("row", "high", "low", "inner")
+GROUP = ("inner", "row", "low", "high")
 
 
 def dot(a, b, contract_a, contract_b):
@@ -200,15 +200,16 @@
 def body(tokens, expert_ids, keep_mask, gate_weights, weight_in, weight_out, grad_output):
     token_rows, width = tokens.shape
     hidden_width = weight_in.shape[2]
-    row_count, outer = lax.axis_size("row"), lax.axis_size("outer")
-    experts = row_count * outer * lax.axis_size("inner")
-    bits = outer.bit_length() - 1
+    row_count, low = lax.axis_size("row"), lax.axis_size("low")
+    experts = row_count * low * 4
+    bits = low.bit_length() - 1
 
     def place_of(expert):
         inner_at = expert & 1
-        outer_at = (expert >> 1) & (outer - 1)
-        row_at = expert >> (bits + 1)
-        return ((row_at * 2 + inner_at) << bits) + outer_at
+        low_at = (expert >> 1) & (low - 1)
+        high_at = (expert >> (bits + 1)) & 1
+        row_at = expert >> (bits + 2)
+        return ((((inner_at * row_count + row_at) << bits) + low_at) << 1) + high_at
 
     capacity = 2 * expert_ids.shape[1] * token_rows // experts
     slot_total = experts * capacity
@@ -300,7 +301,7 @@
 
 def solution(mesh):
     rows, cols = mesh.devices.shape
-    split = Mesh(mesh.devices.reshape(rows, cols // 2, 2), AXES)
+    split = Mesh(mesh.devices.reshape(rows, 2, cols // 4, 2), AXES)
     flat, deep = P(AXES, None), P(AXES, None, None)
     return jax.shard_map(
         body,

time: 105 us -> 108 us (1.029)
  waiting for transfers between devices: 43.4 us -> 46.3 us
    all_to_all x4, waiting for transfers between devices: 43.4 us -> 46.3 us  [shuffle(): lax.all_to_all(shaped, GROUP, split_axis=0, concat_axis=0, tiled=True)]
  transfers between devices with their start and end apart: 4 -> 4, of which waited for: 4 -> 4; matrix products, arithmetic and copies ran while one was open for 0% -> 0% of each run, Pallas kernels for 39% -> 38%
where the time goes in v11:
time: 108 us; the launch traced here: 107 us
  waiting for transfers between devices  46.3 us (43%)
  Pallas kernels  44.1 us (41%)
  starting transfers between devices  15.2 us (14%)
    all_to_all x4, waiting for transfers between devices, shuffle(): lax.all_to_all(shaped, GROUP, split_axis=0, concat_axis=0, tiled=True)  46.3 us
    all_to_all x4, starting transfers between devices, shuffle(): lax.all_to_all(shaped, GROUP, split_axis=0, concat_axis=0, tiled=True)  15.2 us
    pallas_call x1, Pallas kernels, body(): call(forward_kernel, [mid, mid, slots], 2 * product, traffic, 32, grid=gr...  13.4 us
    pallas_call x1, Pallas kernels, body(): call(backward_kernel, [mid, slots], 2 * product, traffic, 32, grid=grid,...  12 us
    pallas_call x1, Pallas kernels, body(): call(weights_kernel, [pltpu.HBM(weight_in.shape, BF16), pltpu.HBM(weight_...  10.7 us
    pallas_call x1, Pallas kernels, body(): call(place_cotangents_kernel, slots, 2 * place_flops, token_bytes + slot_...  2.46 us
    pallas_call x1, Pallas kernels, body(): call(functools.partial(place_tokens_kernel, capacity, place_of), [jax.Sha...  2.42 us
  transfers between devices with their start and end apart: 4, of which 4 were waited for; matrix products, arithmetic and copies ran while one was open for 0% of the time, Pallas kernels for 38%

profile of v11, /device:TPU:0, one launch (start us, length us, event | category | flops | bytes accessed | tf_op | source)
XLA Modules:
  0.0 107.1 jit_solution(8219836398415566142)
XLA Ops:
  0.6 2.4 %shard_map.110 = (f32[8,128]{1,0:T(8,128)S(1)}, bf16[512,768]{1,0:T(8,128)(2,1)}) custom-call(bf16[128,768]{1,0:T(8,128)(2,1)} %tokens_ref.1, s32[2,128]{1,0:T(2,128)} %bitcast.19, s32[2,128]{1,0:T(2,128)} %bitcast.20, f32[2,128]{1,0:T(2,128)} %bitcast.21), custom_call_target="tpu_custom_call" | custom-call | flops 100663296 | bytes 983040 | tf_op jit(solution)/shard_map/pallas_call | solution.py:227
  3.0 7.3 %all-to-all-start = ((bf16[32,16,768]{2,1,0:T(8,128)(2,1)}), bf16[32,16,768]{2,1,0:T(8,128)(2,1)S(1)}, u32[]{:S(2)}, u32[]{:S(2)}) async-start(bf16[32,16,768]{2,1,0:T(8,128)(2,1)} %bitcast.3), calls=%async_computation | async-start | bytes 1572864 | tf_op jit(solution)/shard_map/all_to_all | solution.py:219
  10.4 2.5 %shard_map.113 = bf16[512,768]{1,0:T(8,128)(2,1)} custom-call(bf16[128,768]{1,0:T(8,128)(2,1)} %grad_ref.3, f32[8,128]{1,0:T(8,128)S(1)} %get-tuple-element.18.meta_ref), custom_call_target="tpu_custom_call" | custom-call | flops 201326592 | bytes 983040 | tf_op jit(solution)/shard_map/pallas_call | solution.py:234
  12.8 19.5 %all-to-all-done = bf16[32,16,768]{2,1,0:T(8,128)(2,1)S(1)} async-done(((bf16[32,16,768]{2,1,0:T(8,128)(2,1)}), bf16[32,16,768]{2,1,0:T(8,128)(2,1)S(1)}, u32[]{:S(2)}, u32[]{:S(2)}) %all-to-all-start) | async-done | bytes 786464 | tf_op jit(solution)/shard_map/all_to_all | solution.py:219
  32.3 2.6 %all-to-all-start.2 = ((bf16[32,16,768]{2,1,0:T(8,128)(2,1)}), bf16[32,16,768]{2,1,0:T(8,128)(2,1)S(1)}, u32[]{:S(2)}, u32[]{:S(2)}) async-start(bf16[32,16,768]{2,1,0:T(8,128)(2,1)} %bitcast.7), calls=%async_computation.2 | async-start | bytes 1572864 | tf_op jit(solution)/shard_map/all_to_all | solution.py:219
  35.0 13.4 %shard_map.111 = (bf16[512,4096]{1,0:T(8,128)(2,1)}, bf16[512,4096]{1,0:T(8,128)(2,1)}, bf16[512,768]{1,0:T(8,128)(2,1)}) custom-call(bf16[512,768]{1,0:T(8,128)(2,1)S(1)} %bitcast.14, bf16[1,768,4096]{2,1,0:T(8,128)(2,1)} %w_in_ref.3, bf16[1,4096,768]{2,1,0:T(8,128)(2,1)} %w_out_ref.3), custom_call_target="tpu_custom_call" | custom-call | flops 6442450944 | bytes 22544384 | tf_op jit(solution)/shard_map/pallas_call | solution.py:250
  48.3 8.6 %all-to-all-done.2 = bf16[32,16,768]{2,1,0:T(8,128)(2,1)S(1)} async-done(((bf16[32,16,768]{2,1,0:T(8,128)(2,1)}), bf16[32,16,768]{2,1,0:T(8,128)(2,1)S(1)}, u32[]{:S(2)}, u32[]{:S(2)}) %all-to-all-start.2) | async-done | bytes 786464 | tf_op jit(solution)/shard_map/all_to_all | solution.py:219
  56.9 2.6 %all-to-all-start.1 = ((bf16[32,16,768]{2,1,0:T(8,128)(2,1)}), bf16[32,16,768]{2,1,0:T(8,128)(2,1)S(1)}, u32[]{:S(2)}, u32[]{:S(2)}) async-start(bf16[32,16,768]{2,1,0:T(8,128)(2,1)} %bitcast.5), calls=%async_computation.1 | async-start | bytes 1572864 | tf_op jit(solution)/shard_map/all_to_all | solution.py:219
  59.6 12.0 %shard_map.114 = (bf16[512,4096]{1,0:T(8,128)(2,1)}, bf16[512,768]{1,0:T(8,128)(2,1)S(1)}) custom-call(bf16[512,768]{1,0:T(8,128)(2,1)S(1)} %bitcast.16, bf16[1,768,4096]{2,1,0:T(8,128)(2,1)} %w_in_ref.3, bf16[1,4096,768]{2,1,0:T(8,128)(2,1)} %w_out_ref.3, bf16[512,4096]{1,0:T(8,128)(2,1)} %get-tuple-element.20.slope_ref), custom_call_target="tpu_custom_call" | custom-call | flops 6442450944 | bytes 22544384 | tf_op jit(solution)/shard_map/pallas_call | solution.py:262
  71.6 0.0 copy-start
  71.6 1.0 copy-done
  72.5 9.0 %all-to-all-done.1 = bf16[32,16,768]{2,1,0:T(8,128)(2,1)S(1)} async-done(((bf16[32,16,768]{2,1,0:T(8,128)(2,1)}), bf16[32,16,768]{2,1,0:T(8,128)(2,1)S(1)}, u32[]{:S(2)}, u32[]{:S(2)}) %all-to-all-start.1) | async-done | bytes 786464 | tf_op jit(solution)/shard_map/all_to_all | solution.py:219
  81.5 2.6 %all-to-all-start.3 = ((bf16[32,16,768]{2,1,0:T(8,128)(2,1)}), bf16[32,16,768]{2,1,0:T(8,128)(2,1)S(1)}, u32[]{:S(2)}, u32[]{:S(2)}) async-start(bf16[32,16,768]{2,1,0:T(8,128)(2,1)} %bitcast.18), calls=%async_computation.3 | async-start | bytes 1572864 | tf_op jit(solution)/shard_map/all_to_all | solution.py:219
  84.2 10.7 %shard_map.116 = (bf16[1,768,4096]{2,1,0:T(8,128)(2,1)}, bf16[1,4096,768]{2,1,0:T(8,128)(2,1)}) custom-call(bf16[512,768]{1,0:T(8,128)(2,1)S(1)} %bitcast.15, bf16[512,768]{1,0:T(8,128)(2,1)S(1)} %bitcast.17, bf16[512,4096]{1,0:T(8,128)(2,1)} %get-tuple-element.23.hidden_ref, bf16[512,4096]{1,0:T(8,128)(2,1)} %get-tuple-element.24.grad_pre_ref), custom_call_target="tpu_custom_call" | custom-call | flops 6442450944 | bytes 22544384 | tf_op jit(solution)/shard_map/pallas_call | solution.py:283
  94.9 2.1 %shard_map.112 = (bf16[128,768]{1,0:T(8,128)(2,1)}, f32[2,128]{1,0:T(2,128)}) custom-call(bf16[512,768]{1,0:T(8,128)(2,1)S(1)} %bitcast.12, bf16[128,768]{1,0:T(8,128)(2,1)} %grad_ref.3, f32[8,128]{1,0:T(8,128)S(1)} %get-tuple-element.18.meta_ref), custom_call_target="tpu_custom_call" | custom-call | flops 201326592 | bytes 1179648 | tf_op jit(solution)/shard_map/pallas_call | solution.py:274
  97.0 9.2 %all-to-all-done.3 = bf16[32,16,768]{2,1,0:T(8,128)(2,1)S(1)} async-done(((bf16[32,16,768]{2,1,0:T(8,128)(2,1)}), bf16[32,16,768]{2,1,0:T(8,128)(2,1)S(1)}, u32[]{:S(2)}, u32[]{:S(2)}) %all-to-all-start.3) | async-done | bytes 786464 | tf_op jit(solution)/shard_map/all_to_all | solution.py:219
  106.1 1.0 shard_map.115
Async XLA Ops:
  3.0 29.3 %all-to-all-start = ((bf16[32,16,768]{2,1,0:T(8,128)(2,1)}), bf16[32,16,768]{2,1,0:T(8,128)(2,1)S(1)}, u32[]{:S(2)}, u32[]{:S(2)}) async-start(bf16[32,16,768]{2,1,0:T(8,128)(2,1)} %bitcast.3), calls=%async_computation | async-start | bytes 1572864 | tf_op jit(solution)/shard_map/all_to_all | solution.py:219
  32.3 24.6 %all-to-all-start.2 = ((bf16[32,16,768]{2,1,0:T(8,128)(2,1)}), bf16[32,16,768]{2,1,0:T(8,128)(2,1)S(1)}, u32[]{:S(2)}, u32[]{:S(2)}) async-start(bf16[32,16,768]{2,1,0:T(8,128)(2,1)} %bitcast.7), calls=%async_computation.2 | async-start | bytes 1572864 | tf_op jit(solution)/shard_map/all_to_all | solution.py:219
  56.9 24.6 %all-to-all-start.1 = ((bf16[32,16,768]{2,1,0:T(8,128)(2,1)}), bf16[32,16,768]{2,1,0:T(8,128)(2,1)S(1)}, u32[]{:S(2)}, u32[]{:S(2)}) async-start(bf16[32,16,768]{2,1,0:T(8,128)(2,1)} %bitcast.5), calls=%async_computation.1 | async-start | bytes 1572864 | tf_op jit(solution)/shard_map/all_to_all | solution.py:219
  71.6 1.0 copy-start
  81.5 24.6 %all-to-all-start.3 = ((bf16[32,16,768]{2,1,0:T(8,128)(2,1)}), bf16[32,16,768]{2,1,0:T(8,128)(2,1)S(1)}, u32[]{:S(2)}, u32[]{:S(2)}) async-start(bf16[32,16,768]{2,1,0:T(8,128)(2,1)} %bitcast.18), calls=%async_computation.3 | async-start | bytes 1572864 | tf_op jit(solution)/shard_map/all_to_all | solution.py:219

commit v12 on v7

--- a/solution.py
+++ b/solution.py
@@ -13,8 +13,8 @@
 F32 = jnp.float32
 MIB = 1024 * 1024
 SUB = 256
-AXES = ("row", "outer", "inner")
-GROUP = ("row", "inner", "outer")
+AXES = ("high", "core", "outer", "inner")
+GROUP = ("outer", "high", "inner", "core")
 
 
 def dot(a, b, contract_a, contract_b):
@@ -200,15 +200,16 @@
 def body(tokens, expert_ids, keep_mask, gate_weights, weight_in, weight_out, grad_output):
     token_rows, width = tokens.shape
     hidden_width = weight_in.shape[2]
-    row_count, outer = lax.axis_size("row"), lax.axis_size("outer")
-    experts = row_count * outer * lax.axis_size("inner")
-    bits = outer.bit_length() - 1
+    high, outer = lax.axis_size("high"), lax.axis_size("outer")
+    experts = high * outer * 4
+    high_bits, bits = high.bit_length() - 1, outer.bit_length() - 1
 
     def place_of(expert):
         inner_at = expert & 1
         outer_at = (expert >> 1) & (outer - 1)
-        row_at = expert >> (bits + 1)
-        return ((row_at * 2 + inner_at) << bits) + outer_at
+        core_at = (expert >> (bits + 1)) & 1
+        high_at = expert >> (bits + 2)
+        return (((((outer_at << high_bits) + high_at) << 1) + inner_at) << 1) + core_at
 
     capacity = 2 * expert_ids.shape[1] * token_rows // experts
     slot_total = experts * capacity
@@ -300,7 +301,7 @@
 
 def solution(mesh):
     rows, cols = mesh.devices.shape
-    split = Mesh(mesh.devices.reshape(rows, cols // 2, 2), AXES)
+    split = Mesh(mesh.devices.reshape(rows // 2, 2, cols // 2, 2), AXES)
     flat, deep = P(AXES, None), P(AXES, None, None)
     return jax.shard_map(
         body,

time: 105 us -> 105 us (level)
  starting transfers between devices: 15.2 us -> 18.2 us
  waiting for transfers between devices: 43.4 us -> 40.8 us
    all_to_all x4, starting transfers between devices: 15.2 us -> 18.2 us  [shuffle(): lax.all_to_all(shaped, GROUP, split_axis=0, concat_axis=0, tiled=True)]
    all_to_all x4, waiting for transfers between devices: 43.4 us -> 40.8 us  [shuffle(): lax.all_to_all(shaped, GROUP, split_axis=0, concat_axis=0, tiled=True)]
where the time goes in v12:
time: 105 us
  Pallas kernels  44.1 us (42%)
  waiting for transfers between devices  40.8 us (39%)
  starting transfers between devices  18.2 us (17%)
    all_to_all x4, waiting for transfers between devices, shuffle(): lax.all_to_all(shaped, GROUP, split_axis=0, concat_axis=0, tiled=True)  40.8 us
    all_to_all x4, starting transfers between devices, shuffle(): lax.all_to_all(shaped, GROUP, split_axis=0, concat_axis=0, tiled=True)  18.2 us
    pallas_call x1, Pallas kernels, body(): call(forward_kernel, [mid, mid, slots], 2 * product, traffic, 32, grid=gr...  13.4 us
    pallas_call x1, Pallas kernels, body(): call(backward_kernel, [mid, slots], 2 * product, traffic, 32, grid=grid,...  12 us
    pallas_call x1, Pallas kernels, body(): call(weights_kernel, [pltpu.HBM(weight_in.shape, BF16), pltpu.HBM(weight_...  10.7 us
    pallas_call x1, Pallas kernels, body(): call(place_cotangents_kernel, slots, 2 * place_flops, token_bytes + slot_...  2.46 us
    pallas_call x1, Pallas kernels, body(): call(functools.partial(place_tokens_kernel, capacity, place_of), [jax.Sha...  2.42 us
    pallas_call x1, Pallas kernels, body(): call(pick_outputs_kernel, [jax.ShapeDtypeStruct((token_rows, width), BF16...  2.1 us
  transfers between devices with their start and end apart: 4, of which 4 were waited for; matrix products, arithmetic and copies ran while one was open for 0% of the time, Pallas kernels for 39%

profile of v12, /device:TPU:0, one launch (start us, length us, event | category | flops | bytes accessed | tf_op | source)
XLA Modules:
  0.0 104.7 jit_solution(11986416354189752093)
XLA Ops:
  0.6 2.4 %shard_map.110 = (f32[8,128]{1,0:T(8,128)S(1)}, bf16[512,768]{1,0:T(8,128)(2,1)}) custom-call(bf16[128,768]{1,0:T(8,128)(2,1)} %tokens_ref.1, s32[2,128]{1,0:T(2,128)} %bitcast.19, s32[2,128]{1,0:T(2,128)} %bitcast.20, f32[2,128]{1,0:T(2,128)} %bitcast.21), custom_call_target="tpu_custom_call" | custom-call | flops 100663296 | bytes 983040 | tf_op jit(solution)/shard_map/pallas_call | solution.py:227
  3.0 7.3 %all-to-all-start = ((bf16[32,16,768]{2,1,0:T(8,128)(2,1)}), bf16[32,16,768]{2,1,0:T(8,128)(2,1)S(1)}, u32[]{:S(2)}, u32[]{:S(2)}) async-start(bf16[32,16,768]{2,1,0:T(8,128)(2,1)} %bitcast.3), calls=%async_computation | async-start | bytes 1572864 | tf_op jit(solution)/shard_map/all_to_all | solution.py:219
  10.4 2.5 %shard_map.113 = bf16[512,768]{1,0:T(8,128)(2,1)} custom-call(bf16[128,768]{1,0:T(8,128)(2,1)} %grad_ref.3, f32[8,128]{1,0:T(8,128)S(1)} %get-tuple-element.18.meta_ref), custom_call_target="tpu_custom_call" | custom-call | flops 201326592 | bytes 983040 | tf_op jit(solution)/shard_map/pallas_call | solution.py:234
  12.8 18.2 %all-to-all-done = bf16[32,16,768]{2,1,0:T(8,128)(2,1)S(1)} async-done(((bf16[32,16,768]{2,1,0:T(8,128)(2,1)}), bf16[32,16,768]{2,1,0:T(8,128)(2,1)S(1)}, u32[]{:S(2)}, u32[]{:S(2)}) %all-to-all-start) | async-done | bytes 786464 | tf_op jit(solution)/shard_map/all_to_all | solution.py:219
  31.0 3.6 %all-to-all-start.2 = ((bf16[32,16,768]{2,1,0:T(8,128)(2,1)}), bf16[32,16,768]{2,1,0:T(8,128)(2,1)S(1)}, u32[]{:S(2)}, u32[]{:S(2)}) async-start(bf16[32,16,768]{2,1,0:T(8,128)(2,1)} %bitcast.7), calls=%async_computation.2 | async-start | bytes 1572864 | tf_op jit(solution)/shard_map/all_to_all | solution.py:219
  34.6 13.4 %shard_map.111 = (bf16[512,4096]{1,0:T(8,128)(2,1)}, bf16[512,4096]{1,0:T(8,128)(2,1)}, bf16[512,768]{1,0:T(8,128)(2,1)}) custom-call(bf16[512,768]{1,0:T(8,128)(2,1)S(1)} %bitcast.14, bf16[1,768,4096]{2,1,0:T(8,128)(2,1)} %w_in_ref.3, bf16[1,4096,768]{2,1,0:T(8,128)(2,1)} %w_out_ref.3), custom_call_target="tpu_custom_call" | custom-call | flops 6442450944 | bytes 22544384 | tf_op jit(solution)/shard_map/pallas_call | solution.py:250
  48.0 7.2 %all-to-all-done.2 = bf16[32,16,768]{2,1,0:T(8,128)(2,1)S(1)} async-done(((bf16[32,16,768]{2,1,0:T(8,128)(2,1)}), bf16[32,16,768]{2,1,0:T(8,128)(2,1)S(1)}, u32[]{:S(2)}, u32[]{:S(2)}) %all-to-all-start.2) | async-done | bytes 786464 | tf_op jit(solution)/shard_map/all_to_all | solution.py:219
  55.2 3.6 %all-to-all-start.1 = ((bf16[32,16,768]{2,1,0:T(8,128)(2,1)}), bf16[32,16,768]{2,1,0:T(8,128)(2,1)S(1)}, u32[]{:S(2)}, u32[]{:S(2)}) async-start(bf16[32,16,768]{2,1,0:T(8,128)(2,1)} %bitcast.5), calls=%async_computation.1 | async-start | bytes 1572864 | tf_op jit(solution)/shard_map/all_to_all | solution.py:219
  58.8 12.0 %shard_map.114 = (bf16[512,4096]{1,0:T(8,128)(2,1)}, bf16[512,768]{1,0:T(8,128)(2,1)S(1)}) custom-call(bf16[512,768]{1,0:T(8,128)(2,1)S(1)} %bitcast.16, bf16[1,768,4096]{2,1,0:T(8,128)(2,1)} %w_in_ref.3, bf16[1,4096,768]{2,1,0:T(8,128)(2,1)} %w_out_ref.3, bf16[512,4096]{1,0:T(8,128)(2,1)} %get-tuple-element.20.slope_ref), custom_call_target="tpu_custom_call" | custom-call | flops 6442450944 | bytes 22544384 | tf_op jit(solution)/shard_map/pallas_call | solution.py:262
  70.9 0.0 copy-start
  70.9 1.0 copy-done
  71.8 7.6 %all-to-all-done.1 = bf16[32,16,768]{2,1,0:T(8,128)(2,1)S(1)} async-done(((bf16[32,16,768]{2,1,0:T(8,128)(2,1)}), bf16[32,16,768]{2,1,0:T(8,128)(2,1)S(1)}, u32[]{:S(2)}, u32[]{:S(2)}) %all-to-all-start.1) | async-done | bytes 786464 | tf_op jit(solution)/shard_map/all_to_all | solution.py:219
  79.5 3.6 %all-to-all-start.3 = ((bf16[32,16,768]{2,1,0:T(8,128)(2,1)}), bf16[32,16,768]{2,1,0:T(8,128)(2,1)S(1)}, u32[]{:S(2)}, u32[]{:S(2)}) async-start(bf16[32,16,768]{2,1,0:T(8,128)(2,1)} %bitcast.18), calls=%async_computation.3 | async-start | bytes 1572864 | tf_op jit(solution)/shard_map/all_to_all | solution.py:219
  83.1 10.7 %shard_map.116 = (bf16[1,768,4096]{2,1,0:T(8,128)(2,1)}, bf16[1,4096,768]{2,1,0:T(8,128)(2,1)}) custom-call(bf16[512,768]{1,0:T(8,128)(2,1)S(1)} %bitcast.15, bf16[512,768]{1,0:T(8,128)(2,1)S(1)} %bitcast.17, bf16[512,4096]{1,0:T(8,128)(2,1)} %get-tuple-element.23.hidden_ref, bf16[512,4096]{1,0:T(8,128)(2,1)} %get-tuple-element.24.grad_pre_ref), custom_call_target="tpu_custom_call" | custom-call | flops 6442450944 | bytes 22544384 | tf_op jit(solution)/shard_map/pallas_call | solution.py:283
  93.8 2.1 %shard_map.112 = (bf16[128,768]{1,0:T(8,128)(2,1)}, f32[2,128]{1,0:T(2,128)}) custom-call(bf16[512,768]{1,0:T(8,128)(2,1)S(1)} %bitcast.12, bf16[128,768]{1,0:T(8,128)(2,1)} %grad_ref.3, f32[8,128]{1,0:T(8,128)S(1)} %get-tuple-element.18.meta_ref), custom_call_target="tpu_custom_call" | custom-call | flops 201326592 | bytes 1179648 | tf_op jit(solution)/shard_map/pallas_call | solution.py:274
  95.9 7.8 %all-to-all-done.3 = bf16[32,16,768]{2,1,0:T(8,128)(2,1)S(1)} async-done(((bf16[32,16,768]{2,1,0:T(8,128)(2,1)}), bf16[32,16,768]{2,1,0:T(8,128)(2,1)S(1)}, u32[]{:S(2)}, u32[]{:S(2)}) %all-to-all-start.3) | async-done | bytes 786464 | tf_op jit(solution)/shard_map/all_to_all | solution.py:219
  103.7 1.0 shard_map.115
Async XLA Ops:
  3.0 27.9 %all-to-all-start = ((bf16[32,16,768]{2,1,0:T(8,128)(2,1)}), bf16[32,16,768]{2,1,0:T(8,128)(2,1)S(1)}, u32[]{:S(2)}, u32[]{:S(2)}) async-start(bf16[32,16,768]{2,1,0:T(8,128)(2,1)} %bitcast.3), calls=%async_computation | async-start | bytes 1572864 | tf_op jit(solution)/shard_map/all_to_all | solution.py:219
  31.0 24.2 %all-to-all-start.2 = ((bf16[32,16,768]{2,1,0:T(8,128)(2,1)}), bf16[32,16,768]{2,1,0:T(8,128)(2,1)S(1)}, u32[]{:S(2)}, u32[]{:S(2)}) async-start(bf16[32,16,768]{2,1,0:T(8,128)(2,1)} %bitcast.7), calls=%async_computation.2 | async-start | bytes 1572864 | tf_op jit(solution)/shard_map/all_to_all | solution.py:219
  55.2 24.2 %all-to-all-start.1 = ((bf16[32,16,768]{2,1,0:T(8,128)(2,1)}), bf16[32,16,768]{2,1,0:T(8,128)(2,1)S(1)}, u32[]{:S(2)}, u32[]{:S(2)}) async-start(bf16[32,16,768]{2,1,0:T(8,128)(2,1)} %bitcast.5), calls=%async_computation.1 | async-start | bytes 1572864 | tf_op jit(solution)/shard_map/all_to_all | solution.py:219
  70.9 1.0 copy-start
  79.5 24.2 %all-to-all-start.3 = ((bf16[32,16,768]{2,1,0:T(8,128)(2,1)}), bf16[32,16,768]{2,1,0:T(8,128)(2,1)S(1)}, u32[]{:S(2)}, u32[]{:S(2)}) async-start(bf16[32,16,768]{2,1,0:T(8,128)(2,1)} %bitcast.18), calls=%async_computation.3 | async-start | bytes 1572864 | tf_op jit(solution)/shard_map/all_to_all | solution.py:219

commit v13 on v12

--- a/solution.py
+++ b/solution.py
@@ -14,7 +14,7 @@
 MIB = 1024 * 1024
 SUB = 256
 AXES = ("high", "core", "outer", "inner")
-GROUP = ("outer", "high", "inner", "core")
+GROUP = ("outer", "core", "high", "inner")
 
 
 def dot(a, b, contract_a, contract_b):
@@ -209,7 +209,7 @@
         outer_at = (expert >> 1) & (outer - 1)
         core_at = (expert >> (bits + 1)) & 1
         high_at = expert >> (bits + 2)
-        return (((((outer_at << high_bits) + high_at) << 1) + inner_at) << 1) + core_at
+        return (((((outer_at << 1) + core_at) << high_bits) + high_at) << 1) + inner_at
 
     capacity = 2 * expert_ids.shape[1] * token_rows // experts
     slot_total = experts * capacity

time: 105 us -> 106 us (level)
  waiting for transfers between devices: 40.8 us -> 43.9 us
  starting transfers between devices: 18.2 us -> 15.9 us
    all_to_all x4, waiting for transfers between devices: 40.8 us -> 43.9 us  [shuffle(): lax.all_to_all(shaped, GROUP, split_axis=0, concat_axis=0, tiled=True)]
    all_to_all x4, starting transfers between devices: 18.2 us -> 15.9 us  [shuffle(): lax.all_to_all(shaped, GROUP, split_axis=0, concat_axis=0, tiled=True)]
where the time goes in v13:
time: 106 us; the launch traced here: 105 us
  Pallas kernels  44.1 us (42%)
  waiting for transfers between devices  43.9 us (41%)
  starting transfers between devices  15.9 us (15%)
    all_to_all x4, waiting for transfers between devices, shuffle(): lax.all_to_all(shaped, GROUP, split_axis=0, concat_axis=0, tiled=True)  43.9 us
    all_to_all x4, starting transfers between devices, shuffle(): lax.all_to_all(shaped, GROUP, split_axis=0, concat_axis=0, tiled=True)  15.9 us
    pallas_call x1, Pallas kernels, body(): call(forward_kernel, [mid, mid, slots], 2 * product, traffic, 32, grid=gr...  13.4 us
    pallas_call x1, Pallas kernels, body(): call(backward_kernel, [mid, slots], 2 * product, traffic, 32, grid=grid,...  12 us
    pallas_call x1, Pallas kernels, body(): call(weights_kernel, [pltpu.HBM(weight_in.shape, BF16), pltpu.HBM(weight_...  10.7 us
    pallas_call x1, Pallas kernels, body(): call(place_cotangents_kernel, slots, 2 * place_flops, token_bytes + slot_...  2.46 us
    pallas_call x1, Pallas kernels, body(): call(functools.partial(place_tokens_kernel, capacity, place_of), [jax.Sha...  2.42 us
  transfers between devices with their start and end apart: 4, of which 4 were waited for; matrix products, arithmetic and copies ran while one was open for 0% of the time, Pallas kernels for 39%

profile of v13, /device:TPU:0, one launch (start us, length us, event | category | flops | bytes accessed | tf_op | source)
XLA Modules:
  0.0 105.5 jit_solution(6496907656951023308)
XLA Ops:
  0.6 2.4 %shard_map.110 = (f32[8,128]{1,0:T(8,128)S(1)}, bf16[512,768]{1,0:T(8,128)(2,1)}) custom-call(bf16[128,768]{1,0:T(8,128)(2,1)} %tokens_ref.1, s32[2,128]{1,0:T(2,128)} %bitcast.19, s32[2,128]{1,0:T(2,128)} %bitcast.20, f32[2,128]{1,0:T(2,128)} %bitcast.21), custom_call_target="tpu_custom_call" | custom-call | flops 100663296 | bytes 983040 | tf_op jit(solution)/shard_map/pallas_call | solution.py:227
  3.0 7.3 %all-to-all-start = ((bf16[32,16,768]{2,1,0:T(8,128)(2,1)}), bf16[32,16,768]{2,1,0:T(8,128)(2,1)S(1)}, u32[]{:S(2)}, u32[]{:S(2)}) async-start(bf16[32,16,768]{2,1,0:T(8,128)(2,1)} %bitcast.3), calls=%async_computation | async-start | bytes 1572864 | tf_op jit(solution)/shard_map/all_to_all | solution.py:219
  10.4 2.5 %shard_map.113 = bf16[512,768]{1,0:T(8,128)(2,1)} custom-call(bf16[128,768]{1,0:T(8,128)(2,1)} %grad_ref.3, f32[8,128]{1,0:T(8,128)S(1)} %get-tuple-element.18.meta_ref), custom_call_target="tpu_custom_call" | custom-call | flops 201326592 | bytes 983040 | tf_op jit(solution)/shard_map/pallas_call | solution.py:234
  12.8 18.9 %all-to-all-done = bf16[32,16,768]{2,1,0:T(8,128)(2,1)S(1)} async-done(((bf16[32,16,768]{2,1,0:T(8,128)(2,1)}), bf16[32,16,768]{2,1,0:T(8,128)(2,1)S(1)}, u32[]{:S(2)}, u32[]{:S(2)}) %all-to-all-start) | async-done | bytes 786464 | tf_op jit(solution)/shard_map/all_to_all | solution.py:219
  31.7 2.9 %all-to-all-start.2 = ((bf16[32,16,768]{2,1,0:T(8,128)(2,1)}), bf16[32,16,768]{2,1,0:T(8,128)(2,1)S(1)}, u32[]{:S(2)}, u32[]{:S(2)}) async-start(bf16[32,16,768]{2,1,0:T(8,128)(2,1)} %bitcast.7), calls=%async_computation.2 | async-start | bytes 1572864 | tf_op jit(solution)/shard_map/all_to_all | solution.py:219
  34.6 13.4 %shard_map.111 = (bf16[512,4096]{1,0:T(8,128)(2,1)}, bf16[512,4096]{1,0:T(8,128)(2,1)}, bf16[512,768]{1,0:T(8,128)(2,1)}) custom-call(bf16[512,768]{1,0:T(8,128)(2,1)S(1)} %bitcast.14, bf16[1,768,4096]{2,1,0:T(8,128)(2,1)} %w_in_ref.3, bf16[1,4096,768]{2,1,0:T(8,128)(2,1)} %w_out_ref.3), custom_call_target="tpu_custom_call" | custom-call | flops 6442450944 | bytes 22544384 | tf_op jit(solution)/shard_map/pallas_call | solution.py:250
  48.0 8.0 %all-to-all-done.2 = bf16[32,16,768]{2,1,0:T(8,128)(2,1)S(1)} async-done(((bf16[32,16,768]{2,1,0:T(8,128)(2,1)}), bf16[32,16,768]{2,1,0:T(8,128)(2,1)S(1)}, u32[]{:S(2)}, u32[]{:S(2)}) %all-to-all-start.2) | async-done | bytes 786464 | tf_op jit(solution)/shard_map/all_to_all | solution.py:219
  56.0 2.9 %all-to-all-start.1 = ((bf16[32,16,768]{2,1,0:T(8,128)(2,1)}), bf16[32,16,768]{2,1,0:T(8,128)(2,1)S(1)}, u32[]{:S(2)}, u32[]{:S(2)}) async-start(bf16[32,16,768]{2,1,0:T(8,128)(2,1)} %bitcast.5), calls=%async_computation.1 | async-start | bytes 1572864 | tf_op jit(solution)/shard_map/all_to_all | solution.py:219
  58.8 12.0 %shard_map.114 = (bf16[512,4096]{1,0:T(8,128)(2,1)}, bf16[512,768]{1,0:T(8,128)(2,1)S(1)}) custom-call(bf16[512,768]{1,0:T(8,128)(2,1)S(1)} %bitcast.16, bf16[1,768,4096]{2,1,0:T(8,128)(2,1)} %w_in_ref.3, bf16[1,4096,768]{2,1,0:T(8,128)(2,1)} %w_out_ref.3, bf16[512,4096]{1,0:T(8,128)(2,1)} %get-tuple-element.20.slope_ref), custom_call_target="tpu_custom_call" | custom-call | flops 6442450944 | bytes 22544384 | tf_op jit(solution)/shard_map/pallas_call | solution.py:262
  70.8 0.0 copy-start
  70.8 1.0 copy-done
  71.8 8.4 %all-to-all-done.1 = bf16[32,16,768]{2,1,0:T(8,128)(2,1)S(1)} async-done(((bf16[32,16,768]{2,1,0:T(8,128)(2,1)}), bf16[32,16,768]{2,1,0:T(8,128)(2,1)S(1)}, u32[]{:S(2)}, u32[]{:S(2)}) %all-to-all-start.1) | async-done | bytes 786464 | tf_op jit(solution)/shard_map/all_to_all | solution.py:219
  80.2 2.9 %all-to-all-start.3 = ((bf16[32,16,768]{2,1,0:T(8,128)(2,1)}), bf16[32,16,768]{2,1,0:T(8,128)(2,1)S(1)}, u32[]{:S(2)}, u32[]{:S(2)}) async-start(bf16[32,16,768]{2,1,0:T(8,128)(2,1)} %bitcast.18), calls=%async_computation.3 | async-start | bytes 1572864 | tf_op jit(solution)/shard_map/all_to_all | solution.py:219
  83.1 10.7 %shard_map.116 = (bf16[1,768,4096]{2,1,0:T(8,128)(2,1)}, bf16[1,4096,768]{2,1,0:T(8,128)(2,1)}) custom-call(bf16[512,768]{1,0:T(8,128)(2,1)S(1)} %bitcast.15, bf16[512,768]{1,0:T(8,128)(2,1)S(1)} %bitcast.17, bf16[512,4096]{1,0:T(8,128)(2,1)} %get-tuple-element.23.hidden_ref, bf16[512,4096]{1,0:T(8,128)(2,1)} %get-tuple-element.24.grad_pre_ref), custom_call_target="tpu_custom_call" | custom-call | flops 6442450944 | bytes 22544384 | tf_op jit(solution)/shard_map/pallas_call | solution.py:283
  93.8 2.1 %shard_map.112 = (bf16[128,768]{1,0:T(8,128)(2,1)}, f32[2,128]{1,0:T(2,128)}) custom-call(bf16[512,768]{1,0:T(8,128)(2,1)S(1)} %bitcast.12, bf16[128,768]{1,0:T(8,128)(2,1)} %grad_ref.3, f32[8,128]{1,0:T(8,128)S(1)} %get-tuple-element.18.meta_ref), custom_call_target="tpu_custom_call" | custom-call | flops 201326592 | bytes 1179648 | tf_op jit(solution)/shard_map/pallas_call | solution.py:274
  95.9 8.6 %all-to-all-done.3 = bf16[32,16,768]{2,1,0:T(8,128)(2,1)S(1)} async-done(((bf16[32,16,768]{2,1,0:T(8,128)(2,1)}), bf16[32,16,768]{2,1,0:T(8,128)(2,1)S(1)}, u32[]{:S(2)}, u32[]{:S(2)}) %all-to-all-start.3) | async-done | bytes 786464 | tf_op jit(solution)/shard_map/all_to_all | solution.py:219
  104.5 1.0 shard_map.115
Async XLA Ops:
  3.0 28.7 %all-to-all-start = ((bf16[32,16,768]{2,1,0:T(8,128)(2,1)}), bf16[32,16,768]{2,1,0:T(8,128)(2,1)S(1)}, u32[]{:S(2)}, u32[]{:S(2)}) async-start(bf16[32,16,768]{2,1,0:T(8,128)(2,1)} %bitcast.3), calls=%async_computation | async-start | bytes 1572864 | tf_op jit(solution)/shard_map/all_to_all | solution.py:219
  31.7 24.2 %all-to-all-start.2 = ((bf16[32,16,768]{2,1,0:T(8,128)(2,1)}), bf16[32,16,768]{2,1,0:T(8,128)(2,1)S(1)}, u32[]{:S(2)}, u32[]{:S(2)}) async-start(bf16[32,16,768]{2,1,0:T(8,128)(2,1)} %bitcast.7), calls=%async_computation.2 | async-start | bytes 1572864 | tf_op jit(solution)/shard_map/all_to_all | solution.py:219
  56.0 24.2 %all-to-all-start.1 = ((bf16[32,16,768]{2,1,0:T(8,128)(2,1)}), bf16[32,16,768]{2,1,0:T(8,128)(2,1)S(1)}, u32[]{:S(2)}, u32[]{:S(2)}) async-start(bf16[32,16,768]{2,1,0:T(8,128)(2,1)} %bitcast.5), calls=%async_computation.1 | async-start | bytes 1572864 | tf_op jit(solution)/shard_map/all_to_all | solution.py:219
  70.8 1.0 copy-start
  80.2 24.2 %all-to-all-start.3 = ((bf16[32,16,768]{2,1,0:T(8,128)(2,1)}), bf16[32,16,768]{2,1,0:T(8,128)(2,1)S(1)}, u32[]{:S(2)}, u32[]{:S(2)}) async-start(bf16[32,16,768]{2,1,0:T(8,128)(2,1)} %bitcast.18), calls=%async_computation.3 | async-start | bytes 1572864 | tf_op jit(solution)/shard_map/all_to_all | solution.py:219

commit v14 on v10

--- a/solution.py
+++ b/solution.py
@@ -94,14 +94,10 @@
     return jnp.concatenate(pieces, axis=1)
 
 
-def place_cotangents_kernel(half_ref, both_grads, own_meta, partner_meta, out_ref):
+def place_cotangents_kernel(own_grad, partner_grad, own_meta, partner_meta, out_ref):
     slot_total = out_ref.shape[0]
-    half = half_ref[0]
     total = None
-    for grad_ref, meta_ref in (
-        (both_grads.at[half], own_meta),
-        (both_grads.at[1 - half], partner_meta),
-    ):
+    for grad_ref, meta_ref in ((own_grad, own_meta), (partner_grad, partner_meta)):
         for k in range(2):
             rows = scaled_rows(meta_ref[k + 2 : k + 3, :], grad_ref).astype(BF16)
             part = dot(one_hot(hits(slot_total, meta_ref, k)), rows, 1, 0)
@@ -171,13 +167,12 @@
 
 
 def pick_outputs_kernel(
-    half_ref, back_ref, both_grads, own_meta, partner_meta, own_out, partner_out, own_gates, partner_gates
+    back_ref, own_grad, partner_grad, own_meta, partner_meta, own_out, partner_out, own_gates, partner_gates
 ):
     slot_total = back_ref.shape[0]
-    half = half_ref[0]
     for grad_ref, meta_ref, out_ref, gates_ref in (
-        (both_grads.at[half], own_meta, own_out, own_gates),
-        (both_grads.at[1 - half], partner_meta, partner_out, partner_gates),
+        (own_grad, own_meta, own_out, own_gates),
+        (partner_grad, partner_meta, partner_out, partner_gates),
     ):
         total = None
         for k in range(2):
@@ -248,7 +243,7 @@
     slot_bytes, token_bytes = slot_total * width * 2, token_rows * width * 2
     place_flops = 2 * slot_total * token_rows * width
 
-    both_grads = lax.all_gather(grad_output, "half")
+    partner_grad = exchange(grad_output)
     half = lax.axis_index("half").astype(jnp.int32).reshape(1)
     own_meta, sent_meta, sent = call(
         functools.partial(place_tokens_kernel, rest_count.bit_length() - 1, capacity),
@@ -265,14 +260,9 @@
     )
     x = shuffle(sent, ALL, 2 * members)
     partner_meta = exchange(sent_meta)
-    smem = pl.BlockSpec(memory_space=pltpu.SMEM)
     sent_cot = call(
-        place_cotangents_kernel,
-        slots,
-        4 * place_flops,
-        2 * token_bytes + slot_bytes,
-        in_specs=[smem] + [vmem] * 3,
-    )(half, both_grads, own_meta, partner_meta)
+        place_cotangents_kernel, slots, 4 * place_flops, 2 * token_bytes + slot_bytes
+    )(in_hbm(grad_output), partner_grad, own_meta, partner_meta)
     cot = shuffle(sent_cot, GROUP, members)
 
     chunk = 1024
@@ -293,7 +283,7 @@
         traffic,
         32,
         grid=grid,
-        in_specs=[vmem, in_spec, out_spec],
+        in_specs=[whole, in_spec, out_spec],
         out_specs=[mid_spec, mid_spec, whole],
         scratch_shapes=[total],
     )(x, weight_in, weight_out)
@@ -305,7 +295,7 @@
         traffic,
         32,
         grid=grid,
-        in_specs=[vmem, in_spec, out_spec, mid_spec],
+        in_specs=[whole, in_spec, out_spec, mid_spec],
         out_specs=[mid_spec, whole],
         scratch_shapes=[total],
     )(cot, weight_in, weight_out, in_hbm(slope))
@@ -316,8 +306,7 @@
         [tokens_f32, token_shape, gates_shape, gates_shape],
         4 * place_flops,
         4 * token_bytes + slot_bytes,
-        in_specs=[smem] + [vmem] * 4,
-    )(half, back_out, both_grads, own_meta, partner_meta)
+    )(back_out, in_hbm(grad_output), partner_grad, own_meta, partner_meta)
     grad_pre, partner_out = lax.optimization_barrier((grad_pre, partner_out))
     got_out, got_gates = exchange(partner_out), exchange(partner_gates)
     grad_in_w, grad_out_w = call(
@@ -327,7 +316,7 @@
         traffic,
         32,
         grid=grid,
-        in_specs=[vmem, vmem, mid_spec, mid_spec],
+        in_specs=[whole, whole, mid_spec, mid_spec],
         out_specs=[in_spec, out_spec],
     )(x, cot, in_hbm(hidden), in_hbm(grad_pre))
     combined, grad_gates = call(
@@ -341,7 +330,7 @@
 
 def solution(mesh):
     rows, cols = mesh.devices.shape
-    halves = Mesh(mesh.devices.reshape(rows, 2, cols // 2), AXES)
+    halves = Mesh(mesh.devices.reshape(rows // 2, 2, cols), AXES)
     flat, deep = P(AXES, None), P(AXES, None, None)
     return jax.shard_map(
         body,

time: 111 us -> 106 us (0.955)
  waiting for transfers between devices: 12.2 us -> 39.8 us
  blocking collectives: 26.5 us -> 0 us
  starting transfers between devices: 26.8 us -> 18.6 us
  Pallas kernels: 44 us -> 45.8 us
    all_to_all x4, waiting for transfers between devices: 10.2 us -> 38.6 us  [shuffle(): lax.all_to_all(shaped, group, split_axis=0, concat_axis=0, tiled=True)]
    all_gather x1 -> x0, blocking collectives: 26.5 us -> none  [body(): both_grads = lax.all_gather(grad_output, 'half')]
    ppermute x3 -> x4, starting transfers between devices: 5.66 us -> 1.09 us  [exchange(): return lax.ppermute(values, 'half', ((0, 1), (1, 0)))]
    all_to_all x4, starting transfers between devices: 21.1 us -> 17.5 us  [shuffle(): lax.all_to_all(shaped, group, split_axis=0, concat_axis=0, tiled=True)]
  transfers between devices with their start and end apart: 7 -> 8, of which waited for: 2 -> 6; matrix products, arithmetic and copies ran while one was open for 0% -> 0% of each run, Pallas kernels for 37% -> 40%
where the time goes in v14:
time: 106 us
  Pallas kernels  45.8 us (43%)
  waiting for transfers between devices  39.8 us (38%)
  starting transfers between devices  18.6 us (18%)
    all_to_all x4, waiting for transfers between devices, shuffle(): lax.all_to_all(shaped, group, split_axis=0, concat_axis=0, tiled=True)  38.6 us
    all_to_all x4, starting transfers between devices, shuffle(): lax.all_to_all(shaped, group, split_axis=0, concat_axis=0, tiled=True)  17.5 us
    pallas_call x1, Pallas kernels, body(): call(forward_kernel, [mid, mid, slots], 2 * product, traffic, 32, grid=gr...  13.4 us
    pallas_call x1, Pallas kernels, body(): call(backward_kernel, [mid, slots], 2 * product, traffic, 32, grid=grid,...  12.3 us
    pallas_call x1, Pallas kernels, body(): call(weights_kernel, [pltpu.HBM(weight_in.shape, BF16), pltpu.HBM(weight_...  10.7 us
    pallas_call x1, Pallas kernels, body(): call(place_cotangents_kernel, slots, 4 * place_flops, 2 * token_bytes + s...  2.96 us
    pallas_call x1, Pallas kernels, body(): call(functools.partial(place_tokens_kernel, rest_count.bit_length() - 1,...  2.42 us
    pallas_call x1, Pallas kernels, body(): call(pick_outputs_kernel, [tokens_f32, token_shape, gates_shape, gates_sh...  2.39 us
  transfers between devices with their start and end apart: 8, of which 6 were waited for; matrix products, arithmetic and copies ran while one was open for 0% of the time, Pallas kernels for 40%

profile of v14, /device:TPU:0, one launch (start us, length us, event | category | flops | bytes accessed | tf_op | source)
XLA Modules:
  0.0 105.9 jit_solution(2360103802422833684)
XLA Ops:
  0.6 2.4 %shard_map.110 = (f32[8,128]{1,0:T(8,128)S(1)}, f32[8,128]{1,0:T(8,128)S(1)}, bf16[512,768]{1,0:T(8,128)(2,1)}) custom-call(s32[1]{0:T(128)} %bitcast.half_ref, bf16[128,768]{1,0:T(8,128)(2,1)} %tokens_ref.1, s32[2,128]{1,0:T(2,128)} %bitcast.19, s32[2,128]{1,0:T(2,128)} %bitcast.20, f32[2,128]{1,0:T(2,128)} %bitcast.21), custom_call_target="tpu_custom_call" | custom-call | flops 100663296 | bytes 983040 | tf_op jit(solution)/shard_map/pallas_call | solution.py:248
  3.1 7.3 %all-to-all-start = ((bf16[32,16,768]{2,1,0:T(8,128)(2,1)}), bf16[32,16,768]{2,1,0:T(8,128)(2,1)S(1)}, u32[]{:S(2)}, u32[]{:S(2)}) async-start(bf16[32,16,768]{2,1,0:T(8,128)(2,1)} %bitcast.4), calls=%async_computation | async-start | bytes 1572864 | tf_op jit(solution)/shard_map/all_to_all | solution.py:233
  10.4 0.3 collective-permute-start
  10.7 0.3 collective-permute-start.1
  10.9 0.9 collective-permute-done.1.partner_meta
  11.9 0.2 collective-permute-done.partner_grad
  12.1 0.0 copy-start
  12.1 3.0 %shard_map.113 = bf16[512,768]{1,0:T(8,128)(2,1)} custom-call(bf16[128,768]{1,0:T(8,128)(2,1)} %own_grad.3, bf16[128,768]{1,0:T(8,128)(2,1)S(1)} %collective-permute-done.partner_grad, f32[8,128]{1,0:T(8,128)S(1)} %get-tuple-element.25.own_meta.meta_ref, f32[8,128]{1,0:T(8,128)S(1)} %collective-permute-done.1.partner_meta), custom_call_target="tpu_custom_call" | custom-call | flops 402653184 | bytes 1179648 | tf_op jit(solution)/shard_map/pallas_call | solution.py:263
  15.0 16.9 %all-to-all-done = bf16[32,16,768]{2,1,0:T(8,128)(2,1)S(1)} async-done(((bf16[32,16,768]{2,1,0:T(8,128)(2,1)}), bf16[32,16,768]{2,1,0:T(8,128)(2,1)S(1)}, u32[]{:S(2)}, u32[]{:S(2)}) %all-to-all-start) | async-done | bytes 786464 | tf_op jit(solution)/shard_map/all_to_all | solution.py:233
  31.9 0.0 copy-done
  31.9 3.6 %all-to-all-start.2 = ((bf16[16,32,768]{2,1,0:T(8,128)(2,1)}), bf16[16,32,768]{2,1,0:T(8,128)(2,1)S(1)}, u32[]{:S(2)}, u32[]{:S(2)}) async-start(bf16[16,32,768]{2,1,0:T(8,128)(2,1)} %bitcast.8), calls=%async_computation.2 | async-start | bytes 1572864 | tf_op jit(solution)/shard_map/all_to_all | solution.py:233
  35.5 13.4 %shard_map.111 = (bf16[512,4096]{1,0:T(8,128)(2,1)}, bf16[512,4096]{1,0:T(8,128)(2,1)}, bf16[512,768]{1,0:T(8,128)(2,1)}) custom-call(bf16[512,768]{1,0:T(8,128)(2,1)S(1)} %bitcast.14, bf16[1,768,4096]{2,1,0:T(8,128)(2,1)} %w_in_ref.3, bf16[1,4096,768]{2,1,0:T(8,128)(2,1)} %w_out_ref.3), custom_call_target="tpu_custom_call" | custom-call | flops 6442450944 | bytes 22544384 | tf_op jit(solution)/shard_map/pallas_call | solution.py:279
  48.9 7.0 %all-to-all-done.2 = bf16[16,32,768]{2,1,0:T(8,128)(2,1)S(1)} async-done(((bf16[16,32,768]{2,1,0:T(8,128)(2,1)}), bf16[16,32,768]{2,1,0:T(8,128)(2,1)S(1)}, u32[]{:S(2)}, u32[]{:S(2)}) %all-to-all-start.2) | async-done | bytes 786464 | tf_op jit(solution)/shard_map/all_to_all | solution.py:233
  55.9 3.9 %all-to-all-start.1 = ((bf16[16,32,768]{2,1,0:T(8,128)(2,1)}), bf16[16,32,768]{2,1,0:T(8,128)(2,1)S(1)}, u32[]{:S(2)}, u32[]{:S(2)}) async-start(bf16[16,32,768]{2,1,0:T(8,128)(2,1)} %bitcast.6), calls=%async_computation.1 | async-start | bytes 1572864 | tf_op jit(solution)/shard_map/all_to_all | solution.py:233
  59.7 12.3 %shard_map.114 = (bf16[512,4096]{1,0:T(8,128)(2,1)}, bf16[512,768]{1,0:T(8,128)(2,1)}) custom-call(bf16[512,768]{1,0:T(8,128)(2,1)S(1)} %bitcast.16, bf16[1,768,4096]{2,1,0:T(8,128)(2,1)} %w_in_ref.3, bf16[1,4096,768]{2,1,0:T(8,128)(2,1)} %w_out_ref.3, bf16[512,4096]{1,0:T(8,128)(2,1)} %get-tuple-element.28.slope_ref), custom_call_target="tpu_custom_call" | custom-call | flops 6442450944 | bytes 22544384 | tf_op jit(solution)/shard_map/pallas_call | solution.py:291
  72.0 7.8 %all-to-all-done.1 = bf16[16,32,768]{2,1,0:T(8,128)(2,1)S(1)} async-done(((bf16[16,32,768]{2,1,0:T(8,128)(2,1)}), bf16[16,32,768]{2,1,0:T(8,128)(2,1)S(1)}, u32[]{:S(2)}, u32[]{:S(2)}) %all-to-all-start.1) | async-done | bytes 786464 | tf_op jit(solution)/shard_map/all_to_all | solution.py:233
  79.8 2.8 %all-to-all-start.3 = ((bf16[32,16,768]{2,1,0:T(8,128)(2,1)}), bf16[32,16,768]{2,1,0:T(8,128)(2,1)S(1)}, u32[]{:S(2)}, u32[]{:S(2)}) async-start(bf16[32,16,768]{2,1,0:T(8,128)(2,1)} %bitcast.10), calls=%async_computation.3 | async-start | bytes 1572864 | tf_op jit(solution)/shard_map/all_to_all | solution.py:233
  82.6 0.0 copy-start.1
  82.6 0.9 copy-done.1
  83.5 2.4 %shard_map.112 = (f32[128,768]{1,0:T(8,128)S(1)}, bf16[128,768]{1,0:T(8,128)(2,1)}, f32[2,128]{1,0:T(2,128)S(1)}, f32[2,128]{1,0:T(2,128)S(1)}) custom-call(bf16[512,768]{1,0:T(8,128)(2,1)S(1)} %bitcast.18, bf16[128,768]{1,0:T(8,128)(2,1)} %own_grad.3, bf16[128,768]{1,0:T(8,128)(2,1)S(1)} %copy-done.1, f32[8,128]{1,0:T(8,128)S(1)} %get-tuple-element.25.own_meta.meta_ref, ...), custom_call_target="tpu_custom_call" | custom-call | flops 402653184 | bytes 1572864 | tf_op jit(solution)/shard_map/pallas_call | solution.py:304
  85.9 0.2 collective-permute-start.3
  86.2 0.3 collective-permute-start.2
  86.4 10.7 %shard_map.117 = (bf16[1,768,4096]{2,1,0:T(8,128)(2,1)}, bf16[1,4096,768]{2,1,0:T(8,128)(2,1)}) custom-call(bf16[512,768]{1,0:T(8,128)(2,1)S(1)} %bitcast.15, bf16[512,768]{1,0:T(8,128)(2,1)S(1)} %bitcast.17, bf16[512,4096]{1,0:T(8,128)(2,1)} %get-tuple-element.37.hidden_ref, bf16[512,4096]{1,0:T(8,128)(2,1)} %get-tuple-element.38.grad_pre_ref), custom_call_target="tpu_custom_call" | custom-call | flops 6442450944 | bytes 22544384 | tf_op jit(solution)/shard_map/pallas_call | solution.py:312
  97.1 7.0 %all-to-all-done.3 = bf16[32,16,768]{2,1,0:T(8,128)(2,1)S(1)} async-done(((bf16[32,16,768]{2,1,0:T(8,128)(2,1)}), bf16[32,16,768]{2,1,0:T(8,128)(2,1)S(1)}, u32[]{:S(2)}, u32[]{:S(2)}) %all-to-all-start.3) | async-done | bytes 786464 | tf_op jit(solution)/shard_map/all_to_all | solution.py:233
  104.1 1.0 shard_map.116
  105.1 0.0 collective-permute-done.3.got_gates
  105.1 0.0 collective-permute-done.2.got_out
  105.1 0.7 shard_map.115
Async XLA Ops:
  3.1 28.8 %all-to-all-start = ((bf16[32,16,768]{2,1,0:T(8,128)(2,1)}), bf16[32,16,768]{2,1,0:T(8,128)(2,1)S(1)}, u32[]{:S(2)}, u32[]{:S(2)}) async-start(bf16[32,16,768]{2,1,0:T(8,128)(2,1)} %bitcast.4), calls=%async_computation | async-start | bytes 1572864 | tf_op jit(solution)/shard_map/all_to_all | solution.py:233
  10.4 1.7 %collective-permute-start = (bf16[128,768]{1,0:T(8,128)(2,1)}, bf16[128,768]{1,0:T(8,128)(2,1)S(1)}, u32[]{:S(2)}, u32[]{:S(2)}) collective-permute-start(bf16[128,768]{1,0:T(8,128)(2,1)} %own_grad.3), channel_id=1, source_target_pairs={{0,8},{8,0},{1,9},{9,1},{2,10},{10,2},{3,11},{11,3},{4,12},{12,4},... | collective-permute-start | bytes 589832 | tf_op jit(solution)/shard_map/ppermute | solution.py:229
  10.7 1.2 %collective-permute-start.1 = (f32[8,128]{1,0:T(8,128)S(1)}, f32[8,128]{1,0:T(8,128)S(1)}, u32[]{:S(2)}, u32[]{:S(2)}) collective-permute-start(f32[8,128]{1,0:T(8,128)S(1)} %get-tuple-element.26), channel_id=1, source_target_pairs={{0,8},{8,0},{1,9},{9,1},{2,10},{10,2},{3,11},{11,3},{4,12},{12,4},... | collective-permute-start | bytes 12296 | tf_op jit(solution)/shard_map/ppermute | solution.py:229
  12.1 19.8 %copy-start = (bf16[128,768]{1,0:T(8,128)(2,1)}, bf16[128,768]{1,0:T(8,128)(2,1)S(1)}, u32[]{:S(2)}) copy-start(bf16[128,768]{1,0:T(8,128)(2,1)S(1)} %collective-permute-done.partner_grad) | copy-start | bytes 589828
  31.9 24.0 %all-to-all-start.2 = ((bf16[16,32,768]{2,1,0:T(8,128)(2,1)}), bf16[16,32,768]{2,1,0:T(8,128)(2,1)S(1)}, u32[]{:S(2)}, u32[]{:S(2)}) async-start(bf16[16,32,768]{2,1,0:T(8,128)(2,1)} %bitcast.8), calls=%async_computation.2 | async-start | bytes 1572864 | tf_op jit(solution)/shard_map/all_to_all | solution.py:233
  55.9 24.0 %all-to-all-start.1 = ((bf16[16,32,768]{2,1,0:T(8,128)(2,1)}), bf16[16,32,768]{2,1,0:T(8,128)(2,1)S(1)}, u32[]{:S(2)}, u32[]{:S(2)}) async-start(bf16[16,32,768]{2,1,0:T(8,128)(2,1)} %bitcast.6), calls=%async_computation.1 | async-start | bytes 1572864 | tf_op jit(solution)/shard_map/all_to_all | solution.py:233
  79.8 24.3 %all-to-all-start.3 = ((bf16[32,16,768]{2,1,0:T(8,128)(2,1)}), bf16[32,16,768]{2,1,0:T(8,128)(2,1)S(1)}, u32[]{:S(2)}, u32[]{:S(2)}) async-start(bf16[32,16,768]{2,1,0:T(8,128)(2,1)} %bitcast.10), calls=%async_computation.3 | async-start | bytes 1572864 | tf_op jit(solution)/shard_map/all_to_all | solution.py:233
  82.6 0.9 copy-start.1
  85.9 19.2 %collective-permute-start.3 = (f32[2,128]{1,0:T(2,128)S(1)}, f32[2,128]{1,0:T(2,128)S(1)}, u32[]{:S(2)}, u32[]{:S(2)}) collective-permute-start(f32[2,128]{1,0:T(2,128)S(1)} %get-tuple-element.33), channel_id=1, source_target_pairs={{0,8},{8,0},{1,9},{9,1},{2,10},{10,2},{3,11},{11,3},{4,12},{12,4},... | collective-permute-start | bytes 3080 | tf_op jit(solution)/shard_map/ppermute | solution.py:229
  86.2 19.0 %collective-permute-start.2 = (bf16[128,768]{1,0:T(8,128)(2,1)}, bf16[128,768]{1,0:T(8,128)(2,1)S(1)}, u32[]{:S(2)}, u32[]{:S(2)}) collective-permute-start(bf16[128,768]{1,0:T(8,128)(2,1)} %get-tuple-element.31), channel_id=1, source_target_pairs={{0,8},{8,0},{1,9},{9,1},{2,10},{10,2},{3,11},{11,3},{4,12},{12,4},... | collective-permute-start | bytes 589832 | tf_op jit(solution)/shard_map/ppermute | solution.py:229

commit v15 on v14

--- a/solution.py
+++ b/solution.py
@@ -13,9 +13,9 @@
 F32 = jnp.float32
 MIB = 1024 * 1024
 SUB = 256
-AXES = ("row", "half", "rest")
-ALL = ("row", "rest", "half")
-GROUP = ("row", "rest")
+AXES = ("row", "half", "outer", "inner")
+ALL = ("row", "inner", "outer", "half")
+GROUP = ("row", "inner", "outer")
 
 
 def dot(a, b, contract_a, contract_b):
@@ -44,7 +44,10 @@
         expert = ids_ref[k : k + 1, :]
         kept = keep_ref[k : k + 1, :] > 0
         side = (expert >> rest_bits) & 1
-        local = ((expert >> (rest_bits + 1)) << rest_bits) + (expert & ((1 << rest_bits) - 1))
+        inner_at = expert & 1
+        outer_at = (expert >> 1) & ((1 << (rest_bits - 1)) - 1)
+        row_at = expert >> (rest_bits + 1)
+        local = (((row_at << 1) + inner_at) << (rest_bits - 1)) + outer_at
         base = local * (2 * capacity) + slot
         row = base + half * capacity
         mine_ref[k : k + 1, :] = jnp.where(kept & (side == half), row, -1).astype(F32)
@@ -220,7 +223,7 @@
 def body(tokens, expert_ids, keep_mask, gate_weights, weight_in, weight_out, grad_output):
     token_rows, width = tokens.shape
     hidden_width = weight_in.shape[2]
-    rest_count = lax.axis_size("rest")
+    rest_count = lax.axis_size("outer") * lax.axis_size("inner")
     members = lax.axis_size("row") * rest_count
     capacity = expert_ids.shape[1] * token_rows // members
     slot_total = 2 * members * capacity
@@ -307,8 +310,11 @@
         4 * place_flops,
         4 * token_bytes + slot_bytes,
     )(back_out, in_hbm(grad_output), partner_grad, own_meta, partner_meta)
-    grad_pre, partner_out = lax.optimization_barrier((grad_pre, partner_out))
     got_out, got_gates = exchange(partner_out), exchange(partner_gates)
+    combined, grad_gates = call(
+        finish_outputs_kernel, [token_shape, gates_shape], 0, 6 * token_bytes
+    )(own_out, got_out, own_gates, got_gates)
+    grad_pre, grad_gates = lax.optimization_barrier((grad_pre, grad_gates))
     grad_in_w, grad_out_w = call(
         weights_kernel,
         [pltpu.HBM(weight_in.shape, BF16), pltpu.HBM(weight_out.shape, BF16)],
@@ -319,9 +325,6 @@
         in_specs=[whole, whole, mid_spec, mid_spec],
         out_specs=[in_spec, out_spec],
     )(x, cot, in_hbm(hidden), in_hbm(grad_pre))
-    combined, grad_gates = call(
-        finish_outputs_kernel, [token_shape, gates_shape], 0, 6 * token_bytes
-    )(own_out, got_out, own_gates, got_gates)
     grad_tokens = call(
         pick_gradients_kernel, token_shape, place_flops, slot_bytes + token_bytes
     )(back_grad, own_meta)
@@ -330,7 +333,7 @@
 
 def solution(mesh):
     rows, cols = mesh.devices.shape
-    halves = Mesh(mesh.devices.reshape(rows // 2, 2, cols), AXES)
+    halves = Mesh(mesh.devices.reshape(rows // 2, 2, cols // 2, 2), AXES)
     flat, deep = P(AXES, None), P(AXES, None, None)
     return jax.shard_map(
         body,

time: 106 us -> 120 us (1.13)
  waiting for transfers between devices: 39.8 us -> 55 us
    all_to_all x4, waiting for transfers between devices: 38.6 us -> 52.9 us  [shuffle(): lax.all_to_all(shaped, group, split_axis=0, concat_axis=0, tiled=True)]
  transfers between devices with their start and end apart: 8 -> 8, of which waited for: 6 -> 7; matrix products, arithmetic and copies ran while one was open for 0% -> 0% of each run, Pallas kernels for 40% -> 26%
where the time goes in v15:
time: 120 us; the launch traced here: 119 us
  waiting for transfers between devices  55 us (46%)
  Pallas kernels  45.1 us (38%)
  starting transfers between devices  18.3 us (15%)
    all_to_all x4, waiting for transfers between devices, shuffle(): lax.all_to_all(shaped, group, split_axis=0, concat_axis=0, tiled=True)  52.9 us
    all_to_all x4, starting transfers between devices, shuffle(): lax.all_to_all(shaped, group, split_axis=0, concat_axis=0, tiled=True)  17.1 us
    pallas_call x1, Pallas kernels, body(): call(forward_kernel, [mid, mid, slots], 2 * product, traffic, 32, grid=gr...  13.4 us
    pallas_call x1, Pallas kernels, body(): call(backward_kernel, [mid, slots], 2 * product, traffic, 32, grid=grid,...  12.3 us
    pallas_call x1, Pallas kernels, body(): call(weights_kernel, [pltpu.HBM(weight_in.shape, BF16), pltpu.HBM(weight_...  10.7 us
    pallas_call x1, Pallas kernels, body(): call(place_cotangents_kernel, slots, 4 * place_flops, 2 * token_bytes + s...  2.88 us
    pallas_call x1, Pallas kernels, body(): call(functools.partial(place_tokens_kernel, rest_count.bit_length() - 1,...  2.42 us
  transfers between devices with their start and end apart: 8, of which 7 were waited for; matrix products, arithmetic and copies ran while one was open for 0% of the time, Pallas kernels for 26%

profile of v15, /device:TPU:0, one launch (start us, length us, event | category | flops | bytes accessed | tf_op | source)
XLA Modules:
  0.0 119.0 jit_solution(6233185671385254371)
XLA Ops:
  0.6 2.4 %shard_map.110 = (f32[8,128]{1,0:T(8,128)S(1)}, f32[8,128]{1,0:T(8,128)S(1)}, bf16[512,768]{1,0:T(8,128)(2,1)}) custom-call(s32[1]{0:T(128)} %bitcast.half_ref, bf16[128,768]{1,0:T(8,128)(2,1)} %tokens_ref.1, s32[2,128]{1,0:T(2,128)} %bitcast.19, s32[2,128]{1,0:T(2,128)} %bitcast.20, f32[2,128]{1,0:T(2,128)} %bitcast.21), custom_call_target="tpu_custom_call" | custom-call | flops 100663296 | bytes 983040 | tf_op jit(solution)/shard_map/pallas_call | solution.py:251
  3.1 7.3 %all-to-all-start = ((bf16[32,16,768]{2,1,0:T(8,128)(2,1)}), bf16[32,16,768]{2,1,0:T(8,128)(2,1)S(1)}, u32[]{:S(2)}, u32[]{:S(2)}) async-start(bf16[32,16,768]{2,1,0:T(8,128)(2,1)} %bitcast.4), calls=%async_computation | async-start | bytes 1572864 | tf_op jit(solution)/shard_map/all_to_all | solution.py:236
  10.4 0.3 collective-permute-start
  10.7 0.3 collective-permute-start.1
  10.9 0.9 collective-permute-done.1.partner_meta
  11.9 0.2 collective-permute-done.partner_grad
  12.1 2.9 %shard_map.114 = bf16[512,768]{1,0:T(8,128)(2,1)} custom-call(bf16[128,768]{1,0:T(8,128)(2,1)} %own_grad.3, bf16[128,768]{1,0:T(8,128)(2,1)S(1)} %collective-permute-done.partner_grad, f32[8,128]{1,0:T(8,128)S(1)} %get-tuple-element.25.own_meta.meta_ref, f32[8,128]{1,0:T(8,128)S(1)} %collective-permute-done.1.partner_meta), custom_call_target="tpu_custom_call" | custom-call | flops 402653184 | bytes 1179648 | tf_op jit(solution)/shard_map/pallas_call | solution.py:266
  15.0 17.4 %all-to-all-done = bf16[32,16,768]{2,1,0:T(8,128)(2,1)S(1)} async-done(((bf16[32,16,768]{2,1,0:T(8,128)(2,1)}), bf16[32,16,768]{2,1,0:T(8,128)(2,1)S(1)}, u32[]{:S(2)}, u32[]{:S(2)}) %all-to-all-start) | async-done | bytes 786464 | tf_op jit(solution)/shard_map/all_to_all | solution.py:236
  32.3 3.6 %all-to-all-start.2 = ((bf16[16,32,768]{2,1,0:T(8,128)(2,1)}), bf16[16,32,768]{2,1,0:T(8,128)(2,1)S(1)}, u32[]{:S(2)}, u32[]{:S(2)}) async-start(bf16[16,32,768]{2,1,0:T(8,128)(2,1)} %bitcast.8), calls=%async_computation.2 | async-start | bytes 1572864 | tf_op jit(solution)/shard_map/all_to_all | solution.py:236
  35.9 13.4 %shard_map.111 = (bf16[512,4096]{1,0:T(8,128)(2,1)}, bf16[512,4096]{1,0:T(8,128)(2,1)}, bf16[512,768]{1,0:T(8,128)(2,1)}) custom-call(bf16[512,768]{1,0:T(8,128)(2,1)S(1)} %bitcast.14, bf16[1,768,4096]{2,1,0:T(8,128)(2,1)} %w_in_ref.3, bf16[1,4096,768]{2,1,0:T(8,128)(2,1)} %w_out_ref.3), custom_call_target="tpu_custom_call" | custom-call | flops 6442450944 | bytes 22544384 | tf_op jit(solution)/shard_map/pallas_call | solution.py:282
  49.3 8.6 %all-to-all-done.2 = bf16[16,32,768]{2,1,0:T(8,128)(2,1)S(1)} async-done(((bf16[16,32,768]{2,1,0:T(8,128)(2,1)}), bf16[16,32,768]{2,1,0:T(8,128)(2,1)S(1)}, u32[]{:S(2)}, u32[]{:S(2)}) %all-to-all-start.2) | async-done | bytes 786464 | tf_op jit(solution)/shard_map/all_to_all | solution.py:236
  57.9 3.6 %all-to-all-start.1 = ((bf16[16,32,768]{2,1,0:T(8,128)(2,1)}), bf16[16,32,768]{2,1,0:T(8,128)(2,1)S(1)}, u32[]{:S(2)}, u32[]{:S(2)}) async-start(bf16[16,32,768]{2,1,0:T(8,128)(2,1)} %bitcast.6), calls=%async_computation.1 | async-start | bytes 1572864 | tf_op jit(solution)/shard_map/all_to_all | solution.py:236
  61.5 12.3 %shard_map.115 = (bf16[512,4096]{1,0:T(8,128)(2,1)}, bf16[512,768]{1,0:T(8,128)(2,1)}) custom-call(bf16[512,768]{1,0:T(8,128)(2,1)S(1)} %bitcast.16, bf16[1,768,4096]{2,1,0:T(8,128)(2,1)} %w_in_ref.3, bf16[1,4096,768]{2,1,0:T(8,128)(2,1)} %w_out_ref.3, bf16[512,4096]{1,0:T(8,128)(2,1)} %get-tuple-element.32.slope_ref), custom_call_target="tpu_custom_call" | custom-call | flops 6442450944 | bytes 22544384 | tf_op jit(solution)/shard_map/pallas_call | solution.py:294
  73.8 8.9 %all-to-all-done.1 = bf16[16,32,768]{2,1,0:T(8,128)(2,1)S(1)} async-done(((bf16[16,32,768]{2,1,0:T(8,128)(2,1)}), bf16[16,32,768]{2,1,0:T(8,128)(2,1)S(1)}, u32[]{:S(2)}, u32[]{:S(2)}) %all-to-all-start.1) | async-done | bytes 786464 | tf_op jit(solution)/shard_map/all_to_all | solution.py:236
  82.7 2.6 %all-to-all-start.3 = ((bf16[32,16,768]{2,1,0:T(8,128)(2,1)}), bf16[32,16,768]{2,1,0:T(8,128)(2,1)S(1)}, u32[]{:S(2)}, u32[]{:S(2)}) async-start(bf16[32,16,768]{2,1,0:T(8,128)(2,1)} %bitcast.10), calls=%async_computation.3 | async-start | bytes 1572864 | tf_op jit(solution)/shard_map/all_to_all | solution.py:236
  85.3 1.7 %shard_map.112 = (f32[128,768]{1,0:T(8,128)S(1)}, bf16[128,768]{1,0:T(8,128)(2,1)S(1)}, f32[2,128]{1,0:T(2,128)S(1)}, f32[2,128]{1,0:T(2,128)S(1)}) custom-call(bf16[512,768]{1,0:T(8,128)(2,1)S(1)} %bitcast.18, bf16[128,768]{1,0:T(8,128)(2,1)} %own_grad.3, bf16[128,768]{1,0:T(8,128)(2,1)S(1)} %collective-permute-done.partner_grad, ...), custom_call_target="tpu_custom_call" | custom-call | flops 402653184 | bytes 1572864 | tf_op jit(solution)/shard_map/pallas_call | solution.py:307
  87.0 0.2 collective-permute-start.2
  87.2 0.4 collective-permute-start.3
  87.6 0.9 collective-permute-done.3.got_gates
  88.6 0.0 collective-permute-done.2.got_out
  88.6 0.7 shard_map.113
  89.3 18.0 %all-to-all-done.3 = bf16[32,16,768]{2,1,0:T(8,128)(2,1)S(1)} async-done(((bf16[32,16,768]{2,1,0:T(8,128)(2,1)}), bf16[32,16,768]{2,1,0:T(8,128)(2,1)S(1)}, u32[]{:S(2)}, u32[]{:S(2)}) %all-to-all-start.3) | async-done | bytes 786464 | tf_op jit(solution)/shard_map/all_to_all | solution.py:236
  107.3 1.0 shard_map.116
  108.3 10.7 %shard_map.117 = (bf16[1,768,4096]{2,1,0:T(8,128)(2,1)}, bf16[1,4096,768]{2,1,0:T(8,128)(2,1)}) custom-call(bf16[512,768]{1,0:T(8,128)(2,1)S(1)} %bitcast.15, bf16[512,768]{1,0:T(8,128)(2,1)S(1)} %bitcast.17, bf16[512,4096]{1,0:T(8,128)(2,1)} %get-tuple-element.37.hidden_ref, bf16[512,4096]{1,0:T(8,128)(2,1)} %get-tuple-element.38.grad_pre_ref), custom_call_target="tpu_custom_call" | custom-call | flops 6442450944 | bytes 22544384 | tf_op jit(solution)/shard_map/pallas_call | solution.py:318
Async XLA Ops:
  3.1 29.3 %all-to-all-start = ((bf16[32,16,768]{2,1,0:T(8,128)(2,1)}), bf16[32,16,768]{2,1,0:T(8,128)(2,1)S(1)}, u32[]{:S(2)}, u32[]{:S(2)}) async-start(bf16[32,16,768]{2,1,0:T(8,128)(2,1)} %bitcast.4), calls=%async_computation | async-start | bytes 1572864 | tf_op jit(solution)/shard_map/all_to_all | solution.py:236
  10.4 1.7 %collective-permute-start = (bf16[128,768]{1,0:T(8,128)(2,1)}, bf16[128,768]{1,0:T(8,128)(2,1)S(1)}, u32[]{:S(2)}, u32[]{:S(2)}) collective-permute-start(bf16[128,768]{1,0:T(8,128)(2,1)} %own_grad.3), channel_id=1, source_target_pairs={{0,8},{8,0},{1,9},{9,1},{2,10},{10,2},{3,11},{11,3},{4,12},{12,4},... | collective-permute-start | bytes 589832 | tf_op jit(solution)/shard_map/ppermute | solution.py:232
  10.7 1.2 %collective-permute-start.1 = (f32[8,128]{1,0:T(8,128)S(1)}, f32[8,128]{1,0:T(8,128)S(1)}, u32[]{:S(2)}, u32[]{:S(2)}) collective-permute-start(f32[8,128]{1,0:T(8,128)S(1)} %get-tuple-element.26), channel_id=1, source_target_pairs={{0,8},{8,0},{1,9},{9,1},{2,10},{10,2},{3,11},{11,3},{4,12},{12,4},... | collective-permute-start | bytes 12296 | tf_op jit(solution)/shard_map/ppermute | solution.py:232
  32.3 25.5 %all-to-all-start.2 = ((bf16[16,32,768]{2,1,0:T(8,128)(2,1)}), bf16[16,32,768]{2,1,0:T(8,128)(2,1)S(1)}, u32[]{:S(2)}, u32[]{:S(2)}) async-start(bf16[16,32,768]{2,1,0:T(8,128)(2,1)} %bitcast.8), calls=%async_computation.2 | async-start | bytes 1572864 | tf_op jit(solution)/shard_map/all_to_all | solution.py:236
  57.9 24.8 %all-to-all-start.1 = ((bf16[16,32,768]{2,1,0:T(8,128)(2,1)}), bf16[16,32,768]{2,1,0:T(8,128)(2,1)S(1)}, u32[]{:S(2)}, u32[]{:S(2)}) async-start(bf16[16,32,768]{2,1,0:T(8,128)(2,1)} %bitcast.6), calls=%async_computation.1 | async-start | bytes 1572864 | tf_op jit(solution)/shard_map/all_to_all | solution.py:236
  82.7 24.6 %all-to-all-start.3 = ((bf16[32,16,768]{2,1,0:T(8,128)(2,1)}), bf16[32,16,768]{2,1,0:T(8,128)(2,1)S(1)}, u32[]{:S(2)}, u32[]{:S(2)}) async-start(bf16[32,16,768]{2,1,0:T(8,128)(2,1)} %bitcast.10), calls=%async_computation.3 | async-start | bytes 1572864 | tf_op jit(solution)/shard_map/all_to_all | solution.py:236
  87.0 1.5 %collective-permute-start.2 = (bf16[128,768]{1,0:T(8,128)(2,1)S(1)}, bf16[128,768]{1,0:T(8,128)(2,1)S(1)}, u32[]{:S(2)}, u32[]{:S(2)}) collective-permute-start(bf16[128,768]{1,0:T(8,128)(2,1)S(1)} %get-tuple-element.28), channel_id=1, source_target_pairs={{0,8},{8,0},{1,9},{9,1},{2,10},{10,2},{3,11},{11,3},{4,12},{12,4},... | collective-permute-start | bytes 589832 | tf_op jit(solution)/shard_map/ppermute | solution.py:232
  87.2 1.3 %collective-permute-start.3 = (f32[2,128]{1,0:T(2,128)S(1)}, f32[2,128]{1,0:T(2,128)S(1)}, u32[]{:S(2)}, u32[]{:S(2)}) collective-permute-start(f32[2,128]{1,0:T(2,128)S(1)} %get-tuple-element.30), channel_id=1, source_target_pairs={{0,8},{8,0},{1,9},{9,1},{2,10},{10,2},{3,11},{11,3},{4,12},{12,4},... | collective-permute-start | bytes 3080 | tf_op jit(solution)/shard_map/ppermute | solution.py:232

commit v16 on v7

--- a/solution.py
+++ b/solution.py
@@ -66,11 +66,22 @@
     return jnp.concatenate(pieces, axis=1)
 
 
-def place_tokens_kernel(capacity, place_of, tokens_ref, ids_ref, keep_ref, gates_ref, meta_ref, out_ref):
-    route(ids_ref, keep_ref, gates_ref, meta_ref, capacity, place_of)
-    slot_total = out_ref.shape[0]
-    mask = hits(slot_total, meta_ref, 0) | hits(slot_total, meta_ref, 1)
-    out_ref[...] = dot(one_hot(mask), restore(tokens_ref), 1, 0).astype(BF16)
+def place_tokens_kernel(
+    capacity, place_of, tokens_ref, ids_ref, keep_ref, gates_ref, meta_ref, out_ref, restored
+):
+    step = pl.program_id(0)
+
+    @pl.when(step == 0)
+    def _():
+        route(ids_ref, keep_ref, gates_ref, meta_ref, capacity, place_of)
+        restored[...] = restore(tokens_ref)
+
+    rows, token_rows = out_ref.shape[0], meta_ref.shape[1]
+    index = lax.broadcasted_iota(jnp.int32, (rows, token_rows), 0) + step * rows
+    mask = (index == meta_ref[0:1, :].astype(jnp.int32)) | (
+        index == meta_ref[1:2, :].astype(jnp.int32)
+    )
+    out_ref[...] = dot(one_hot(mask), restored[...], 1, 0).astype(BF16)
 
 
 def scaled_rows(gate_row, grad_ref):
@@ -228,6 +239,14 @@
         [jax.ShapeDtypeStruct((8, token_rows), F32), slots],
         place_flops,
         token_bytes + slot_bytes,
+        grid=(2,),
+        in_specs=[pl.BlockSpec((token_rows, width), lambda i: (0, 0))]
+        + [pl.BlockSpec((2, token_rows), lambda i: (0, 0))] * 3,
+        out_specs=[
+            pl.BlockSpec((8, token_rows), lambda i: (0, 0)),
+            pl.BlockSpec((slot_total // 2, width), lambda i: (i, 0)),
+        ],
+        scratch_shapes=[pltpu.VMEM((token_rows, width), BF16)],
     )(in_hbm(tokens), in_hbm(expert_ids.T), in_hbm(keep_mask.T), in_hbm(gate_weights.T))
     x = shuffle(sent)
     sent_cot = call(

time: 105 us -> 105 us (level)
  no operation moved by 1% of the time
where the time goes in v16:
time: 105 us; the launch traced here: 104 us
  Pallas kernels  44.2 us (42%)
  waiting for transfers between devices  43.4 us (41%)
  starting transfers between devices  15.2 us (14%)
    all_to_all x4, waiting for transfers between devices, shuffle(): lax.all_to_all(shaped, GROUP, split_axis=0, concat_axis=0, tiled=True)  43.4 us
    all_to_all x4, starting transfers between devices, shuffle(): lax.all_to_all(shaped, GROUP, split_axis=0, concat_axis=0, tiled=True)  15.2 us
    pallas_call x1, Pallas kernels, body(): call(forward_kernel, [mid, mid, slots], 2 * product, traffic, 32, grid=gr...  13.4 us
    pallas_call x1, Pallas kernels, body(): call(backward_kernel, [mid, slots], 2 * product, traffic, 32, grid=grid,...  12 us
    pallas_call x1, Pallas kernels, body(): call(weights_kernel, [pltpu.HBM(weight_in.shape, BF16), pltpu.HBM(weight_...  10.7 us
    pallas_call x1, Pallas kernels, body(): call(functools.partial(place_tokens_kernel, capacity, place_of), [jax.Sha...  2.51 us
    pallas_call x1, Pallas kernels, body(): call(place_cotangents_kernel, slots, 2 * place_flops, token_bytes + slot_...  2.46 us
  transfers between devices with their start and end apart: 4, of which 4 were waited for; matrix products, arithmetic and copies ran while one was open for 0% of the time, Pallas kernels for 39%

profile of v16, /device:TPU:0, one launch (start us, length us, event | category | flops | bytes accessed | tf_op | source)
XLA Modules:
  0.0 104.3 jit_solution(8877946974296276244)
XLA Ops:
  0.6 2.5 %shard_map.110 = (f32[8,128]{1,0:T(8,128)S(1)}, bf16[512,768]{1,0:T(8,128)(2,1)}) custom-call(bf16[128,768]{1,0:T(8,128)(2,1)} %tokens_ref.1, s32[2,128]{1,0:T(2,128)} %bitcast.19, s32[2,128]{1,0:T(2,128)} %bitcast.20, f32[2,128]{1,0:T(2,128)} %bitcast.21), custom_call_target="tpu_custom_call" | custom-call | flops 100663296 | bytes 983040 | tf_op jit(solution)/shard_map/pallas_call | solution.py:237
  3.1 7.3 %all-to-all-start = ((bf16[32,16,768]{2,1,0:T(8,128)(2,1)}), bf16[32,16,768]{2,1,0:T(8,128)(2,1)S(1)}, u32[]{:S(2)}, u32[]{:S(2)}) async-start(bf16[32,16,768]{2,1,0:T(8,128)(2,1)} %bitcast.3), calls=%async_computation | async-start | bytes 1572864 | tf_op jit(solution)/shard_map/all_to_all | solution.py:229
  10.4 2.5 %shard_map.113 = bf16[512,768]{1,0:T(8,128)(2,1)} custom-call(bf16[128,768]{1,0:T(8,128)(2,1)} %grad_ref.3, f32[8,128]{1,0:T(8,128)S(1)} %get-tuple-element.18.meta_ref), custom_call_target="tpu_custom_call" | custom-call | flops 201326592 | bytes 983040 | tf_op jit(solution)/shard_map/pallas_call | solution.py:252
  12.9 18.8 %all-to-all-done = bf16[32,16,768]{2,1,0:T(8,128)(2,1)S(1)} async-done(((bf16[32,16,768]{2,1,0:T(8,128)(2,1)}), bf16[32,16,768]{2,1,0:T(8,128)(2,1)S(1)}, u32[]{:S(2)}, u32[]{:S(2)}) %all-to-all-start) | async-done | bytes 786464 | tf_op jit(solution)/shard_map/all_to_all | solution.py:229
  31.7 2.6 %all-to-all-start.2 = ((bf16[32,16,768]{2,1,0:T(8,128)(2,1)}), bf16[32,16,768]{2,1,0:T(8,128)(2,1)S(1)}, u32[]{:S(2)}, u32[]{:S(2)}) async-start(bf16[32,16,768]{2,1,0:T(8,128)(2,1)} %bitcast.7), calls=%async_computation.2 | async-start | bytes 1572864 | tf_op jit(solution)/shard_map/all_to_all | solution.py:229
  34.3 13.4 %shard_map.111 = (bf16[512,4096]{1,0:T(8,128)(2,1)}, bf16[512,4096]{1,0:T(8,128)(2,1)}, bf16[512,768]{1,0:T(8,128)(2,1)}) custom-call(bf16[512,768]{1,0:T(8,128)(2,1)S(1)} %bitcast.14, bf16[1,768,4096]{2,1,0:T(8,128)(2,1)} %w_in_ref.3, bf16[1,4096,768]{2,1,0:T(8,128)(2,1)} %w_out_ref.3), custom_call_target="tpu_custom_call" | custom-call | flops 6442450944 | bytes 22544384 | tf_op jit(solution)/shard_map/pallas_call | solution.py:268
  47.7 7.9 %all-to-all-done.2 = bf16[32,16,768]{2,1,0:T(8,128)(2,1)S(1)} async-done(((bf16[32,16,768]{2,1,0:T(8,128)(2,1)}), bf16[32,16,768]{2,1,0:T(8,128)(2,1)S(1)}, u32[]{:S(2)}, u32[]{:S(2)}) %all-to-all-start.2) | async-done | bytes 786464 | tf_op jit(solution)/shard_map/all_to_all | solution.py:229
  55.6 2.6 %all-to-all-start.1 = ((bf16[32,16,768]{2,1,0:T(8,128)(2,1)}), bf16[32,16,768]{2,1,0:T(8,128)(2,1)S(1)}, u32[]{:S(2)}, u32[]{:S(2)}) async-start(bf16[32,16,768]{2,1,0:T(8,128)(2,1)} %bitcast.5), calls=%async_computation.1 | async-start | bytes 1572864 | tf_op jit(solution)/shard_map/all_to_all | solution.py:229
  58.2 12.0 %shard_map.114 = (bf16[512,4096]{1,0:T(8,128)(2,1)}, bf16[512,768]{1,0:T(8,128)(2,1)S(1)}) custom-call(bf16[512,768]{1,0:T(8,128)(2,1)S(1)} %bitcast.16, bf16[1,768,4096]{2,1,0:T(8,128)(2,1)} %w_in_ref.3, bf16[1,4096,768]{2,1,0:T(8,128)(2,1)} %w_out_ref.3, bf16[512,4096]{1,0:T(8,128)(2,1)} %get-tuple-element.20.slope_ref), custom_call_target="tpu_custom_call" | custom-call | flops 6442450944 | bytes 22544384 | tf_op jit(solution)/shard_map/pallas_call | solution.py:280
  70.2 0.0 copy-start
  70.2 1.0 copy-done
  71.2 8.3 %all-to-all-done.1 = bf16[32,16,768]{2,1,0:T(8,128)(2,1)S(1)} async-done(((bf16[32,16,768]{2,1,0:T(8,128)(2,1)}), bf16[32,16,768]{2,1,0:T(8,128)(2,1)S(1)}, u32[]{:S(2)}, u32[]{:S(2)}) %all-to-all-start.1) | async-done | bytes 786464 | tf_op jit(solution)/shard_map/all_to_all | solution.py:229
  79.5 2.6 %all-to-all-start.3 = ((bf16[32,16,768]{2,1,0:T(8,128)(2,1)}), bf16[32,16,768]{2,1,0:T(8,128)(2,1)S(1)}, u32[]{:S(2)}, u32[]{:S(2)}) async-start(bf16[32,16,768]{2,1,0:T(8,128)(2,1)} %bitcast.18), calls=%async_computation.3 | async-start | bytes 1572864 | tf_op jit(solution)/shard_map/all_to_all | solution.py:229
  82.1 10.7 %shard_map.116 = (bf16[1,768,4096]{2,1,0:T(8,128)(2,1)}, bf16[1,4096,768]{2,1,0:T(8,128)(2,1)}) custom-call(bf16[512,768]{1,0:T(8,128)(2,1)S(1)} %bitcast.15, bf16[512,768]{1,0:T(8,128)(2,1)S(1)} %bitcast.17, bf16[512,4096]{1,0:T(8,128)(2,1)} %get-tuple-element.23.hidden_ref, bf16[512,4096]{1,0:T(8,128)(2,1)} %get-tuple-element.24.grad_pre_ref), custom_call_target="tpu_custom_call" | custom-call | flops 6442450944 | bytes 22544384 | tf_op jit(solution)/shard_map/pallas_call | solution.py:301
  92.8 2.1 %shard_map.112 = (bf16[128,768]{1,0:T(8,128)(2,1)}, f32[2,128]{1,0:T(2,128)}) custom-call(bf16[512,768]{1,0:T(8,128)(2,1)S(1)} %bitcast.12, bf16[128,768]{1,0:T(8,128)(2,1)} %grad_ref.3, f32[8,128]{1,0:T(8,128)S(1)} %get-tuple-element.18.meta_ref), custom_call_target="tpu_custom_call" | custom-call | flops 201326592 | bytes 1179648 | tf_op jit(solution)/shard_map/pallas_call | solution.py:292
  94.9 8.4 %all-to-all-done.3 = bf16[32,16,768]{2,1,0:T(8,128)(2,1)S(1)} async-done(((bf16[32,16,768]{2,1,0:T(8,128)(2,1)}), bf16[32,16,768]{2,1,0:T(8,128)(2,1)S(1)}, u32[]{:S(2)}, u32[]{:S(2)}) %all-to-all-start.3) | async-done | bytes 786464 | tf_op jit(solution)/shard_map/all_to_all | solution.py:229
  103.3 1.0 shard_map.115
Async XLA Ops:
  3.1 28.6 %all-to-all-start = ((bf16[32,16,768]{2,1,0:T(8,128)(2,1)}), bf16[32,16,768]{2,1,0:T(8,128)(2,1)S(1)}, u32[]{:S(2)}, u32[]{:S(2)}) async-start(bf16[32,16,768]{2,1,0:T(8,128)(2,1)} %bitcast.3), calls=%async_computation | async-start | bytes 1572864 | tf_op jit(solution)/shard_map/all_to_all | solution.py:229
  31.7 23.9 %all-to-all-start.2 = ((bf16[32,16,768]{2,1,0:T(8,128)(2,1)}), bf16[32,16,768]{2,1,0:T(8,128)(2,1)S(1)}, u32[]{:S(2)}, u32[]{:S(2)}) async-start(bf16[32,16,768]{2,1,0:T(8,128)(2,1)} %bitcast.7), calls=%async_computation.2 | async-start | bytes 1572864 | tf_op jit(solution)/shard_map/all_to_all | solution.py:229
  55.6 23.9 %all-to-all-start.1 = ((bf16[32,16,768]{2,1,0:T(8,128)(2,1)}), bf16[32,16,768]{2,1,0:T(8,128)(2,1)S(1)}, u32[]{:S(2)}, u32[]{:S(2)}) async-start(bf16[32,16,768]{2,1,0:T(8,128)(2,1)} %bitcast.5), calls=%async_computation.1 | async-start | bytes 1572864 | tf_op jit(solution)/shard_map/all_to_all | solution.py:229
  70.2 1.0 copy-start
  79.5 23.9 %all-to-all-start.3 = ((bf16[32,16,768]{2,1,0:T(8,128)(2,1)}), bf16[32,16,768]{2,1,0:T(8,128)(2,1)S(1)}, u32[]{:S(2)}, u32[]{:S(2)}) async-start(bf16[32,16,768]{2,1,0:T(8,128)(2,1)} %bitcast.18), calls=%async_computation.3 | async-start | bytes 1572864 | tf_op jit(solution)/shard_map/all_to_all | solution.py:229
